TPU v7x, 768 devices: a whole 4x8x12 slice. The times are simulated.
768 devices in a mesh: dp: 24 (over z, core), group: 32 (over x, y).
Axes of the slice: x: 4, y: 8, z: 12, core: 2. Of those that a mesh axis runs over, the one named last changes fastest.
Arguments:
- query_layer_input: bfloat16 [49152, 4096], P(('dp', 'group')), may hold values from -6 to 6
- query_frozen_base: bfloat16 [49152, 4096], P(('dp', 'group')), may hold values from -6 to 6
- passage_layer_input: bfloat16 [49152, 4096], P(('dp', 'group')), may hold values from -6 to 6
- passage_frozen_base: bfloat16 [49152, 4096], P(('dp', 'group')), may hold values from -6 to 6
- adapter_down_weight: bfloat16 [4096, 64], replicated, may hold values from -0.09375 to 0.09375
- adapter_up_weight: bfloat16 [64, 4096], replicated, may hold values from -0.75 to 0.75
- positive_passage_index: int32 [49152], P(('dp', 'group')), may hold values from 0 to 63
- hard_negative_slots: int32 [49152, 32], P(('dp', 'group')), may hold values from 0 to 255
- group_peer_rows: int32 [18432, 8], P(('dp', 'group')), may hold values from 0 to 63
- remote_group_rows: int32 [24576, 2], P(('dp', 'group')), may hold values from 0 to 63
Outputs:
- lora_down_grad: float32 [4096, 64], replicated
- lora_up_grad: float32 [64, 4096], replicated
- loss: float32 [], replicated
All inputs are finite; a program needn't handle non-finite values.
Results may differ from a plain program's by a relative error of at most 0.008.
Values may be sent and summed in bfloat16 or wider, within the bound.
No kernel may reach another device: no remote copies, remote signals or barrier semaphores. Data moves between devices by JAX's collectives and lax.ppermute only.
A program may use at most 32 MiB of HBM per device.

v0:
```python
import math

import jax
import jax.numpy as jnp
from jax import lax
from jax.sharding import PartitionSpec as P

adapter_scale = 2.0
logit_divisor = 0.05
epsilon = 1e-06


def embedding_rows(hidden_state, frozen_output, adapter_down_weight, adapter_up_weight):
    adapter_latent = jnp.dot(
        hidden_state, adapter_down_weight, preferred_element_type=jnp.float32
    ).astype(jnp.bfloat16)
    unnormalized_rows = frozen_output.astype(jnp.float32) + adapter_scale * jnp.dot(
        adapter_latent, adapter_up_weight, preferred_element_type=jnp.float32
    )
    inverse = lax.rsqrt(
        jnp.sum(unnormalized_rows * unnormalized_rows, axis=-1, keepdims=True) + epsilon
    )
    unit_rows = (unnormalized_rows * inverse).astype(jnp.bfloat16)
    scaled = (adapter_latent.astype(jnp.float32) * inverse).astype(jnp.bfloat16)
    return (unit_rows, scaled, inverse)


def tangent_of(grad_rows, unit_rows):
    unit_f = unit_rows.astype(jnp.float32)
    radial = jnp.sum(unit_f * grad_rows, axis=-1, keepdims=True)
    return (grad_rows - unit_f * radial).astype(jnp.bfloat16)


def backward_projection(tangent_row_block, adapter_up_weight):
    return jnp.dot(
        tangent_row_block, adapter_up_weight.T, preferred_element_type=jnp.float32
    ).astype(jnp.bfloat16)


def up_weight_term(scaled, tangent_row_block):
    return jnp.dot(scaled.T, tangent_row_block, preferred_element_type=jnp.float32)


def score_rows(
    request_normalized_directions, match_entries, collected_entries, slots, loss_slope_coefficient
):
    slot_count = collected_entries.shape[0]
    match_similarities = (
        jnp.dot(request_normalized_directions, match_entries.T, preferred_element_type=jnp.float32)
        / logit_divisor
    )
    similarity_table = (
        jnp.dot(
            request_normalized_directions, collected_entries.T, preferred_element_type=jnp.float32
        )
        / logit_divisor
    )
    hard_scores = jnp.take_along_axis(similarity_table, slots, axis=1)
    maximal_logit_offset = 1.0 / logit_divisor
    match_exponential = jnp.exp(match_similarities - maximal_logit_offset)
    distractor_exponential = jnp.exp(hard_scores - maximal_logit_offset)
    partition_function = jnp.sum(match_exponential, axis=1, keepdims=True) + jnp.sum(
        distractor_exponential, axis=1, keepdims=True
    )
    loss_sum = jnp.sum(
        jnp.log(partition_function[:, 0]) + maximal_logit_offset - jnp.diagonal(match_similarities)
    )
    match_indicator = jnp.eye(match_similarities.shape[0], dtype=jnp.float32)
    match_slope = (
        (match_exponential / partition_function - match_indicator)
        * (loss_slope_coefficient / logit_divisor)
    ).astype(jnp.bfloat16)
    distractor_probability = (
        distractor_exponential / partition_function * (loss_slope_coefficient / logit_divisor)
    )
    row_match = (
        slots[:, :, None] == jnp.arange(slot_count, dtype=jnp.int32)[None, None, :]
    ).astype(jnp.float32)
    hard_grad = jnp.sum(row_match * distractor_probability[:, :, None], axis=1).astype(jnp.bfloat16)
    return (loss_sum, match_slope, hard_grad)


def body(
    query_layer_input,
    query_frozen_base,
    passage_layer_input,
    passage_frozen_base,
    adapter_down_weight,
    adapter_up_weight,
    positive_passage_index,
    hard_negative_slots,
    group_peer_rows,
    remote_group_rows,
):
    n_dp = lax.axis_size("dp")
    n_group = lax.axis_size("group")
    queries = query_layer_input.shape[0] * n_dp * n_group
    loss_slope_coefficient = 16.0 / math.sqrt(queries)
    feature_width = query_layer_input.shape[1]
    adapter_rank_width = adapter_down_weight.shape[1]
    pool_rows = passage_layer_input.shape[0]
    near_count = group_peer_rows.shape[0] * group_peer_rows.shape[1]
    query_unit_rows, query_scaled_rows, query_inverse_norm = embedding_rows(
        query_layer_input, query_frozen_base, adapter_down_weight, adapter_up_weight
    )
    passage_unit_rows, passage_scaled_rows, passage_inverse_norm = embedding_rows(
        passage_layer_input, passage_frozen_base, adapter_down_weight, adapter_up_weight
    )
    near_send = jnp.take(passage_unit_rows, group_peer_rows, axis=0)
    far_send = jnp.take(passage_unit_rows, remote_group_rows, axis=0)
    near_own_latent = jnp.take(passage_scaled_rows, group_peer_rows, axis=0)
    far_own_latent = jnp.take(passage_scaled_rows, remote_group_rows, axis=0)
    near_block = lax.all_to_all(near_send, "dp", split_axis=0, concat_axis=0, tiled=True)
    far_block = lax.all_to_all(far_send, "group", split_axis=0, concat_axis=0, tiled=True)
    collected_entries = jnp.concatenate(
        [near_block.reshape(-1, feature_width), far_block.reshape(-1, feature_width)], axis=0
    )
    match_entries = jnp.take(passage_unit_rows, positive_passage_index, axis=0)
    positive_latent = jnp.take(passage_scaled_rows, positive_passage_index, axis=0)
    loss_sum, match_slope, hard_grad = score_rows(
        query_unit_rows,
        match_entries,
        collected_entries,
        hard_negative_slots,
        loss_slope_coefficient,
    )
    query_grad = jnp.dot(match_slope, match_entries, preferred_element_type=jnp.float32) + jnp.dot(
        hard_grad, collected_entries, preferred_element_type=jnp.float32
    )
    pos_slot_grad = jnp.dot(match_slope.T, query_unit_rows, preferred_element_type=jnp.float32)
    fetched_grad = jnp.dot(hard_grad.T, query_unit_rows, preferred_element_type=jnp.float32)
    query_tangent_rows = tangent_of(query_grad, query_unit_rows)
    positive_tangent = tangent_of(pos_slot_grad, match_entries)
    gathered_tangent_rows = tangent_of(fetched_grad, collected_entries)
    up_weight_gradient = adapter_scale * (
        up_weight_term(query_scaled_rows, query_tangent_rows)
        + up_weight_term(positive_latent, positive_tangent)
    )
    query_back_rows = backward_projection(query_tangent_rows, adapter_up_weight)
    positive_back_rows = backward_projection(positive_tangent, adapter_up_weight)
    near_tangent = lax.all_to_all(
        gathered_tangent_rows[:near_count].reshape(n_dp, -1, feature_width),
        "dp",
        split_axis=0,
        concat_axis=0,
        tiled=True,
    )
    far_tangent = lax.all_to_all(
        gathered_tangent_rows[near_count:].reshape(n_group, -1, feature_width),
        "group",
        split_axis=0,
        concat_axis=0,
        tiled=True,
    )
    local_tangent_rows = jnp.concatenate(
        [near_tangent.reshape(-1, feature_width), far_tangent.reshape(-1, feature_width)], axis=0
    )
    local_latent_rows = jnp.concatenate(
        [
            near_own_latent.reshape(-1, adapter_rank_width),
            far_own_latent.reshape(-1, adapter_rank_width),
        ],
        axis=0,
    )
    up_weight_gradient = up_weight_gradient + adapter_scale * up_weight_term(
        local_latent_rows, local_tangent_rows
    )
    local_back_rows = backward_projection(local_tangent_rows, adapter_up_weight)
    near_back = local_back_rows[:near_count]
    far_back = local_back_rows[near_count:]
    back_rows = jnp.concatenate([near_back, far_back, positive_back_rows], axis=0)
    owner_ids = jnp.concatenate(
        [group_peer_rows.reshape(-1), remote_group_rows.reshape(-1), positive_passage_index], axis=0
    )
    row_match = (owner_ids[:, None] == jnp.arange(pool_rows, dtype=jnp.int32)[None, :]).astype(
        jnp.bfloat16
    )
    row_total_sum = jnp.dot(row_match.T, back_rows, preferred_element_type=jnp.float32)
    passage_output_gradient = (adapter_scale * passage_inverse_norm * row_total_sum).astype(
        jnp.bfloat16
    )
    query_embedding_gradient = (
        adapter_scale * query_inverse_norm * query_back_rows.astype(jnp.float32)
    ).astype(jnp.bfloat16)
    down_grad = jnp.dot(
        query_layer_input.T, query_embedding_gradient, preferred_element_type=jnp.float32
    ) + jnp.dot(passage_layer_input.T, passage_output_gradient, preferred_element_type=jnp.float32)
    down_total, up_total, loss_total = lax.psum(
        (down_grad, up_weight_gradient, loss_sum), ("dp", "group")
    )
    return (down_total, up_total, loss_total / queries)


def solution(mesh):
    placed = (
        P(("dp", "group"), None),
        P(("dp", "group"), None),
        P(("dp", "group"), None),
        P(("dp", "group"), None),
        P(),
        P(),
        P(("dp", "group")),
        P(("dp", "group"), None),
        P(("dp", "group"), None),
        P(("dp", "group"), None),
    )
    return jax.shard_map(
        body, mesh=mesh, in_specs=placed, out_specs=(P(), P(), P()), check_vma=False
    )
```

profile of v0, /device:TPU:1, one launch (start us, length us, event | category | flops | bytes accessed | tf_op | source)
XLA Modules:
  0.0 722.1 jit_solution(2024917296185620867)
XLA Ops:
  7.2 0.7 compare_select_fusion.2
  7.9 0.7 compare_and_fusion.1
  8.6 1.5 convolution_convert_fusion.2
  10.1 1.5 multiply_reduce_fusion
  11.9 0.9 gather_fusion.2
  13.3 1.4 broadcast_select_fusion
  14.6 10.5 %all-to-all-start.1 = ((bf16[32,2,4096]{2,1,0:T(2,128)(2,1)}), bf16[32,2,4096]{2,1,0:T(2,128)(2,1)S(1)}, u32[]{:S(2)}, u32[]{:S(2)}) async-start(bf16[32,2,4096]{2,1,0:T(2,128)(2,1)} %broadcast_select_fusion), calls=%async_computation.1 | async-start | bytes 1048576 | tf_op jit(solution)/shard_map/all_to_all | solution.py:114
  25.3 1.5 gather_fusion.1
  27.0 1.4 bitcast_select_fusion
  28.3 8.5 %all-to-all-done.1 = bf16[32,2,4096]{2,1,0:T(2,128)(2,1)S(1)} async-done(((bf16[32,2,4096]{2,1,0:T(2,128)(2,1)}), bf16[32,2,4096]{2,1,0:T(2,128)(2,1)S(1)}, u32[]{:S(2)}, u32[]{:S(2)}) %all-to-all-start.1) | async-done | bytes 524320 | tf_op jit(solution)/shard_map/all_to_all | solution.py:114
  36.8 21.3 %all-to-all-start = ((bf16[24,8,4096]{2,1,0:T(8,128)(2,1)}), bf16[24,8,4096]{2,1,0:T(8,128)(2,1)S(1)}, u32[]{:S(2)}, u32[]{:S(2)}) async-start(bf16[24,8,4096]{2,1,0:T(8,128)(2,1)} %bitcast_select_fusion), calls=%async_computation | async-start | bytes 3145728 | tf_op jit(solution)/shard_map/all_to_all | solution.py:113
  58.4 0.9 gather_fusion
  59.3 1.7 convolution_convert_fusion.3
  60.9 1.5 multiply_reduce_fusion.1
  62.4 1.0 copy-done.1
  63.9 0.8 gather_fusion.6
  64.7 1.2 reshape.105
  66.0 48.5 %all-to-all-done = bf16[24,8,4096]{2,1,0:T(8,128)(2,1)S(1)} async-done(((bf16[24,8,4096]{2,1,0:T(8,128)(2,1)}), bf16[24,8,4096]{2,1,0:T(8,128)(2,1)S(1)}, u32[]{:S(2)}, u32[]{:S(2)}) %all-to-all-start) | async-done | bytes 1572896 | tf_op jit(solution)/shard_map/all_to_all | solution.py:113
  114.5 0.8 convolution_multiply_fusion.2
  115.2 16.6 %gather_fusion.7 = f32[2048]{0:T(1024)S(1)} fusion(f32[64,256]{1,0:T(8,128)S(1)} %convolution_multiply_fusion.2, s32[2048]{0:T(1024)S(1)} %reshape.167), kind=kCustom, calls=%fused_computation.7 | custom fusion | bytes 32768 | tf_op jit(solution)/shard_map/jit(take_along_axis)/gather | solution.py:58
  132.1 0.6 subtract_reduce_fusion
  132.8 0.7 select_reduce_fusion
  133.5 0.8 fusion.4
  134.3 0.9 fusion.6
  135.2 1.3 copy-done.3
  136.6 0.8 slice.28
  137.4 2.2 reshape.111
  139.6 5.5 all-to-all-start.3
  145.1 2.7 slice_bitcast_fusion
  147.8 10.2 %all-to-all-done.3 = bf16[32,2,4096]{2,1,0:T(2,128)(2,1)} async-done(((bf16[32,2,4096]{2,1,0:T(2,128)(2,1)}), bf16[32,2,4096]{2,1,0:T(2,128)(2,1)}, u32[]{:S(2)}, u32[]{:S(2)}) %all-to-all-start.3) | async-done | bytes 524320 | tf_op jit(solution)/shard_map/all_to_all | solution.py:148
  158.0 10.2 %all-to-all-start.2 = ((bf16[24,8,4096]{2,1,0:T(8,128)(2,1)}), bf16[24,8,4096]{2,1,0:T(8,128)(2,1)}, u32[]{:S(2)}, u32[]{:S(2)}) async-start(bf16[24,8,4096]{2,1,0:T(8,128)(2,1)} %slice_bitcast_fusion), calls=%async_computation.2 | async-start | bytes 3145728 | tf_op jit(solution)/shard_map/all_to_all | solution.py:141
  168.5 0.6 gather_fusion.3
  169.1 0.8 gather_fusion.4
  170.0 0.6 gather_fusion.5
  171.4 1.4 fusion.17
  174.2 0.6 fusion.14
  175.6 1.4 fusion.35
  177.0 0.8 fusion.13
  177.9 2.6 convolution_add_fusion.1
  180.5 1.2 reshape.112
  181.7 42.9 %all-to-all-done.2 = bf16[24,8,4096]{2,1,0:T(8,128)(2,1)} async-done(((bf16[24,8,4096]{2,1,0:T(8,128)(2,1)}), bf16[24,8,4096]{2,1,0:T(8,128)(2,1)}, u32[]{:S(2)}, u32[]{:S(2)}) %all-to-all-start.2) | async-done | bytes 1572896 | tf_op jit(solution)/shard_map/all_to_all | solution.py:141
  224.6 2.3 fusion.8
  226.9 3.0 fusion.3
  229.8 1.6 fusion.2
  231.4 106.8 %psum.23 = f32[]{:T(128)} all-reduce(f32[]{:T(128)} %get-tuple-element.5), channel_id=1, replica_groups=mesh['dp'=24,'group'=32] {'dp','group'}, use_global_device_ids=true, to_apply=%region_11.12 | all-reduce | flops 1 | bytes 8 | tf_op jit(solution)/shard_map/psum | solution.py:188
  338.9 371.9 %all-reduce.3.cloned.1.call-done = (f32[4096,64]{0,1:T(8,128)}, f32[64,4096]{1,0:T(8,128)}) async-done(((f32[4096,64]{0,1:T(8,128)}, f32[64,4096]{1,0:T(8,128)}), (f32[4096,64]{0,1:T(8,128)}, f32[64,4096]{1,0:T(8,128)})) %all-reduce.3.cloned.1.call-update) | async-done | bytes 2097168 | tf_op jit(solution)/shard_map/psum | solution.py:188
  710.8 2.4 copy.46
  713.2 1.0 copy.47
  (74 shorter events, 5.3 us)
Async XLA Ops:
  7.2 2.9 copy-start
  12.8 12.3 %copy-start.13 = (s32[24,8]{0,1:T(8,128)S(1)}, s32[24,8]{0,1:T(8,128)}, u32[]{:S(2)}) copy-start(s32[24,8]{0,1:T(8,128)} %param.18) | copy-start | bytes 2308
  14.6 22.2 %all-to-all-start.1 = ((bf16[32,2,4096]{2,1,0:T(2,128)(2,1)}), bf16[32,2,4096]{2,1,0:T(2,128)(2,1)S(1)}, u32[]{:S(2)}, u32[]{:S(2)}) async-start(bf16[32,2,4096]{2,1,0:T(2,128)(2,1)} %broadcast_select_fusion), calls=%async_computation.1 | async-start | bytes 1048576 | tf_op jit(solution)/shard_map/all_to_all | solution.py:114
  28.3 29.8 %copy-start.14 = (s32[64,32]{0,1:T(8,128)S(1)}, s32[64,32]{0,1:T(8,128)}, u32[]{:S(2)}) copy-start(s32[64,32]{0,1:T(8,128)} %param.17) | copy-start | bytes 24580
  28.3 30.0 %copy-start.16 = (s32[64]{0:T(128)S(1)}, s32[64]{0:T(128)}, u32[]{:S(2)}) copy-start(s32[64]{0:T(128)} %param.16) | copy-start | bytes 772
  36.8 21.6 %copy-start.10 = (bf16[32,2,4096]{2,1,0:T(2,128)(2,1)}, bf16[32,2,4096]{2,1,0:T(2,128)(2,1)S(1)}, u32[]{:S(2)}) copy-start(bf16[32,2,4096]{2,1,0:T(2,128)(2,1)S(1)} %all-to-all-done.1) | copy-start | bytes 1572868
  36.8 77.7 %all-to-all-start = ((bf16[24,8,4096]{2,1,0:T(8,128)(2,1)}), bf16[24,8,4096]{2,1,0:T(8,128)(2,1)S(1)}, u32[]{:S(2)}, u32[]{:S(2)}) async-start(bf16[24,8,4096]{2,1,0:T(8,128)(2,1)} %bitcast_select_fusion), calls=%async_computation | async-start | bytes 3145728 | tf_op jit(solution)/shard_map/all_to_all | solution.py:113
  59.2 4.3 copy-start.4
  62.4 1.0 copy-start.1
  135.2 1.4 copy-start.3
  139.6 18.4 %all-to-all-start.3 = ((bf16[32,2,4096]{2,1,0:T(2,128)(2,1)}), bf16[32,2,4096]{2,1,0:T(2,128)(2,1)}, u32[]{:S(2)}, u32[]{:S(2)}) async-start(bf16[32,2,4096]{2,1,0:T(2,128)(2,1)} %reshape.111), calls=%async_computation.3 | async-start | bytes 1048576 | tf_op jit(solution)/shard_map/all_to_all | solution.py:148
  147.8 22.9 %copy-start.15 = (s32[32,2]{0,1:T(2,128)S(1)}, s32[32,2]{0,1:T(2,128)}, u32[]{:S(2)}) copy-start(s32[32,2]{0,1:T(2,128)} %param.19) | copy-start | bytes 772
  158.0 66.6 %all-to-all-start.2 = ((bf16[24,8,4096]{2,1,0:T(8,128)(2,1)}), bf16[24,8,4096]{2,1,0:T(8,128)(2,1)}, u32[]{:S(2)}, u32[]{:S(2)}) async-start(bf16[24,8,4096]{2,1,0:T(8,128)(2,1)} %slice_bitcast_fusion), calls=%async_computation.2 | async-start | bytes 3145728 | tf_op jit(solution)/shard_map/all_to_all | solution.py:141
  168.2 542.7 %all-reduce.3.cloned.1.call-start = ((), (), s32[]{:S(2)}) async-start(), calls=%async_computation.4 | async-start | bytes 4194304 | tf_op jit(solution)/shard_map/psum | solution.py:188
  171.1 1.7 copy-start.5
  173.1 0.8 copy-start.6
  174.2 1.2 copy-start.2
  175.4 1.6 copy-start.11
  175.6 2.2 copy-start.7
  224.6 2.3 copy-start.8
  226.9 3.0 copy-start.9
  710.8 2.4 copy-start.12
Sparse Core Ops, SparseCore 0:
  231.6 479.2 all-reduce.2
where the time goes:
time: 724 us; the launch traced here: 722 us
  waiting for transfers between devices  482 us (67%)
  blocking collectives  107 us (15%)
  starting transfers between devices  47.7 us (7%)
  local copies, waits for them, and re-layouts  39.4 us (5%)
  matrix products  22.3 us (3%)
  between operations  16.2 us (2%)
  other arithmetic  7.68 us (1%)
    psum x1, waiting for transfers between devices, body(): lax.psum((down_grad, up_weight_gradient, loss_sum), ('dp', 'group'))  372 us
    psum x1, blocking collectives, body(): lax.psum((down_grad, up_weight_gradient, loss_sum), ('dp', 'group'))  107 us
    all_to_all x1, waiting for transfers between devices, body(): lax.all_to_all(near_send, 'dp', split_axis=0, concat_axis=0, tiled=True)  48.5 us
    all_to_all x1, waiting for transfers between devices, body(): lax.all_to_all(gathered_tangent_rows[:near_count].reshape(n_dp, -1, featu...  42.9 us
    all_to_all x1, starting transfers between devices, body(): lax.all_to_all(near_send, 'dp', split_axis=0, concat_axis=0, tiled=True)  21.3 us
    gather x3, local copies, waits for them, and re-layouts, score_rows(): hard_scores = jnp.take_along_axis(similarity_table, slots, axis=1)  16.8 us
  transfers between devices with their start and end apart: 5, of which 5 were waited for; matrix products, arithmetic and copies ran while one was open for 3% of the time, Pallas kernels for 0%

commit v1 on v0

v1 whole, which is shorter than its diff:
```python
import math

import jax
import jax.numpy as jnp
from jax import lax
from jax.experimental import pallas as pl
from jax.experimental.pallas import tpu as pltpu
from jax.sharding import PartitionSpec as P

f32 = jnp.float32
bf16 = jnp.bfloat16
adapter_scale = 2.0
logit_divisor = 0.05
epsilon = 1e-06
offset = 1.0 / logit_divisor
tile = 512
lanes = 128


def dot(a, b, ca=1, cb=0):
    return lax.dot_general(a, b, (((ca,), (cb,)), ((), ())), preferred_element_type=f32)


def iota(shape, dim):
    return lax.broadcasted_iota(jnp.int32, shape, dim)


def eye(n, m):
    return (iota((n, m), 0) == iota((n, m), 1)).astype(bf16)


def flip(a):
    return dot(eye(a.shape[1], a.shape[1]), a, 1, 1).astype(bf16)


def column_tiles(width):
    step = min(tile, width)
    return [slice(c, c + step) for c in range(0, width, step)]


def embed(x_ref, base_ref, down_ref, up_ref, unit_ref, ext_ref, inv_ref, raw_ref):
    rows, width = x_ref.shape
    rank = up_ref.shape[0]
    latent = dot(x_ref[...], down_ref[...], 1, 1).astype(bf16)
    squares = jnp.zeros((rows, 1), f32)
    for cols in column_tiles(width):
        raw = base_ref[:, cols].astype(f32) + adapter_scale * dot(latent, up_ref[:, cols])
        raw_ref[:, cols] = raw
        squares = squares + jnp.sum(raw * raw, axis=1, keepdims=True)
    inverse = lax.rsqrt(squares + epsilon)
    for cols in column_tiles(width):
        unit_ref[:, cols] = (raw_ref[:, cols] * inverse).astype(bf16)
    scaled = (latent.astype(f32) * inverse).astype(bf16)
    high = inverse.astype(bf16).astype(f32)
    lane = iota((rows, lanes), 1)
    ext = dot(scaled, eye(rank, lanes))
    ext = jnp.where(lane == rank, high, ext)
    ext = jnp.where(lane == rank + 1, inverse - high, ext)
    ext_ref[...] = ext.astype(bf16)
    inv_ref[...] = jnp.broadcast_to(inverse, inv_ref.shape)


def passage_kernel(
    grid_x, grid_y, place_ref, x_ref, base_ref, down_ref, up_ref, near_ids_ref, far_ids_ref,
    near_ref, far_ref, unit_ref, ext_ref, inv_ref, pick_ref, raw_ref,
):
    embed(x_ref, base_ref, down_ref, up_ref, unit_ref, ext_ref, inv_ref, raw_ref)
    rows, width = x_ref.shape
    half = width // 2
    per_near, n_near = near_ids_ref.shape
    count = per_near * n_near
    ids = near_ids_ref[...].astype(f32).astype(bf16)
    spread = (iota((count, n_near), 0) // per_near == iota((count, n_near), 1)).astype(bf16)
    table = dot(spread, ids, 1, 1)
    mine = iota((count, per_near), 0) % per_near == iota((count, per_near), 1)
    wanted = jnp.sum(jnp.where(mine, table, 0.0), axis=1, keepdims=True).astype(jnp.int32)
    pick = (iota((count, rows), 1) == wanted).astype(bf16)
    pick_ref[...] = pick
    for cols in column_tiles(width):
        near_ref[:, cols] = dot(pick, unit_ref[:, cols]).astype(bf16)
    near_ref[:, width:] = dot(pick, ext_ref[...]).astype(bf16)
    n_far = far_ids_ref.shape[1]
    total = n_far * 8
    where_x, where_y = place_ref[0], place_ref[1]
    ids = far_ids_ref[...].astype(f32).astype(bf16)
    block = iota((total, n_far), 0) // 8
    to_x = (where_x + block // grid_y) % grid_x
    to_y = (where_y + block % grid_y) % grid_y
    spread = (to_x * grid_y + to_y == iota((total, n_far), 1)).astype(bf16)
    table = dot(spread, ids, 1, 1)
    mine = iota((total, 2), 0) % 2 == iota((total, 2), 1)
    wanted = jnp.sum(jnp.where(mine, table, 0.0), axis=1, keepdims=True).astype(jnp.int32)
    kind = (iota((total, 4 * rows), 0) // 2) % 4
    source = iota((total, 4 * rows), 1)
    choose = ((source // rows == kind) & (source % rows == wanted)).astype(bf16)
    for cols in column_tiles(half):
        later = slice(half + cols.start, half + cols.stop)
        stack = jnp.concatenate(
            [unit_ref[:, cols], unit_ref[:, later], x_ref[:, cols], x_ref[:, later]], axis=0
        )
        far_ref[:, cols] = dot(choose, stack).astype(bf16)
    first = jnp.where(iota((total, rows), 0) // 2 % 4 == 0, wanted, -1)
    far_ref[:, half:] = dot((iota((total, rows), 1) == first).astype(bf16), ext_ref[...]).astype(
        bf16
    )


def query_kernel(
    grid_x, grid_y, place_ref, x_ref, base_ref, down_ref, up_ref, slots_ref,
    unit_ref, ext_ref, inv_ref, near_count_ref, other_count_ref, raw_ref,
):
    embed(x_ref, base_ref, down_ref, up_ref, unit_ref, ext_ref, inv_ref, raw_ref)
    hard, rows = slots_ref.shape
    n_near = near_count_ref.shape[1]
    n_other = other_count_ref.shape[1]
    n_far = n_other - rows
    where_x, where_y = place_ref[0], place_ref[1]
    near_slot = iota((n_near, rows), 0)
    spot = iota((n_other, rows), 0)
    block = spot // 2
    from_x = (where_x + grid_x - block % grid_x) % grid_x
    from_y = (where_y + grid_y - (block // grid_x) % grid_y) % grid_y
    far_slot = n_near + (from_x * grid_y + from_y) * 2 + spot % 2
    far_slot = jnp.where(spot < n_far, far_slot, -1)
    near_count = jnp.zeros((n_near, rows), f32)
    other_count = jnp.zeros((n_other, rows), f32)
    for k in range(hard):
        slot = slots_ref[k : k + 1, :]
        near_count = near_count + (near_slot == slot).astype(f32)
        other_count = other_count + (far_slot == slot).astype(f32)
    other_count = jnp.where(spot < n_far, other_count, 1.0)
    unit = eye(rows, rows)
    near_count_ref[...] = dot(unit, near_count.astype(bf16), 1, 1)
    other_count_ref[...] = dot(unit, other_count.astype(bf16), 1, 1)


def store_blocks(ref, cols, value):
    size = ref.shape[2]
    step = min(size, cols.stop - cols.start)
    for c in range(cols.start, cols.stop, step):
        at = c % size
        ref[c // size, :, at : at + step] = value[:, c - cols.start : c - cols.start + step]


def load_blocks(ref, cols):
    size = ref.shape[2]
    step = min(size, cols.stop - cols.start)
    parts = []
    for c in range(cols.start, cols.stop, step):
        parts.append(ref[c // size, :, c % size : c % size + step])
    return parts[0] if len(parts) == 1 else jnp.concatenate(parts, axis=1)


def score_kernel(
    slope, near_ref, far_ref, q_ref, q_ext_ref, q_inv_ref, unit_ref, p_ext_ref, positive_ref,
    near_count_ref, other_count_ref, up_ref,
    ret_ref, up_out_ref, row_ref, dz_q_ref, dz_f_ref, x_far_ref, o_ref,
):
    rows, width = q_ref.shape
    rank = up_ref.shape[0]
    half = width // 2
    total = far_ref.shape[0]
    n_far = total // 4
    n_near = near_ref.shape[0]
    out_row = iota((total, total), 0)
    in_row = iota((total, total), 1)
    spot = out_row % n_far
    undo = (
        (in_row // 8 == spot // 2)
        & (in_row % 2 == spot % 2)
        & ((in_row // 2) % 4 == out_row // n_far)
    ).astype(bf16)
    for cols in column_tiles(half):
        later = slice(half + cols.start, half + cols.stop)
        got = dot(undo, far_ref[:, cols]).astype(bf16)
        o_ref[0:n_far, cols] = got[0:n_far]
        o_ref[0:n_far, later] = got[n_far : 2 * n_far]
        x_far_ref[:, cols] = got[2 * n_far : 3 * n_far]
        x_far_ref[:, later] = got[3 * n_far :]
    far_ext = dot(undo[0:n_far], far_ref[:, half:])
    own = (iota((rows, rows), 0) == positive_ref[...]).astype(bf16)
    own_t = flip(own)
    for cols in column_tiles(width):
        o_ref[n_far:, cols] = dot(own_t, unit_ref[:, cols]).astype(bf16)
    pos_ext = dot(own_t, p_ext_ref[...])

    q_all = q_ref[...]
    near_raw = dot(q_all, near_ref[:, :width], 1, 1)
    other_raw = dot(q_all, o_ref[...], 1, 1)
    near_raw_t = dot(near_ref[:, :width], q_all, 1, 1)
    other_raw_t = dot(o_ref[...], q_all, 1, 1)
    near_exp = jnp.exp(near_raw / logit_divisor - offset) * near_count_ref[...]
    other_exp = jnp.exp(other_raw / logit_divisor - offset) * other_count_ref[...]
    partition = jnp.sum(near_exp, axis=1, keepdims=True) + jnp.sum(
        other_exp, axis=1, keepdims=True
    )
    same = iota(other_raw.shape, 1) == iota(other_raw.shape, 0) + n_far
    matched = jnp.sum(jnp.where(same, other_raw, 0.0), axis=1, keepdims=True) / logit_divisor
    loss = jnp.sum(jnp.log(partition) + offset - matched, axis=0, keepdims=True)
    near_g = (near_exp / partition * slope).astype(bf16)
    other_g = ((other_exp / partition - same.astype(f32)) * slope).astype(bf16)
    near_gt = flip(near_g)
    other_gt = flip(other_g)
    q_radial = jnp.sum(near_g.astype(f32) * near_raw, axis=1, keepdims=True) + jnp.sum(
        other_g.astype(f32) * other_raw, axis=1, keepdims=True
    )
    near_radial = jnp.sum(near_gt.astype(f32) * near_raw_t, axis=1, keepdims=True)
    other_radial = jnp.sum(other_gt.astype(f32) * other_raw_t, axis=1, keepdims=True)
    q_lat = flip(q_ext_ref[...])[0:rank]
    near_lat = flip(near_ref[:, width:])[0:rank]
    other_lat = flip(jnp.concatenate([far_ext, pos_ext], axis=0).astype(bf16))[0:rank]
    q_back = jnp.zeros((rows, rank), f32)
    near_back = jnp.zeros((n_near, rank), f32)
    other_back = jnp.zeros((n_far + rows, rank), f32)
    for cols in column_tiles(width):
        q = q_ref[:, cols]
        near = near_ref[:, cols]
        other = o_ref[:, cols]
        up = up_ref[:, cols]
        q_t = dot(near_g, near) + dot(other_g, other) - q.astype(f32) * q_radial
        near_t = dot(near_gt, q) - near.astype(f32) * near_radial
        other_t = dot(other_gt, q) - other.astype(f32) * other_radial
        q_t, near_t, other_t = q_t.astype(bf16), near_t.astype(bf16), other_t.astype(bf16)
        q_back = q_back + dot(q_t, up, 1, 1)
        near_back = near_back + dot(near_t, up, 1, 1)
        other_back = other_back + dot(other_t, up, 1, 1)
        grad = dot(q_lat, q_t) + dot(near_lat, near_t) + dot(other_lat, other_t)
        store_blocks(up_out_ref, cols, adapter_scale * grad)
    back = dot(near_back.astype(bf16), eye(rank, lanes))
    lane = iota((n_near, lanes), 1)
    high = loss.astype(bf16).astype(f32)
    back = jnp.where(lane == rank, high, back)
    back = jnp.where(lane == rank + 1, loss - high, back)
    ret_ref[...] = back.astype(bf16)
    other_back = other_back.astype(bf16)
    row_ref[...] = dot(own, other_back[n_far:])
    dz_q_ref[...] = (adapter_scale * q_inv_ref[:, 0:1] * q_back.astype(bf16).astype(f32)).astype(
        bf16
    )
    far_inv = far_ext[:, rank : rank + 1] + far_ext[:, rank + 1 : rank + 2]
    dz_f_ref[...] = (adapter_scale * far_inv * other_back[0:n_far].astype(f32)).astype(bf16)


def down_kernel(
    per_near, place_ref, ret_ref, pick_ref, row_ref, p_inv_ref, dz_q_ref, dz_f_ref, x_q_ref, x_p_ref,
    x_far_ref, up_part_ref, keep_ref, send_ref, loss_ref,
):
    rank = row_ref.shape[1]
    ret = ret_ref[...]
    row_sum = dot(flip(pick_ref[...]), ret)[:, 0:rank] + row_ref[...]
    dz_p = (adapter_scale * p_inv_ref[:, 0:1] * row_sum).astype(bf16)
    dz_pt, dz_qt, dz_ft = flip(dz_p), flip(dz_q_ref[...]), flip(dz_f_ref[...])
    even = place_ref[2] == 0
    for cols in column_tiles(x_q_ref.shape[1]):
        grad = (
            dot(dz_qt, x_q_ref[:, cols])
            + dot(dz_pt, x_p_ref[:, cols])
            + dot(dz_ft, x_far_ref[:, cols])
        )
        other = load_blocks(up_part_ref, cols)
        store_blocks(keep_ref, cols, jnp.where(even, grad, other))
        store_blocks(send_ref, cols, jnp.where(even, other, grad).astype(bf16))
    first = iota(ret.shape, 0) % per_near == 0
    lane = iota(ret.shape, 1)
    chosen = first & ((lane == rank) | (lane == rank + 1))
    part = jnp.sum(jnp.where(chosen, ret.astype(f32), 0.0), axis=1, keepdims=True)
    loss_ref[...] = jnp.broadcast_to(jnp.sum(part, axis=0, keepdims=True), loss_ref.shape)


def add_kernel(keep_ref, got_ref, out_ref):
    for i in range(keep_ref.shape[0]):
        out_ref[i] = (keep_ref[i] + got_ref[i].astype(f32)).astype(bf16)


def sum_blocks(ref):
    acc = ref[0].astype(f32)
    for i in range(1, ref.shape[0]):
        acc = acc + ref[i].astype(f32)
    return acc


def spread_kernel(in_ref, out_ref):
    value = sum_blocks(in_ref).astype(bf16)
    for i in range(out_ref.shape[0]):
        out_ref[i] = value


def finish_kernel(in_ref, loss_ref, out_ref):
    loss = loss_ref[...]
    high = loss.astype(bf16).astype(f32)
    row = iota(loss.shape, 0)
    tail = jnp.where(row == 0, high, jnp.where(row == 1, loss - high, 0.0))
    if out_ref.shape[2] > lanes:
        tail = jnp.concatenate([tail] * (out_ref.shape[2] // lanes), axis=1)
    value = jnp.concatenate([sum_blocks(in_ref), tail], axis=0).astype(bf16)
    for i in range(out_ref.shape[0]):
        out_ref[i] = value


def output_kernel(place_ref, mine_ref, other_ref, down_ref, up_ref, loss_ref):
    rank = down_ref.shape[0]
    size = mine_ref.shape[2]
    even = place_ref[2] == 0
    loss = jnp.zeros((8, lanes), f32)
    for i in range(mine_ref.shape[0]):
        mine, other = mine_ref[i].astype(f32), other_ref[i].astype(f32)
        cols = slice(i * size, (i + 1) * size)
        down_ref[:, cols] = jnp.where(even, mine[0:rank], other[0:rank])
        up_ref[:, cols] = jnp.where(even, other[0:rank], mine[0:rank])
        loss = loss + mine[rank:, 0:lanes]
    loss_ref[...] = jnp.broadcast_to(jnp.sum(loss, axis=0, keepdims=True), loss.shape)


def call(kernel, outs, args, scratch=(), flops=0, moved=0):
    specs = []
    for a in args:
        space = pltpu.SMEM if a.dtype == jnp.int32 and a.ndim == 1 else pltpu.VMEM
        specs.append(pl.BlockSpec(memory_space=space))
    shapes = [jax.ShapeDtypeStruct(s, d) for s, d in outs]
    return pl.pallas_call(
        kernel,
        out_shape=shapes,
        in_specs=specs,
        out_specs=[pl.BlockSpec(memory_space=pltpu.VMEM) for _ in shapes],
        scratch_shapes=[pltpu.VMEM(s, d) for s, d in scratch],
        compiler_params=pltpu.CompilerParams(vmem_limit_bytes=40 * 1024 * 1024),
        cost_estimate=pl.CostEstimate(flops=flops, bytes_accessed=moved, transcendentals=0),
    )(*args)


def exchange(x, axis, groups=None):
    return lax.all_to_all(
        x, axis, split_axis=0, concat_axis=0, tiled=True, axis_index_groups=groups
    )


def far_exchange(blocks, grid_x, grid_y):
    rows, width = blocks.shape
    group = [(x, y) for x in range(grid_x) for y in range(grid_y)]
    line = blocks.reshape(grid_x, grid_y, 8, width)
    got = [line[0]]
    for dx in range(1, grid_x):
        pairs = [(x * grid_y + y, (x + dx) % grid_x * grid_y + y) for x, y in group]
        got.append(lax.ppermute(line[dx], "group", pairs))
    ended = []
    for dy in range(grid_y):
        piece = jnp.concatenate([g[dy] for g in got], axis=0)
        if dy:
            pairs = [(x * grid_y + y, x * grid_y + (y + dy) % grid_y) for x, y in group]
            piece = lax.ppermute(piece, "group", pairs)
        ended.append(piece)
    return jnp.concatenate(ended, axis=0)


def make_body(grid_x, grid_y):
    def body(
        query_layer_input,
        query_frozen_base,
        passage_layer_input,
        passage_frozen_base,
        adapter_down_weight,
        adapter_up_weight,
        positive_passage_index,
        hard_negative_slots,
        group_peer_rows,
        remote_group_rows,
    ):
        n_dp = lax.axis_size("dp")
        n_group = lax.axis_size("group")
        rows, width = query_layer_input.shape
        rank = adapter_up_weight.shape[0]
        queries = rows * n_dp * n_group
        slope = 16.0 / math.sqrt(queries) / logit_divisor
        g = lax.axis_index("group")
        place = jnp.stack([g // grid_y, g % grid_y, lax.axis_index("dp") % 2]).astype(jnp.int32)
        down_t = adapter_down_weight.T
        per_near = group_peer_rows.shape[1]
        n_near = n_dp * per_near
        n_far = n_group * 2
        half = width // 2
        block = width // n_group
        near, far, p_unit, p_ext, p_inv, pick = call(
            lambda *refs: passage_kernel(grid_x, grid_y, *refs),
            [
                ((n_near, width + lanes), bf16),
                ((n_far * 4, half + lanes), bf16),
                ((rows, width), bf16),
                ((rows, lanes), bf16),
                ((rows, lanes), f32),
                ((n_near, rows), bf16),
            ],
            (
                place, passage_layer_input, passage_frozen_base, down_t, adapter_up_weight,
                group_peer_rows.T, remote_group_rows.T,
            ),
            [((rows, width), f32)], flops=400_000_000, moved=6_000_000,
        )
        near = exchange(near.reshape(n_dp, per_near, width + lanes), "dp")
        near = near.reshape(n_near, width + lanes)
        far = far_exchange(far, grid_x, grid_y)
        q_unit, q_ext, q_inv, near_count, other_count = call(
            lambda *refs: query_kernel(grid_x, grid_y, *refs),
            [
                ((rows, width), bf16),
                ((rows, lanes), bf16),
                ((rows, lanes), f32),
                ((rows, n_near), f32),
                ((rows, n_far + rows), f32),
            ],
            (
                place, query_layer_input, query_frozen_base, down_t, adapter_up_weight,
                hard_negative_slots.T,
            ),
            [((rows, width), f32)], flops=100_000_000, moved=3_000_000,
        )
        ret, up_part, row_part, dz_q, dz_f, x_far = call(
            lambda *refs: score_kernel(slope, *refs),
            [
                ((n_near, lanes), bf16),
                ((n_group, rank, block), f32),
                ((rows, rank), f32),
                ((rows, rank), bf16),
                ((n_far, rank), bf16),
                ((n_far, width), bf16),
            ],
            (
                near, far, q_unit, q_ext, q_inv, p_unit, p_ext,
                positive_passage_index.reshape(1, rows), near_count, other_count,
                adapter_up_weight,
            ),
            [((n_far + rows, width), bf16)], flops=1_500_000_000, moved=8_000_000,
        )
        ret = exchange(ret.reshape(n_dp, per_near, lanes), "dp").reshape(n_near, lanes)
        keep, send, loss = call(
            lambda *refs: down_kernel(per_near, *refs),
            [
                ((n_group, rank, block), f32),
                ((n_group, rank, block), bf16),
                ((8, lanes), f32),
            ],
            (
                place, ret, pick, row_part, p_inv, dz_q, dz_f, query_layer_input,
                passage_layer_input, x_far, up_part,
            ),
            flops=200_000_000, moved=5_000_000,
        )
        swap = [(i, i ^ 1) for i in range(n_dp)]
        got = lax.ppermute(send, "dp", swap)
        (part,) = call(add_kernel, [((n_group, rank, block), bf16)], (keep, got), moved=2_500_000)
        part = exchange(part, "group")
        cores = [list(range(c, n_dp, 2)) for c in range(2)]
        (part,) = call(
            spread_kernel, [((n_dp // 2, rank, block), bf16)], (part,), moved=1_000_000
        )
        part = exchange(part, "dp", cores)
        (part,) = call(
            finish_kernel, [((n_group, rank + 8, block), bf16)], (part, loss), moved=1_000_000
        )
        part = exchange(part, "group")
        other = lax.ppermute(part, "dp", swap)
        down, up, loss = call(
            output_kernel,
            [((rank, width), f32), ((rank, width), f32), ((8, lanes), f32)],
            (place, part, other),
            moved=3_500_000,
        )
        return (down.T, up, loss[0, 0] / queries)

    return body


def solution(mesh):
    n_group = mesh.shape["group"]
    grid_x = {32: 4, 4: 2}[n_group]
    both = P(("dp", "group"), None)
    placed = (both, both, both, both, P(), P(), P(("dp", "group")), both, both, both)
    return jax.shard_map(
        make_body(grid_x, n_group // grid_x),
        mesh=mesh,
        in_specs=placed,
        out_specs=(P(), P(), P()),
        check_vma=False,
    )
```

time: 724 us -> 198 us (0.27)
  waiting for transfers between devices: 482 us -> 21.9 us
  blocking collectives: 107 us -> 78.9 us
  local copies, waits for them, and re-layouts: 39.4 us -> 14 us
  matrix products: 22.3 us -> 0 us
  starting transfers between devices: 47.7 us -> 65.4 us
  Pallas kernels: 0 us -> 13.5 us
  between operations: 16.2 us -> 2.85 us
  other arithmetic: 7.68 us -> 0.17 us
    psum x1 -> x0, waiting for transfers between devices: 372 us -> none  [body(): lax.psum((down_grad, up_weight_gradient, loss_sum), ('dp', 'group'))]
    all_to_all x4 -> x1, waiting for transfers between devices: 110 us -> 0.01 us  [exchange(): lax.all_to_all(x, axis, split_axis=0, concat_axis=0, tiled=True, axis_ind...]
    psum x1 -> x0, blocking collectives: 107 us -> none  [body(): lax.psum((down_grad, up_weight_gradient, loss_sum), ('dp', 'group'))]
    all_to_all x0 -> x4, blocking collectives: none -> 78.9 us  [exchange(): lax.all_to_all(x, axis, split_axis=0, concat_axis=0, tiled=True, axis_ind...]
    ppermute x0 -> x12, starting transfers between devices: none -> 48.7 us  [the longest x7 28.4 us: far_exchange(): piece = lax.ppermute(piece, 'group', pairs)]
    all_to_all x4 -> x1, starting transfers between devices: 47.5 us -> 16.7 us  [exchange(): lax.all_to_all(x, axis, split_axis=0, concat_axis=0, tiled=True, axis_ind...]
    gather x11 -> x0, local copies, waits for them, and re-layouts: 23.3 us -> none  [the longest x3 16.8 us: score_rows(): hard_scores = jnp.take_along_axis(similarity_table, slots, axis=1)]
    dot_general x17 -> x0, matrix products: 22.3 us -> none  [the longest x3 6.93 us: up_weight_term(): jnp.dot(scaled.T, tangent_row_block, preferred_element_type=jnp.float32)]
  transfers between devices with their start and end apart: 5 -> 13, of which waited for: 5 -> 7; matrix products, arithmetic and copies ran while one was open for 3% -> 1% of each run, Pallas kernels for 0% -> 1%
where the time goes in v1:
time: 198 us; the launch traced here: 197 us
  blocking collectives  78.9 us (40%)
  starting transfers between devices  65.4 us (33%)
  waiting for transfers between devices  21.9 us (11%)
  local copies, waits for them, and re-layouts  14 us (7%)
  Pallas kernels  13.5 us (7%)
  between operations  2.85 us (1%)
    all_to_all x4, blocking collectives, exchange(): lax.all_to_all(x, axis, split_axis=0, concat_axis=0, tiled=True, axis_ind...  78.9 us
    ppermute x7, starting transfers between devices, far_exchange(): piece = lax.ppermute(piece, 'group', pairs)  28.4 us
    all_to_all x1, starting transfers between devices, exchange(): lax.all_to_all(x, axis, split_axis=0, concat_axis=0, tiled=True, axis_ind...  16.7 us
    pallas_call x8, Pallas kernels, call(): pl.pallas_call(kernel, out_shape=shapes, in_specs=specs, out_specs=[pl.Bl...  13.5 us
    ppermute x7, waiting for transfers between devices, far_exchange(): piece = lax.ppermute(piece, 'group', pairs)  12.9 us
    unnamed x47, local copies, waits for them, and re-layouts  11.2 us
    ppermute x3, starting transfers between devices, far_exchange(): got.append(lax.ppermute(line[dx], 'group', pairs))  10.6 us
    ppermute x1, starting transfers between devices, body(): other = lax.ppermute(part, 'dp', swap)  7.32 us
  transfers between devices with their start and end apart: 13, of which 7 were waited for; matrix products, arithmetic and copies ran while one was open for 1% of the time, Pallas kernels for 1%

profile of v1, /device:TPU:1, one launch (start us, length us, event | category | flops | bytes accessed | tf_op | source)
XLA Modules:
  0.0 196.6 jit_solution(16095460285529436684)
XLA Ops:
  0.7 0.1 pad_add_fusion.refs_0_.place_ref
  0.7 1.0 copy-done
  1.8 1.0 copy-done.2
  2.8 1.0 copy-done.5
  3.9 1.0 copy-done.10
  4.9 0.7 copy-done.12
  5.6 0.7 copy-done.15
  6.3 2.5 %shard_map.121 = (bf16[192,4224]{1,0:T(8,128)(2,1)S(1)}, bf16[256,2176]{1,0:T(8,128)(2,1)S(1)}, bf16[64,4096]{1,0:T(8,128)(2,1)S(1)}, bf16[64,128]{1,0:T(8,128)(...) custom-call(s32[3]{0:T(128)S(1)} %pad_add_fusion.refs_0_.place_ref, bf16[64,4096]{1,0:T(8,128)(2,1)S(1)} %copy-done.5, ...), custom_call_target="tpu_custom_call" | custom-call | flops 400000000 | bytes 6000000 | tf_op jit(solution)/shard_map/pallas_call | solution.py:320
  8.8 1.2 copy-done.7
  10.0 1.0 copy-done.8
  11.0 16.7 %all-to-all-start = ((bf16[24,8,4224]{2,1,0:T(8,128)(2,1)}), bf16[24,8,4224]{2,1,0:T(8,128)(2,1)S(1)}, u32[]{:S(2)}, u32[]{:S(2)}) async-start(bf16[24,8,4224]{2,1,0:T(8,128)(2,1)} %bitcast.77), calls=%async_computation | async-start | bytes 3244032 | tf_op jit(solution)/shard_map/all_to_all | solution.py:332
  27.7 0.0 copy-start.1
  27.8 1.3 slice_bitcast_fusion
  29.1 3.1 %collective-permute-start = (bf16[8,8,2176]{2,1,0:T(8,128)(2,1)S(1)}, bf16[8,8,2176]{2,1,0:T(8,128)(2,1)S(1)}, u32[]{:S(2)}, u32[]{:S(2)}) collective-permute-start(bf16[8,8,2176]{2,1,0:T(8,128)(2,1)S(1)} %get-tuple-element.59), channel_id=1, source_target_pairs={{0,8},{1,9},{2,10},{3,11},{4,12},{5,13},{6,14},{7,15},{8,16},{9,17... | collective-permute-start | bytes 835592 | tf_op jit(solution)/shard_map/ppermute | solution.py:344
  32.2 4.3 %collective-permute-start.1 = (bf16[8,8,2176]{2,1,0:T(8,128)(2,1)S(1)}, bf16[8,8,2176]{2,1,0:T(8,128)(2,1)S(1)}, u32[]{:S(2)}, u32[]{:S(2)}) collective-permute-start(bf16[8,8,2176]{2,1,0:T(8,128)(2,1)S(1)} %get-tuple-element.58), channel_id=1, source_target_pairs={{0,16},{1,17},{2,18},{3,19},{4,20},{5,21},{6,22},{7,23},{8,24},{9,... | collective-permute-start | bytes 835592 | tf_op jit(solution)/shard_map/ppermute | solution.py:344
  36.6 3.1 %collective-permute-start.2 = (bf16[8,8,2176]{2,1,0:T(8,128)(2,1)S(1)}, bf16[8,8,2176]{2,1,0:T(8,128)(2,1)S(1)}, u32[]{:S(2)}, u32[]{:S(2)}) collective-permute-start(bf16[8,8,2176]{2,1,0:T(8,128)(2,1)S(1)} %get-tuple-element.57), channel_id=1, source_target_pairs={{0,24},{1,25},{2,26},{3,27},{4,28},{5,29},{6,30},{7,31},{8,0},{9,1... | collective-permute-start | bytes 835592 | tf_op jit(solution)/shard_map/ppermute | solution.py:344
  39.7 0.9 fusion.3
  40.6 2.0 %shard_map.122 = (bf16[64,4096]{1,0:T(8,128)(2,1)S(1)}, bf16[64,128]{1,0:T(8,128)(2,1)S(1)}, f32[64,128]{1,0:T(8,128)S(1)}, f32[64,192]{1,0:T(8,128)S(1)}, f32[64,128]{1,0:T(8,128)S(1)}) custom-call(s32[3]{0:T(128)S(1)} %pad_add_fusion.refs_0_.place_ref, bf16[64,4096]{1,0:T(8,128)(2,1)S(1)} %copy-done.4, bf16[64,4096]{1,0:T(8,128)(2,1)S(1)} %copy-done.9, ...), custom_call_target="tpu_custom_call" | custom-call | flops 100000000 | bytes 3000000 | tf_op jit(solution)/shard_map/pallas_call | solution.py:320
  42.6 5.8 %collective-permute-done.2 = bf16[8,8,2176]{2,1,0:T(8,128)(2,1)S(1)} collective-permute-done((bf16[8,8,2176]{2,1,0:T(8,128)(2,1)S(1)}, bf16[8,8,2176]{2,1,0:T(8,128)(2,1)S(1)}, u32[]{:S(2)}, u32[]{:S(2)}) %collective-permute-start.2) | collective-permute-done | bytes 278560 | tf_op jit(solution)/shard_map/ppermute | solution.py:344
  48.5 3.2 %collective-permute-start.3 = (bf16[32,2176]{1,0:T(8,128)(2,1)S(1)}, bf16[32,2176]{1,0:T(8,128)(2,1)S(1)}, u32[]{:S(2)}, u32[]{:S(2)}) collective-permute-start(bf16[32,2176]{1,0:T(8,128)(2,1)S(1)} %pad_maximum_fusion), channel_id=1, source_target_pairs={{0,1},{1,2},{2,3},{3,4},{4,5},{5,6},{6,7},{7,0},{8,9},{9,10},{10,1... | collective-permute-start | bytes 417800 | tf_op jit(solution)/shard_map/ppermute | solution.py:350
  51.8 4.2 %collective-permute-start.4 = (bf16[32,2176]{1,0:T(8,128)(2,1)S(1)}, bf16[32,2176]{1,0:T(8,128)(2,1)S(1)}, u32[]{:S(2)}, u32[]{:S(2)}) collective-permute-start(bf16[32,2176]{1,0:T(8,128)(2,1)S(1)} %pad_maximum_fusion.1), channel_id=1, source_target_pairs={{0,2},{1,3},{2,4},{3,5},{4,6},{5,7},{6,0},{7,1},{8,10},{9,11},{10,... | collective-permute-start | bytes 417800 | tf_op jit(solution)/shard_map/ppermute | solution.py:350
  56.0 4.6 %collective-permute-start.5 = (bf16[32,2176]{1,0:T(8,128)(2,1)S(1)}, bf16[32,2176]{1,0:T(8,128)(2,1)S(1)}, u32[]{:S(2)}, u32[]{:S(2)}) collective-permute-start(bf16[32,2176]{1,0:T(8,128)(2,1)S(1)} %pad_maximum_fusion.2), channel_id=1, source_target_pairs={{0,3},{1,4},{2,5},{3,6},{4,7},{5,0},{6,1},{7,2},{8,11},{9,12},{10,... | collective-permute-start | bytes 417800 | tf_op jit(solution)/shard_map/ppermute | solution.py:350
  60.7 3.5 %collective-permute-start.6 = (bf16[32,2176]{1,0:T(8,128)(2,1)S(1)}, bf16[32,2176]{1,0:T(8,128)(2,1)S(1)}, u32[]{:S(2)}, u32[]{:S(2)}) collective-permute-start(bf16[32,2176]{1,0:T(8,128)(2,1)S(1)} %pad_maximum_fusion.3), channel_id=1, source_target_pairs={{0,4},{1,5},{2,6},{3,7},{4,0},{5,1},{6,2},{7,3},{8,12},{9,13},{10,... | collective-permute-start | bytes 417800 | tf_op jit(solution)/shard_map/ppermute | solution.py:350
  64.3 4.9 %collective-permute-start.7 = (bf16[32,2176]{1,0:T(8,128)(2,1)S(1)}, bf16[32,2176]{1,0:T(8,128)(2,1)S(1)}, u32[]{:S(2)}, u32[]{:S(2)}) collective-permute-start(bf16[32,2176]{1,0:T(8,128)(2,1)S(1)} %pad_maximum_fusion.4), channel_id=1, source_target_pairs={{0,5},{1,6},{2,7},{3,0},{4,1},{5,2},{6,3},{7,4},{8,13},{9,14},{10,... | collective-permute-start | bytes 417800 | tf_op jit(solution)/shard_map/ppermute | solution.py:350
  69.3 5.0 %collective-permute-start.8 = (bf16[32,2176]{1,0:T(8,128)(2,1)S(1)}, bf16[32,2176]{1,0:T(8,128)(2,1)S(1)}, u32[]{:S(2)}, u32[]{:S(2)}) collective-permute-start(bf16[32,2176]{1,0:T(8,128)(2,1)S(1)} %pad_maximum_fusion.5), channel_id=1, source_target_pairs={{0,6},{1,7},{2,0},{3,1},{4,2},{5,3},{6,4},{7,5},{8,14},{9,15},{10,... | collective-permute-start | bytes 417800 | tf_op jit(solution)/shard_map/ppermute | solution.py:350
  74.3 3.0 %collective-permute-start.9 = (bf16[32,2176]{1,0:T(8,128)(2,1)S(1)}, bf16[32,2176]{1,0:T(8,128)(2,1)S(1)}, u32[]{:S(2)}, u32[]{:S(2)}) collective-permute-start(bf16[32,2176]{1,0:T(8,128)(2,1)S(1)} %pad_maximum_fusion.6), channel_id=1, source_target_pairs={{0,7},{1,0},{2,1},{3,2},{4,3},{5,4},{6,5},{7,6},{8,15},{9,8},{10,9... | collective-permute-start | bytes 417800 | tf_op jit(solution)/shard_map/ppermute | solution.py:350
  77.3 0.2 collective-permute-done.6
  77.6 5.4 %collective-permute-done.7 = bf16[32,2176]{1,0:T(8,128)(2,1)S(1)} collective-permute-done((bf16[32,2176]{1,0:T(8,128)(2,1)S(1)}, bf16[32,2176]{1,0:T(8,128)(2,1)S(1)}, u32[]{:S(2)}, u32[]{:S(2)}) %collective-permute-start.7) | collective-permute-done | bytes 139296 | tf_op jit(solution)/shard_map/ppermute | solution.py:350
  83.0 5.9 %collective-permute-done.8 = bf16[32,2176]{1,0:T(8,128)(2,1)S(1)} collective-permute-done((bf16[32,2176]{1,0:T(8,128)(2,1)S(1)}, bf16[32,2176]{1,0:T(8,128)(2,1)S(1)}, u32[]{:S(2)}, u32[]{:S(2)}) %collective-permute-start.8) | collective-permute-done | bytes 139296 | tf_op jit(solution)/shard_map/ppermute | solution.py:350
  89.0 1.4 collective-permute-done.9
  90.3 1.0 copy-done.13
  91.3 1.2 copy-done.14
  92.6 1.0 copy-done.17
  93.6 5.1 %shard_map.123 = (bf16[192,128]{1,0:T(8,128)(2,1)S(1)}, f32[32,64,128]{2,1,0:T(8,128)S(1)}, f32[64,64]{1,0:T(8,128)S(1)}, bf16[64,64]{1,0:T(8,128)(2,1)S(1)}, bf...) custom-call(bf16[192,4224]{1,0:T(8,128)(2,1)S(1)} %bitcast.76, bf16[256,2176]{1,0:T(8,128)(2,1)S(1)} %copy-done.14, ...), custom_call_target="tpu_custom_call" | custom-call | flops 1500000000 | bytes 8000000 | tf_op jit(solution)/shard_map/pallas_call | solution.py:320
  98.7 20.7 %all_to_all.25 = bf16[24,8,128]{2,1,0:T(8,128)(2,1)S(1)} all-to-all(bf16[24,8,128]{2,1,0:T(8,128)(2,1)S(1)} %bitcast.79), channel_id=1, replica_groups=mesh['dp'=24,'group'=32] {'dp'}, dimensions={0} | all-to-all | bytes 98304 | tf_op jit(solution)/shard_map/all_to_all | solution.py:332
  119.4 1.5 shard_map.124
  121.0 2.4 %collective-permute-start.10 = (bf16[32,64,128]{2,1,0:T(8,128)(2,1)S(1)}, bf16[32,64,128]{2,1,0:T(8,128)(2,1)S(1)}, u32[]{:S(2)}, u32[]{:S(2)}) collective-permute-start(bf16[32,64,128]{2,1,0:T(8,128)(2,1)S(1)} %get-tuple-element.44), channel_id=1, source_target_pairs={{0,32},{32,0},{64,96},{96,64},{128,160},{160,128},{192,224},{224,1... | collective-permute-start | bytes 1572872 | tf_op jit(solution)/shard_map/ppermute | solution.py:448
  123.4 1.5 collective-permute-done.10.got_ref
  124.9 0.1 shard_map.125
  125.0 20.5 %all_to_all.26.in_ref = bf16[32,64,128]{2,1,0:T(8,128)(2,1)S(1)} all-to-all(bf16[32,64,128]{2,1,0:T(8,128)(2,1)S(1)} %shard_map.125), channel_id=1, replica_groups=mesh['dp'=24,'group'=32] {'group'}, dimensions={0} | all-to-all | bytes 1048576 | tf_op jit(solution)/shard_map/all_to_all | solution.py:332
  145.5 0.1 shard_map.126
  145.6 13.6 %all_to_all.27.in_ref = bf16[12,64,128]{2,1,0:T(8,128)(2,1)S(1)} all-to-all(bf16[12,64,128]{2,1,0:T(8,128)(2,1)S(1)} %shard_map.126), channel_id=1, replica_groups={{0,64,128,192,256,320,384,448,512,576,640,704},{32,96,160,224,288,352,4..., dimensions={0} | all-to-all | bytes 393216 | tf_op jit(solution)/shard_map/all_to_all | solution.py:332
  159.3 0.1 shard_map.127
  159.3 24.0 %all_to_all.28.mine_ref = bf16[32,72,128]{2,1,0:T(8,128)(2,1)S(1)} all-to-all(bf16[32,72,128]{2,1,0:T(8,128)(2,1)S(1)} %shard_map.127), channel_id=1, replica_groups=mesh['dp'=24,'group'=32] {'group'}, dimensions={0} | all-to-all | bytes 1179648 | tf_op jit(solution)/shard_map/all_to_all | solution.py:332
  183.3 7.3 %collective-permute-start.11 = (bf16[32,72,128]{2,1,0:T(8,128)(2,1)S(1)}, bf16[32,72,128]{2,1,0:T(8,128)(2,1)S(1)}, u32[]{:S(2)}, u32[]{:S(2)}) collective-permute-start(bf16[32,72,128]{2,1,0:T(8,128)(2,1)S(1)} %all_to_all.28.mine_ref), channel_id=1, source_target_pairs={{0,32},{32,0},{64,96},{96,64},{128,160},{160,128},{192,224},{224,1... | collective-permute-start | bytes 1769480 | tf_op jit(solution)/shard_map/ppermute | solution.py:460
  190.7 1.6 collective-permute-done.11.other_ref
  192.3 2.1 %shard_map.128 = (f32[64,4096]{1,0:T(8,128)}, f32[64,4096]{1,0:T(8,128)}, f32[8,128]{1,0:T(8,128)S(1)}) custom-call(s32[3]{0:T(128)S(1)} %pad_add_fusion.refs_0_.place_ref, bf16[32,72,128]{2,1,0:T(8,128)(2,1)S(1)} %all_to_all.28.mine_ref, bf16[32,72,128]{2,1,0:T(8,128)(2,1)S(1)} %collective-permute-done.11.other_ref), custom_call_target="tpu_custom_call" | custom-call | bytes 3500000 | tf_op jit(solution)/shard_map/pallas_call | solution.py:320
  194.3 0.5 slice.164
  (52 shorter events, 0.4 us)
Async XLA Ops:
  0.7 1.0 copy-start
  1.8 1.0 copy-start.2
  2.8 1.0 copy-start.5
  3.9 1.0 copy-start.10
  4.9 0.7 copy-start.12
  5.6 0.7 copy-start.15
  8.8 1.2 copy-start.7
  10.0 1.0 copy-start.8
  11.0 80.3 %all-to-all-start = ((bf16[24,8,4224]{2,1,0:T(8,128)(2,1)}), bf16[24,8,4224]{2,1,0:T(8,128)(2,1)S(1)}, u32[]{:S(2)}, u32[]{:S(2)}) async-start(bf16[24,8,4224]{2,1,0:T(8,128)(2,1)} %bitcast.77), calls=%async_computation | async-start | bytes 3244032 | tf_op jit(solution)/shard_map/all_to_all | solution.py:332
  27.7 12.9 %copy-start.1 = (bf16[4096,64]{0,1:T(8,128)(2,1)S(1)}, bf16[4096,64]{0,1:T(8,128)(2,1)}, u32[]{:S(2)}) copy-start(bf16[4096,64]{0,1:T(8,128)(2,1)} %param.14) | copy-start | bytes 1572868
  27.7 12.9 %copy-start.3 = (bf16[64,4096]{1,0:T(8,128)(2,1)S(1)}, bf16[64,4096]{1,0:T(8,128)(2,1)}, u32[]{:S(2)}) copy-start(bf16[64,4096]{1,0:T(8,128)(2,1)} %refs_10_.1) | copy-start | bytes 1572868
  27.7 12.9 %copy-start.4 = (bf16[64,4096]{1,0:T(8,128)(2,1)S(1)}, bf16[64,4096]{1,0:T(8,128)(2,1)}, u32[]{:S(2)}) copy-start(bf16[64,4096]{1,0:T(8,128)(2,1)} %refs_7_.1) | copy-start | bytes 1572868
  27.7 12.9 %copy-start.9 = (bf16[64,4096]{1,0:T(8,128)(2,1)S(1)}, bf16[64,4096]{1,0:T(8,128)(2,1)}, u32[]{:S(2)}) copy-start(bf16[64,4096]{1,0:T(8,128)(2,1)} %refs_2_.3) | copy-start | bytes 1572868
  27.7 12.9 %copy-start.11 = (s32[64,32]{0,1:T(8,128)S(1)}, s32[64,32]{0,1:T(8,128)}, u32[]{:S(2)}) copy-start(s32[64,32]{0,1:T(8,128)} %param.17) | copy-start | bytes 24580
  29.1 19.4 %collective-permute-start = (bf16[8,8,2176]{2,1,0:T(8,128)(2,1)S(1)}, bf16[8,8,2176]{2,1,0:T(8,128)(2,1)S(1)}, u32[]{:S(2)}, u32[]{:S(2)}) collective-permute-start(bf16[8,8,2176]{2,1,0:T(8,128)(2,1)S(1)} %get-tuple-element.59), channel_id=1, source_target_pairs={{0,8},{1,9},{2,10},{3,11},{4,12},{5,13},{6,14},{7,15},{8,16},{9,17... | collective-permute-start | bytes 835592 | tf_op jit(solution)/shard_map/ppermute | solution.py:344
  32.2 16.2 %collective-permute-start.1 = (bf16[8,8,2176]{2,1,0:T(8,128)(2,1)S(1)}, bf16[8,8,2176]{2,1,0:T(8,128)(2,1)S(1)}, u32[]{:S(2)}, u32[]{:S(2)}) collective-permute-start(bf16[8,8,2176]{2,1,0:T(8,128)(2,1)S(1)} %get-tuple-element.58), channel_id=1, source_target_pairs={{0,16},{1,17},{2,18},{3,19},{4,20},{5,21},{6,22},{7,23},{8,24},{9,... | collective-permute-start | bytes 835592 | tf_op jit(solution)/shard_map/ppermute | solution.py:344
  36.6 11.8 %collective-permute-start.2 = (bf16[8,8,2176]{2,1,0:T(8,128)(2,1)S(1)}, bf16[8,8,2176]{2,1,0:T(8,128)(2,1)S(1)}, u32[]{:S(2)}, u32[]{:S(2)}) collective-permute-start(bf16[8,8,2176]{2,1,0:T(8,128)(2,1)S(1)} %get-tuple-element.57), channel_id=1, source_target_pairs={{0,24},{1,25},{2,26},{3,27},{4,28},{5,29},{6,30},{7,31},{8,0},{9,1... | collective-permute-start | bytes 835592 | tf_op jit(solution)/shard_map/ppermute | solution.py:344
  42.6 13.4 %copy-start.16 = (bf16[64,4096]{1,0:T(8,128)(2,1)}, bf16[64,4096]{1,0:T(8,128)(2,1)S(1)}, u32[]{:S(2)}) copy-start(bf16[64,4096]{1,0:T(8,128)(2,1)S(1)} %get-tuple-element.28.refs_2_) | copy-start | bytes 1572868
  48.5 20.7 %collective-permute-start.3 = (bf16[32,2176]{1,0:T(8,128)(2,1)S(1)}, bf16[32,2176]{1,0:T(8,128)(2,1)S(1)}, u32[]{:S(2)}, u32[]{:S(2)}) collective-permute-start(bf16[32,2176]{1,0:T(8,128)(2,1)S(1)} %pad_maximum_fusion), channel_id=1, source_target_pairs={{0,1},{1,2},{2,3},{3,4},{4,5},{5,6},{6,7},{7,0},{8,9},{9,10},{10,1... | collective-permute-start | bytes 417800 | tf_op jit(solution)/shard_map/ppermute | solution.py:350
  51.8 22.5 %collective-permute-start.4 = (bf16[32,2176]{1,0:T(8,128)(2,1)S(1)}, bf16[32,2176]{1,0:T(8,128)(2,1)S(1)}, u32[]{:S(2)}, u32[]{:S(2)}) collective-permute-start(bf16[32,2176]{1,0:T(8,128)(2,1)S(1)} %pad_maximum_fusion.1), channel_id=1, source_target_pairs={{0,2},{1,3},{2,4},{3,5},{4,6},{5,7},{6,0},{7,1},{8,10},{9,11},{10,... | collective-permute-start | bytes 417800 | tf_op jit(solution)/shard_map/ppermute | solution.py:350
  56.0 21.3 %collective-permute-start.5 = (bf16[32,2176]{1,0:T(8,128)(2,1)S(1)}, bf16[32,2176]{1,0:T(8,128)(2,1)S(1)}, u32[]{:S(2)}, u32[]{:S(2)}) collective-permute-start(bf16[32,2176]{1,0:T(8,128)(2,1)S(1)} %pad_maximum_fusion.2), channel_id=1, source_target_pairs={{0,3},{1,4},{2,5},{3,6},{4,7},{5,0},{6,1},{7,2},{8,11},{9,12},{10,... | collective-permute-start | bytes 417800 | tf_op jit(solution)/shard_map/ppermute | solution.py:350
  60.7 16.8 %collective-permute-start.6 = (bf16[32,2176]{1,0:T(8,128)(2,1)S(1)}, bf16[32,2176]{1,0:T(8,128)(2,1)S(1)}, u32[]{:S(2)}, u32[]{:S(2)}) collective-permute-start(bf16[32,2176]{1,0:T(8,128)(2,1)S(1)} %pad_maximum_fusion.3), channel_id=1, source_target_pairs={{0,4},{1,5},{2,6},{3,7},{4,0},{5,1},{6,2},{7,3},{8,12},{9,13},{10,... | collective-permute-start | bytes 417800 | tf_op jit(solution)/shard_map/ppermute | solution.py:350
  64.3 18.7 %collective-permute-start.7 = (bf16[32,2176]{1,0:T(8,128)(2,1)S(1)}, bf16[32,2176]{1,0:T(8,128)(2,1)S(1)}, u32[]{:S(2)}, u32[]{:S(2)}) collective-permute-start(bf16[32,2176]{1,0:T(8,128)(2,1)S(1)} %pad_maximum_fusion.4), channel_id=1, source_target_pairs={{0,5},{1,6},{2,7},{3,0},{4,1},{5,2},{6,3},{7,4},{8,13},{9,14},{10,... | collective-permute-start | bytes 417800 | tf_op jit(solution)/shard_map/ppermute | solution.py:350
  69.2 22.1 %copy-start.18 = (s32[64]{0:T(128)S(1)}, s32[64]{0:T(128)}, u32[]{:S(2)}) copy-start(s32[64]{0:T(128)} %param.16) | copy-start | bytes 772
  69.3 19.7 %collective-permute-start.8 = (bf16[32,2176]{1,0:T(8,128)(2,1)S(1)}, bf16[32,2176]{1,0:T(8,128)(2,1)S(1)}, u32[]{:S(2)}, u32[]{:S(2)}) collective-permute-start(bf16[32,2176]{1,0:T(8,128)(2,1)S(1)} %pad_maximum_fusion.5), channel_id=1, source_target_pairs={{0,6},{1,7},{2,0},{3,1},{4,2},{5,3},{6,4},{7,5},{8,14},{9,15},{10,... | collective-permute-start | bytes 417800 | tf_op jit(solution)/shard_map/ppermute | solution.py:350
  74.3 16.0 %collective-permute-start.9 = (bf16[32,2176]{1,0:T(8,128)(2,1)S(1)}, bf16[32,2176]{1,0:T(8,128)(2,1)S(1)}, u32[]{:S(2)}, u32[]{:S(2)}) collective-permute-start(bf16[32,2176]{1,0:T(8,128)(2,1)S(1)} %pad_maximum_fusion.6), channel_id=1, source_target_pairs={{0,7},{1,0},{2,1},{3,2},{4,3},{5,4},{6,5},{7,6},{8,15},{9,8},{10,9... | collective-permute-start | bytes 417800 | tf_op jit(solution)/shard_map/ppermute | solution.py:350
  90.3 1.0 copy-start.13
  91.3 1.2 copy-start.14
  92.6 1.0 copy-start.17
  93.6 25.8 %copy-start.6 = (bf16[64,4096]{1,0:T(8,128)(2,1)S(1)}, bf16[64,4096]{1,0:T(8,128)(2,1)}, u32[]{:S(2)}) copy-start(bf16[64,4096]{1,0:T(8,128)(2,1)} %refs_8_.1) | copy-start | bytes 1572868
  121.0 3.9 %collective-permute-start.10 = (bf16[32,64,128]{2,1,0:T(8,128)(2,1)S(1)}, bf16[32,64,128]{2,1,0:T(8,128)(2,1)S(1)}, u32[]{:S(2)}, u32[]{:S(2)}) collective-permute-start(bf16[32,64,128]{2,1,0:T(8,128)(2,1)S(1)} %get-tuple-element.44), channel_id=1, source_target_pairs={{0,32},{32,0},{64,96},{96,64},{128,160},{160,128},{192,224},{224,1... | collective-permute-start | bytes 1572872 | tf_op jit(solution)/shard_map/ppermute | solution.py:448
  183.3 8.9 %collective-permute-start.11 = (bf16[32,72,128]{2,1,0:T(8,128)(2,1)S(1)}, bf16[32,72,128]{2,1,0:T(8,128)(2,1)S(1)}, u32[]{:S(2)}, u32[]{:S(2)}) collective-permute-start(bf16[32,72,128]{2,1,0:T(8,128)(2,1)S(1)} %all_to_all.28.mine_ref), channel_id=1, source_target_pairs={{0,32},{32,0},{64,96},{96,64},{128,160},{160,128},{192,224},{224,1... | collective-permute-start | bytes 1769480 | tf_op jit(solution)/shard_map/ppermute | solution.py:460

commit v2 on v1

v2 whole, which is shorter than its diff:
```python
import math

import jax
import jax.numpy as jnp
from jax import lax
from jax.experimental import pallas as pl
from jax.experimental.pallas import tpu as pltpu
from jax.sharding import PartitionSpec as P

f32 = jnp.float32
bf16 = jnp.bfloat16
adapter_scale = 2.0
logit_divisor = 0.05
epsilon = 1e-06
offset = 1.0 / logit_divisor
tile = 512
lanes = 128


def dot(a, b, ca=1, cb=0):
    return lax.dot_general(a, b, (((ca,), (cb,)), ((), ())), preferred_element_type=f32)


def iota(shape, dim):
    return lax.broadcasted_iota(jnp.int32, shape, dim)


def eye(n, m):
    return (iota((n, m), 0) == iota((n, m), 1)).astype(bf16)


def flip(a):
    return dot(eye(a.shape[1], a.shape[1]), a, 1, 1).astype(bf16)


def column_tiles(width):
    step = min(tile, width)
    return [slice(c, c + step) for c in range(0, width, step)]


def embed(x_ref, base_ref, down_ref, up_ref, unit_ref, ext_ref, inv_ref, raw_ref, ready=None):
    rows, width = x_ref.shape
    rank = up_ref.shape[0]
    latent = dot(x_ref[...], down_ref[...], 1, 1).astype(bf16)
    if ready is not None:
        ready()
    squares = jnp.zeros((rows, 1), f32)
    for cols in column_tiles(width):
        raw = base_ref[:, cols].astype(f32) + adapter_scale * dot(latent, up_ref[:, cols])
        raw_ref[:, cols] = raw
        squares = squares + jnp.sum(raw * raw, axis=1, keepdims=True)
    inverse = lax.rsqrt(squares + epsilon)
    for cols in column_tiles(width):
        unit_ref[:, cols] = (raw_ref[:, cols] * inverse).astype(bf16)
    scaled = (latent.astype(f32) * inverse).astype(bf16)
    high = inverse.astype(bf16).astype(f32)
    lane = iota((rows, lanes), 1)
    ext = dot(scaled, eye(rank, lanes))
    ext = jnp.where(lane == rank, high, ext)
    ext = jnp.where(lane == rank + 1, inverse - high, ext)
    ext_ref[...] = ext.astype(bf16)
    inv_ref[...] = jnp.broadcast_to(inverse, inv_ref.shape)


def passage_kernel(
    grid_x, grid_y, place_ref, x_hbm, base_hbm, down_hbm, up_hbm, near_ids_hbm, far_ids_hbm, *refs
):
    near_ref, *far_refs = refs[: 1 + grid_y]
    unit_ref, ext_ref, inv_ref, pick_ref = refs[1 + grid_y : 5 + grid_y]
    (x_ref, base_ref, down_ref, up_ref, near_ids_ref, far_ids_ref, raw_ref, sems) = refs[5 + grid_y :]
    pairs = [
        (x_hbm, x_ref), (down_hbm, down_ref), (base_hbm, base_ref), (up_hbm, up_ref),
        (near_ids_hbm, near_ids_ref), (far_ids_hbm, far_ids_ref),
    ]
    copies = [pltpu.make_async_copy(a, b, sems.at[i]) for i, (a, b) in enumerate(pairs)]
    for c in copies:
        c.start()
    copies[0].wait()
    copies[1].wait()

    def ready():
        copies[2].wait()
        copies[3].wait()

    embed(x_ref, base_ref, down_ref, up_ref, unit_ref, ext_ref, inv_ref, raw_ref, ready)
    copies[4].wait()
    copies[5].wait()
    rows, width = x_ref.shape
    half = width // 2
    per_near, n_near = near_ids_ref.shape
    count = per_near * n_near
    ids = near_ids_ref[...].astype(f32).astype(bf16)
    spread = (iota((count, n_near), 0) // per_near == iota((count, n_near), 1)).astype(bf16)
    table = dot(spread, ids, 1, 1)
    mine = iota((count, per_near), 0) % per_near == iota((count, per_near), 1)
    wanted = jnp.sum(jnp.where(mine, table, 0.0), axis=1, keepdims=True).astype(jnp.int32)
    pick = (iota((count, rows), 1) == wanted).astype(bf16)
    pick_ref[...] = pick
    for cols in column_tiles(width):
        near_ref[:, cols] = dot(pick, unit_ref[:, cols]).astype(bf16)
    near_ref[:, width:] = dot(pick, ext_ref[...]).astype(bf16)
    n_far = far_ids_ref.shape[1]
    total = n_far * 8
    size = grid_x * 8
    where_x, where_y = place_ref[0], place_ref[1]
    ids = far_ids_ref[...].astype(f32).astype(bf16)
    block = iota((total, n_far), 0) // 8
    to_x = (where_x + block % grid_x) % grid_x
    to_y = (where_y + block // grid_x) % grid_y
    spread = (to_x * grid_y + to_y == iota((total, n_far), 1)).astype(bf16)
    table = dot(spread, ids, 1, 1)
    mine = iota((total, 2), 0) % 2 == iota((total, 2), 1)
    wanted = jnp.sum(jnp.where(mine, table, 0.0), axis=1, keepdims=True).astype(jnp.int32)
    kind = (iota((total, 4 * rows), 0) // 2) % 4
    source = iota((total, 4 * rows), 1)
    choose = ((source // rows == kind) & (source % rows == wanted)).astype(bf16)
    for cols in column_tiles(half):
        later = slice(half + cols.start, half + cols.stop)
        stack = jnp.concatenate(
            [unit_ref[:, cols], unit_ref[:, later], x_ref[:, cols], x_ref[:, later]], axis=0
        )
        got = dot(choose, stack).astype(bf16)
        for dy in range(grid_y):
            far_refs[dy][:, cols] = got[dy * size : (dy + 1) * size]
    first = jnp.where(iota((total, rows), 0) // 2 % 4 == 0, wanted, -1)
    got = dot((iota((total, rows), 1) == first).astype(bf16), ext_ref[...]).astype(bf16)
    for dy in range(grid_y):
        far_refs[dy][:, half:] = got[dy * size : (dy + 1) * size]


def query_kernel(
    grid_x, grid_y, place_ref, x_ref, base_ref, down_ref, up_ref, slots_ref,
    unit_ref, ext_ref, inv_ref, near_count_ref, other_count_ref, raw_ref,
):
    embed(x_ref, base_ref, down_ref, up_ref, unit_ref, ext_ref, inv_ref, raw_ref)
    hard, rows = slots_ref.shape
    n_near = near_count_ref.shape[0]
    n_other = other_count_ref.shape[0]
    n_far = n_other - rows
    where_x, where_y = place_ref[0], place_ref[1]
    near_slot = iota((n_near, rows), 0)
    spot = iota((n_other, rows), 0)
    block = spot // 2
    from_x = (where_x + grid_x - (block // grid_y) % grid_x) % grid_x
    from_y = (where_y + grid_y - block % grid_y) % grid_y
    far_slot = n_near + (from_x * grid_y + from_y) * 2 + spot % 2
    far_slot = jnp.where(spot < n_far, far_slot, -1)
    near_count = jnp.zeros((n_near, rows), f32)
    other_count = jnp.zeros((n_other, rows), f32)
    for k in range(hard):
        slot = slots_ref[k : k + 1, :]
        near_count = near_count + (near_slot == slot).astype(f32)
        other_count = other_count + (far_slot == slot).astype(f32)
    near_count_ref[...] = near_count
    other_count_ref[...] = jnp.where(spot < n_far, other_count, 1.0)


def store_blocks(ref, cols, value):
    size = ref.shape[2]
    step = min(size, cols.stop - cols.start)
    for c in range(cols.start, cols.stop, step):
        at = c % size
        ref[c // size, :, at : at + step] = value[:, c - cols.start : c - cols.start + step]


def load_blocks(ref, cols):
    size = ref.shape[2]
    step = min(size, cols.stop - cols.start)
    parts = []
    for c in range(cols.start, cols.stop, step):
        parts.append(ref[c // size, :, c % size : c % size + step])
    return parts[0] if len(parts) == 1 else jnp.concatenate(parts, axis=1)


def far_kernel(count, *refs):
    far_refs = refs[:count]
    q_ref, unit_ref, p_ext_ref, positive_ref = refs[count : count + 4]
    o_ref, ext_ref, x_far_ref, raw_ref = refs[count + 4 :]
    rows, width = q_ref.shape
    half = width // 2
    total = far_refs[0].shape[0]
    each = total // 4
    n_far = each * count
    out_row = iota((total, total), 0)
    in_row = iota((total, total), 1)
    spot = out_row % each
    undo = (
        (in_row // 8 == spot // 2)
        & (in_row % 2 == spot % 2)
        & ((in_row // 2) % 4 == out_row // each)
    ).astype(bf16)
    for i, far_ref in enumerate(far_refs):
        at = slice(i * each, (i + 1) * each)
        for cols in column_tiles(half):
            later = slice(half + cols.start, half + cols.stop)
            got = dot(undo, far_ref[:, cols]).astype(bf16)
            o_ref[at, cols] = got[0:each]
            o_ref[at, later] = got[each : 2 * each]
            x_far_ref[at, cols] = got[2 * each : 3 * each]
            x_far_ref[at, later] = got[3 * each :]
        ext_ref[at, :] = dot(undo[0:each], far_ref[:, half:]).astype(bf16)
    own = (iota((rows, rows), 0) == positive_ref[...]).astype(bf16)
    own_t = flip(own)
    for cols in column_tiles(width):
        o_ref[n_far:, cols] = dot(own_t, unit_ref[:, cols]).astype(bf16)
    ext_ref[n_far:, :] = dot(own_t, p_ext_ref[...]).astype(bf16)
    raw_ref[...] = dot(o_ref[...], q_ref[...], 1, 1)


def score_kernel(
    slope, rank, near_ref, q_ref, other_raw_hbm, near_count_ref, other_count_ref, up_ref,
    ret_ref, near_g_ref, other_g_ref, near_radial_ref, other_radial_ref, q_radial_ref,
    other_raw_ref, sem,
):
    copy = pltpu.make_async_copy(other_raw_hbm, other_raw_ref, sem)
    copy.start()
    rows, width = q_ref.shape
    n_near = near_ref.shape[0]
    near_raw = dot(near_ref[:, :width], q_ref[...], 1, 1)
    copy.wait()
    other_raw = other_raw_ref[...]
    n_far = other_raw.shape[0] - rows
    near_exp = jnp.exp(near_raw / logit_divisor - offset) * near_count_ref[...]
    other_exp = jnp.exp(other_raw / logit_divisor - offset) * other_count_ref[...]
    partition = jnp.sum(near_exp, axis=0, keepdims=True) + jnp.sum(
        other_exp, axis=0, keepdims=True
    )
    same = iota(other_raw.shape, 0) == iota(other_raw.shape, 1) + n_far
    matched = jnp.sum(jnp.where(same, other_raw, 0.0), axis=0, keepdims=True) / logit_divisor
    loss = jnp.sum(jnp.log(partition) + offset - matched, axis=1, keepdims=True)
    near_g = (near_exp / partition * slope).astype(bf16)
    other_g = ((other_exp / partition - same.astype(f32)) * slope).astype(bf16)
    near_g_ref[...] = near_g
    other_g_ref[...] = other_g
    near_part = near_g.astype(f32) * near_raw
    other_part = other_g.astype(f32) * other_raw
    near_radial = jnp.sum(near_part, axis=1, keepdims=True)
    near_radial_ref[...] = near_radial
    other_radial_ref[...] = jnp.sum(other_part, axis=1, keepdims=True)
    q_radial = jnp.sum(near_part, axis=0, keepdims=True) + jnp.sum(
        other_part, axis=0, keepdims=True
    )
    square = iota((rows, rows), 0) == iota((rows, rows), 1)
    q_radial_ref[...] = jnp.sum(jnp.where(square, q_radial, 0.0), axis=1, keepdims=True)
    back = jnp.zeros((n_near, rank), f32)
    for cols in column_tiles(width):
        tangent = dot(near_g, q_ref[:, cols]) - near_ref[:, cols].astype(f32) * near_radial
        back = back + dot(tangent.astype(bf16), up_ref[:, cols], 1, 1)
    back = dot(back.astype(bf16), eye(rank, lanes))
    lane = iota((n_near, lanes), 1)
    high = loss.astype(bf16).astype(f32)
    back = jnp.where(lane == rank, high, back)
    back = jnp.where(lane == rank + 1, loss - high, back)
    ret_ref[...] = back.astype(bf16)


def local_kernel(
    place_ref, near_ref, o_ref, o_ext_ref, x_far_ref, q_ref, q_ext_ref, q_inv_ref, p_inv_ref, x_q_ref,
    positive_ref, near_g_ref, other_g_ref, near_radial_ref, other_radial_ref, q_radial_ref, up_ref,
    up_keep_ref, up_send_ref, down_ref, row_ref,
):
    rows, width = q_ref.shape
    rank = up_ref.shape[0]
    part = rank // 2
    n_far = o_ref.shape[0] - rows
    even = place_ref[2] == 0
    near_gt, other_gt = near_g_ref[...], other_g_ref[...]
    near_g, other_g = flip(near_gt), flip(other_gt)
    q_lat = flip(q_ext_ref[...])[0:rank]
    near_lat = flip(near_ref[:, width:])[0:rank]
    other_lat = flip(o_ext_ref[...])[0:rank]
    q_back = jnp.zeros((rows, rank), f32)
    other_back = jnp.zeros((n_far + rows, rank), f32)
    for cols in column_tiles(width):
        q = q_ref[:, cols]
        near = near_ref[:, cols]
        other = o_ref[:, cols]
        up = up_ref[:, cols]
        q_t = dot(near_g, near) + dot(other_g, other) - q.astype(f32) * q_radial_ref[...]
        near_t = dot(near_gt, q) - near.astype(f32) * near_radial_ref[...]
        other_t = dot(other_gt, q) - other.astype(f32) * other_radial_ref[...]
        q_t, near_t, other_t = q_t.astype(bf16), near_t.astype(bf16), other_t.astype(bf16)
        q_back = q_back + dot(q_t, up, 1, 1)
        other_back = other_back + dot(other_t, up, 1, 1)
        grad = dot(q_lat, q_t) + dot(near_lat, near_t) + dot(other_lat, other_t)
        grad = adapter_scale * grad
        top, low = grad[0:part], grad[part:]
        store_blocks(up_keep_ref, cols, jnp.where(even, top, low))
        store_blocks(up_send_ref, cols, jnp.where(even, low, top).astype(bf16))
    other_back = other_back.astype(bf16)
    own = (iota((rows, rows), 0) == positive_ref[...]).astype(bf16)
    wide = dot(other_back[n_far:], eye(rank, lanes)).astype(bf16)
    row_sum = dot(own, wide)
    row_ref[...] = jnp.where(iota(row_sum.shape, 1) < rank, row_sum, p_inv_ref[...])
    q_back = q_back.astype(bf16).astype(f32)
    dz_q = (adapter_scale * q_inv_ref[:, 0:1] * q_back).astype(bf16)
    far_ext = o_ext_ref[0:n_far, :].astype(f32)
    far_inv = far_ext[:, rank : rank + 1] + far_ext[:, rank + 1 : rank + 2]
    dz_f = (adapter_scale * far_inv * other_back[0:n_far].astype(f32)).astype(bf16)
    dz_qt, dz_ft = flip(dz_q), flip(dz_f)
    for cols in column_tiles(width):
        down_ref[:, cols] = dot(dz_qt, x_q_ref[:, cols]) + dot(dz_ft, x_far_ref[:, cols])


def down_kernel(
    per_near, place_ref, ret_ref, pick_ref, row_hbm, x_p_ref, down_hbm,
    keep_ref, send_ref, loss_ref, row_ref, down_ref, sems,
):
    row_copy = pltpu.make_async_copy(row_hbm, row_ref, sems.at[0])
    down_copy = pltpu.make_async_copy(down_hbm, down_ref, sems.at[1])
    row_copy.start()
    down_copy.start()
    rank = down_ref.shape[0]
    part = rank // 2
    ret = ret_ref[...]
    row_sum = dot(flip(pick_ref[...]), ret)[:, 0:rank]
    row_copy.wait()
    row_sum = row_sum + row_ref[:, 0:rank]
    dz_t = flip((adapter_scale * row_ref[:, rank : rank + 1] * row_sum).astype(bf16))
    down_copy.wait()
    even = place_ref[2] == 0
    for cols in column_tiles(x_p_ref.shape[1]):
        grad = dot(dz_t, x_p_ref[:, cols]) + down_ref[:, cols]
        top, low = grad[0:part], grad[part:]
        store_blocks(keep_ref, cols, jnp.where(even, top, low))
        store_blocks(send_ref, cols, jnp.where(even, low, top).astype(bf16))
    first = iota(ret.shape, 0) % per_near == 0
    lane = iota(ret.shape, 1)
    chosen = first & ((lane == rank) | (lane == rank + 1))
    share = jnp.sum(jnp.where(chosen, ret.astype(f32), 0.0), axis=1, keepdims=True)
    loss_ref[...] = jnp.broadcast_to(jnp.sum(share, axis=0, keepdims=True), loss_ref.shape)


def add_kernel(down_ref, got_down_ref, up_ref, got_up_ref, out_ref):
    part = down_ref.shape[1]
    for i in range(down_ref.shape[0]):
        out_ref[i, 0:part] = (down_ref[i] + got_down_ref[i].astype(f32)).astype(bf16)
        out_ref[i, part:] = (up_ref[i] + got_up_ref[i].astype(f32)).astype(bf16)


def sum_blocks(ref, *at):
    acc = ref[(0, *at)].astype(f32)
    for i in range(1, ref.shape[0]):
        acc = acc + ref[(i, *at)].astype(f32)
    return acc


def sum_kernel(in_ref, out_ref):
    for j in range(out_ref.shape[0]):
        out_ref[j] = sum_blocks(in_ref, j).astype(bf16)


def spread_kernel(in_ref, out_ref):
    value = sum_blocks(in_ref).astype(bf16)
    for i in range(out_ref.shape[0]):
        out_ref[i] = value


def copy_kernel(in_ref, out_ref):
    for i in range(out_ref.shape[0]):
        out_ref[i] = in_ref[...]


def finish_kernel(in_ref, loss_ref, out_ref):
    loss = loss_ref[...]
    high = loss.astype(bf16).astype(f32)
    row = iota(loss.shape, 0)
    tail = jnp.where(row == 0, high, jnp.where(row == 1, loss - high, 0.0))
    if out_ref.shape[2] > lanes:
        tail = jnp.concatenate([tail] * (out_ref.shape[2] // lanes), axis=1)
    value = jnp.concatenate([sum_blocks(in_ref), tail], axis=0).astype(bf16)
    for i in range(out_ref.shape[0]):
        out_ref[i] = value


def output_kernel(queries, place_ref, mine_ref, other_ref, down_ref, up_ref, loss_ref):
    rank = down_ref.shape[0]
    part = rank // 2
    size = mine_ref.shape[3]
    even = place_ref[2] == 0
    loss = jnp.zeros((8, lanes), f32)
    for i in range(mine_ref.shape[0]):
        for j in range(mine_ref.shape[1]):
            mine, other = mine_ref[i, j].astype(f32), other_ref[i, j].astype(f32)
            at = (i * mine_ref.shape[1] + j) * size
            cols = slice(at, at + size)
            top = jnp.where(even, mine[0:rank], other[0:rank])
            low = jnp.where(even, other[0:rank], mine[0:rank])
            down_ref[0:part, cols] = top[0:part]
            down_ref[part:, cols] = low[0:part]
            up_ref[0:part, cols] = top[part:]
            up_ref[part:, cols] = low[part:]
            loss = loss + mine[rank:, 0:lanes]
    loss_ref[...] = jnp.sum(loss, axis=0, keepdims=True)[:, 0:1] / queries


def call(kernel, outs, args, scratch=(), flops=0, moved=0, hbm=(), out_hbm=(), limit=16):
    specs = []
    for i, a in enumerate(args):
        space = pltpu.SMEM if a.dtype == jnp.int32 and a.ndim == 1 else pltpu.VMEM
        specs.append(pl.BlockSpec(memory_space=pltpu.HBM if i in hbm else space))
    args = [
        pltpu.with_memory_space_constraint(a, pltpu.HBM) if i in hbm else a
        for i, a in enumerate(args)
    ]
    shapes = [
        pltpu.HBM(s, d) if i in out_hbm else jax.ShapeDtypeStruct(s, d)
        for i, (s, d) in enumerate(outs)
    ]
    return pl.pallas_call(
        kernel,
        out_shape=shapes,
        in_specs=specs,
        out_specs=[pl.BlockSpec(memory_space=pltpu.VMEM) for _ in shapes],
        scratch_shapes=[pltpu.VMEM(*s) if isinstance(s, tuple) else s for s in scratch],
        compiler_params=pltpu.CompilerParams(vmem_limit_bytes=limit * 1024 * 1024),
        cost_estimate=pl.CostEstimate(flops=flops, bytes_accessed=moved, transcendentals=0),
    )(*args)


def exchange(x, axis, groups=None):
    return lax.all_to_all(
        x, axis, split_axis=0, concat_axis=0, tiled=True, axis_index_groups=groups
    )


def far_exchange(pieces, grid_x, grid_y):
    group = [(x, y) for x in range(grid_x) for y in range(grid_y)]
    got = [pieces[0]]
    for dy in range(1, grid_y):
        pairs = [(x * grid_y + y, x * grid_y + (y + dy) % grid_y) for x, y in group]
        got.append(lax.ppermute(pieces[dy], "group", pairs))
    ended = []
    for dx in range(grid_x):
        piece = jnp.concatenate([g[dx * 8 : (dx + 1) * 8] for g in got], axis=0)
        if dx:
            pairs = [(x * grid_y + y, (x + dx) % grid_x * grid_y + y) for x, y in group]
            piece = lax.ppermute(piece, "group", pairs)
        ended.append(piece)
    return ended


def make_body(grid_x, grid_y):
    def body(
        query_layer_input,
        query_frozen_base,
        passage_layer_input,
        passage_frozen_base,
        adapter_down_weight,
        adapter_up_weight,
        positive_passage_index,
        hard_negative_slots,
        group_peer_rows,
        remote_group_rows,
    ):
        n_dp = lax.axis_size("dp")
        n_group = lax.axis_size("group")
        rows, width = query_layer_input.shape
        rank = adapter_up_weight.shape[0]
        part = rank // 2
        queries = rows * n_dp * n_group
        slope = 16.0 / math.sqrt(queries) / logit_divisor
        g = lax.axis_index("group")
        place = jnp.stack([g // grid_y, g % grid_y, lax.axis_index("dp") % 2]).astype(jnp.int32)
        down_t = adapter_down_weight.T
        near_ids, far_ids = group_peer_rows.T, remote_group_rows.T
        per_near = group_peer_rows.shape[1]
        n_near = n_dp * per_near
        n_far = n_group * 2
        n_other = n_far + rows
        half = width // 2
        block = width // n_group
        near, *rest = call(
            lambda *refs: passage_kernel(grid_x, grid_y, *refs),
            [((n_near, width + lanes), bf16)]
            + [((grid_x * 8, half + lanes), bf16)] * grid_y
            + [
                ((rows, width), bf16),
                ((rows, lanes), bf16),
                ((rows, lanes), f32),
                ((n_near, rows), bf16),
            ],
            (
                place, passage_layer_input, passage_frozen_base, down_t, adapter_up_weight,
                near_ids, far_ids,
            ),
            [
                ((rows, width), bf16),
                ((rows, width), bf16),
                (down_t.shape, bf16),
                (adapter_up_weight.shape, bf16),
                (near_ids.shape, jnp.int32),
                (far_ids.shape, jnp.int32),
                ((rows, width), f32),
                pltpu.SemaphoreType.DMA((6,)),
            ],
            flops=400_000_000, moved=6_000_000, hbm=range(1, 7),
        )
        far, (p_unit, p_ext, p_inv, pick) = rest[:grid_y], rest[grid_y:]
        near = exchange(near.reshape(n_dp, per_near, width + lanes), "dp")
        near = near.reshape(n_near, width + lanes)
        far = far_exchange(far, grid_x, grid_y)
        q_unit, q_ext, q_inv, near_count, other_count = call(
            lambda *refs: query_kernel(grid_x, grid_y, *refs),
            [
                ((rows, width), bf16),
                ((rows, lanes), bf16),
                ((rows, lanes), f32),
                ((n_near, rows), f32),
                ((n_other, rows), f32),
            ],
            (
                place, query_layer_input, query_frozen_base, down_t, adapter_up_weight,
                hard_negative_slots.T,
            ),
            [((rows, width), f32)], flops=100_000_000, moved=3_000_000,
        )
        positive = positive_passage_index.reshape(1, rows)
        other, other_ext, x_far, other_raw = call(
            lambda *refs: far_kernel(grid_x, *refs),
            [
                ((n_other, width), bf16),
                ((n_other, lanes), bf16),
                ((n_far, width), bf16),
                ((n_other, rows), f32),
            ],
            (*far, q_unit, p_unit, p_ext, positive),
            flops=300_000_000, moved=4_000_000, out_hbm=(3,),
        )
        ret, near_g, other_g, near_radial, other_radial, q_radial = call(
            lambda *refs: score_kernel(slope, rank, *refs),
            [
                ((n_near, lanes), bf16),
                ((n_near, rows), bf16),
                ((n_other, rows), bf16),
                ((n_near, 1), f32),
                ((n_other, 1), f32),
                ((rows, 1), f32),
            ],
            (near, q_unit, other_raw, near_count, other_count, adapter_up_weight),
            [((n_other, rows), f32), pltpu.SemaphoreType.DMA(())],
            flops=300_000_000, moved=3_000_000, hbm=(2,),
        )
        ret = exchange(ret.reshape(n_dp, per_near, lanes), "dp").reshape(n_near, lanes)
        up_keep, up_send, down_part, row_part = call(
            local_kernel,
            [
                ((n_group, part, block), f32),
                ((n_group, part, block), bf16),
                ((rank, width), f32),
                ((rows, lanes), f32),
            ],
            (
                place, near, other, other_ext, x_far, q_unit, q_ext, q_inv, p_inv, query_layer_input,
                positive, near_g, other_g, near_radial, other_radial, q_radial, adapter_up_weight,
            ),
            flops=900_000_000, moved=9_000_000, out_hbm=(2, 3),
        )
        swap = [(i, i ^ 1) for i in range(n_dp)]
        up_got = lax.ppermute(up_send, "dp", swap)
        keep, send, loss = call(
            lambda *refs: down_kernel(per_near, *refs),
            [
                ((n_group, part, block), f32),
                ((n_group, part, block), bf16),
                ((8, lanes), f32),
            ],
            (place, ret, pick, row_part, passage_layer_input, down_part),
            [((rows, lanes), f32), ((rank, width), f32), pltpu.SemaphoreType.DMA((2,))],
            flops=100_000_000, moved=3_000_000, hbm=(3, 5),
        )
        got = lax.ppermute(send, "dp", swap)
        (sums,) = call(
            add_kernel,
            [((n_group, rank, block), bf16)],
            (keep, got, up_keep, up_got),
            moved=2_500_000,
        )
        cores = [list(range(c, n_dp, 2)) for c in range(2)]
        along_x = [[x * grid_y + y for x in range(grid_x)] for y in range(grid_y)]
        along_y = [[x * grid_y + y for y in range(grid_y)] for x in range(grid_x)]
        sums = exchange(sums.reshape(grid_x, grid_y, rank, block), "group", along_x)
        (sums,) = call(sum_kernel, [((grid_y, rank, block), bf16)], (sums,), moved=600_000)
        sums = exchange(sums, "group", along_y)
        (sums,) = call(
            spread_kernel, [((n_dp // 2, rank, block), bf16)], (sums,), moved=600_000
        )
        sums = exchange(sums, "dp", cores)
        (sums,) = call(
            finish_kernel, [((grid_y, rank + 8, block), bf16)], (sums, loss), moved=600_000
        )
        sums = exchange(sums, "group", along_y)
        (sums,) = call(
            copy_kernel, [((grid_x, grid_y, rank + 8, block), bf16)], (sums,), moved=600_000
        )
        sums = exchange(sums, "group", along_x)
        other_sums = lax.ppermute(sums, "dp", swap)
        down, up, loss = call(
            lambda *refs: output_kernel(queries, *refs),
            [((rank, width), f32), ((rank, width), f32), ((1, 1), f32)],
            (place, sums, other_sums),
            moved=3_500_000,
        )
        return (down.T, up, loss.reshape(()))

    return body


def solution(mesh):
    n_group = mesh.shape["group"]
    grid_x = {32: 4, 4: 2}[n_group]
    both = P(("dp", "group"), None)
    placed = (both, both, both, both, P(), P(), P(("dp", "group")), both, both, both)
    return jax.shard_map(
        make_body(grid_x, n_group // grid_x),
        mesh=mesh,
        in_specs=placed,
        out_specs=(P(), P(), P()),
        check_vma=False,
    )
```

time: 198 us -> 216 us (1.091)
  blocking collectives: 78.9 us -> 66.1 us
  starting transfers between devices: 65.4 us -> 75.8 us
  waiting for transfers between devices: 21.9 us -> 31.5 us
  Pallas kernels: 13.5 us -> 21.2 us
  local copies, waits for them, and re-layouts: 14 us -> 18.4 us
    ppermute x4 -> x9, starting transfers between devices: 17.9 us -> 40.2 us  [the longest x7 29.4 us: far_exchange(): got.append(lax.ppermute(pieces[dy], 'group', pairs))]
    all_to_all x1 -> x2, waiting for transfers between devices: 0.01 us -> 21.4 us  [exchange(): lax.all_to_all(x, axis, split_axis=0, concat_axis=0, tiled=True, axis_ind...]
    ppermute x7 -> x3, starting transfers between devices: 28.4 us -> 10.5 us  [far_exchange(): piece = lax.ppermute(piece, 'group', pairs)]
    all_to_all x4 -> x5, blocking collectives: 78.9 us -> 66.1 us  [exchange(): lax.all_to_all(x, axis, split_axis=0, concat_axis=0, tiled=True, axis_ind...]
    pallas_call x8 -> x12, Pallas kernels: 13.5 us -> 21.2 us  [call(): pl.pallas_call(kernel, out_shape=shapes, in_specs=specs, out_specs=[pl.Bl...]
    unnamed x47 -> x71, local copies, waits for them, and re-layouts: 11.2 us -> 18.4 us
    ppermute x7 -> x3, waiting for transfers between devices: 12.9 us -> 5.78 us  [far_exchange(): piece = lax.ppermute(piece, 'group', pairs)]
    all_to_all x1 -> x2, starting transfers between devices: 16.7 us -> 22.9 us  [exchange(): lax.all_to_all(x, axis, split_axis=0, concat_axis=0, tiled=True, axis_ind...]
  transfers between devices with their start and end apart: 13 -> 15, of which waited for: 7 -> 6; matrix products, arithmetic and copies ran while one was open for 1% -> 2% of each run, Pallas kernels for 1% -> 5%
where the time goes in v2:
time: 216 us; the launch traced here: 214 us
  starting transfers between devices  75.8 us (35%)
  blocking collectives  66.1 us (31%)
  waiting for transfers between devices  31.5 us (15%)
  Pallas kernels  21.2 us (10%)
  local copies, waits for them, and re-layouts  18.4 us (9%)
    all_to_all x5, blocking collectives, exchange(): lax.all_to_all(x, axis, split_axis=0, concat_axis=0, tiled=True, axis_ind...  66.1 us
    ppermute x7, starting transfers between devices, far_exchange(): got.append(lax.ppermute(pieces[dy], 'group', pairs))  29.4 us
    all_to_all x2, starting transfers between devices, exchange(): lax.all_to_all(x, axis, split_axis=0, concat_axis=0, tiled=True, axis_ind...  22.9 us
    all_to_all x2, waiting for transfers between devices, exchange(): lax.all_to_all(x, axis, split_axis=0, concat_axis=0, tiled=True, axis_ind...  21.4 us
    pallas_call x12, Pallas kernels, call(): pl.pallas_call(kernel, out_shape=shapes, in_specs=specs, out_specs=[pl.Bl...  21.2 us
    unnamed x71, local copies, waits for them, and re-layouts  18.4 us
    ppermute x3, starting transfers between devices, far_exchange(): piece = lax.ppermute(piece, 'group', pairs)  10.5 us
    ppermute x1, starting transfers between devices, body(): other_sums = lax.ppermute(sums, 'dp', swap)  8.58 us
  transfers between devices with their start and end apart: 15, of which 6 were waited for; matrix products, arithmetic and copies ran while one was open for 2% of the time, Pallas kernels for 5%

profile of v2, /device:TPU:1, one launch (start us, length us, event | category | flops | bytes accessed | tf_op | source)
XLA Modules:
  0.0 214.2 jit_solution(4683114786724843898)
XLA Ops:
  0.7 5.0 %shard_map.121 = (bf16[192,4224]{1,0:T(8,128)(2,1)}, bf16[32,2176]{1,0:T(8,128)(2,1)S(1)}, bf16[32,2176]{1,0:T(8,128)(2,1)}, bf16[32,2176]{1,0:T(8,128)(2,1)}, b...) custom-call(s32[3]{0:T(128)S(1)} %pad_add_fusion.refs_0_.place_ref, ...), custom_call_target="tpu_custom_call" | custom-call | flops 400000000 | bytes 6000000 | tf_op jit(solution)/shard_map/pallas_call | solution.py:410
  6.3 4.0 %collective-permute-start = (bf16[32,2176]{1,0:T(8,128)(2,1)}, bf16[32,2176]{1,0:T(8,128)(2,1)}, u32[]{:S(2)}, u32[]{:S(2)}) collective-permute-start(bf16[32,2176]{1,0:T(8,128)(2,1)} %get-tuple-element.44), channel_id=1, source_target_pairs={{0,1},{1,2},{2,3},{3,4},{4,5},{5,6},{6,7},{7,0},{8,9},{9,10},{10,1... | collective-permute-start | bytes 417800 | tf_op jit(solution)/shard_map/ppermute | solution.py:432
  10.4 4.2 %collective-permute-start.1 = (bf16[32,2176]{1,0:T(8,128)(2,1)}, bf16[32,2176]{1,0:T(8,128)(2,1)}, u32[]{:S(2)}, u32[]{:S(2)}) collective-permute-start(bf16[32,2176]{1,0:T(8,128)(2,1)} %get-tuple-element.45), channel_id=1, source_target_pairs={{0,2},{1,3},{2,4},{3,5},{4,6},{5,7},{6,0},{7,1},{8,10},{9,11},{10,... | collective-permute-start | bytes 417800 | tf_op jit(solution)/shard_map/ppermute | solution.py:432
  14.6 4.6 %collective-permute-start.2 = (bf16[32,2176]{1,0:T(8,128)(2,1)}, bf16[32,2176]{1,0:T(8,128)(2,1)}, u32[]{:S(2)}, u32[]{:S(2)}) collective-permute-start(bf16[32,2176]{1,0:T(8,128)(2,1)} %get-tuple-element.46), channel_id=1, source_target_pairs={{0,3},{1,4},{2,5},{3,6},{4,7},{5,0},{6,1},{7,2},{8,11},{9,12},{10,... | collective-permute-start | bytes 417800 | tf_op jit(solution)/shard_map/ppermute | solution.py:432
  19.2 3.5 %collective-permute-start.3 = (bf16[32,2176]{1,0:T(8,128)(2,1)}, bf16[32,2176]{1,0:T(8,128)(2,1)}, u32[]{:S(2)}, u32[]{:S(2)}) collective-permute-start(bf16[32,2176]{1,0:T(8,128)(2,1)} %get-tuple-element.47), channel_id=1, source_target_pairs={{0,4},{1,5},{2,6},{3,7},{4,0},{5,1},{6,2},{7,3},{8,12},{9,13},{10,... | collective-permute-start | bytes 417800 | tf_op jit(solution)/shard_map/ppermute | solution.py:432
  22.8 4.9 %collective-permute-start.4 = (bf16[32,2176]{1,0:T(8,128)(2,1)S(1)}, bf16[32,2176]{1,0:T(8,128)(2,1)}, u32[]{:S(2)}, u32[]{:S(2)}) collective-permute-start(bf16[32,2176]{1,0:T(8,128)(2,1)S(1)} %get-tuple-element.48), channel_id=1, source_target_pairs={{0,5},{1,6},{2,7},{3,0},{4,1},{5,2},{6,3},{7,4},{8,13},{9,14},{10,... | collective-permute-start | bytes 417800 | tf_op jit(solution)/shard_map/ppermute | solution.py:432
  27.7 17.3 %all-to-all-start = ((bf16[24,8,4224]{2,1,0:T(8,128)(2,1)}), bf16[24,8,4224]{2,1,0:T(8,128)(2,1)S(1)}, u32[]{:S(2)}, u32[]{:S(2)}) async-start(bf16[24,8,4224]{2,1,0:T(8,128)(2,1)} %bitcast.6), calls=%async_computation | async-start | bytes 3244032 | tf_op jit(solution)/shard_map/all_to_all | solution.py:422
  45.0 5.1 %collective-permute-start.5 = (bf16[32,2176]{1,0:T(8,128)(2,1)S(1)}, bf16[32,2176]{1,0:T(8,128)(2,1)S(1)}, u32[]{:S(2)}, u32[]{:S(2)}) collective-permute-start(bf16[32,2176]{1,0:T(8,128)(2,1)S(1)} %get-tuple-element.49), channel_id=1, source_target_pairs={{0,6},{1,7},{2,0},{3,1},{4,2},{5,3},{6,4},{7,5},{8,14},{9,15},{10,... | collective-permute-start | bytes 417800 | tf_op jit(solution)/shard_map/ppermute | solution.py:432
  50.1 0.8 constant_dynamic-update-slice_fusion.30
  51.0 3.0 %collective-permute-start.6 = (bf16[32,2176]{1,0:T(8,128)(2,1)S(1)}, bf16[32,2176]{1,0:T(8,128)(2,1)S(1)}, u32[]{:S(2)}, u32[]{:S(2)}) collective-permute-start(bf16[32,2176]{1,0:T(8,128)(2,1)S(1)} %get-tuple-element.50), channel_id=1, source_target_pairs={{0,7},{1,0},{2,1},{3,2},{4,3},{5,4},{6,5},{7,6},{8,15},{9,8},{10,9... | collective-permute-start | bytes 417800 | tf_op jit(solution)/shard_map/ppermute | solution.py:432
  54.0 0.8 constant_dynamic-update-slice_fusion.29
  54.8 0.8 constant_dynamic-update-slice_fusion.28
  55.7 0.8 constant_dynamic-update-slice_fusion.27
  56.5 0.8 constant_dynamic-update-slice_fusion.26
  57.4 1.6 collective-permute-done.6
  59.0 3.1 %collective-permute-start.7 = (bf16[64,2176]{1,0:T(8,128)(2,1)S(1)}, bf16[64,2176]{1,0:T(8,128)(2,1)S(1)}, u32[]{:S(2)}, u32[]{:S(2)}) collective-permute-start(bf16[64,2176]{1,0:T(8,128)(2,1)S(1)} %get-tuple-element.81), channel_id=1, source_target_pairs={{0,8},{1,9},{2,10},{3,11},{4,12},{5,13},{6,14},{7,15},{8,16},{9,17... | collective-permute-start | bytes 835592 | tf_op jit(solution)/shard_map/ppermute | solution.py:438
  62.1 4.4 %collective-permute-start.8 = (bf16[64,2176]{1,0:T(8,128)(2,1)S(1)}, bf16[64,2176]{1,0:T(8,128)(2,1)S(1)}, u32[]{:S(2)}, u32[]{:S(2)}) collective-permute-start(bf16[64,2176]{1,0:T(8,128)(2,1)S(1)} %get-tuple-element.80), channel_id=1, source_target_pairs={{0,16},{1,17},{2,18},{3,19},{4,20},{5,21},{6,22},{7,23},{8,24},{9,... | collective-permute-start | bytes 835592 | tf_op jit(solution)/shard_map/ppermute | solution.py:438
  66.5 3.1 %collective-permute-start.9 = (bf16[64,2176]{1,0:T(8,128)(2,1)S(1)}, bf16[64,2176]{1,0:T(8,128)(2,1)S(1)}, u32[]{:S(2)}, u32[]{:S(2)}) collective-permute-start(bf16[64,2176]{1,0:T(8,128)(2,1)S(1)} %get-tuple-element.79), channel_id=1, source_target_pairs={{0,24},{1,25},{2,26},{3,27},{4,28},{5,29},{6,30},{7,31},{8,0},{9,1... | collective-permute-start | bytes 835592 | tf_op jit(solution)/shard_map/ppermute | solution.py:438
  69.6 2.1 shard_map.122
  71.7 4.6 %collective-permute-done.8.refs_2_ = bf16[64,2176]{1,0:T(8,128)(2,1)S(1)} collective-permute-done((bf16[64,2176]{1,0:T(8,128)(2,1)S(1)}, bf16[64,2176]{1,0:T(8,128)(2,1)S(1)}, u32[]{:S(2)}, u32[]{:S(2)}) %collective-permute-start.8) | collective-permute-done | bytes 278560 | tf_op jit(solution)/shard_map/ppermute | solution.py:438
  76.3 1.2 collective-permute-done.9.refs_3_
  77.5 1.6 shard_map.123
  79.1 1.0 copy-done.5
  80.1 0.8 copy-done.10
  81.5 21.4 %all-to-all-done = bf16[24,8,4224]{2,1,0:T(8,128)(2,1)S(1)} async-done(((bf16[24,8,4224]{2,1,0:T(8,128)(2,1)}), bf16[24,8,4224]{2,1,0:T(8,128)(2,1)S(1)}, u32[]{:S(2)}, u32[]{:S(2)}) %all-to-all-start) | async-done | bytes 1622048 | tf_op jit(solution)/shard_map/all_to_all | solution.py:422
  102.9 3.3 %shard_map.124 = (bf16[192,128]{1,0:T(8,128)(2,1)}, bf16[192,64]{1,0:T(8,128)(2,1)S(1)}, bf16[128,64]{1,0:T(8,128)(2,1)S(1)}, f32[192,1]{1,0:T(8,128)S(1)}, f32[128,1]{1,0:T(8,128)S(1)}, /*index=5*/f32[64,1]{1,0:T(8,128)S(1)}) custom-call(bf16[192,4224]{1,0:T(8,128)(2,1)S(1)} %bitcast.15, bf16[64,4096]{1,0:T(8,128)(2,1)S(1)} %get-tuple-element.42.refs_4_.refs_1_.q_ref, ...), custom_call_target="tpu_custom_call" | custom-call | flops 300000000 | bytes 3000000 | tf_op jit(solution)/shard_map/pallas_call | solution.py:410
  107.4 5.6 %all-to-all-start.1 = ((bf16[24,8,128]{2,1,0:T(8,128)(2,1)}), bf16[24,8,128]{2,1,0:T(8,128)(2,1)S(1)}, u32[]{:S(2)}, u32[]{:S(2)}) async-start(bf16[24,8,128]{2,1,0:T(8,128)(2,1)} %bitcast.10), calls=%async_computation.1 | async-start | bytes 98304 | tf_op jit(solution)/shard_map/all_to_all | solution.py:422
  113.0 1.0 copy-done.4
  114.1 1.2 copy-done.6
  115.3 1.0 copy-done.11
  116.3 0.8 copy-done.13
  117.1 0.8 copy-done.17
  117.9 0.8 copy-done.19
  118.7 0.8 copy-done.21
  122.2 4.9 %shard_map.125 = (f32[32,32,128]{2,1,0:T(8,128)S(1)}, bf16[32,32,128]{2,1,0:T(8,128)(2,1)}, f32[64,4096]{1,0:T(8,128)}, f32[64,128]{1,0:T(8,128)}) custom-call(s32[3]{0:T(128)S(1)} %copy-done.25, bf16[192,4224]{1,0:T(8,128)(2,1)S(1)} %bitcast.16, bf16[128,4096]{1,0:T(8,128)(2,1)S(1)} %copy-done.6, bf16[128,128]{1,0:T(8,128)(2,1)S(1)} %copy-done.19, ...), custom_call_target="tpu_custom_call" | custom-call | flops 900000000 | bytes 9000000 | tf_op jit(solution)/shard_map/pallas_call | solution.py:410
  127.1 0.8 copy-done.8
  127.9 2.2 %collective-permute-start.11 = (bf16[32,32,128]{2,1,0:T(8,128)(2,1)}, bf16[32,32,128]{2,1,0:T(8,128)(2,1)S(1)}, u32[]{:S(2)}, u32[]{:S(2)}) collective-permute-start(bf16[32,32,128]{2,1,0:T(8,128)(2,1)} %get-tuple-element.74), channel_id=1, source_target_pairs={{0,32},{32,0},{64,96},{96,64},{128,160},{160,128},{192,224},{224,1... | collective-permute-start | bytes 786440 | tf_op jit(solution)/shard_map/ppermute | solution.py:560
  130.2 2.1 shard_map.126
  132.3 2.2 %collective-permute-start.10 = (bf16[32,32,128]{2,1,0:T(8,128)(2,1)S(1)}, bf16[32,32,128]{2,1,0:T(8,128)(2,1)S(1)}, u32[]{:S(2)}, u32[]{:S(2)}) collective-permute-start(bf16[32,32,128]{2,1,0:T(8,128)(2,1)S(1)} %get-tuple-element.72), channel_id=1, source_target_pairs={{0,32},{32,0},{64,96},{96,64},{128,160},{160,128},{192,224},{224,1... | collective-permute-start | bytes 786440 | tf_op jit(solution)/shard_map/ppermute | solution.py:572
  134.5 1.2 collective-permute-done.10.got_down_ref
  135.8 12.5 %all_to_all.35.in_ref = bf16[4,8,64,128]{3,2,1,0:T(8,128)(2,1)S(1)} all-to-all(bf16[4,8,64,128]{3,2,1,0:T(8,128)(2,1)S(1)} %bitcast.19), channel_id=1, replica_groups={{0,8,16,24},{1,9,17,25},{2,10,18,26},{3,11,19,27},{4,12,20,28},{5,13,21..., dimensions={0} | all-to-all | bytes 1048576 | tf_op jit(solution)/shard_map/all_to_all | solution.py:422
  148.4 12.9 %all_to_all.36.in_ref = bf16[8,64,128]{2,1,0:T(8,128)(2,1)S(1)} all-to-all(bf16[8,64,128]{2,1,0:T(8,128)(2,1)S(1)} %shard_map.128), channel_id=1, replica_groups={{0,1,2,3,4,5,6,7},{8,9,10,11,12,13,14,15},{16,17,18,19,20,21,22,23},{24..., dimensions={0} | all-to-all | bytes 262144 | tf_op jit(solution)/shard_map/all_to_all | solution.py:422
  161.3 20.5 %all_to_all.37.in_ref = bf16[12,64,128]{2,1,0:T(8,128)(2,1)S(1)} all-to-all(bf16[12,64,128]{2,1,0:T(8,128)(2,1)S(1)} %shard_map.129), channel_id=1, replica_groups={{0,64,128,192,256,320,384,448,512,576,640,704},{32,96,160,224,288,352,4..., dimensions={0} | all-to-all | bytes 393216 | tf_op jit(solution)/shard_map/all_to_all | solution.py:422
  181.9 10.5 %all_to_all.38.in_ref = bf16[8,72,128]{2,1,0:T(8,128)(2,1)S(1)} all-to-all(bf16[8,72,128]{2,1,0:T(8,128)(2,1)S(1)} %shard_map.130), channel_id=1, replica_groups={{0,1,2,3,4,5,6,7},{8,9,10,11,12,13,14,15},{16,17,18,19,20,21,22,23},{24..., dimensions={0} | all-to-all | bytes 294912 | tf_op jit(solution)/shard_map/all_to_all | solution.py:422
  192.4 9.7 %all_to_all.39.refs_1_ = bf16[4,8,72,128]{3,2,1,0:T(8,128)(2,1)S(1)} all-to-all(bf16[4,8,72,128]{3,2,1,0:T(8,128)(2,1)S(1)} %shard_map.131), channel_id=1, replica_groups={{0,8,16,24},{1,9,17,25},{2,10,18,26},{3,11,19,27},{4,12,20,28},{5,13,21..., dimensions={0} | all-to-all | bytes 1179648 | tf_op jit(solution)/shard_map/all_to_all | solution.py:422
  202.1 8.6 %collective-permute-start.12 = (bf16[4,8,72,128]{3,2,1,0:T(8,128)(2,1)S(1)}, bf16[4,8,72,128]{3,2,1,0:T(8,128)(2,1)S(1)}, u32[]{:S(2)}, u32[]{:S(2)}) collective-permute-start(bf16[4,8,72,128]{3,2,1,0:T(8,128)(2,1)S(1)} %all_to_all.39.refs_1_), channel_id=1, source_target_pairs={{0,32},{32,0},{64,96},{96,64},{128,160},{160,128},{192,224},{224,1... | collective-permute-start | bytes 1769480 | tf_op jit(solution)/shard_map/ppermute | solution.py:597
  210.7 1.6 collective-permute-done.12.refs_2_
  212.3 1.9 shard_map.132
  (72 shorter events, 5.8 us)
Async XLA Ops:
  0.7 68.8 %copy-start.24 = (s32[3]{0:T(128)}, s32[3]{0:T(128)S(1)}, u32[]{:S(2)}) copy-start(s32[3]{0:T(128)S(1)} %pad_add_fusion.refs_0_.place_ref) | copy-start | bytes 40
  5.7 0.6 copy-start.14
  6.3 38.7 %collective-permute-start = (bf16[32,2176]{1,0:T(8,128)(2,1)}, bf16[32,2176]{1,0:T(8,128)(2,1)}, u32[]{:S(2)}, u32[]{:S(2)}) collective-permute-start(bf16[32,2176]{1,0:T(8,128)(2,1)} %get-tuple-element.44), channel_id=1, source_target_pairs={{0,1},{1,2},{2,3},{3,4},{4,5},{5,6},{6,7},{7,0},{8,9},{9,10},{10,1... | collective-permute-start | bytes 417800 | tf_op jit(solution)/shard_map/ppermute | solution.py:432
  10.4 40.6 %collective-permute-start.1 = (bf16[32,2176]{1,0:T(8,128)(2,1)}, bf16[32,2176]{1,0:T(8,128)(2,1)}, u32[]{:S(2)}, u32[]{:S(2)}) collective-permute-start(bf16[32,2176]{1,0:T(8,128)(2,1)} %get-tuple-element.45), channel_id=1, source_target_pairs={{0,2},{1,3},{2,4},{3,5},{4,6},{5,7},{6,0},{7,1},{8,10},{9,11},{10,... | collective-permute-start | bytes 417800 | tf_op jit(solution)/shard_map/ppermute | solution.py:432
  14.6 40.2 %collective-permute-start.2 = (bf16[32,2176]{1,0:T(8,128)(2,1)}, bf16[32,2176]{1,0:T(8,128)(2,1)}, u32[]{:S(2)}, u32[]{:S(2)}) collective-permute-start(bf16[32,2176]{1,0:T(8,128)(2,1)} %get-tuple-element.46), channel_id=1, source_target_pairs={{0,3},{1,4},{2,5},{3,6},{4,7},{5,0},{6,1},{7,2},{8,11},{9,12},{10,... | collective-permute-start | bytes 417800 | tf_op jit(solution)/shard_map/ppermute | solution.py:432
  19.2 36.4 %collective-permute-start.3 = (bf16[32,2176]{1,0:T(8,128)(2,1)}, bf16[32,2176]{1,0:T(8,128)(2,1)}, u32[]{:S(2)}, u32[]{:S(2)}) collective-permute-start(bf16[32,2176]{1,0:T(8,128)(2,1)} %get-tuple-element.47), channel_id=1, source_target_pairs={{0,4},{1,5},{2,6},{3,7},{4,0},{5,1},{6,2},{7,3},{8,12},{9,13},{10,... | collective-permute-start | bytes 417800 | tf_op jit(solution)/shard_map/ppermute | solution.py:432
  22.8 33.7 %collective-permute-start.4 = (bf16[32,2176]{1,0:T(8,128)(2,1)S(1)}, bf16[32,2176]{1,0:T(8,128)(2,1)}, u32[]{:S(2)}, u32[]{:S(2)}) collective-permute-start(bf16[32,2176]{1,0:T(8,128)(2,1)S(1)} %get-tuple-element.48), channel_id=1, source_target_pairs={{0,5},{1,6},{2,7},{3,0},{4,1},{5,2},{6,3},{7,4},{8,13},{9,14},{10,... | collective-permute-start | bytes 417800 | tf_op jit(solution)/shard_map/ppermute | solution.py:432
  27.7 75.2 %all-to-all-start = ((bf16[24,8,4224]{2,1,0:T(8,128)(2,1)}), bf16[24,8,4224]{2,1,0:T(8,128)(2,1)S(1)}, u32[]{:S(2)}, u32[]{:S(2)}) async-start(bf16[24,8,4224]{2,1,0:T(8,128)(2,1)} %bitcast.6), calls=%async_computation | async-start | bytes 3244032 | tf_op jit(solution)/shard_map/all_to_all | solution.py:422
  44.9 24.6 %copy-start = (bf16[64,4096]{1,0:T(8,128)(2,1)S(1)}, bf16[64,4096]{1,0:T(8,128)(2,1)}, u32[]{:S(2)}) copy-start(bf16[64,4096]{1,0:T(8,128)(2,1)} %up_ref.1) | copy-start | bytes 1572868
  45.0 24.6 %copy-start.1 = (bf16[4096,64]{0,1:T(8,128)(2,1)S(1)}, bf16[4096,64]{0,1:T(8,128)(2,1)}, u32[]{:S(2)}) copy-start(bf16[4096,64]{0,1:T(8,128)(2,1)} %param.14) | copy-start | bytes 1572868
  45.0 24.6 %copy-start.3 = (bf16[64,4096]{1,0:T(8,128)(2,1)S(1)}, bf16[64,4096]{1,0:T(8,128)(2,1)}, u32[]{:S(2)}) copy-start(bf16[64,4096]{1,0:T(8,128)(2,1)} %x_q_ref.1) | copy-start | bytes 1572868
  45.0 24.6 %copy-start.7 = (bf16[64,4096]{1,0:T(8,128)(2,1)S(1)}, bf16[64,4096]{1,0:T(8,128)(2,1)}, u32[]{:S(2)}) copy-start(bf16[64,4096]{1,0:T(8,128)(2,1)} %refs_2_.3) | copy-start | bytes 1572868
  45.0 24.6 %copy-start.27 = (s32[64,32]{0,1:T(8,128)S(1)}, s32[64,32]{0,1:T(8,128)}, u32[]{:S(2)}) copy-start(s32[64,32]{0,1:T(8,128)} %param.17) | copy-start | bytes 24580
  45.0 12.3 %collective-permute-start.5 = (bf16[32,2176]{1,0:T(8,128)(2,1)S(1)}, bf16[32,2176]{1,0:T(8,128)(2,1)S(1)}, u32[]{:S(2)}, u32[]{:S(2)}) collective-permute-start(bf16[32,2176]{1,0:T(8,128)(2,1)S(1)} %get-tuple-element.49), channel_id=1, source_target_pairs={{0,6},{1,7},{2,0},{3,1},{4,2},{5,3},{6,4},{7,5},{8,14},{9,15},{10,... | collective-permute-start | bytes 417800 | tf_op jit(solution)/shard_map/ppermute | solution.py:432
  51.0 8.0 %collective-permute-start.6 = (bf16[32,2176]{1,0:T(8,128)(2,1)S(1)}, bf16[32,2176]{1,0:T(8,128)(2,1)S(1)}, u32[]{:S(2)}, u32[]{:S(2)}) collective-permute-start(bf16[32,2176]{1,0:T(8,128)(2,1)S(1)} %get-tuple-element.50), channel_id=1, source_target_pairs={{0,7},{1,0},{2,1},{3,2},{4,3},{5,4},{6,5},{7,6},{8,15},{9,8},{10,9... | collective-permute-start | bytes 417800 | tf_op jit(solution)/shard_map/ppermute | solution.py:432
  55.7 21.8 %copy-start.30 = (s32[64]{0:T(128)S(1)}, s32[64]{0:T(128)}, u32[]{:S(2)}) copy-start(s32[64]{0:T(128)} %param.16) | copy-start | bytes 772
  59.0 12.7 %collective-permute-start.7 = (bf16[64,2176]{1,0:T(8,128)(2,1)S(1)}, bf16[64,2176]{1,0:T(8,128)(2,1)S(1)}, u32[]{:S(2)}, u32[]{:S(2)}) collective-permute-start(bf16[64,2176]{1,0:T(8,128)(2,1)S(1)} %get-tuple-element.81), channel_id=1, source_target_pairs={{0,8},{1,9},{2,10},{3,11},{4,12},{5,13},{6,14},{7,15},{8,16},{9,17... | collective-permute-start | bytes 835592 | tf_op jit(solution)/shard_map/ppermute | solution.py:438
  62.1 14.2 %collective-permute-start.8 = (bf16[64,2176]{1,0:T(8,128)(2,1)S(1)}, bf16[64,2176]{1,0:T(8,128)(2,1)S(1)}, u32[]{:S(2)}, u32[]{:S(2)}) collective-permute-start(bf16[64,2176]{1,0:T(8,128)(2,1)S(1)} %get-tuple-element.80), channel_id=1, source_target_pairs={{0,16},{1,17},{2,18},{3,19},{4,20},{5,21},{6,22},{7,23},{8,24},{9,... | collective-permute-start | bytes 835592 | tf_op jit(solution)/shard_map/ppermute | solution.py:438
  66.5 11.0 %collective-permute-start.9 = (bf16[64,2176]{1,0:T(8,128)(2,1)S(1)}, bf16[64,2176]{1,0:T(8,128)(2,1)S(1)}, u32[]{:S(2)}, u32[]{:S(2)}) collective-permute-start(bf16[64,2176]{1,0:T(8,128)(2,1)S(1)} %get-tuple-element.79), channel_id=1, source_target_pairs={{0,24},{1,25},{2,26},{3,27},{4,28},{5,29},{6,30},{7,31},{8,0},{9,1... | collective-permute-start | bytes 835592 | tf_op jit(solution)/shard_map/ppermute | solution.py:438
  71.7 31.2 %copy-start.16 = (f32[64,128]{1,0:T(8,128)}, f32[64,128]{1,0:T(8,128)S(1)}, u32[]{:S(2)}) copy-start(f32[64,128]{1,0:T(8,128)S(1)} %get-tuple-element.62.q_inv_ref) | copy-start | bytes 98308
  71.7 31.2 %copy-start.28 = (bf16[64,128]{1,0:T(8,128)(2,1)}, bf16[64,128]{1,0:T(8,128)(2,1)S(1)}, u32[]{:S(2)}) copy-start(bf16[64,128]{1,0:T(8,128)(2,1)S(1)} %get-tuple-element.61.q_ext_ref) | copy-start | bytes 49156
  79.1 1.0 copy-start.5
  80.1 0.8 copy-start.10
  80.9 0.6 copy-start.18
  106.2 0.6 copy-start.12
  106.8 0.6 copy-start.20
  107.4 5.6 %copy-start.22 = (f32[64,1]{1,0:T(8,128)}, f32[64,1]{1,0:T(8,128)S(1)}, u32[]{:S(2)}) copy-start(f32[64,1]{1,0:T(8,128)S(1)} %get-tuple-element.68.q_radial_ref) | copy-start | bytes 772
  107.4 22.7 %all-to-all-start.1 = ((bf16[24,8,128]{2,1,0:T(8,128)(2,1)}), bf16[24,8,128]{2,1,0:T(8,128)(2,1)S(1)}, u32[]{:S(2)}, u32[]{:S(2)}) async-start(bf16[24,8,128]{2,1,0:T(8,128)(2,1)} %bitcast.10), calls=%async_computation.1 | async-start | bytes 98304 | tf_op jit(solution)/shard_map/all_to_all | solution.py:422
  113.0 1.0 copy-start.4
  114.1 1.2 copy-start.6
  115.3 1.0 copy-start.11
  116.3 0.8 copy-start.13
  117.1 0.8 copy-start.17
  117.9 0.8 copy-start.19
  118.6 0.8 copy-start.21
  119.4 0.8 copy-start.23
  120.2 0.7 copy-start.25
  120.8 0.7 copy-start.29
  121.5 0.7 copy-start.31
  122.2 7.9 %copy-start.2 = (bf16[64,4096]{1,0:T(8,128)(2,1)S(1)}, bf16[64,4096]{1,0:T(8,128)(2,1)}, u32[]{:S(2)}) copy-start(bf16[64,4096]{1,0:T(8,128)(2,1)} %refs_4_.5) | copy-start | bytes 1572868
  122.2 8.0 %copy-start.15 = (bf16[192,64]{1,0:T(8,128)(2,1)S(1)}, bf16[192,64]{1,0:T(8,128)(2,1)}, u32[]{:S(2)}) copy-start(bf16[192,64]{1,0:T(8,128)(2,1)} %copy-done.14) | copy-start | bytes 73732
  122.2 8.0 %copy-start.26 = (s32[3]{0:T(128)S(1)}, s32[3]{0:T(128)}, u32[]{:S(2)}) copy-start(s32[3]{0:T(128)} %copy-done.24) | copy-start | bytes 40
  127.1 0.8 copy-start.8
  127.9 7.8 %copy-start.9 = (f32[32,32,128]{2,1,0:T(8,128)S(1)}, f32[32,32,128]{2,1,0:T(8,128)}, u32[]{:S(2)}) copy-start(f32[32,32,128]{2,1,0:T(8,128)} %copy-done.8) | copy-start | bytes 1572868
  127.9 6.6 %collective-permute-start.11 = (bf16[32,32,128]{2,1,0:T(8,128)(2,1)}, bf16[32,32,128]{2,1,0:T(8,128)(2,1)S(1)}, u32[]{:S(2)}, u32[]{:S(2)}) collective-permute-start(bf16[32,32,128]{2,1,0:T(8,128)(2,1)} %get-tuple-element.74), channel_id=1, source_target_pairs={{0,32},{32,0},{64,96},{96,64},{128,160},{160,128},{192,224},{224,1... | collective-permute-start | bytes 786440 | tf_op jit(solution)/shard_map/ppermute | solution.py:560
  132.3 3.4 %collective-permute-start.10 = (bf16[32,32,128]{2,1,0:T(8,128)(2,1)S(1)}, bf16[32,32,128]{2,1,0:T(8,128)(2,1)S(1)}, u32[]{:S(2)}, u32[]{:S(2)}) collective-permute-start(bf16[32,32,128]{2,1,0:T(8,128)(2,1)S(1)} %get-tuple-element.72), channel_id=1, source_target_pairs={{0,32},{32,0},{64,96},{96,64},{128,160},{160,128},{192,224},{224,1... | collective-permute-start | bytes 786440 | tf_op jit(solution)/shard_map/ppermute | solution.py:572
  202.1 10.2 %collective-permute-start.12 = (bf16[4,8,72,128]{3,2,1,0:T(8,128)(2,1)S(1)}, bf16[4,8,72,128]{3,2,1,0:T(8,128)(2,1)S(1)}, u32[]{:S(2)}, u32[]{:S(2)}) collective-permute-start(bf16[4,8,72,128]{3,2,1,0:T(8,128)(2,1)S(1)} %all_to_all.39.refs_1_), channel_id=1, source_target_pairs={{0,32},{32,0},{64,96},{96,64},{128,160},{160,128},{192,224},{224,1... | collective-permute-start | bytes 1769480 | tf_op jit(solution)/shard_map/ppermute | solution.py:597

commit v3 on v2

--- a/solution.py
+++ b/solution.py
@@ -51,7 +51,7 @@
         squares = squares + jnp.sum(raw * raw, axis=1, keepdims=True)
     inverse = lax.rsqrt(squares + epsilon)
     for cols in column_tiles(width):
-        unit_ref[:, cols] = (raw_ref[:, cols] * inverse).astype(bf16)
+        unit_ref[0:rows, cols] = (raw_ref[:, cols] * inverse).astype(bf16)
     scaled = (latent.astype(f32) * inverse).astype(bf16)
     high = inverse.astype(bf16).astype(f32)
     lane = iota((rows, lanes), 1)
@@ -62,19 +62,23 @@
     inv_ref[...] = jnp.broadcast_to(inverse, inv_ref.shape)
 
 
-def passage_kernel(
-    grid_x, grid_y, place_ref, x_hbm, base_hbm, down_hbm, up_hbm, near_ids_hbm, far_ids_hbm, *refs
-):
-    near_ref, *far_refs = refs[: 1 + grid_y]
-    unit_ref, ext_ref, inv_ref, pick_ref = refs[1 + grid_y : 5 + grid_y]
-    (x_ref, base_ref, down_ref, up_ref, near_ids_ref, far_ids_ref, raw_ref, sems) = refs[5 + grid_y :]
-    pairs = [
-        (x_hbm, x_ref), (down_hbm, down_ref), (base_hbm, base_ref), (up_hbm, up_ref),
-        (near_ids_hbm, near_ids_ref), (far_ids_hbm, far_ids_ref),
-    ]
+def fetch(pairs, sems):
     copies = [pltpu.make_async_copy(a, b, sems.at[i]) for i, (a, b) in enumerate(pairs)]
     for c in copies:
         c.start()
+    return copies
+
+
+def passage_kernel(
+    x_hbm, base_hbm, down_hbm, up_hbm, near_ids_hbm,
+    near_hbm, unit_ref, ext_ref, inv_ref, pick_ref,
+    x_ref, base_ref, down_ref, up_ref, near_ids_ref, raw_ref, near_ref, sems, out_sems,
+):
+    pairs = [
+        (x_hbm, x_ref), (down_hbm, down_ref), (base_hbm, base_ref), (up_hbm, up_ref),
+        (near_ids_hbm, near_ids_ref),
+    ]
+    copies = fetch(pairs, sems)
     copies[0].wait()
     copies[1].wait()
 
@@ -84,9 +88,7 @@
 
     embed(x_ref, base_ref, down_ref, up_ref, unit_ref, ext_ref, inv_ref, raw_ref, ready)
     copies[4].wait()
-    copies[5].wait()
     rows, width = x_ref.shape
-    half = width // 2
     per_near, n_near = near_ids_ref.shape
     count = per_near * n_near
     ids = near_ids_ref[...].astype(f32).astype(bf16)
@@ -96,9 +98,21 @@
     wanted = jnp.sum(jnp.where(mine, table, 0.0), axis=1, keepdims=True).astype(jnp.int32)
     pick = (iota((count, rows), 1) == wanted).astype(bf16)
     pick_ref[...] = pick
-    for cols in column_tiles(width):
-        near_ref[:, cols] = dot(pick, unit_ref[:, cols]).astype(bf16)
     near_ref[:, width:] = dot(pick, ext_ref[...]).astype(bf16)
+    sent = []
+    for i, cols in enumerate([slice(width, width + lanes), *column_tiles(width)]):
+        if i:
+            near_ref[:, cols] = dot(pick, unit_ref[:, cols]).astype(bf16)
+        copy = pltpu.make_async_copy(near_ref.at[:, cols], near_hbm.at[:, cols], out_sems.at[i])
+        copy.start()
+        sent.append(copy)
+    for copy in sent:
+        copy.wait()
+
+
+def far_pick_kernel(grid_x, grid_y, place_ref, x_ref, unit_ref, ext_ref, far_ids_ref, *far_refs):
+    rows, width = x_ref.shape
+    half = width // 2
     n_far = far_ids_ref.shape[1]
     total = n_far * 8
     size = grid_x * 8
@@ -130,10 +144,15 @@
 
 def query_kernel(
     grid_x, grid_y, place_ref, x_ref, base_ref, down_ref, up_ref, slots_ref,
-    unit_ref, ext_ref, inv_ref, near_count_ref, other_count_ref, raw_ref,
+    pair_ref, ext_ref, inv_ref, near_count_ref, other_count_ref, shadow_ref, raw_ref,
 ):
-    embed(x_ref, base_ref, down_ref, up_ref, unit_ref, ext_ref, inv_ref, raw_ref)
     hard, rows = slots_ref.shape
+    embed(x_ref, base_ref, down_ref, up_ref, pair_ref, ext_ref, inv_ref, raw_ref)
+    pair_ref[rows:, :] = up_ref[...]
+    product = dot(pair_ref[0:rows, :], up_ref[...], 1, 1)
+    high = product.astype(bf16)
+    shadow_ref[0:rows, :] = high
+    shadow_ref[rows:, :] = (product - high.astype(f32)).astype(bf16)
     n_near = near_count_ref.shape[0]
     n_other = other_count_ref.shape[0]
     n_far = n_other - rows
@@ -172,11 +191,23 @@
     return parts[0] if len(parts) == 1 else jnp.concatenate(parts, axis=1)
 
 
+def regroup_kernel(*refs):
+    size = 8
+    count = refs[0].shape[0] // size
+    n_in = len(refs) - count
+    for dx in range(0, count, 2):
+        for dy in range(0, n_in, 2):
+            a, b = [refs[dy + i][dx * size : (dx + 2) * size, :] for i in range(2)]
+            at = slice(dy * size, (dy + 2) * size)
+            refs[n_in + dx][at, :] = jnp.concatenate([a[:size], b[:size]], axis=0)
+            refs[n_in + dx + 1][at, :] = jnp.concatenate([a[size:], b[size:]], axis=0)
+
+
 def far_kernel(count, *refs):
     far_refs = refs[:count]
     q_ref, unit_ref, p_ext_ref, positive_ref = refs[count : count + 4]
     o_ref, ext_ref, x_far_ref, raw_ref = refs[count + 4 :]
-    rows, width = q_ref.shape
+    rows, width = unit_ref.shape
     half = width // 2
     total = far_refs[0].shape[0]
     each = total // 4
@@ -204,22 +235,23 @@
     for cols in column_tiles(width):
         o_ref[n_far:, cols] = dot(own_t, unit_ref[:, cols]).astype(bf16)
     ext_ref[n_far:, :] = dot(own_t, p_ext_ref[...]).astype(bf16)
-    raw_ref[...] = dot(o_ref[...], q_ref[...], 1, 1)
+    raw_ref[...] = dot(o_ref[...], q_ref[0:rows, :], 1, 1)
 
 
 def score_kernel(
-    slope, rank, near_ref, q_ref, other_raw_hbm, near_count_ref, other_count_ref, up_ref,
-    ret_ref, near_g_ref, other_g_ref, near_radial_ref, other_radial_ref, q_radial_ref,
-    other_raw_ref, sem,
+    slope, rank, near_ref, pair_ref, other_raw_hbm, near_count_ref, other_count_ref, shadow_ref,
+    ret_ref, g_ref, radial_ref, other_raw_ref, sem,
 ):
     copy = pltpu.make_async_copy(other_raw_hbm, other_raw_ref, sem)
     copy.start()
-    rows, width = q_ref.shape
-    n_near = near_ref.shape[0]
-    near_raw = dot(near_ref[:, :width], q_ref[...], 1, 1)
+    width = pair_ref.shape[1]
+    n_near, rows = near_count_ref.shape
+    both = dot(near_ref[:, :width], pair_ref[...], 1, 1)
+    near_raw, near_up = both[:, 0:rows], both[:, rows:]
     copy.wait()
     other_raw = other_raw_ref[...]
-    n_far = other_raw.shape[0] - rows
+    n_other = other_raw.shape[0]
+    n_far = n_other - rows
     near_exp = jnp.exp(near_raw / logit_divisor - offset) * near_count_ref[...]
     other_exp = jnp.exp(other_raw / logit_divisor - offset) * other_count_ref[...]
     partition = jnp.sum(near_exp, axis=0, keepdims=True) + jnp.sum(
@@ -230,22 +262,22 @@
     loss = jnp.sum(jnp.log(partition) + offset - matched, axis=1, keepdims=True)
     near_g = (near_exp / partition * slope).astype(bf16)
     other_g = ((other_exp / partition - same.astype(f32)) * slope).astype(bf16)
-    near_g_ref[...] = near_g
-    other_g_ref[...] = other_g
+    g_ref[0:n_near, :] = near_g
+    g_ref[n_near:, :] = other_g
     near_part = near_g.astype(f32) * near_raw
     other_part = other_g.astype(f32) * other_raw
     near_radial = jnp.sum(near_part, axis=1, keepdims=True)
-    near_radial_ref[...] = near_radial
-    other_radial_ref[...] = jnp.sum(other_part, axis=1, keepdims=True)
+    radial_ref[0:n_near, :] = near_radial
+    radial_ref[n_near : n_near + n_other, :] = jnp.sum(other_part, axis=1, keepdims=True)
     q_radial = jnp.sum(near_part, axis=0, keepdims=True) + jnp.sum(
         other_part, axis=0, keepdims=True
     )
     square = iota((rows, rows), 0) == iota((rows, rows), 1)
-    q_radial_ref[...] = jnp.sum(jnp.where(square, q_radial, 0.0), axis=1, keepdims=True)
-    back = jnp.zeros((n_near, rank), f32)
-    for cols in column_tiles(width):
-        tangent = dot(near_g, q_ref[:, cols]) - near_ref[:, cols].astype(f32) * near_radial
-        back = back + dot(tangent.astype(bf16), up_ref[:, cols], 1, 1)
+    radial_ref[n_near + n_other :, :] = jnp.sum(
+        jnp.where(square, q_radial, 0.0), axis=1, keepdims=True
+    )
+    back = dot(near_g, shadow_ref[0:rows, :]) + dot(near_g, shadow_ref[rows:, :])
+    back = back - near_radial * near_up
     back = dot(back.astype(bf16), eye(rank, lanes))
     lane = iota((n_near, lanes), 1)
     high = loss.astype(bf16).astype(f32)
@@ -255,30 +287,45 @@
 
 
 def local_kernel(
-    place_ref, near_ref, o_ref, o_ext_ref, x_far_ref, q_ref, q_ext_ref, q_inv_ref, p_inv_ref, x_q_ref,
-    positive_ref, near_g_ref, other_g_ref, near_radial_ref, other_radial_ref, q_radial_ref, up_ref,
+    near_ref, pair_ref, o_hbm, o_ext_hbm, x_far_hbm, q_ext_hbm, q_inv_hbm, p_inv_hbm, x_q_hbm,
+    positive_hbm, g_hbm, radial_hbm, place_hbm,
     up_keep_ref, up_send_ref, down_ref, row_ref,
+    o_ref, o_ext_ref, x_far_ref, q_ext_ref, q_inv_ref, p_inv_ref, x_q_ref, positive_ref, g_ref,
+    radial_ref, place_ref, sems,
 ):
-    rows, width = q_ref.shape
-    rank = up_ref.shape[0]
+    pairs = [
+        (g_hbm, g_ref), (radial_hbm, radial_ref), (o_hbm, o_ref), (o_ext_hbm, o_ext_ref),
+        (q_ext_hbm, q_ext_ref), (place_hbm, place_ref), (positive_hbm, positive_ref),
+        (q_inv_hbm, q_inv_ref), (p_inv_hbm, p_inv_ref), (x_far_hbm, x_far_ref), (x_q_hbm, x_q_ref),
+    ]
+    copies = fetch(pairs, sems)
+    for c in copies[:6]:
+        c.wait()
+    rows, width = x_q_ref.shape
+    rank = pair_ref.shape[0] - rows
     part = rank // 2
+    n_near = near_ref.shape[0]
     n_far = o_ref.shape[0] - rows
-    even = place_ref[2] == 0
-    near_gt, other_gt = near_g_ref[...], other_g_ref[...]
+    n_all = n_near + n_far + rows
+    even = place_ref[0:1, 2:3] == 0
+    near_gt, other_gt = g_ref[0:n_near, :], g_ref[n_near:, :]
     near_g, other_g = flip(near_gt), flip(other_gt)
+    near_radial = radial_ref[0:n_near, :]
+    other_radial = radial_ref[n_near:n_all, :]
+    q_radial = radial_ref[n_all:, :]
     q_lat = flip(q_ext_ref[...])[0:rank]
     near_lat = flip(near_ref[:, width:])[0:rank]
     other_lat = flip(o_ext_ref[...])[0:rank]
     q_back = jnp.zeros((rows, rank), f32)
     other_back = jnp.zeros((n_far + rows, rank), f32)
     for cols in column_tiles(width):
-        q = q_ref[:, cols]
+        q = pair_ref[0:rows, cols]
         near = near_ref[:, cols]
         other = o_ref[:, cols]
-        up = up_ref[:, cols]
-        q_t = dot(near_g, near) + dot(other_g, other) - q.astype(f32) * q_radial_ref[...]
-        near_t = dot(near_gt, q) - near.astype(f32) * near_radial_ref[...]
-        other_t = dot(other_gt, q) - other.astype(f32) * other_radial_ref[...]
+        up = pair_ref[rows:, cols]
+        q_t = dot(near_g, near) + dot(other_g, other) - q.astype(f32) * q_radial
+        near_t = dot(near_gt, q) - near.astype(f32) * near_radial
+        other_t = dot(other_gt, q) - other.astype(f32) * other_radial
         q_t, near_t, other_t = q_t.astype(bf16), near_t.astype(bf16), other_t.astype(bf16)
         q_back = q_back + dot(q_t, up, 1, 1)
         other_back = other_back + dot(other_t, up, 1, 1)
@@ -287,6 +334,8 @@
         top, low = grad[0:part], grad[part:]
         store_blocks(up_keep_ref, cols, jnp.where(even, top, low))
         store_blocks(up_send_ref, cols, jnp.where(even, low, top).astype(bf16))
+    for c in copies[6:]:
+        c.wait()
     other_back = other_back.astype(bf16)
     own = (iota((rows, rows), 0) == positive_ref[...]).astype(bf16)
     wide = dot(other_back[n_far:], eye(rank, lanes)).astype(bf16)
@@ -345,20 +394,10 @@
     return acc
 
 
-def sum_kernel(in_ref, out_ref):
-    for j in range(out_ref.shape[0]):
-        out_ref[j] = sum_blocks(in_ref, j).astype(bf16)
-
-
 def spread_kernel(in_ref, out_ref):
     value = sum_blocks(in_ref).astype(bf16)
     for i in range(out_ref.shape[0]):
         out_ref[i] = value
-
-
-def copy_kernel(in_ref, out_ref):
-    for i in range(out_ref.shape[0]):
-        out_ref[i] = in_ref[...]
 
 
 def finish_kernel(in_ref, loss_ref, out_ref):
@@ -376,25 +415,23 @@
 def output_kernel(queries, place_ref, mine_ref, other_ref, down_ref, up_ref, loss_ref):
     rank = down_ref.shape[0]
     part = rank // 2
-    size = mine_ref.shape[3]
+    size = mine_ref.shape[2]
     even = place_ref[2] == 0
     loss = jnp.zeros((8, lanes), f32)
     for i in range(mine_ref.shape[0]):
-        for j in range(mine_ref.shape[1]):
-            mine, other = mine_ref[i, j].astype(f32), other_ref[i, j].astype(f32)
-            at = (i * mine_ref.shape[1] + j) * size
-            cols = slice(at, at + size)
-            top = jnp.where(even, mine[0:rank], other[0:rank])
-            low = jnp.where(even, other[0:rank], mine[0:rank])
-            down_ref[0:part, cols] = top[0:part]
-            down_ref[part:, cols] = low[0:part]
-            up_ref[0:part, cols] = top[part:]
-            up_ref[part:, cols] = low[part:]
-            loss = loss + mine[rank:, 0:lanes]
+        mine, other = mine_ref[i].astype(f32), other_ref[i].astype(f32)
+        cols = slice(i * size, (i + 1) * size)
+        top = jnp.where(even, mine[0:rank], other[0:rank])
+        low = jnp.where(even, other[0:rank], mine[0:rank])
+        down_ref[0:part, cols] = top[0:part]
+        down_ref[part:, cols] = low[0:part]
+        up_ref[0:part, cols] = top[part:]
+        up_ref[part:, cols] = low[part:]
+        loss = loss + mine[rank:, 0:lanes]
     loss_ref[...] = jnp.sum(loss, axis=0, keepdims=True)[:, 0:1] / queries
 
 
-def call(kernel, outs, args, scratch=(), flops=0, moved=0, hbm=(), out_hbm=(), limit=16):
+def call(kernel, outs, args, scratch=(), flops=0, moved=0, hbm=(), out_hbm=(), out_raw=(), limit=16):
     specs = []
     for i, a in enumerate(args):
         space = pltpu.SMEM if a.dtype == jnp.int32 and a.ndim == 1 else pltpu.VMEM
@@ -411,7 +448,10 @@
         kernel,
         out_shape=shapes,
         in_specs=specs,
-        out_specs=[pl.BlockSpec(memory_space=pltpu.VMEM) for _ in shapes],
+        out_specs=[
+            pl.BlockSpec(memory_space=pltpu.HBM if i in out_raw else pltpu.VMEM)
+            for i in range(len(shapes))
+        ],
         scratch_shapes=[pltpu.VMEM(*s) if isinstance(s, tuple) else s for s in scratch],
         compiler_params=pltpu.CompilerParams(vmem_limit_bytes=limit * 1024 * 1024),
         cost_estimate=pl.CostEstimate(flops=flops, bytes_accessed=moved, transcendentals=0),
@@ -430,9 +470,9 @@
     for dy in range(1, grid_y):
         pairs = [(x * grid_y + y, x * grid_y + (y + dy) % grid_y) for x, y in group]
         got.append(lax.ppermute(pieces[dy], "group", pairs))
+    lines = call(regroup_kernel, [((grid_y * 8, got[0].shape[1]), bf16)] * grid_x, got, moved=1000)
     ended = []
-    for dx in range(grid_x):
-        piece = jnp.concatenate([g[dx * 8 : (dx + 1) * 8] for g in got], axis=0)
+    for dx, piece in enumerate(lines):
         if dx:
             pairs = [(x * grid_y + y, (x + dx) % grid_x * grid_y + y) for x, y in group]
             piece = lax.ppermute(piece, "group", pairs)
@@ -470,50 +510,53 @@
         n_other = n_far + rows
         half = width // 2
         block = width // n_group
-        near, *rest = call(
-            lambda *refs: passage_kernel(grid_x, grid_y, *refs),
-            [((n_near, width + lanes), bf16)]
-            + [((grid_x * 8, half + lanes), bf16)] * grid_y
-            + [
+        near, p_unit, p_ext, p_inv, pick = call(
+            passage_kernel,
+            [
+                ((n_near, width + lanes), bf16),
                 ((rows, width), bf16),
                 ((rows, lanes), bf16),
                 ((rows, lanes), f32),
                 ((n_near, rows), bf16),
             ],
-            (
-                place, passage_layer_input, passage_frozen_base, down_t, adapter_up_weight,
-                near_ids, far_ids,
-            ),
+            (passage_layer_input, passage_frozen_base, down_t, adapter_up_weight, near_ids),
             [
                 ((rows, width), bf16),
                 ((rows, width), bf16),
                 (down_t.shape, bf16),
                 (adapter_up_weight.shape, bf16),
                 (near_ids.shape, jnp.int32),
-                (far_ids.shape, jnp.int32),
                 ((rows, width), f32),
-                pltpu.SemaphoreType.DMA((6,)),
-            ],
-            flops=400_000_000, moved=6_000_000, hbm=range(1, 7),
-        )
-        far, (p_unit, p_ext, p_inv, pick) = rest[:grid_y], rest[grid_y:]
+                ((n_near, width + lanes), bf16),
+                pltpu.SemaphoreType.DMA((5,)),
+                pltpu.SemaphoreType.DMA((1 + len(column_tiles(width)),)),
+            ],
+            flops=300_000_000, moved=5_000_000, hbm=range(5), out_hbm=(0, 3), out_raw=(0,),
+        )
+        far = call(
+            lambda *refs: far_pick_kernel(grid_x, grid_y, *refs),
+            [((grid_x * 8, half + lanes), bf16)] * grid_y,
+            (place, passage_layer_input, p_unit, p_ext, far_ids),
+            flops=1000, moved=1000,
+        )
         near = exchange(near.reshape(n_dp, per_near, width + lanes), "dp")
         near = near.reshape(n_near, width + lanes)
         far = far_exchange(far, grid_x, grid_y)
-        q_unit, q_ext, q_inv, near_count, other_count = call(
+        q_pair, q_ext, q_inv, near_count, other_count, shadow = call(
             lambda *refs: query_kernel(grid_x, grid_y, *refs),
             [
-                ((rows, width), bf16),
+                ((rows + rank, width), bf16),
                 ((rows, lanes), bf16),
                 ((rows, lanes), f32),
                 ((n_near, rows), f32),
                 ((n_other, rows), f32),
+                ((2 * rows, rank), bf16),
             ],
             (
                 place, query_layer_input, query_frozen_base, down_t, adapter_up_weight,
                 hard_negative_slots.T,
             ),
-            [((rows, width), f32)], flops=100_000_000, moved=3_000_000,
+            [((rows, width), f32)], flops=1000, moved=1000, out_hbm=(1, 2),
         )
         positive = positive_passage_index.reshape(1, rows)
         other, other_ext, x_far, other_raw = call(
@@ -524,22 +567,19 @@
                 ((n_far, width), bf16),
                 ((n_other, rows), f32),
             ],
-            (*far, q_unit, p_unit, p_ext, positive),
-            flops=300_000_000, moved=4_000_000, out_hbm=(3,),
-        )
-        ret, near_g, other_g, near_radial, other_radial, q_radial = call(
+            (*far, q_pair, p_unit, p_ext, positive),
+            flops=1000, moved=1000, out_hbm=range(4),
+        )
+        ret, weights, radial = call(
             lambda *refs: score_kernel(slope, rank, *refs),
             [
                 ((n_near, lanes), bf16),
-                ((n_near, rows), bf16),
-                ((n_other, rows), bf16),
-                ((n_near, 1), f32),
-                ((n_other, 1), f32),
-                ((rows, 1), f32),
-            ],
-            (near, q_unit, other_raw, near_count, other_count, adapter_up_weight),
+                ((n_near + n_other, rows), bf16),
+                ((n_near + n_other + rows, 1), f32),
+            ],
+            (near, q_pair, other_raw, near_count, other_count, shadow),
             [((n_other, rows), f32), pltpu.SemaphoreType.DMA(())],
-            flops=300_000_000, moved=3_000_000, hbm=(2,),
+            flops=200_000_000, moved=3_000_000, hbm=(2,), out_hbm=(1, 2),
         )
         ret = exchange(ret.reshape(n_dp, per_near, lanes), "dp").reshape(n_near, lanes)
         up_keep, up_send, down_part, row_part = call(
@@ -551,10 +591,24 @@
                 ((rows, lanes), f32),
             ],
             (
-                place, near, other, other_ext, x_far, q_unit, q_ext, q_inv, p_inv, query_layer_input,
-                positive, near_g, other_g, near_radial, other_radial, q_radial, adapter_up_weight,
+                near, q_pair, other, other_ext, x_far, q_ext, q_inv, p_inv, query_layer_input,
+                positive, weights, radial, place.reshape(1, 3),
             ),
-            flops=900_000_000, moved=9_000_000, out_hbm=(2, 3),
+            [
+                ((n_other, width), bf16),
+                ((n_other, lanes), bf16),
+                ((n_far, width), bf16),
+                ((rows, lanes), bf16),
+                ((rows, lanes), f32),
+                ((rows, lanes), f32),
+                ((rows, width), bf16),
+                ((1, rows), jnp.int32),
+                (weights.shape, bf16),
+                (radial.shape, f32),
+                ((1, 3), jnp.int32),
+                pltpu.SemaphoreType.DMA((11,)),
+            ],
+            flops=900_000_000, moved=9_000_000, hbm=range(2, 13), out_hbm=(2, 3),
         )
         swap = [(i, i ^ 1) for i in range(n_dp)]
         up_got = lax.ppermute(up_send, "dp", swap)
@@ -577,23 +631,15 @@
             moved=2_500_000,
         )
         cores = [list(range(c, n_dp, 2)) for c in range(2)]
-        along_x = [[x * grid_y + y for x in range(grid_x)] for y in range(grid_y)]
-        along_y = [[x * grid_y + y for y in range(grid_y)] for x in range(grid_x)]
-        sums = exchange(sums.reshape(grid_x, grid_y, rank, block), "group", along_x)
-        (sums,) = call(sum_kernel, [((grid_y, rank, block), bf16)], (sums,), moved=600_000)
-        sums = exchange(sums, "group", along_y)
+        sums = exchange(sums, "group")
         (sums,) = call(
-            spread_kernel, [((n_dp // 2, rank, block), bf16)], (sums,), moved=600_000
+            spread_kernel, [((n_dp // 2, rank, block), bf16)], (sums,), moved=1_000_000
         )
         sums = exchange(sums, "dp", cores)
         (sums,) = call(
-            finish_kernel, [((grid_y, rank + 8, block), bf16)], (sums, loss), moved=600_000
-        )
-        sums = exchange(sums, "group", along_y)
-        (sums,) = call(
-            copy_kernel, [((grid_x, grid_y, rank + 8, block), bf16)], (sums,), moved=600_000
-        )
-        sums = exchange(sums, "group", along_x)
+            finish_kernel, [((n_group, rank + 8, block), bf16)], (sums, loss), moved=1_000_000
+        )
+        sums = exchange(sums, "group")
         other_sums = lax.ppermute(sums, "dp", swap)
         down, up, loss = call(
             lambda *refs: output_kernel(queries, *refs),

time: 216 us -> 192 us (0.89)
  waiting for transfers between devices: 31.5 us -> 17.3 us
  local copies, waits for them, and re-layouts: 18.4 us -> 4.99 us
  starting transfers between devices: 75.8 us -> 80.2 us
  blocking collectives: 66.1 us -> 62.9 us
    all_to_all x2, waiting for transfers between devices: 21.4 us -> 0.57 us  [exchange(): lax.all_to_all(x, axis, split_axis=0, concat_axis=0, tiled=True, axis_ind...]
    unnamed x71 -> x24, local copies, waits for them, and re-layouts: 18.4 us -> 4.99 us
    ppermute x7, waiting for transfers between devices: 1.59 us -> 12.9 us  [far_exchange(): got.append(lax.ppermute(pieces[dy], 'group', pairs))]
    all_to_all x2, starting transfers between devices: 22.9 us -> 28.5 us  [exchange(): lax.all_to_all(x, axis, split_axis=0, concat_axis=0, tiled=True, axis_ind...]
    ppermute x3, waiting for transfers between devices: 5.78 us -> 1.18 us  [far_exchange(): piece = lax.ppermute(piece, 'group', pairs)]
    all_to_all x5 -> x3, blocking collectives: 66.1 us -> 62.9 us  [exchange(): lax.all_to_all(x, axis, split_axis=0, concat_axis=0, tiled=True, axis_ind...]
  transfers between devices with their start and end apart: 15 -> 15, of which waited for: 6 -> 8; matrix products, arithmetic and copies ran while one was open for 2% -> 0% of each run, Pallas kernels for 5% -> 7%
where the time goes in v3:
time: 192 us; the launch traced here: 190 us
  starting transfers between devices  80.2 us (42%)
  blocking collectives  62.9 us (33%)
  Pallas kernels  23 us (12%)
  waiting for transfers between devices  17.3 us (9%)
  local copies, waits for them, and re-layouts  4.99 us (3%)
    all_to_all x3, blocking collectives, exchange(): lax.all_to_all(x, axis, split_axis=0, concat_axis=0, tiled=True, axis_ind...  62.9 us
    ppermute x7, starting transfers between devices, far_exchange(): got.append(lax.ppermute(pieces[dy], 'group', pairs))  28.5 us
    all_to_all x2, starting transfers between devices, exchange(): lax.all_to_all(x, axis, split_axis=0, concat_axis=0, tiled=True, axis_ind...  28.5 us
    pallas_call x12, Pallas kernels, call(): pl.pallas_call(kernel, out_shape=shapes, in_specs=specs, out_specs=[pl.Bl...  23 us
    ppermute x7, waiting for transfers between devices, far_exchange(): got.append(lax.ppermute(pieces[dy], 'group', pairs))  12.9 us
    ppermute x3, starting transfers between devices, far_exchange(): piece = lax.ppermute(piece, 'group', pairs)  10.5 us
    ppermute x1, starting transfers between devices, body(): other_sums = lax.ppermute(sums, 'dp', swap)  8.04 us
    unnamed x24, local copies, waits for them, and re-layouts  4.99 us
  transfers between devices with their start and end apart: 15, of which 8 were waited for; matrix products, arithmetic and copies ran while one was open for 0% of the time, Pallas kernels for 7%

profile of v3, /device:TPU:1, one launch (start us, length us, event | category | flops | bytes accessed | tf_op | source)
XLA Modules:
  0.0 190.1 jit_solution(3465042741702261263)
XLA Ops:
  0.6 4.6 %shard_map.121 = (bf16[192,4224]{1,0:T(8,128)(2,1)}, bf16[64,4096]{1,0:T(8,128)(2,1)S(1)}, bf16[64,128]{1,0:T(8,128)(2,1)S(1)}, f32[64,128]{1,0:T(8,128)}, bf16[192,64]{1,0:T(8,128)(2,1)S(1)}) custom-call(bf16[64,4096]{1,0:T(8,128)(2,1)} %refs_4_.3, bf16[64,4096]{1,0:T(8,128)(2,1)} %base_hbm.1, bf16[64,4096]{1,0:T(8,128)(2,1)} %bitcast.18, ...), custom_call_target="tpu_custom_call" | custom-call | flops 300000000 | bytes 5000000 | tf_op jit(solution)/shard_map/pallas_call | solution.py:447
  5.2 0.0 copy-start
  5.3 0.0 copy-start.11
  5.3 16.8 %all-to-all-start = ((bf16[24,8,4224]{2,1,0:T(8,128)(2,1)}), bf16[24,8,4224]{2,1,0:T(8,128)(2,1)S(1)}, u32[]{:S(2)}, u32[]{:S(2)}) async-start(bf16[24,8,4224]{2,1,0:T(8,128)(2,1)} %bitcast.25), calls=%async_computation | async-start | bytes 3244032 | tf_op jit(solution)/shard_map/all_to_all | solution.py:462
  22.2 0.1 pad_add_fusion.refs_0_
  22.2 1.3 shard_map.123
  23.5 3.2 %collective-permute-start = (bf16[32,2176]{1,0:T(8,128)(2,1)S(1)}, bf16[32,2176]{1,0:T(8,128)(2,1)S(1)}, u32[]{:S(2)}, u32[]{:S(2)}) collective-permute-start(bf16[32,2176]{1,0:T(8,128)(2,1)S(1)} %get-tuple-element.48), channel_id=1, source_target_pairs={{0,1},{1,2},{2,3},{3,4},{4,5},{5,6},{6,7},{7,0},{8,9},{9,10},{10,1... | collective-permute-start | bytes 417800 | tf_op jit(solution)/shard_map/ppermute | solution.py:472
  26.7 4.2 %collective-permute-start.1 = (bf16[32,2176]{1,0:T(8,128)(2,1)S(1)}, bf16[32,2176]{1,0:T(8,128)(2,1)S(1)}, u32[]{:S(2)}, u32[]{:S(2)}) collective-permute-start(bf16[32,2176]{1,0:T(8,128)(2,1)S(1)} %get-tuple-element.49), channel_id=1, source_target_pairs={{0,2},{1,3},{2,4},{3,5},{4,6},{5,7},{6,0},{7,1},{8,10},{9,11},{10,... | collective-permute-start | bytes 417800 | tf_op jit(solution)/shard_map/ppermute | solution.py:472
  30.9 4.6 %collective-permute-start.2 = (bf16[32,2176]{1,0:T(8,128)(2,1)S(1)}, bf16[32,2176]{1,0:T(8,128)(2,1)S(1)}, u32[]{:S(2)}, u32[]{:S(2)}) collective-permute-start(bf16[32,2176]{1,0:T(8,128)(2,1)S(1)} %get-tuple-element.50), channel_id=1, source_target_pairs={{0,3},{1,4},{2,5},{3,6},{4,7},{5,0},{6,1},{7,2},{8,11},{9,12},{10,... | collective-permute-start | bytes 417800 | tf_op jit(solution)/shard_map/ppermute | solution.py:472
  35.6 3.5 %collective-permute-start.3 = (bf16[32,2176]{1,0:T(8,128)(2,1)S(1)}, bf16[32,2176]{1,0:T(8,128)(2,1)S(1)}, u32[]{:S(2)}, u32[]{:S(2)}) collective-permute-start(bf16[32,2176]{1,0:T(8,128)(2,1)S(1)} %get-tuple-element.51), channel_id=1, source_target_pairs={{0,4},{1,5},{2,6},{3,7},{4,0},{5,1},{6,2},{7,3},{8,12},{9,13},{10,... | collective-permute-start | bytes 417800 | tf_op jit(solution)/shard_map/ppermute | solution.py:472
  39.1 4.9 %collective-permute-start.4 = (bf16[32,2176]{1,0:T(8,128)(2,1)S(1)}, bf16[32,2176]{1,0:T(8,128)(2,1)S(1)}, u32[]{:S(2)}, u32[]{:S(2)}) collective-permute-start(bf16[32,2176]{1,0:T(8,128)(2,1)S(1)} %get-tuple-element.52), channel_id=1, source_target_pairs={{0,5},{1,6},{2,7},{3,0},{4,1},{5,2},{6,3},{7,4},{8,13},{9,14},{10,... | collective-permute-start | bytes 417800 | tf_op jit(solution)/shard_map/ppermute | solution.py:472
  44.0 5.0 %collective-permute-start.5 = (bf16[32,2176]{1,0:T(8,128)(2,1)S(1)}, bf16[32,2176]{1,0:T(8,128)(2,1)S(1)}, u32[]{:S(2)}, u32[]{:S(2)}) collective-permute-start(bf16[32,2176]{1,0:T(8,128)(2,1)S(1)} %get-tuple-element.53), channel_id=1, source_target_pairs={{0,6},{1,7},{2,0},{3,1},{4,2},{5,3},{6,4},{7,5},{8,14},{9,15},{10,... | collective-permute-start | bytes 417800 | tf_op jit(solution)/shard_map/ppermute | solution.py:472
  49.0 0.0 copy-start.4
  49.0 3.1 %collective-permute-start.6 = (bf16[32,2176]{1,0:T(8,128)(2,1)S(1)}, bf16[32,2176]{1,0:T(8,128)(2,1)S(1)}, u32[]{:S(2)}, u32[]{:S(2)}) collective-permute-start(bf16[32,2176]{1,0:T(8,128)(2,1)S(1)} %get-tuple-element.54), channel_id=1, source_target_pairs={{0,7},{1,0},{2,1},{3,2},{4,3},{5,4},{6,5},{7,6},{8,15},{9,8},{10,9... | collective-permute-start | bytes 417800 | tf_op jit(solution)/shard_map/ppermute | solution.py:472
  52.2 0.5 collective-permute-done.3.refs_4_
  52.7 1.8 collective-permute-done.4.refs_5_
  54.5 9.8 %collective-permute-done.5.refs_6_ = bf16[32,2176]{1,0:T(8,128)(2,1)S(1)} collective-permute-done((bf16[32,2176]{1,0:T(8,128)(2,1)S(1)}, bf16[32,2176]{1,0:T(8,128)(2,1)S(1)}, u32[]{:S(2)}, u32[]{:S(2)}) %collective-permute-start.5) | collective-permute-done | bytes 139296 | tf_op jit(solution)/shard_map/ppermute | solution.py:472
  64.2 0.8 collective-permute-done.6.refs_7_
  65.0 0.2 shard_map.124
  65.2 3.1 %collective-permute-start.7 = (bf16[64,2176]{1,0:T(8,128)(2,1)S(1)}, bf16[64,2176]{1,0:T(8,128)(2,1)S(1)}, u32[]{:S(2)}, u32[]{:S(2)}) collective-permute-start(bf16[64,2176]{1,0:T(8,128)(2,1)S(1)} %get-tuple-element.56), channel_id=1, source_target_pairs={{0,8},{1,9},{2,10},{3,11},{4,12},{5,13},{6,14},{7,15},{8,16},{9,17... | collective-permute-start | bytes 835592 | tf_op jit(solution)/shard_map/ppermute | solution.py:478
  68.3 4.3 %collective-permute-start.8 = (bf16[64,2176]{1,0:T(8,128)(2,1)S(1)}, bf16[64,2176]{1,0:T(8,128)(2,1)S(1)}, u32[]{:S(2)}, u32[]{:S(2)}) collective-permute-start(bf16[64,2176]{1,0:T(8,128)(2,1)S(1)} %get-tuple-element.57), channel_id=1, source_target_pairs={{0,16},{1,17},{2,18},{3,19},{4,20},{5,21},{6,22},{7,23},{8,24},{9,... | collective-permute-start | bytes 835592 | tf_op jit(solution)/shard_map/ppermute | solution.py:478
  72.7 3.1 %collective-permute-start.9 = (bf16[64,2176]{1,0:T(8,128)(2,1)S(1)}, bf16[64,2176]{1,0:T(8,128)(2,1)S(1)}, u32[]{:S(2)}, u32[]{:S(2)}) collective-permute-start(bf16[64,2176]{1,0:T(8,128)(2,1)S(1)} %get-tuple-element.58), channel_id=1, source_target_pairs={{0,24},{1,25},{2,26},{3,27},{4,28},{5,29},{6,30},{7,31},{8,0},{9,1... | collective-permute-start | bytes 835592 | tf_op jit(solution)/shard_map/ppermute | solution.py:478
  75.8 1.0 copy-done.1
  76.8 1.0 copy-done.2
  77.8 1.0 copy-done.5
  78.9 1.0 copy-done.6
  79.9 2.6 %shard_map.122 = (bf16[128,4096]{1,0:T(8,128)(2,1)S(1)}, bf16[64,128]{1,0:T(8,128)(2,1)}, f32[64,128]{1,0:T(8,128)}, f32[192,64]{1,0:T(8,128)S(1)}, f32[128,64]{1,0:T(8,128)S(1)}, /*index=5*/bf16[128,64]{1,0:T(8,128)(2,1)S(1)}) custom-call(s32[3]{0:T(128)S(1)} %pad_add_fusion.refs_0_, bf16[64,4096]{1,0:T(8,128)(2,1)S(1)} %copy-done.5, ...), custom_call_target="tpu_custom_call" | custom-call | flops 1000 | bytes 1000 | tf_op jit(solution)/shard_map/pallas_call | solution.py:447
  82.5 1.2 collective-permute-done.9.refs_3_
  83.7 1.9 shard_map.125
  85.6 2.2 %shard_map.126 = (bf16[192,128]{1,0:T(8,128)(2,1)}, bf16[320,64]{1,0:T(8,128)(2,1)}, f32[384,1]{1,0:T(8,128)}) custom-call(bf16[192,4224]{1,0:T(8,128)(2,1)S(1)} %bitcast.16, bf16[128,4096]{1,0:T(8,128)(2,1)S(1)} %get-tuple-element.44.refs_4_.refs_1_.pair_ref, f32[128,64]{1,0:T(8,128)} %get-tuple-element.59.refs_2_, ...), custom_call_target="tpu_custom_call" | custom-call | flops 200000000 | bytes 3000000 | tf_op jit(solution)/shard_map/pallas_call | solution.py:447
  87.8 11.7 %all-to-all-start.1 = ((bf16[24,8,128]{2,1,0:T(8,128)(2,1)}), bf16[24,8,128]{2,1,0:T(8,128)(2,1)S(1)}, u32[]{:S(2)}, u32[]{:S(2)}) async-start(bf16[24,8,128]{2,1,0:T(8,128)(2,1)} %bitcast.10), calls=%async_computation.1 | async-start | bytes 98304 | tf_op jit(solution)/shard_map/all_to_all | solution.py:462
  99.5 0.6 fusion.place_hbm
  100.1 6.0 %shard_map.127 = (f32[32,32,128]{2,1,0:T(8,128)S(1)}, bf16[32,32,128]{2,1,0:T(8,128)(2,1)}, f32[64,4096]{1,0:T(8,128)}, f32[64,128]{1,0:T(8,128)}) custom-call(bf16[192,4224]{1,0:T(8,128)(2,1)S(1)} %bitcast.17, bf16[128,4096]{1,0:T(8,128)(2,1)S(1)} %get-tuple-element.44.refs_4_.refs_1_.pair_ref, bf16[128,4096]{1,0:T(8,128)(2,1)} %get-tuple-element.65.o_hbm, ...), custom_call_target="tpu_custom_call" | custom-call | flops 900000000 | bytes 9000000 | tf_op jit(solution)/shard_map/pallas_call | solution.py:447
  106.1 0.8 copy-done.7
  106.9 2.2 %collective-permute-start.11 = (bf16[32,32,128]{2,1,0:T(8,128)(2,1)}, bf16[32,32,128]{2,1,0:T(8,128)(2,1)S(1)}, u32[]{:S(2)}, u32[]{:S(2)}) collective-permute-start(bf16[32,32,128]{2,1,0:T(8,128)(2,1)} %get-tuple-element.78), channel_id=1, source_target_pairs={{0,32},{32,0},{64,96},{96,64},{128,160},{160,128},{192,224},{224,1... | collective-permute-start | bytes 786440 | tf_op jit(solution)/shard_map/ppermute | solution.py:614
  109.1 0.6 all-to-all-done.1
  109.6 2.1 %shard_map.128 = (f32[32,32,128]{2,1,0:T(8,128)S(1)}, bf16[32,32,128]{2,1,0:T(8,128)(2,1)S(1)}, f32[8,128]{1,0:T(8,128)S(1)}) custom-call(s32[3]{0:T(128)S(1)} %pad_add_fusion.refs_0_, bf16[192,128]{1,0:T(8,128)(2,1)S(1)} %bitcast.20, bf16[192,64]{1,0:T(8,128)(2,1)S(1)} %get-tuple-element.64.refs_2_, f32[64,128]{1,0:T(8,128)} %get-tuple-element.73.refs_3_, ...), custom_call_target="tpu_custom_call" | custom-call | flops 100000000 | bytes 3000000 | tf_op jit(solution)/shard_map/pallas_call | solution.py:447
  111.7 2.4 %collective-permute-start.10 = (bf16[32,32,128]{2,1,0:T(8,128)(2,1)S(1)}, bf16[32,32,128]{2,1,0:T(8,128)(2,1)S(1)}, u32[]{:S(2)}, u32[]{:S(2)}) collective-permute-start(bf16[32,32,128]{2,1,0:T(8,128)(2,1)S(1)} %get-tuple-element.76), channel_id=1, source_target_pairs={{0,32},{32,0},{64,96},{96,64},{128,160},{160,128},{192,224},{224,1... | collective-permute-start | bytes 786440 | tf_op jit(solution)/shard_map/ppermute | solution.py:626
  114.2 1.1 collective-permute-done.10.got_down_ref
  115.3 0.1 shard_map.129
  115.4 21.0 %all_to_all.25.in_ref = bf16[32,64,128]{2,1,0:T(8,128)(2,1)S(1)} all-to-all(bf16[32,64,128]{2,1,0:T(8,128)(2,1)S(1)} %shard_map.129), channel_id=1, replica_groups=mesh['dp'=24,'group'=32] {'group'}, dimensions={0} | all-to-all | bytes 1048576 | tf_op jit(solution)/shard_map/all_to_all | solution.py:462
  136.4 0.1 shard_map.130
  136.5 20.0 %all_to_all.26.in_ref = bf16[12,64,128]{2,1,0:T(8,128)(2,1)S(1)} all-to-all(bf16[12,64,128]{2,1,0:T(8,128)(2,1)S(1)} %shard_map.130), channel_id=1, replica_groups={{0,64,128,192,256,320,384,448,512,576,640,704},{32,96,160,224,288,352,4..., dimensions={0} | all-to-all | bytes 393216 | tf_op jit(solution)/shard_map/all_to_all | solution.py:462
  156.6 0.1 shard_map.131
  156.6 21.9 %all_to_all.27.refs_1_ = bf16[32,72,128]{2,1,0:T(8,128)(2,1)S(1)} all-to-all(bf16[32,72,128]{2,1,0:T(8,128)(2,1)S(1)} %shard_map.131), channel_id=1, replica_groups=mesh['dp'=24,'group'=32] {'group'}, dimensions={0} | all-to-all | bytes 1179648 | tf_op jit(solution)/shard_map/all_to_all | solution.py:462
  178.5 8.0 %collective-permute-start.12 = (bf16[32,72,128]{2,1,0:T(8,128)(2,1)S(1)}, bf16[32,72,128]{2,1,0:T(8,128)(2,1)S(1)}, u32[]{:S(2)}, u32[]{:S(2)}) collective-permute-start(bf16[32,72,128]{2,1,0:T(8,128)(2,1)S(1)} %all_to_all.27.refs_1_), channel_id=1, source_target_pairs={{0,32},{32,0},{64,96},{96,64},{128,160},{160,128},{192,224},{224,1... | collective-permute-start | bytes 1769480 | tf_op jit(solution)/shard_map/ppermute | solution.py:643
  186.5 1.6 collective-permute-done.12.refs_2_
  188.2 1.9 %shard_map.132 = (f32[64,4096]{1,0:T(8,128)}, f32[64,4096]{1,0:T(8,128)}, f32[1,1]{1,0:T(1,128)}) custom-call(s32[3]{0:T(128)S(1)} %pad_add_fusion.refs_0_, bf16[32,72,128]{2,1,0:T(8,128)(2,1)S(1)} %all_to_all.27.refs_1_, bf16[32,72,128]{2,1,0:T(8,128)(2,1)S(1)} %collective-permute-done.12.refs_2_), custom_call_target="tpu_custom_call" | custom-call | bytes 3500000 | tf_op jit(solution)/shard_map/pallas_call | solution.py:447
  (23 shorter events, 0.1 us)
Async XLA Ops:
  5.2 17.0 %copy-start.3 = (bf16[64,4096]{1,0:T(8,128)(2,1)}, bf16[64,4096]{1,0:T(8,128)(2,1)S(1)}, u32[]{:S(2)}) copy-start(bf16[64,4096]{1,0:T(8,128)(2,1)S(1)} %get-tuple-element.45.refs_2_.refs_5_) | copy-start | bytes 1572868
  5.2 17.0 %copy-start = (bf16[64,4096]{1,0:T(8,128)(2,1)S(1)}, bf16[64,4096]{1,0:T(8,128)(2,1)}, u32[]{:S(2)}) copy-start(bf16[64,4096]{1,0:T(8,128)(2,1)} %refs_4_.3) | copy-start | bytes 1572868
  5.3 17.0 %copy-start.11 = (s32[32,2]{0,1:T(2,128)S(1)}, s32[32,2]{0,1:T(2,128)}, u32[]{:S(2)}) copy-start(s32[32,2]{0,1:T(2,128)} %param.19) | copy-start | bytes 772
  5.3 80.3 %all-to-all-start = ((bf16[24,8,4224]{2,1,0:T(8,128)(2,1)}), bf16[24,8,4224]{2,1,0:T(8,128)(2,1)S(1)}, u32[]{:S(2)}, u32[]{:S(2)}) async-start(bf16[24,8,4224]{2,1,0:T(8,128)(2,1)} %bitcast.25), calls=%async_computation | async-start | bytes 3244032 | tf_op jit(solution)/shard_map/all_to_all | solution.py:462
  22.1 53.6 %copy-start.9 = (s32[64,32]{0,1:T(8,128)S(1)}, s32[64,32]{0,1:T(8,128)}, u32[]{:S(2)}) copy-start(s32[64,32]{0,1:T(8,128)} %param.17) | copy-start | bytes 24580
  23.5 20.5 %collective-permute-start = (bf16[32,2176]{1,0:T(8,128)(2,1)S(1)}, bf16[32,2176]{1,0:T(8,128)(2,1)S(1)}, u32[]{:S(2)}, u32[]{:S(2)}) collective-permute-start(bf16[32,2176]{1,0:T(8,128)(2,1)S(1)} %get-tuple-element.48), channel_id=1, source_target_pairs={{0,1},{1,2},{2,3},{3,4},{4,5},{5,6},{6,7},{7,0},{8,9},{9,10},{10,1... | collective-permute-start | bytes 417800 | tf_op jit(solution)/shard_map/ppermute | solution.py:472
  26.7 22.3 %collective-permute-start.1 = (bf16[32,2176]{1,0:T(8,128)(2,1)S(1)}, bf16[32,2176]{1,0:T(8,128)(2,1)S(1)}, u32[]{:S(2)}, u32[]{:S(2)}) collective-permute-start(bf16[32,2176]{1,0:T(8,128)(2,1)S(1)} %get-tuple-element.49), channel_id=1, source_target_pairs={{0,2},{1,3},{2,4},{3,5},{4,6},{5,7},{6,0},{7,1},{8,10},{9,11},{10,... | collective-permute-start | bytes 417800 | tf_op jit(solution)/shard_map/ppermute | solution.py:472
  30.9 21.2 %collective-permute-start.2 = (bf16[32,2176]{1,0:T(8,128)(2,1)S(1)}, bf16[32,2176]{1,0:T(8,128)(2,1)S(1)}, u32[]{:S(2)}, u32[]{:S(2)}) collective-permute-start(bf16[32,2176]{1,0:T(8,128)(2,1)S(1)} %get-tuple-element.50), channel_id=1, source_target_pairs={{0,3},{1,4},{2,5},{3,6},{4,7},{5,0},{6,1},{7,2},{8,11},{9,12},{10,... | collective-permute-start | bytes 417800 | tf_op jit(solution)/shard_map/ppermute | solution.py:472
  35.6 17.1 %collective-permute-start.3 = (bf16[32,2176]{1,0:T(8,128)(2,1)S(1)}, bf16[32,2176]{1,0:T(8,128)(2,1)S(1)}, u32[]{:S(2)}, u32[]{:S(2)}) collective-permute-start(bf16[32,2176]{1,0:T(8,128)(2,1)S(1)} %get-tuple-element.51), channel_id=1, source_target_pairs={{0,4},{1,5},{2,6},{3,7},{4,0},{5,1},{6,2},{7,3},{8,12},{9,13},{10,... | collective-permute-start | bytes 417800 | tf_op jit(solution)/shard_map/ppermute | solution.py:472
  39.1 15.3 %collective-permute-start.4 = (bf16[32,2176]{1,0:T(8,128)(2,1)S(1)}, bf16[32,2176]{1,0:T(8,128)(2,1)S(1)}, u32[]{:S(2)}, u32[]{:S(2)}) collective-permute-start(bf16[32,2176]{1,0:T(8,128)(2,1)S(1)} %get-tuple-element.52), channel_id=1, source_target_pairs={{0,5},{1,6},{2,7},{3,0},{4,1},{5,2},{6,3},{7,4},{8,13},{9,14},{10,... | collective-permute-start | bytes 417800 | tf_op jit(solution)/shard_map/ppermute | solution.py:472
  44.0 20.2 %collective-permute-start.5 = (bf16[32,2176]{1,0:T(8,128)(2,1)S(1)}, bf16[32,2176]{1,0:T(8,128)(2,1)S(1)}, u32[]{:S(2)}, u32[]{:S(2)}) collective-permute-start(bf16[32,2176]{1,0:T(8,128)(2,1)S(1)} %get-tuple-element.53), channel_id=1, source_target_pairs={{0,6},{1,7},{2,0},{3,1},{4,2},{5,3},{6,4},{7,5},{8,14},{9,15},{10,... | collective-permute-start | bytes 417800 | tf_op jit(solution)/shard_map/ppermute | solution.py:472
  49.0 34.7 %copy-start.4 = (bf16[64,4096]{1,0:T(8,128)(2,1)S(1)}, bf16[64,4096]{1,0:T(8,128)(2,1)}, u32[]{:S(2)}) copy-start(bf16[64,4096]{1,0:T(8,128)(2,1)} %copy-done.3) | copy-start | bytes 1572868
  49.0 34.7 %copy-start.10 = (s32[64]{0:T(128)S(1)}, s32[64]{0:T(128)}, u32[]{:S(2)}) copy-start(s32[64]{0:T(128)} %param.16) | copy-start | bytes 772
  49.0 16.0 %collective-permute-start.6 = (bf16[32,2176]{1,0:T(8,128)(2,1)S(1)}, bf16[32,2176]{1,0:T(8,128)(2,1)S(1)}, u32[]{:S(2)}, u32[]{:S(2)}) collective-permute-start(bf16[32,2176]{1,0:T(8,128)(2,1)S(1)} %get-tuple-element.54), channel_id=1, source_target_pairs={{0,7},{1,0},{2,1},{3,2},{4,3},{5,4},{6,5},{7,6},{8,15},{9,8},{10,9... | collective-permute-start | bytes 417800 | tf_op jit(solution)/shard_map/ppermute | solution.py:472
  65.2 17.3 %collective-permute-start.7 = (bf16[64,2176]{1,0:T(8,128)(2,1)S(1)}, bf16[64,2176]{1,0:T(8,128)(2,1)S(1)}, u32[]{:S(2)}, u32[]{:S(2)}) collective-permute-start(bf16[64,2176]{1,0:T(8,128)(2,1)S(1)} %get-tuple-element.56), channel_id=1, source_target_pairs={{0,8},{1,9},{2,10},{3,11},{4,12},{5,13},{6,14},{7,15},{8,16},{9,17... | collective-permute-start | bytes 835592 | tf_op jit(solution)/shard_map/ppermute | solution.py:478
  68.3 14.2 %collective-permute-start.8 = (bf16[64,2176]{1,0:T(8,128)(2,1)S(1)}, bf16[64,2176]{1,0:T(8,128)(2,1)S(1)}, u32[]{:S(2)}, u32[]{:S(2)}) collective-permute-start(bf16[64,2176]{1,0:T(8,128)(2,1)S(1)} %get-tuple-element.57), channel_id=1, source_target_pairs={{0,16},{1,17},{2,18},{3,19},{4,20},{5,21},{6,22},{7,23},{8,24},{9,... | collective-permute-start | bytes 835592 | tf_op jit(solution)/shard_map/ppermute | solution.py:478
  72.7 11.0 %collective-permute-start.9 = (bf16[64,2176]{1,0:T(8,128)(2,1)S(1)}, bf16[64,2176]{1,0:T(8,128)(2,1)S(1)}, u32[]{:S(2)}, u32[]{:S(2)}) collective-permute-start(bf16[64,2176]{1,0:T(8,128)(2,1)S(1)} %get-tuple-element.58), channel_id=1, source_target_pairs={{0,24},{1,25},{2,26},{3,27},{4,28},{5,29},{6,30},{7,31},{8,0},{9,1... | collective-permute-start | bytes 835592 | tf_op jit(solution)/shard_map/ppermute | solution.py:478
  75.7 1.0 copy-start.1
  76.8 1.0 copy-start.2
  77.8 1.0 copy-start.5
  78.9 1.0 copy-start.6
  87.8 21.8 %all-to-all-start.1 = ((bf16[24,8,128]{2,1,0:T(8,128)(2,1)}), bf16[24,8,128]{2,1,0:T(8,128)(2,1)S(1)}, u32[]{:S(2)}, u32[]{:S(2)}) async-start(bf16[24,8,128]{2,1,0:T(8,128)(2,1)} %bitcast.10), calls=%async_computation.1 | async-start | bytes 98304 | tf_op jit(solution)/shard_map/all_to_all | solution.py:462
  106.1 0.8 copy-start.7
  106.9 8.4 %copy-start.8 = (f32[32,32,128]{2,1,0:T(8,128)S(1)}, f32[32,32,128]{2,1,0:T(8,128)}, u32[]{:S(2)}) copy-start(f32[32,32,128]{2,1,0:T(8,128)} %copy-done.7) | copy-start | bytes 1572868
  106.9 7.3 %collective-permute-start.11 = (bf16[32,32,128]{2,1,0:T(8,128)(2,1)}, bf16[32,32,128]{2,1,0:T(8,128)(2,1)S(1)}, u32[]{:S(2)}, u32[]{:S(2)}) collective-permute-start(bf16[32,32,128]{2,1,0:T(8,128)(2,1)} %get-tuple-element.78), channel_id=1, source_target_pairs={{0,32},{32,0},{64,96},{96,64},{128,160},{160,128},{192,224},{224,1... | collective-permute-start | bytes 786440 | tf_op jit(solution)/shard_map/ppermute | solution.py:614
  111.7 3.6 %collective-permute-start.10 = (bf16[32,32,128]{2,1,0:T(8,128)(2,1)S(1)}, bf16[32,32,128]{2,1,0:T(8,128)(2,1)S(1)}, u32[]{:S(2)}, u32[]{:S(2)}) collective-permute-start(bf16[32,32,128]{2,1,0:T(8,128)(2,1)S(1)} %get-tuple-element.76), channel_id=1, source_target_pairs={{0,32},{32,0},{64,96},{96,64},{128,160},{160,128},{192,224},{224,1... | collective-permute-start | bytes 786440 | tf_op jit(solution)/shard_map/ppermute | solution.py:626
  178.5 9.7 %collective-permute-start.12 = (bf16[32,72,128]{2,1,0:T(8,128)(2,1)S(1)}, bf16[32,72,128]{2,1,0:T(8,128)(2,1)S(1)}, u32[]{:S(2)}, u32[]{:S(2)}) collective-permute-start(bf16[32,72,128]{2,1,0:T(8,128)(2,1)S(1)} %all_to_all.27.refs_1_), channel_id=1, source_target_pairs={{0,32},{32,0},{64,96},{96,64},{128,160},{160,128},{192,224},{224,1... | collective-permute-start | bytes 1769480 | tf_op jit(solution)/shard_map/ppermute | solution.py:643

commit v4 on v3

--- a/solution.py
+++ b/solution.py
@@ -179,22 +179,15 @@
     step = min(size, cols.stop - cols.start)
     for c in range(cols.start, cols.stop, step):
         at = c % size
-        ref[c // size, :, at : at + step] = value[:, c - cols.start : c - cols.start + step]
-
-
-def load_blocks(ref, cols):
-    size = ref.shape[2]
-    step = min(size, cols.stop - cols.start)
-    parts = []
-    for c in range(cols.start, cols.stop, step):
-        parts.append(ref[c // size, :, c % size : c % size + step])
-    return parts[0] if len(parts) == 1 else jnp.concatenate(parts, axis=1)
-
-
-def regroup_kernel(*refs):
+        block = value[:, c - cols.start : c - cols.start + step]
+        ref[c // size, 0 : value.shape[0], at : at + step] = block
+
+
+def regroup_kernel(order, *refs):
     size = 8
     count = refs[0].shape[0] // size
-    n_in = len(refs) - count
+    n_in = len(order)
+    refs = [refs[order.index(dy)] for dy in range(n_in)] + list(refs[n_in:])
     for dx in range(0, count, 2):
         for dy in range(0, n_in, 2):
             a, b = [refs[dy + i][dx * size : (dx + 2) * size, :] for i in range(2)]
@@ -204,9 +197,10 @@
 
 
 def far_kernel(count, *refs):
-    far_refs = refs[:count]
-    q_ref, unit_ref, p_ext_ref, positive_ref = refs[count : count + 4]
-    o_ref, ext_ref, x_far_ref, raw_ref = refs[count + 4 :]
+    order = far_order(count)
+    far_refs = [refs[order.index(dx)] for dx in range(count)]
+    pair_ref, unit_ref, p_ext_ref, positive_ref = refs[count : count + 4]
+    o_ref, ext_ref, x_far_ref, both_ref = refs[count + 4 :]
     rows, width = unit_ref.shape
     half = width // 2
     total = far_refs[0].shape[0]
@@ -235,21 +229,22 @@
     for cols in column_tiles(width):
         o_ref[n_far:, cols] = dot(own_t, unit_ref[:, cols]).astype(bf16)
     ext_ref[n_far:, :] = dot(own_t, p_ext_ref[...]).astype(bf16)
-    raw_ref[...] = dot(o_ref[...], q_ref[0:rows, :], 1, 1)
+    both_ref[...] = dot(o_ref[...], pair_ref[...], 1, 1)
 
 
 def score_kernel(
-    slope, rank, near_ref, pair_ref, other_raw_hbm, near_count_ref, other_count_ref, shadow_ref,
-    ret_ref, g_ref, radial_ref, other_raw_ref, sem,
+    slope, rank, near_ref, pair_ref, other_both_hbm, near_count_ref, other_count_ref, shadow_hbm,
+    ret_ref, g_ref, radial_ref, near_up_ref, other_both_ref, shadow_ref, sems,
 ):
-    copy = pltpu.make_async_copy(other_raw_hbm, other_raw_ref, sem)
-    copy.start()
+    copies = fetch([(other_both_hbm, other_both_ref), (shadow_hbm, shadow_ref)], sems)
     width = pair_ref.shape[1]
     n_near, rows = near_count_ref.shape
     both = dot(near_ref[:, :width], pair_ref[...], 1, 1)
     near_raw, near_up = both[:, 0:rows], both[:, rows:]
-    copy.wait()
-    other_raw = other_raw_ref[...]
+    near_up_ref[...] = near_up
+    for c in copies:
+        c.wait()
+    other_raw = other_both_ref[:, 0:rows]
     n_other = other_raw.shape[0]
     n_far = n_other - rows
     near_exp = jnp.exp(near_raw / logit_divisor - offset) * near_count_ref[...]
@@ -286,20 +281,31 @@
     ret_ref[...] = back.astype(bf16)
 
 
+def halves(value):
+    high = value.astype(bf16)
+    return high, (value - high.astype(f32)).astype(bf16)
+
+
+def wide_dot(a, value):
+    high, low = halves(value)
+    return dot(a, high) + dot(a, low)
+
+
 def local_kernel(
-    near_ref, pair_ref, o_hbm, o_ext_hbm, x_far_hbm, q_ext_hbm, q_inv_hbm, p_inv_hbm, x_q_hbm,
-    positive_hbm, g_hbm, radial_hbm, place_hbm,
+    place_ref, near_ref, pair_ref, shadow_hbm, o_hbm, o_ext_hbm, x_far_hbm, q_ext_hbm, q_inv_hbm,
+    p_inv_hbm, x_q_hbm, positive_hbm, g_hbm, radial_hbm, near_up_hbm, other_both_hbm,
     up_keep_ref, up_send_ref, down_ref, row_ref,
-    o_ref, o_ext_ref, x_far_ref, q_ext_ref, q_inv_ref, p_inv_ref, x_q_ref, positive_ref, g_ref,
-    radial_ref, place_ref, sems,
+    shadow_ref, o_ref, o_ext_ref, x_far_ref, q_ext_ref, q_inv_ref, p_inv_ref, x_q_ref,
+    positive_ref, g_ref, radial_ref, near_up_ref, other_both_ref, sems,
 ):
     pairs = [
-        (g_hbm, g_ref), (radial_hbm, radial_ref), (o_hbm, o_ref), (o_ext_hbm, o_ext_ref),
-        (q_ext_hbm, q_ext_ref), (place_hbm, place_ref), (positive_hbm, positive_ref),
-        (q_inv_hbm, q_inv_ref), (p_inv_hbm, p_inv_ref), (x_far_hbm, x_far_ref), (x_q_hbm, x_q_ref),
+        (g_hbm, g_ref), (radial_hbm, radial_ref), (q_ext_hbm, q_ext_ref), (o_ext_hbm, o_ext_ref),
+        (o_hbm, o_ref), (positive_hbm, positive_ref), (q_inv_hbm, q_inv_ref), (p_inv_hbm, p_inv_ref),
+        (shadow_hbm, shadow_ref), (near_up_hbm, near_up_ref), (other_both_hbm, other_both_ref),
+        (x_far_hbm, x_far_ref), (x_q_hbm, x_q_ref),
     ]
     copies = fetch(pairs, sems)
-    for c in copies[:6]:
+    for c in copies[:4]:
         c.wait()
     rows, width = x_q_ref.shape
     rank = pair_ref.shape[0] - rows
@@ -307,43 +313,46 @@
     n_near = near_ref.shape[0]
     n_far = o_ref.shape[0] - rows
     n_all = n_near + n_far + rows
-    even = place_ref[0:1, 2:3] == 0
+    even = place_ref[2] == 0
     near_gt, other_gt = g_ref[0:n_near, :], g_ref[n_near:, :]
     near_g, other_g = flip(near_gt), flip(other_gt)
     near_radial = radial_ref[0:n_near, :]
     other_radial = radial_ref[n_near:n_all, :]
     q_radial = radial_ref[n_all:, :]
-    q_lat = flip(q_ext_ref[...])[0:rank]
-    near_lat = flip(near_ref[:, width:])[0:rank]
-    other_lat = flip(o_ext_ref[...])[0:rank]
-    q_back = jnp.zeros((rows, rank), f32)
-    other_back = jnp.zeros((n_far + rows, rank), f32)
+    q_ext, near_ext, o_ext = q_ext_ref[...], near_ref[:, width:], o_ext_ref[...]
+
+    def spread(value):
+        high, low = halves(value)
+        return jnp.concatenate([flip(high)[0:rank], flip(low)[0:rank]], axis=0)
+
+    near_a = spread(dot(near_gt, q_ext) - near_ext.astype(f32) * near_radial)
+    other_a = spread(dot(other_gt, q_ext) - o_ext.astype(f32) * other_radial)
+    q_a = spread(dot(near_g, near_ext) + dot(other_g, o_ext) - q_ext.astype(f32) * q_radial)
+    copies[4].wait()
     for cols in column_tiles(width):
-        q = pair_ref[0:rows, cols]
-        near = near_ref[:, cols]
-        other = o_ref[:, cols]
-        up = pair_ref[rows:, cols]
-        q_t = dot(near_g, near) + dot(other_g, other) - q.astype(f32) * q_radial
-        near_t = dot(near_gt, q) - near.astype(f32) * near_radial
-        other_t = dot(other_gt, q) - other.astype(f32) * other_radial
-        q_t, near_t, other_t = q_t.astype(bf16), near_t.astype(bf16), other_t.astype(bf16)
-        q_back = q_back + dot(q_t, up, 1, 1)
-        other_back = other_back + dot(other_t, up, 1, 1)
-        grad = dot(q_lat, q_t) + dot(near_lat, near_t) + dot(other_lat, other_t)
-        grad = adapter_scale * grad
+        grad = (
+            dot(near_a, near_ref[:, cols])
+            + dot(other_a, o_ref[:, cols])
+            + dot(q_a, pair_ref[0:rows, cols])
+        )
+        grad = adapter_scale * (grad[0:rank] + grad[rank:])
         top, low = grad[0:part], grad[part:]
         store_blocks(up_keep_ref, cols, jnp.where(even, top, low))
         store_blocks(up_send_ref, cols, jnp.where(even, low, top).astype(bf16))
-    for c in copies[6:]:
+    for c in copies[5:]:
         c.wait()
-    other_back = other_back.astype(bf16)
+    other_up = other_both_ref[:, rows:]
+    q_back = wide_dot(near_g, near_up_ref[...]) + wide_dot(other_g, other_up)
+    q_up = shadow_ref[0:rows, :].astype(f32) + shadow_ref[rows:, :].astype(f32)
+    q_back = (q_back - q_up * q_radial).astype(bf16).astype(f32)
+    other_back = dot(other_gt, shadow_ref[0:rows, :]) + dot(other_gt, shadow_ref[rows:, :])
+    other_back = (other_back - other_up * other_radial).astype(bf16)
     own = (iota((rows, rows), 0) == positive_ref[...]).astype(bf16)
     wide = dot(other_back[n_far:], eye(rank, lanes)).astype(bf16)
     row_sum = dot(own, wide)
     row_ref[...] = jnp.where(iota(row_sum.shape, 1) < rank, row_sum, p_inv_ref[...])
-    q_back = q_back.astype(bf16).astype(f32)
     dz_q = (adapter_scale * q_inv_ref[:, 0:1] * q_back).astype(bf16)
-    far_ext = o_ext_ref[0:n_far, :].astype(f32)
+    far_ext = o_ext[0:n_far, :].astype(f32)
     far_inv = far_ext[:, rank : rank + 1] + far_ext[:, rank + 1 : rank + 2]
     dz_f = (adapter_scale * far_inv * other_back[0:n_far].astype(f32)).astype(bf16)
     dz_qt, dz_ft = flip(dz_q), flip(dz_f)
@@ -352,21 +361,22 @@
 
 
 def down_kernel(
-    per_near, place_ref, ret_ref, pick_ref, row_hbm, x_p_ref, down_hbm,
+    per_near, place_ref, ret_ref, pick_ref, row_hbm, x_p_ref, down_hbm, up_keep_hbm, up_send_hbm,
     keep_ref, send_ref, loss_ref, row_ref, down_ref, sems,
 ):
-    row_copy = pltpu.make_async_copy(row_hbm, row_ref, sems.at[0])
-    down_copy = pltpu.make_async_copy(down_hbm, down_ref, sems.at[1])
-    row_copy.start()
-    down_copy.start()
     rank = down_ref.shape[0]
     part = rank // 2
+    pairs = [
+        (row_hbm, row_ref), (down_hbm, down_ref),
+        (up_send_hbm, send_ref.at[:, part:]), (up_keep_hbm, keep_ref.at[:, part:]),
+    ]
+    copies = fetch(pairs, sems)
     ret = ret_ref[...]
     row_sum = dot(flip(pick_ref[...]), ret)[:, 0:rank]
-    row_copy.wait()
+    copies[0].wait()
     row_sum = row_sum + row_ref[:, 0:rank]
     dz_t = flip((adapter_scale * row_ref[:, rank : rank + 1] * row_sum).astype(bf16))
-    down_copy.wait()
+    copies[1].wait()
     even = place_ref[2] == 0
     for cols in column_tiles(x_p_ref.shape[1]):
         grad = dot(dz_t, x_p_ref[:, cols]) + down_ref[:, cols]
@@ -378,13 +388,13 @@
     chosen = first & ((lane == rank) | (lane == rank + 1))
     share = jnp.sum(jnp.where(chosen, ret.astype(f32), 0.0), axis=1, keepdims=True)
     loss_ref[...] = jnp.broadcast_to(jnp.sum(share, axis=0, keepdims=True), loss_ref.shape)
-
-
-def add_kernel(down_ref, got_down_ref, up_ref, got_up_ref, out_ref):
-    part = down_ref.shape[1]
-    for i in range(down_ref.shape[0]):
-        out_ref[i, 0:part] = (down_ref[i] + got_down_ref[i].astype(f32)).astype(bf16)
-        out_ref[i, part:] = (up_ref[i] + got_up_ref[i].astype(f32)).astype(bf16)
+    copies[2].wait()
+    copies[3].wait()
+
+
+def add_kernel(keep_ref, got_ref, out_ref):
+    for i in range(keep_ref.shape[0]):
+        out_ref[i] = (keep_ref[i] + got_ref[i].astype(f32)).astype(bf16)
 
 
 def sum_blocks(ref, *at):
@@ -464,20 +474,37 @@
     )
 
 
+def both_ways(size):
+    ahead = [1] + list(range(size // 2, 1, -1))
+    behind = [size - 1] + list(range(size // 2 + 1, size - 1))
+    order = []
+    for i in range(len(ahead)):
+        order += ahead[i : i + 1] + behind[i : i + 1]
+    return [d for i, d in enumerate(order) if d not in order[:i]]
+
+
 def far_exchange(pieces, grid_x, grid_y):
     group = [(x, y) for x in range(grid_x) for y in range(grid_y)]
+    order = [0, *both_ways(grid_y)]
     got = [pieces[0]]
-    for dy in range(1, grid_y):
+    for dy in order[1:]:
         pairs = [(x * grid_y + y, x * grid_y + (y + dy) % grid_y) for x, y in group]
         got.append(lax.ppermute(pieces[dy], "group", pairs))
-    lines = call(regroup_kernel, [((grid_y * 8, got[0].shape[1]), bf16)] * grid_x, got, moved=1000)
-    ended = []
-    for dx, piece in enumerate(lines):
-        if dx:
-            pairs = [(x * grid_y + y, (x + dx) % grid_x * grid_y + y) for x, y in group]
-            piece = lax.ppermute(piece, "group", pairs)
-        ended.append(piece)
+    lines = call(
+        lambda *refs: regroup_kernel(order, *refs),
+        [((grid_y * 8, got[0].shape[1]), bf16)] * grid_x,
+        got,
+        moved=1000,
+    )
+    ended = [lines[0]]
+    for dx in far_order(grid_x)[1:]:
+        pairs = [(x * grid_y + y, (x + dx) % grid_x * grid_y + y) for x, y in group]
+        ended.append(lax.ppermute(lines[dx], "group", pairs))
     return ended
+
+
+def far_order(size):
+    return [0, *sorted(range(1, size), key=lambda d: -min(d, size - d))]
 
 
 def make_body(grid_x, grid_y):
@@ -556,30 +583,35 @@
                 place, query_layer_input, query_frozen_base, down_t, adapter_up_weight,
                 hard_negative_slots.T,
             ),
-            [((rows, width), f32)], flops=1000, moved=1000, out_hbm=(1, 2),
+            [((rows, width), f32)], flops=1000, moved=1000, out_hbm=(1, 2, 5),
         )
         positive = positive_passage_index.reshape(1, rows)
-        other, other_ext, x_far, other_raw = call(
+        other, other_ext, x_far, other_both = call(
             lambda *refs: far_kernel(grid_x, *refs),
             [
                 ((n_other, width), bf16),
                 ((n_other, lanes), bf16),
                 ((n_far, width), bf16),
-                ((n_other, rows), f32),
+                ((n_other, rows + rank), f32),
             ],
             (*far, q_pair, p_unit, p_ext, positive),
             flops=1000, moved=1000, out_hbm=range(4),
         )
-        ret, weights, radial = call(
+        ret, weights, radial, near_up = call(
             lambda *refs: score_kernel(slope, rank, *refs),
             [
                 ((n_near, lanes), bf16),
                 ((n_near + n_other, rows), bf16),
                 ((n_near + n_other + rows, 1), f32),
-            ],
-            (near, q_pair, other_raw, near_count, other_count, shadow),
-            [((n_other, rows), f32), pltpu.SemaphoreType.DMA(())],
-            flops=200_000_000, moved=3_000_000, hbm=(2,), out_hbm=(1, 2),
+                ((n_near, rank), f32),
+            ],
+            (near, q_pair, other_both, near_count, other_count, shadow),
+            [
+                ((n_other, rows + rank), f32),
+                (shadow.shape, bf16),
+                pltpu.SemaphoreType.DMA((2,)),
+            ],
+            flops=200_000_000, moved=3_000_000, hbm=(2, 5), out_hbm=(1, 2, 3),
         )
         ret = exchange(ret.reshape(n_dp, per_near, lanes), "dp").reshape(n_near, lanes)
         up_keep, up_send, down_part, row_part = call(
@@ -591,10 +623,11 @@
                 ((rows, lanes), f32),
             ],
             (
-                near, q_pair, other, other_ext, x_far, q_ext, q_inv, p_inv, query_layer_input,
-                positive, weights, radial, place.reshape(1, 3),
+                place, near, q_pair, shadow, other, other_ext, x_far, q_ext, q_inv, p_inv,
+                query_layer_input, positive, weights, radial, near_up, other_both,
             ),
             [
+                (shadow.shape, bf16),
                 ((n_other, width), bf16),
                 ((n_other, lanes), bf16),
                 ((n_far, width), bf16),
@@ -605,31 +638,26 @@
                 ((1, rows), jnp.int32),
                 (weights.shape, bf16),
                 (radial.shape, f32),
-                ((1, 3), jnp.int32),
-                pltpu.SemaphoreType.DMA((11,)),
-            ],
-            flops=900_000_000, moved=9_000_000, hbm=range(2, 13), out_hbm=(2, 3),
+                (near_up.shape, f32),
+                (other_both.shape, f32),
+                pltpu.SemaphoreType.DMA((13,)),
+            ],
+            flops=900_000_000, moved=9_000_000, hbm=range(3, 16), out_hbm=range(4),
         )
         swap = [(i, i ^ 1) for i in range(n_dp)]
-        up_got = lax.ppermute(up_send, "dp", swap)
         keep, send, loss = call(
             lambda *refs: down_kernel(per_near, *refs),
             [
-                ((n_group, part, block), f32),
-                ((n_group, part, block), bf16),
+                ((n_group, rank, block), f32),
+                ((n_group, rank, block), bf16),
                 ((8, lanes), f32),
             ],
-            (place, ret, pick, row_part, passage_layer_input, down_part),
-            [((rows, lanes), f32), ((rank, width), f32), pltpu.SemaphoreType.DMA((2,))],
-            flops=100_000_000, moved=3_000_000, hbm=(3, 5),
+            (place, ret, pick, row_part, passage_layer_input, down_part, up_keep, up_send),
+            [((rows, lanes), f32), ((rank, width), f32), pltpu.SemaphoreType.DMA((4,))],
+            flops=100_000_000, moved=3_000_000, hbm=(3, 5, 6, 7),
         )
         got = lax.ppermute(send, "dp", swap)
-        (sums,) = call(
-            add_kernel,
-            [((n_group, rank, block), bf16)],
-            (keep, got, up_keep, up_got),
-            moved=2_500_000,
-        )
+        (sums,) = call(add_kernel, [((n_group, rank, block), bf16)], (keep, got), moved=2_500_000)
         cores = [list(range(c, n_dp, 2)) for c in range(2)]
         sums = exchange(sums, "group")
         (sums,) = call(

time: 192 us -> 180 us (0.938)
  blocking collectives: 62.9 us -> 57.8 us
  starting transfers between devices: 80.2 us -> 76.2 us
    all_to_all x3, blocking collectives: 62.9 us -> 57.8 us  [exchange(): lax.all_to_all(x, axis, split_axis=0, concat_axis=0, tiled=True, axis_ind...]
    all_to_all x2, waiting for transfers between devices: 0.57 us -> 5.66 us  [exchange(): lax.all_to_all(x, axis, split_axis=0, concat_axis=0, tiled=True, axis_ind...]
    ppermute x7, waiting for transfers between devices: 12.9 us -> 8.01 us  [far_exchange(): got.append(lax.ppermute(pieces[dy], 'group', pairs))]
    ppermute x4 -> x3, starting transfers between devices: 12.7 us -> 11.1 us  [far_exchange(): ended.append(lax.ppermute(lines[dx], 'group', pairs))]
    unnamed x24 -> x20, local copies, waits for them, and re-layouts: 4.99 us -> 4.2 us
  transfers between devices with their start and end apart: 15 -> 14, of which waited for: 8 -> 7; matrix products, arithmetic and copies ran while one was open for 0% -> 0% of each run, Pallas kernels for 7% -> 6%
where the time goes in v4:
time: 180 us; the launch traced here: 178 us
  starting transfers between devices  76.2 us (42%)
  blocking collectives  57.8 us (32%)
  Pallas kernels  22.5 us (12%)
  waiting for transfers between devices  16.8 us (9%)
  local copies, waits for them, and re-layouts  4.2 us (2%)
    all_to_all x3, blocking collectives, exchange(): lax.all_to_all(x, axis, split_axis=0, concat_axis=0, tiled=True, axis_ind...  57.8 us
    ppermute x7, starting transfers between devices, far_exchange(): got.append(lax.ppermute(pieces[dy], 'group', pairs))  27.3 us
    all_to_all x2, starting transfers between devices, exchange(): lax.all_to_all(x, axis, split_axis=0, concat_axis=0, tiled=True, axis_ind...  27.2 us
    pallas_call x12, Pallas kernels, call(): pl.pallas_call(kernel, out_shape=shapes, in_specs=specs, out_specs=[pl.Bl...  22.5 us
    ppermute x3, starting transfers between devices, far_exchange(): ended.append(lax.ppermute(lines[dx], 'group', pairs))  11.1 us
    ppermute x1, starting transfers between devices, body(): other_sums = lax.ppermute(sums, 'dp', swap)  8.06 us
    ppermute x7, waiting for transfers between devices, far_exchange(): got.append(lax.ppermute(pieces[dy], 'group', pairs))  8.01 us
    all_to_all x2, waiting for transfers between devices, exchange(): lax.all_to_all(x, axis, split_axis=0, concat_axis=0, tiled=True, axis_ind...  5.66 us
  transfers between devices with their start and end apart: 14, of which 7 were waited for; matrix products, arithmetic and copies ran while one was open for 0% of the time, Pallas kernels for 6%

profile of v4, /device:TPU:1, one launch (start us, length us, event | category | flops | bytes accessed | tf_op | source)
XLA Modules:
  0.0 178.5 jit_solution(42173038083281573)
XLA Ops:
  0.6 4.6 %shard_map.121 = (bf16[192,4224]{1,0:T(8,128)(2,1)}, bf16[64,4096]{1,0:T(8,128)(2,1)S(1)}, bf16[64,128]{1,0:T(8,128)(2,1)S(1)}, f32[64,128]{1,0:T(8,128)}, bf16[192,64]{1,0:T(8,128)(2,1)S(1)}) custom-call(bf16[64,4096]{1,0:T(8,128)(2,1)} %refs_4_.3, bf16[64,4096]{1,0:T(8,128)(2,1)} %base_hbm.1, bf16[64,4096]{1,0:T(8,128)(2,1)} %bitcast.16, ...), custom_call_target="tpu_custom_call" | custom-call | flops 300000000 | bytes 5000000 | tf_op jit(solution)/shard_map/pallas_call | solution.py:457
  5.2 0.0 copy-start.4
  5.2 0.0 copy-start
  5.3 0.0 copy-start.9
  5.3 16.8 %all-to-all-start = ((bf16[24,8,4224]{2,1,0:T(8,128)(2,1)}), bf16[24,8,4224]{2,1,0:T(8,128)(2,1)S(1)}, u32[]{:S(2)}, u32[]{:S(2)}) async-start(bf16[24,8,4224]{2,1,0:T(8,128)(2,1)} %bitcast.23), calls=%async_computation | async-start | bytes 3244032 | tf_op jit(solution)/shard_map/all_to_all | solution.py:472
  22.1 0.0 copy-start.7
  22.2 0.1 pad_add_fusion.refs_0_.place_ref
  22.2 1.3 shard_map.123
  23.5 3.2 %collective-permute-start = (bf16[32,2176]{1,0:T(8,128)(2,1)S(1)}, bf16[32,2176]{1,0:T(8,128)(2,1)S(1)}, u32[]{:S(2)}, u32[]{:S(2)}) collective-permute-start(bf16[32,2176]{1,0:T(8,128)(2,1)S(1)} %get-tuple-element.49), channel_id=1, source_target_pairs={{0,1},{1,2},{2,3},{3,4},{4,5},{5,6},{6,7},{7,0},{8,9},{9,10},{10,1... | collective-permute-start | bytes 417800 | tf_op jit(solution)/shard_map/ppermute | solution.py:492
  26.7 3.8 %collective-permute-start.1 = (bf16[32,2176]{1,0:T(8,128)(2,1)S(1)}, bf16[32,2176]{1,0:T(8,128)(2,1)S(1)}, u32[]{:S(2)}, u32[]{:S(2)}) collective-permute-start(bf16[32,2176]{1,0:T(8,128)(2,1)S(1)} %get-tuple-element.50), channel_id=1, source_target_pairs={{0,7},{1,0},{2,1},{3,2},{4,3},{5,4},{6,5},{7,6},{8,15},{9,8},{10,9... | collective-permute-start | bytes 417800 | tf_op jit(solution)/shard_map/ppermute | solution.py:492
  30.5 6.9 %collective-permute-start.2 = (bf16[32,2176]{1,0:T(8,128)(2,1)S(1)}, bf16[32,2176]{1,0:T(8,128)(2,1)S(1)}, u32[]{:S(2)}, u32[]{:S(2)}) collective-permute-start(bf16[32,2176]{1,0:T(8,128)(2,1)S(1)} %get-tuple-element.51), channel_id=1, source_target_pairs={{0,4},{1,5},{2,6},{3,7},{4,0},{5,1},{6,2},{7,3},{8,12},{9,13},{10,... | collective-permute-start | bytes 417800 | tf_op jit(solution)/shard_map/ppermute | solution.py:492
  37.5 1.9 %collective-permute-start.3 = (bf16[32,2176]{1,0:T(8,128)(2,1)S(1)}, bf16[32,2176]{1,0:T(8,128)(2,1)S(1)}, u32[]{:S(2)}, u32[]{:S(2)}) collective-permute-start(bf16[32,2176]{1,0:T(8,128)(2,1)S(1)} %get-tuple-element.52), channel_id=1, source_target_pairs={{0,5},{1,6},{2,7},{3,0},{4,1},{5,2},{6,3},{7,4},{8,13},{9,14},{10,... | collective-permute-start | bytes 417800 | tf_op jit(solution)/shard_map/ppermute | solution.py:492
  39.4 5.2 %collective-permute-start.4 = (bf16[32,2176]{1,0:T(8,128)(2,1)S(1)}, bf16[32,2176]{1,0:T(8,128)(2,1)S(1)}, u32[]{:S(2)}, u32[]{:S(2)}) collective-permute-start(bf16[32,2176]{1,0:T(8,128)(2,1)S(1)} %get-tuple-element.53), channel_id=1, source_target_pairs={{0,3},{1,4},{2,5},{3,6},{4,7},{5,0},{6,1},{7,2},{8,11},{9,12},{10,... | collective-permute-start | bytes 417800 | tf_op jit(solution)/shard_map/ppermute | solution.py:492
  44.6 2.0 %collective-permute-start.5 = (bf16[32,2176]{1,0:T(8,128)(2,1)S(1)}, bf16[32,2176]{1,0:T(8,128)(2,1)S(1)}, u32[]{:S(2)}, u32[]{:S(2)}) collective-permute-start(bf16[32,2176]{1,0:T(8,128)(2,1)S(1)} %get-tuple-element.54), channel_id=1, source_target_pairs={{0,6},{1,7},{2,0},{3,1},{4,2},{5,3},{6,4},{7,5},{8,14},{9,15},{10,... | collective-permute-start | bytes 417800 | tf_op jit(solution)/shard_map/ppermute | solution.py:492
  46.6 0.0 copy-start.5
  46.6 0.0 copy-start.8
  46.6 4.3 %collective-permute-start.6 = (bf16[32,2176]{1,0:T(8,128)(2,1)S(1)}, bf16[32,2176]{1,0:T(8,128)(2,1)S(1)}, u32[]{:S(2)}, u32[]{:S(2)}) collective-permute-start(bf16[32,2176]{1,0:T(8,128)(2,1)S(1)} %get-tuple-element.55), channel_id=1, source_target_pairs={{0,2},{1,3},{2,4},{3,5},{4,6},{5,7},{6,0},{7,1},{8,10},{9,11},{10,... | collective-permute-start | bytes 417800 | tf_op jit(solution)/shard_map/ppermute | solution.py:492
  51.0 1.5 collective-permute-done.3.refs_4_
  52.4 1.6 collective-permute-done.4.refs_5_
  54.0 5.0 %collective-permute-done.5.refs_6_ = bf16[32,2176]{1,0:T(8,128)(2,1)S(1)} collective-permute-done((bf16[32,2176]{1,0:T(8,128)(2,1)S(1)}, bf16[32,2176]{1,0:T(8,128)(2,1)S(1)}, u32[]{:S(2)}, u32[]{:S(2)}) %collective-permute-start.5) | collective-permute-done | bytes 139296 | tf_op jit(solution)/shard_map/ppermute | solution.py:492
  59.0 0.2 shard_map.124
  59.1 4.6 %collective-permute-start.7 = (bf16[64,2176]{1,0:T(8,128)(2,1)S(1)}, bf16[64,2176]{1,0:T(8,128)(2,1)S(1)}, u32[]{:S(2)}, u32[]{:S(2)}) collective-permute-start(bf16[64,2176]{1,0:T(8,128)(2,1)S(1)} %get-tuple-element.57), channel_id=1, source_target_pairs={{0,16},{1,17},{2,18},{3,19},{4,20},{5,21},{6,22},{7,23},{8,24},{9,... | collective-permute-start | bytes 835592 | tf_op jit(solution)/shard_map/ppermute | solution.py:502
  63.8 2.2 %collective-permute-start.8 = (bf16[64,2176]{1,0:T(8,128)(2,1)S(1)}, bf16[64,2176]{1,0:T(8,128)(2,1)S(1)}, u32[]{:S(2)}, u32[]{:S(2)}) collective-permute-start(bf16[64,2176]{1,0:T(8,128)(2,1)S(1)} %get-tuple-element.58), channel_id=1, source_target_pairs={{0,8},{1,9},{2,10},{3,11},{4,12},{5,13},{6,14},{7,15},{8,16},{9,17... | collective-permute-start | bytes 835592 | tf_op jit(solution)/shard_map/ppermute | solution.py:502
  66.0 4.3 %collective-permute-start.9 = (bf16[64,2176]{1,0:T(8,128)(2,1)S(1)}, bf16[64,2176]{1,0:T(8,128)(2,1)S(1)}, u32[]{:S(2)}, u32[]{:S(2)}) collective-permute-start(bf16[64,2176]{1,0:T(8,128)(2,1)S(1)} %get-tuple-element.59), channel_id=1, source_target_pairs={{0,24},{1,25},{2,26},{3,27},{4,28},{5,29},{6,30},{7,31},{8,0},{9,1... | collective-permute-start | bytes 835592 | tf_op jit(solution)/shard_map/ppermute | solution.py:502
  70.3 0.0 copy-start.1
  70.3 1.0 copy-done.1
  71.3 1.0 copy-done.2
  72.4 1.0 copy-done.3
  73.4 1.0 copy-done.6
  74.5 2.9 %shard_map.122 = (bf16[128,4096]{1,0:T(8,128)(2,1)S(1)}, bf16[64,128]{1,0:T(8,128)(2,1)}, f32[64,128]{1,0:T(8,128)}, f32[192,64]{1,0:T(8,128)S(1)}, f32[128,64]{1,0:T(8,128)S(1)}, /*index=5*/bf16[128,64]{1,0:T(8,128)(2,1)}) custom-call(s32[3]{0:T(128)S(1)} %pad_add_fusion.refs_0_.place_ref, bf16[64,4096]{1,0:T(8,128)(2,1)S(1)} %copy-done.1, ...), custom_call_target="tpu_custom_call" | custom-call | flops 1000 | bytes 1000 | tf_op jit(solution)/shard_map/pallas_call | solution.py:457
  77.4 1.9 %shard_map.125 = (bf16[128,4096]{1,0:T(8,128)(2,1)}, bf16[128,128]{1,0:T(8,128)(2,1)}, bf16[64,4096]{1,0:T(8,128)(2,1)}, f32[128,128]{1,0:T(8,128)}) custom-call(bf16[64,2176]{1,0:T(8,128)(2,1)S(1)} %get-tuple-element.56.refs_0_, bf16[64,2176]{1,0:T(8,128)(2,1)S(1)} %collective-permute-done.7.refs_1_, bf16[64,2176]{1,0:T(8,128)(2,1)S(1)} %collective-permute-done.8.refs_2_, ...), custom_call_target="tpu_custom_call" | custom-call | flops 1000 | bytes 1000 | tf_op jit(solution)/shard_map/pallas_call | solution.py:457
  79.2 0.8 all-to-all-done
  80.1 2.2 %shard_map.126 = (bf16[192,128]{1,0:T(8,128)(2,1)}, bf16[320,64]{1,0:T(8,128)(2,1)}, f32[384,1]{1,0:T(8,128)}, f32[192,64]{1,0:T(8,128)}) custom-call(bf16[192,4224]{1,0:T(8,128)(2,1)S(1)} %bitcast.14, bf16[128,4096]{1,0:T(8,128)(2,1)S(1)} %get-tuple-element.45.refs_4_.refs_1_.pair_ref, f32[128,128]{1,0:T(8,128)} %get-tuple-element.60.refs_2_.other_both_hbm, ...), custom_call_target="tpu_custom_call" | custom-call | flops 200000000 | bytes 3000000 | tf_op jit(solution)/shard_map/pallas_call | solution.py:457
  82.3 10.4 %all-to-all-start.1 = ((bf16[24,8,128]{2,1,0:T(8,128)(2,1)}), bf16[24,8,128]{2,1,0:T(8,128)(2,1)S(1)}, u32[]{:S(2)}, u32[]{:S(2)}) async-start(bf16[24,8,128]{2,1,0:T(8,128)(2,1)} %bitcast.10), calls=%async_computation.1 | async-start | bytes 98304 | tf_op jit(solution)/shard_map/all_to_all | solution.py:472
  92.7 5.2 %shard_map.127 = (f32[32,32,128]{2,1,0:T(8,128)}, bf16[32,32,128]{2,1,0:T(8,128)(2,1)}, f32[64,4096]{1,0:T(8,128)}, f32[64,128]{1,0:T(8,128)}) custom-call(s32[3]{0:T(128)S(1)} %pad_add_fusion.refs_0_.place_ref, bf16[192,4224]{1,0:T(8,128)(2,1)S(1)} %bitcast.15, bf16[128,4096]{1,0:T(8,128)(2,1)S(1)} %get-tuple-element.45.refs_4_.refs_1_.pair_ref, ...), custom_call_target="tpu_custom_call" | custom-call | flops 900000000 | bytes 9000000 | tf_op jit(solution)/shard_map/pallas_call | solution.py:457
  97.9 4.8 %all-to-all-done.1 = bf16[24,8,128]{2,1,0:T(8,128)(2,1)S(1)} async-done(((bf16[24,8,128]{2,1,0:T(8,128)(2,1)}), bf16[24,8,128]{2,1,0:T(8,128)(2,1)S(1)}, u32[]{:S(2)}, u32[]{:S(2)}) %all-to-all-start.1) | async-done | bytes 49184 | tf_op jit(solution)/shard_map/all_to_all | solution.py:472
  102.7 2.1 %shard_map.128 = (f32[32,64,128]{2,1,0:T(8,128)S(1)}, bf16[32,64,128]{2,1,0:T(8,128)(2,1)S(1)}, f32[8,128]{1,0:T(8,128)S(1)}) custom-call(s32[3]{0:T(128)S(1)} %pad_add_fusion.refs_0_.place_ref, bf16[192,128]{1,0:T(8,128)(2,1)S(1)} %bitcast.18, bf16[192,64]{1,0:T(8,128)(2,1)S(1)} %get-tuple-element.65.refs_2_, f32[64,128]{1,0:T(8,128)} %get-tuple-element.75.refs_3_, ...), custom_call_target="tpu_custom_call" | custom-call | flops 100000000 | bytes 3000000 | tf_op jit(solution)/shard_map/pallas_call | solution.py:457
  104.9 2.4 %collective-permute-start.10 = (bf16[32,64,128]{2,1,0:T(8,128)(2,1)S(1)}, bf16[32,64,128]{2,1,0:T(8,128)(2,1)S(1)}, u32[]{:S(2)}, u32[]{:S(2)}) collective-permute-start(bf16[32,64,128]{2,1,0:T(8,128)(2,1)S(1)} %get-tuple-element.80), channel_id=1, source_target_pairs={{0,32},{32,0},{64,96},{96,64},{128,160},{160,128},{192,224},{224,1... | collective-permute-start | bytes 1572872 | tf_op jit(solution)/shard_map/ppermute | solution.py:659
  107.3 1.5 collective-permute-done.10.got_ref
  108.8 0.1 shard_map.129
  108.9 20.4 %all_to_all.25.in_ref = bf16[32,64,128]{2,1,0:T(8,128)(2,1)S(1)} all-to-all(bf16[32,64,128]{2,1,0:T(8,128)(2,1)S(1)} %shard_map.129), channel_id=1, replica_groups=mesh['dp'=24,'group'=32] {'group'}, dimensions={0} | all-to-all | bytes 1048576 | tf_op jit(solution)/shard_map/all_to_all | solution.py:472
  129.3 0.1 shard_map.130
  129.4 14.9 %all_to_all.26.in_ref = bf16[12,64,128]{2,1,0:T(8,128)(2,1)S(1)} all-to-all(bf16[12,64,128]{2,1,0:T(8,128)(2,1)S(1)} %shard_map.130), channel_id=1, replica_groups={{0,64,128,192,256,320,384,448,512,576,640,704},{32,96,160,224,288,352,4..., dimensions={0} | all-to-all | bytes 393216 | tf_op jit(solution)/shard_map/all_to_all | solution.py:472
  144.4 0.1 shard_map.131
  144.4 22.4 %all_to_all.27.refs_1_ = bf16[32,72,128]{2,1,0:T(8,128)(2,1)S(1)} all-to-all(bf16[32,72,128]{2,1,0:T(8,128)(2,1)S(1)} %shard_map.131), channel_id=1, replica_groups=mesh['dp'=24,'group'=32] {'group'}, dimensions={0} | all-to-all | bytes 1179648 | tf_op jit(solution)/shard_map/all_to_all | solution.py:472
  166.9 8.1 %collective-permute-start.11 = (bf16[32,72,128]{2,1,0:T(8,128)(2,1)S(1)}, bf16[32,72,128]{2,1,0:T(8,128)(2,1)S(1)}, u32[]{:S(2)}, u32[]{:S(2)}) collective-permute-start(bf16[32,72,128]{2,1,0:T(8,128)(2,1)S(1)} %all_to_all.27.refs_1_), channel_id=1, source_target_pairs={{0,32},{32,0},{64,96},{96,64},{128,160},{160,128},{192,224},{224,1... | collective-permute-start | bytes 1769480 | tf_op jit(solution)/shard_map/ppermute | solution.py:671
  174.9 1.6 collective-permute-done.11.refs_2_
  176.5 1.9 %shard_map.132 = (f32[64,4096]{1,0:T(8,128)}, f32[64,4096]{1,0:T(8,128)}, f32[1,1]{1,0:T(1,128)}) custom-call(s32[3]{0:T(128)S(1)} %pad_add_fusion.refs_0_.place_ref, bf16[32,72,128]{2,1,0:T(8,128)(2,1)S(1)} %all_to_all.27.refs_1_, bf16[32,72,128]{2,1,0:T(8,128)(2,1)S(1)} %collective-permute-done.11.refs_2_), custom_call_target="tpu_custom_call" | custom-call | bytes 3500000 | tf_op jit(solution)/shard_map/pallas_call | solution.py:457
  (16 shorter events, 0.0 us)
Async XLA Ops:
  5.2 17.0 %copy-start.4 = (bf16[64,4096]{1,0:T(8,128)(2,1)}, bf16[64,4096]{1,0:T(8,128)(2,1)S(1)}, u32[]{:S(2)}) copy-start(bf16[64,4096]{1,0:T(8,128)(2,1)S(1)} %get-tuple-element.46.refs_2_.refs_5_) | copy-start | bytes 1572868
  5.2 17.0 %copy-start = (bf16[64,4096]{1,0:T(8,128)(2,1)S(1)}, bf16[64,4096]{1,0:T(8,128)(2,1)}, u32[]{:S(2)}) copy-start(bf16[64,4096]{1,0:T(8,128)(2,1)} %refs_4_.3) | copy-start | bytes 1572868
  5.3 17.0 %copy-start.9 = (s32[32,2]{0,1:T(2,128)S(1)}, s32[32,2]{0,1:T(2,128)}, u32[]{:S(2)}) copy-start(s32[32,2]{0,1:T(2,128)} %param.19) | copy-start | bytes 772
  5.3 74.8 %all-to-all-start = ((bf16[24,8,4224]{2,1,0:T(8,128)(2,1)}), bf16[24,8,4224]{2,1,0:T(8,128)(2,1)S(1)}, u32[]{:S(2)}, u32[]{:S(2)}) async-start(bf16[24,8,4224]{2,1,0:T(8,128)(2,1)} %bitcast.23), calls=%async_computation | async-start | bytes 3244032 | tf_op jit(solution)/shard_map/all_to_all | solution.py:472
  22.1 48.2 %copy-start.7 = (s32[64,32]{0,1:T(8,128)S(1)}, s32[64,32]{0,1:T(8,128)}, u32[]{:S(2)}) copy-start(s32[64,32]{0,1:T(8,128)} %param.17) | copy-start | bytes 24580
  23.5 21.1 %collective-permute-start = (bf16[32,2176]{1,0:T(8,128)(2,1)S(1)}, bf16[32,2176]{1,0:T(8,128)(2,1)S(1)}, u32[]{:S(2)}, u32[]{:S(2)}) collective-permute-start(bf16[32,2176]{1,0:T(8,128)(2,1)S(1)} %get-tuple-element.49), channel_id=1, source_target_pairs={{0,1},{1,2},{2,3},{3,4},{4,5},{5,6},{6,7},{7,0},{8,9},{9,10},{10,1... | collective-permute-start | bytes 417800 | tf_op jit(solution)/shard_map/ppermute | solution.py:492
  26.7 19.8 %collective-permute-start.1 = (bf16[32,2176]{1,0:T(8,128)(2,1)S(1)}, bf16[32,2176]{1,0:T(8,128)(2,1)S(1)}, u32[]{:S(2)}, u32[]{:S(2)}) collective-permute-start(bf16[32,2176]{1,0:T(8,128)(2,1)S(1)} %get-tuple-element.50), channel_id=1, source_target_pairs={{0,7},{1,0},{2,1},{3,2},{4,3},{5,4},{6,5},{7,6},{8,15},{9,8},{10,9... | collective-permute-start | bytes 417800 | tf_op jit(solution)/shard_map/ppermute | solution.py:492
  30.5 20.4 %collective-permute-start.2 = (bf16[32,2176]{1,0:T(8,128)(2,1)S(1)}, bf16[32,2176]{1,0:T(8,128)(2,1)S(1)}, u32[]{:S(2)}, u32[]{:S(2)}) collective-permute-start(bf16[32,2176]{1,0:T(8,128)(2,1)S(1)} %get-tuple-element.51), channel_id=1, source_target_pairs={{0,4},{1,5},{2,6},{3,7},{4,0},{5,1},{6,2},{7,3},{8,12},{9,13},{10,... | collective-permute-start | bytes 417800 | tf_op jit(solution)/shard_map/ppermute | solution.py:492
  37.5 14.9 %collective-permute-start.3 = (bf16[32,2176]{1,0:T(8,128)(2,1)S(1)}, bf16[32,2176]{1,0:T(8,128)(2,1)S(1)}, u32[]{:S(2)}, u32[]{:S(2)}) collective-permute-start(bf16[32,2176]{1,0:T(8,128)(2,1)S(1)} %get-tuple-element.52), channel_id=1, source_target_pairs={{0,5},{1,6},{2,7},{3,0},{4,1},{5,2},{6,3},{7,4},{8,13},{9,14},{10,... | collective-permute-start | bytes 417800 | tf_op jit(solution)/shard_map/ppermute | solution.py:492
  39.4 14.6 %collective-permute-start.4 = (bf16[32,2176]{1,0:T(8,128)(2,1)S(1)}, bf16[32,2176]{1,0:T(8,128)(2,1)S(1)}, u32[]{:S(2)}, u32[]{:S(2)}) collective-permute-start(bf16[32,2176]{1,0:T(8,128)(2,1)S(1)} %get-tuple-element.53), channel_id=1, source_target_pairs={{0,3},{1,4},{2,5},{3,6},{4,7},{5,0},{6,1},{7,2},{8,11},{9,12},{10,... | collective-permute-start | bytes 417800 | tf_op jit(solution)/shard_map/ppermute | solution.py:492
  44.6 14.4 %collective-permute-start.5 = (bf16[32,2176]{1,0:T(8,128)(2,1)S(1)}, bf16[32,2176]{1,0:T(8,128)(2,1)S(1)}, u32[]{:S(2)}, u32[]{:S(2)}) collective-permute-start(bf16[32,2176]{1,0:T(8,128)(2,1)S(1)} %get-tuple-element.54), channel_id=1, source_target_pairs={{0,6},{1,7},{2,0},{3,1},{4,2},{5,3},{6,4},{7,5},{8,14},{9,15},{10,... | collective-permute-start | bytes 417800 | tf_op jit(solution)/shard_map/ppermute | solution.py:492
  46.6 30.8 %copy-start.5 = (bf16[64,4096]{1,0:T(8,128)(2,1)S(1)}, bf16[64,4096]{1,0:T(8,128)(2,1)}, u32[]{:S(2)}) copy-start(bf16[64,4096]{1,0:T(8,128)(2,1)} %copy-done.4) | copy-start | bytes 1572868
  46.6 30.8 %copy-start.8 = (s32[64]{0:T(128)S(1)}, s32[64]{0:T(128)}, u32[]{:S(2)}) copy-start(s32[64]{0:T(128)} %param.16) | copy-start | bytes 772
  46.6 12.4 %collective-permute-start.6 = (bf16[32,2176]{1,0:T(8,128)(2,1)S(1)}, bf16[32,2176]{1,0:T(8,128)(2,1)S(1)}, u32[]{:S(2)}, u32[]{:S(2)}) collective-permute-start(bf16[32,2176]{1,0:T(8,128)(2,1)S(1)} %get-tuple-element.55), channel_id=1, source_target_pairs={{0,2},{1,3},{2,4},{3,5},{4,6},{5,7},{6,0},{7,1},{8,10},{9,11},{10,... | collective-permute-start | bytes 417800 | tf_op jit(solution)/shard_map/ppermute | solution.py:492
  59.1 18.2 %collective-permute-start.7 = (bf16[64,2176]{1,0:T(8,128)(2,1)S(1)}, bf16[64,2176]{1,0:T(8,128)(2,1)S(1)}, u32[]{:S(2)}, u32[]{:S(2)}) collective-permute-start(bf16[64,2176]{1,0:T(8,128)(2,1)S(1)} %get-tuple-element.57), channel_id=1, source_target_pairs={{0,16},{1,17},{2,18},{3,19},{4,20},{5,21},{6,22},{7,23},{8,24},{9,... | collective-permute-start | bytes 835592 | tf_op jit(solution)/shard_map/ppermute | solution.py:502
  63.8 13.6 %collective-permute-start.8 = (bf16[64,2176]{1,0:T(8,128)(2,1)S(1)}, bf16[64,2176]{1,0:T(8,128)(2,1)S(1)}, u32[]{:S(2)}, u32[]{:S(2)}) collective-permute-start(bf16[64,2176]{1,0:T(8,128)(2,1)S(1)} %get-tuple-element.58), channel_id=1, source_target_pairs={{0,8},{1,9},{2,10},{3,11},{4,12},{5,13},{6,14},{7,15},{8,16},{9,17... | collective-permute-start | bytes 835592 | tf_op jit(solution)/shard_map/ppermute | solution.py:502
  66.0 11.3 %collective-permute-start.9 = (bf16[64,2176]{1,0:T(8,128)(2,1)S(1)}, bf16[64,2176]{1,0:T(8,128)(2,1)S(1)}, u32[]{:S(2)}, u32[]{:S(2)}) collective-permute-start(bf16[64,2176]{1,0:T(8,128)(2,1)S(1)} %get-tuple-element.59), channel_id=1, source_target_pairs={{0,24},{1,25},{2,26},{3,27},{4,28},{5,29},{6,30},{7,31},{8,0},{9,1... | collective-permute-start | bytes 835592 | tf_op jit(solution)/shard_map/ppermute | solution.py:502
  70.3 1.0 copy-start.1
  71.3 1.0 copy-start.2
  72.4 1.0 copy-start.3
  73.4 1.0 copy-start.6
  82.3 20.5 %all-to-all-start.1 = ((bf16[24,8,128]{2,1,0:T(8,128)(2,1)}), bf16[24,8,128]{2,1,0:T(8,128)(2,1)S(1)}, u32[]{:S(2)}, u32[]{:S(2)}) async-start(bf16[24,8,128]{2,1,0:T(8,128)(2,1)} %bitcast.10), calls=%async_computation.1 | async-start | bytes 98304 | tf_op jit(solution)/shard_map/all_to_all | solution.py:472
  104.9 3.9 %collective-permute-start.10 = (bf16[32,64,128]{2,1,0:T(8,128)(2,1)S(1)}, bf16[32,64,128]{2,1,0:T(8,128)(2,1)S(1)}, u32[]{:S(2)}, u32[]{:S(2)}) collective-permute-start(bf16[32,64,128]{2,1,0:T(8,128)(2,1)S(1)} %get-tuple-element.80), channel_id=1, source_target_pairs={{0,32},{32,0},{64,96},{96,64},{128,160},{160,128},{192,224},{224,1... | collective-permute-start | bytes 1572872 | tf_op jit(solution)/shard_map/ppermute | solution.py:659
  166.9 9.7 %collective-permute-start.11 = (bf16[32,72,128]{2,1,0:T(8,128)(2,1)S(1)}, bf16[32,72,128]{2,1,0:T(8,128)(2,1)S(1)}, u32[]{:S(2)}, u32[]{:S(2)}) collective-permute-start(bf16[32,72,128]{2,1,0:T(8,128)(2,1)S(1)} %all_to_all.27.refs_1_), channel_id=1, source_target_pairs={{0,32},{32,0},{64,96},{96,64},{128,160},{160,128},{192,224},{224,1... | collective-permute-start | bytes 1769480 | tf_op jit(solution)/shard_map/ppermute | solution.py:671

commit v5 on v4

--- a/solution.py
+++ b/solution.py
@@ -69,6 +69,15 @@
     return copies
 
 
+def stride_of(chips):
+    return {12: 5, 8: 3, 3: 2}.get(chips, 1)
+
+
+def ring_spot(position, n_dp):
+    chips = n_dp // 2
+    return (position // 2 * stride_of(chips)) % chips * 2 + position % 2
+
+
 def passage_kernel(
     x_hbm, base_hbm, down_hbm, up_hbm, near_ids_hbm,
     near_hbm, unit_ref, ext_ref, inv_ref, pick_ref,
@@ -92,7 +101,8 @@
     per_near, n_near = near_ids_ref.shape
     count = per_near * n_near
     ids = near_ids_ref[...].astype(f32).astype(bf16)
-    spread = (iota((count, n_near), 0) // per_near == iota((count, n_near), 1)).astype(bf16)
+    spot = ring_spot(iota((count, n_near), 0) // per_near, n_near)
+    spread = (spot == iota((count, n_near), 1)).astype(bf16)
     table = dot(spread, ids, 1, 1)
     mine = iota((count, per_near), 0) % per_near == iota((count, per_near), 1)
     wanted = jnp.sum(jnp.where(mine, table, 0.0), axis=1, keepdims=True).astype(jnp.int32)
@@ -143,9 +153,16 @@
 
 
 def query_kernel(
-    grid_x, grid_y, place_ref, x_ref, base_ref, down_ref, up_ref, slots_ref,
-    pair_ref, ext_ref, inv_ref, near_count_ref, other_count_ref, shadow_ref, raw_ref,
+    grid_x, grid_y, per_near, place_ref, x_hbm, base_hbm, down_hbm, up_hbm, slots_hbm,
+    pair_ref, ext_ref, inv_ref, near_count_ref, other_count_ref, shadow_ref,
+    x_ref, base_ref, down_ref, up_ref, slots_ref, raw_ref, sems,
 ):
+    pairs = [
+        (x_hbm, x_ref), (down_hbm, down_ref), (base_hbm, base_ref), (up_hbm, up_ref),
+        (slots_hbm, slots_ref),
+    ]
+    for c in fetch(pairs, sems):
+        c.wait()
     hard, rows = slots_ref.shape
     embed(x_ref, base_ref, down_ref, up_ref, pair_ref, ext_ref, inv_ref, raw_ref)
     pair_ref[rows:, :] = up_ref[...]
@@ -158,6 +175,7 @@
     n_far = n_other - rows
     where_x, where_y = place_ref[0], place_ref[1]
     near_slot = iota((n_near, rows), 0)
+    near_slot = ring_spot(near_slot // per_near, n_near // per_near) * per_near + near_slot % per_near
     spot = iota((n_other, rows), 0)
     block = spot // 2
     from_x = (where_x + grid_x - (block // grid_y) % grid_x) % grid_x
@@ -566,11 +584,14 @@
             (place, passage_layer_input, p_unit, p_ext, far_ids),
             flops=1000, moved=1000,
         )
-        near = exchange(near.reshape(n_dp, per_near, width + lanes), "dp")
+        ring = [ring_spot(i, n_dp) for i in range(n_dp)]
+        step = stride_of(grid_y)
+        plane = [x * grid_y + y * step % grid_y for x in range(grid_x) for y in range(grid_y)]
+        near = exchange(near.reshape(n_dp, per_near, width + lanes), "dp", [ring])
         near = near.reshape(n_near, width + lanes)
         far = far_exchange(far, grid_x, grid_y)
         q_pair, q_ext, q_inv, near_count, other_count, shadow = call(
-            lambda *refs: query_kernel(grid_x, grid_y, *refs),
+            lambda *refs: query_kernel(grid_x, grid_y, per_near, *refs),
             [
                 ((rows + rank, width), bf16),
                 ((rows, lanes), bf16),
@@ -583,7 +604,16 @@
                 place, query_layer_input, query_frozen_base, down_t, adapter_up_weight,
                 hard_negative_slots.T,
             ),
-            [((rows, width), f32)], flops=1000, moved=1000, out_hbm=(1, 2, 5),
+            [
+                ((rows, width), bf16),
+                ((rows, width), bf16),
+                (down_t.shape, bf16),
+                (adapter_up_weight.shape, bf16),
+                (hard_negative_slots.T.shape, jnp.int32),
+                ((rows, width), f32),
+                pltpu.SemaphoreType.DMA((5,)),
+            ],
+            flops=1000, moved=1000, hbm=range(1, 6), out_hbm=(1, 2, 5),
         )
         positive = positive_passage_index.reshape(1, rows)
         other, other_ext, x_far, other_both = call(
@@ -613,7 +643,7 @@
             ],
             flops=200_000_000, moved=3_000_000, hbm=(2, 5), out_hbm=(1, 2, 3),
         )
-        ret = exchange(ret.reshape(n_dp, per_near, lanes), "dp").reshape(n_near, lanes)
+        ret = exchange(ret.reshape(n_dp, per_near, lanes), "dp", [ring]).reshape(n_near, lanes)
         up_keep, up_send, down_part, row_part = call(
             local_kernel,
             [
@@ -658,8 +688,8 @@
         )
         got = lax.ppermute(send, "dp", swap)
         (sums,) = call(add_kernel, [((n_group, rank, block), bf16)], (keep, got), moved=2_500_000)
-        cores = [list(range(c, n_dp, 2)) for c in range(2)]
-        sums = exchange(sums, "group")
+        cores = [ring[c::2] for c in range(2)]
+        sums = exchange(sums, "group", [plane])
         (sums,) = call(
             spread_kernel, [((n_dp // 2, rank, block), bf16)], (sums,), moved=1_000_000
         )
@@ -667,7 +697,7 @@
         (sums,) = call(
             finish_kernel, [((n_group, rank + 8, block), bf16)], (sums, loss), moved=1_000_000
         )
-        sums = exchange(sums, "group")
+        sums = exchange(sums, "group", [plane])
         other_sums = lax.ppermute(sums, "dp", swap)
         down, up, loss = call(
             lambda *refs: output_kernel(queries, *refs),

time: 180 us -> 179 us (level)
  local copies, waits for them, and re-layouts: 4.2 us -> 0.03 us
  waiting for transfers between devices: 16.8 us -> 19.6 us
    unnamed x20 -> x10, local copies, waits for them, and re-layouts: 4.2 us -> 0.03 us
  transfers between devices with their start and end apart: 14 -> 14, of which waited for: 7 -> 8; matrix products, arithmetic and copies ran while one was open for 0% -> 0% of each run, Pallas kernels for 6% -> 7%
where the time goes in v5:
time: 179 us; the launch traced here: 178 us
  starting transfers between devices  75.2 us (42%)
  blocking collectives  58.6 us (33%)
  Pallas kernels  24.1 us (13%)
  waiting for transfers between devices  19.6 us (11%)
    all_to_all x3, blocking collectives, exchange(): lax.all_to_all(x, axis, split_axis=0, concat_axis=0, tiled=True, axis_ind...  58.6 us
    ppermute x7, starting transfers between devices, far_exchange(): got.append(lax.ppermute(pieces[dy], 'group', pairs))  27.3 us
    all_to_all x2, starting transfers between devices, exchange(): lax.all_to_all(x, axis, split_axis=0, concat_axis=0, tiled=True, axis_ind...  25.7 us
    pallas_call x12, Pallas kernels, call(): pl.pallas_call(kernel, out_shape=shapes, in_specs=specs, out_specs=[pl.Bl...  24.1 us
    ppermute x3, starting transfers between devices, far_exchange(): ended.append(lax.ppermute(lines[dx], 'group', pairs))  11.1 us
    ppermute x1, starting transfers between devices, body(): other_sums = lax.ppermute(sums, 'dp', swap)  8.74 us
    ppermute x7, waiting for transfers between devices, far_exchange(): got.append(lax.ppermute(pieces[dy], 'group', pairs))  7.99 us
    all_to_all x2, waiting for transfers between devices, exchange(): lax.all_to_all(x, axis, split_axis=0, concat_axis=0, tiled=True, axis_ind...  6.84 us
  transfers between devices with their start and end apart: 14, of which 8 were waited for; matrix products, arithmetic and copies ran while one was open for 0% of the time, Pallas kernels for 7%

profile of v5, /device:TPU:1, one launch (start us, length us, event | category | flops | bytes accessed | tf_op | source)
XLA Modules:
  0.0 178.5 jit_solution(16838837980785789508)
XLA Ops:
  0.6 4.6 %shard_map.121 = (bf16[192,4224]{1,0:T(8,128)(2,1)}, bf16[64,4096]{1,0:T(8,128)(2,1)S(1)}, bf16[64,128]{1,0:T(8,128)(2,1)S(1)}, f32[64,128]{1,0:T(8,128)}, bf16[192,64]{1,0:T(8,128)(2,1)S(1)}) custom-call(bf16[64,4096]{1,0:T(8,128)(2,1)} %refs_4_.3, bf16[64,4096]{1,0:T(8,128)(2,1)} %base_hbm.1, bf16[64,4096]{1,0:T(8,128)(2,1)} %bitcast.20, ...), custom_call_target="tpu_custom_call" | custom-call | flops 300000000 | bytes 5000000 | tf_op jit(solution)/shard_map/pallas_call | solution.py:475
  5.3 0.0 copy-start.1
  5.3 0.0 copy-start
  5.3 0.0 copy-start.4
  5.3 16.8 %all-to-all-start = ((bf16[24,8,4224]{2,1,0:T(8,128)(2,1)}), bf16[24,8,4224]{2,1,0:T(8,128)(2,1)S(1)}, u32[]{:S(2)}, u32[]{:S(2)}) async-start(bf16[24,8,4224]{2,1,0:T(8,128)(2,1)} %bitcast.22), calls=%async_computation | async-start | bytes 3244032 | tf_op jit(solution)/shard_map/all_to_all | solution.py:490
  22.2 0.1 pad_add_fusion.refs_0_.place_ref
  22.3 1.3 shard_map.123
  23.5 3.2 %collective-permute-start = (bf16[32,2176]{1,0:T(8,128)(2,1)S(1)}, bf16[32,2176]{1,0:T(8,128)(2,1)S(1)}, u32[]{:S(2)}, u32[]{:S(2)}) collective-permute-start(bf16[32,2176]{1,0:T(8,128)(2,1)S(1)} %get-tuple-element.49), channel_id=1, source_target_pairs={{0,1},{1,2},{2,3},{3,4},{4,5},{5,6},{6,7},{7,0},{8,9},{9,10},{10,1... | collective-permute-start | bytes 417800 | tf_op jit(solution)/shard_map/ppermute | solution.py:510
  26.7 3.8 %collective-permute-start.1 = (bf16[32,2176]{1,0:T(8,128)(2,1)S(1)}, bf16[32,2176]{1,0:T(8,128)(2,1)S(1)}, u32[]{:S(2)}, u32[]{:S(2)}) collective-permute-start(bf16[32,2176]{1,0:T(8,128)(2,1)S(1)} %get-tuple-element.50), channel_id=1, source_target_pairs={{0,7},{1,0},{2,1},{3,2},{4,3},{5,4},{6,5},{7,6},{8,15},{9,8},{10,9... | collective-permute-start | bytes 417800 | tf_op jit(solution)/shard_map/ppermute | solution.py:510
  30.6 6.9 %collective-permute-start.2 = (bf16[32,2176]{1,0:T(8,128)(2,1)S(1)}, bf16[32,2176]{1,0:T(8,128)(2,1)S(1)}, u32[]{:S(2)}, u32[]{:S(2)}) collective-permute-start(bf16[32,2176]{1,0:T(8,128)(2,1)S(1)} %get-tuple-element.51), channel_id=1, source_target_pairs={{0,4},{1,5},{2,6},{3,7},{4,0},{5,1},{6,2},{7,3},{8,12},{9,13},{10,... | collective-permute-start | bytes 417800 | tf_op jit(solution)/shard_map/ppermute | solution.py:510
  37.5 1.9 %collective-permute-start.3 = (bf16[32,2176]{1,0:T(8,128)(2,1)S(1)}, bf16[32,2176]{1,0:T(8,128)(2,1)S(1)}, u32[]{:S(2)}, u32[]{:S(2)}) collective-permute-start(bf16[32,2176]{1,0:T(8,128)(2,1)S(1)} %get-tuple-element.52), channel_id=1, source_target_pairs={{0,5},{1,6},{2,7},{3,0},{4,1},{5,2},{6,3},{7,4},{8,13},{9,14},{10,... | collective-permute-start | bytes 417800 | tf_op jit(solution)/shard_map/ppermute | solution.py:510
  39.4 5.2 %collective-permute-start.4 = (bf16[32,2176]{1,0:T(8,128)(2,1)S(1)}, bf16[32,2176]{1,0:T(8,128)(2,1)S(1)}, u32[]{:S(2)}, u32[]{:S(2)}) collective-permute-start(bf16[32,2176]{1,0:T(8,128)(2,1)S(1)} %get-tuple-element.53), channel_id=1, source_target_pairs={{0,3},{1,4},{2,5},{3,6},{4,7},{5,0},{6,1},{7,2},{8,11},{9,12},{10,... | collective-permute-start | bytes 417800 | tf_op jit(solution)/shard_map/ppermute | solution.py:510
  44.6 0.0 collective-permute-done.refs_1_
  44.6 2.0 %collective-permute-start.5 = (bf16[32,2176]{1,0:T(8,128)(2,1)S(1)}, bf16[32,2176]{1,0:T(8,128)(2,1)S(1)}, u32[]{:S(2)}, u32[]{:S(2)}) collective-permute-start(bf16[32,2176]{1,0:T(8,128)(2,1)S(1)} %get-tuple-element.54), channel_id=1, source_target_pairs={{0,6},{1,7},{2,0},{3,1},{4,2},{5,3},{6,4},{7,5},{8,14},{9,15},{10,... | collective-permute-start | bytes 417800 | tf_op jit(solution)/shard_map/ppermute | solution.py:510
  46.6 0.0 collective-permute-done.1.refs_2_
  46.6 0.0 copy-start.2
  46.6 0.0 copy-start.3
  46.6 4.4 %collective-permute-start.6 = (bf16[32,2176]{1,0:T(8,128)(2,1)S(1)}, bf16[32,2176]{1,0:T(8,128)(2,1)S(1)}, u32[]{:S(2)}, u32[]{:S(2)}) collective-permute-start(bf16[32,2176]{1,0:T(8,128)(2,1)S(1)} %get-tuple-element.55), channel_id=1, source_target_pairs={{0,2},{1,3},{2,4},{3,5},{4,6},{5,7},{6,0},{7,1},{8,10},{9,11},{10,... | collective-permute-start | bytes 417800 | tf_op jit(solution)/shard_map/ppermute | solution.py:510
  51.0 0.0 collective-permute-done.2.refs_3_
  51.0 1.4 collective-permute-done.3.refs_4_
  52.4 1.6 collective-permute-done.4.refs_5_
  54.0 4.9 %collective-permute-done.5.refs_6_ = bf16[32,2176]{1,0:T(8,128)(2,1)S(1)} collective-permute-done((bf16[32,2176]{1,0:T(8,128)(2,1)S(1)}, bf16[32,2176]{1,0:T(8,128)(2,1)S(1)}, u32[]{:S(2)}, u32[]{:S(2)}) %collective-permute-start.5) | collective-permute-done | bytes 139296 | tf_op jit(solution)/shard_map/ppermute | solution.py:510
  59.0 0.2 shard_map.124
  59.1 4.7 %collective-permute-start.7 = (bf16[64,2176]{1,0:T(8,128)(2,1)S(1)}, bf16[64,2176]{1,0:T(8,128)(2,1)S(1)}, u32[]{:S(2)}, u32[]{:S(2)}) collective-permute-start(bf16[64,2176]{1,0:T(8,128)(2,1)S(1)} %get-tuple-element.57), channel_id=1, source_target_pairs={{0,16},{1,17},{2,18},{3,19},{4,20},{5,21},{6,22},{7,23},{8,24},{9,... | collective-permute-start | bytes 835592 | tf_op jit(solution)/shard_map/ppermute | solution.py:520
  63.8 2.2 %collective-permute-start.8 = (bf16[64,2176]{1,0:T(8,128)(2,1)S(1)}, bf16[64,2176]{1,0:T(8,128)(2,1)S(1)}, u32[]{:S(2)}, u32[]{:S(2)}) collective-permute-start(bf16[64,2176]{1,0:T(8,128)(2,1)S(1)} %get-tuple-element.58), channel_id=1, source_target_pairs={{0,8},{1,9},{2,10},{3,11},{4,12},{5,13},{6,14},{7,15},{8,16},{9,17... | collective-permute-start | bytes 835592 | tf_op jit(solution)/shard_map/ppermute | solution.py:520
  66.0 4.3 %collective-permute-start.9 = (bf16[64,2176]{1,0:T(8,128)(2,1)S(1)}, bf16[64,2176]{1,0:T(8,128)(2,1)S(1)}, u32[]{:S(2)}, u32[]{:S(2)}) collective-permute-start(bf16[64,2176]{1,0:T(8,128)(2,1)S(1)} %get-tuple-element.59), channel_id=1, source_target_pairs={{0,24},{1,25},{2,26},{3,27},{4,28},{5,29},{6,30},{7,31},{8,0},{9,1... | collective-permute-start | bytes 835592 | tf_op jit(solution)/shard_map/ppermute | solution.py:520
  70.3 4.5 %shard_map.122 = (bf16[128,4096]{1,0:T(8,128)(2,1)S(1)}, bf16[64,128]{1,0:T(8,128)(2,1)}, f32[64,128]{1,0:T(8,128)}, f32[192,64]{1,0:T(8,128)S(1)}, f32[128,64]{1,0:T(8,128)S(1)}, /*index=5*/bf16[128,64]{1,0:T(8,128)(2,1)}) custom-call(s32[3]{0:T(128)S(1)} %pad_add_fusion.refs_0_.place_ref, bf16[64,4096]{1,0:T(8,128)(2,1)} %x_q_hbm.1, ...), custom_call_target="tpu_custom_call" | custom-call | flops 1000 | bytes 1000 | tf_op jit(solution)/shard_map/pallas_call | solution.py:475
  74.8 0.0 collective-permute-done.7.refs_1_
  74.8 1.6 collective-permute-done.8.refs_2_
  76.4 0.0 collective-permute-done.9.refs_3_
  76.4 1.9 %shard_map.125 = (bf16[128,4096]{1,0:T(8,128)(2,1)}, bf16[128,128]{1,0:T(8,128)(2,1)}, bf16[64,4096]{1,0:T(8,128)(2,1)}, f32[128,128]{1,0:T(8,128)}) custom-call(bf16[64,2176]{1,0:T(8,128)(2,1)S(1)} %get-tuple-element.56.refs_0_, bf16[64,2176]{1,0:T(8,128)(2,1)S(1)} %collective-permute-done.7.refs_1_, bf16[64,2176]{1,0:T(8,128)(2,1)S(1)} %collective-permute-done.8.refs_2_, ...), custom_call_target="tpu_custom_call" | custom-call | flops 1000 | bytes 1000 | tf_op jit(solution)/shard_map/pallas_call | solution.py:475
  78.3 1.7 all-to-all-done
  80.0 2.2 %shard_map.126 = (bf16[192,128]{1,0:T(8,128)(2,1)}, bf16[320,64]{1,0:T(8,128)(2,1)}, f32[384,1]{1,0:T(8,128)}, f32[192,64]{1,0:T(8,128)}) custom-call(bf16[192,4224]{1,0:T(8,128)(2,1)S(1)} %bitcast.14, bf16[128,4096]{1,0:T(8,128)(2,1)S(1)} %get-tuple-element.45.refs_4_.refs_1_.pair_ref, f32[128,128]{1,0:T(8,128)} %get-tuple-element.60.refs_2_.other_both_hbm, ...), custom_call_target="tpu_custom_call" | custom-call | flops 200000000 | bytes 3000000 | tf_op jit(solution)/shard_map/pallas_call | solution.py:475
  82.2 8.9 %all-to-all-start.1 = ((bf16[24,8,128]{2,1,0:T(8,128)(2,1)}), bf16[24,8,128]{2,1,0:T(8,128)(2,1)S(1)}, u32[]{:S(2)}, u32[]{:S(2)}) async-start(bf16[24,8,128]{2,1,0:T(8,128)(2,1)} %bitcast.10), calls=%async_computation.1 | async-start | bytes 98304 | tf_op jit(solution)/shard_map/all_to_all | solution.py:490
  91.1 5.2 %shard_map.127 = (f32[32,32,128]{2,1,0:T(8,128)}, bf16[32,32,128]{2,1,0:T(8,128)(2,1)}, f32[64,4096]{1,0:T(8,128)}, f32[64,128]{1,0:T(8,128)}) custom-call(s32[3]{0:T(128)S(1)} %pad_add_fusion.refs_0_.place_ref, bf16[192,4224]{1,0:T(8,128)(2,1)S(1)} %bitcast.15, bf16[128,4096]{1,0:T(8,128)(2,1)S(1)} %get-tuple-element.45.refs_4_.refs_1_.pair_ref, ...), custom_call_target="tpu_custom_call" | custom-call | flops 900000000 | bytes 9000000 | tf_op jit(solution)/shard_map/pallas_call | solution.py:475
  96.3 5.1 %all-to-all-done.1 = bf16[24,8,128]{2,1,0:T(8,128)(2,1)S(1)} async-done(((bf16[24,8,128]{2,1,0:T(8,128)(2,1)}), bf16[24,8,128]{2,1,0:T(8,128)(2,1)S(1)}, u32[]{:S(2)}, u32[]{:S(2)}) %all-to-all-start.1) | async-done | bytes 49184 | tf_op jit(solution)/shard_map/all_to_all | solution.py:490
  101.4 2.1 %shard_map.128 = (f32[32,64,128]{2,1,0:T(8,128)S(1)}, bf16[32,64,128]{2,1,0:T(8,128)(2,1)S(1)}, f32[8,128]{1,0:T(8,128)S(1)}) custom-call(s32[3]{0:T(128)S(1)} %pad_add_fusion.refs_0_.place_ref, bf16[192,128]{1,0:T(8,128)(2,1)S(1)} %bitcast.16, bf16[192,64]{1,0:T(8,128)(2,1)S(1)} %get-tuple-element.65.refs_2_, f32[64,128]{1,0:T(8,128)} %get-tuple-element.75.refs_3_, ...), custom_call_target="tpu_custom_call" | custom-call | flops 100000000 | bytes 3000000 | tf_op jit(solution)/shard_map/pallas_call | solution.py:475
  103.6 2.3 %collective-permute-start.10 = (bf16[32,64,128]{2,1,0:T(8,128)(2,1)S(1)}, bf16[32,64,128]{2,1,0:T(8,128)(2,1)S(1)}, u32[]{:S(2)}, u32[]{:S(2)}) collective-permute-start(bf16[32,64,128]{2,1,0:T(8,128)(2,1)S(1)} %get-tuple-element.80), channel_id=1, source_target_pairs={{0,32},{32,0},{64,96},{96,64},{128,160},{160,128},{192,224},{224,1... | collective-permute-start | bytes 1572872 | tf_op jit(solution)/shard_map/ppermute | solution.py:689
  105.8 1.5 collective-permute-done.10.got_ref
  107.4 0.1 shard_map.129
  107.5 23.2 %all_to_all.25.in_ref = bf16[32,64,128]{2,1,0:T(8,128)(2,1)S(1)} all-to-all(bf16[32,64,128]{2,1,0:T(8,128)(2,1)S(1)} %shard_map.129), channel_id=1, replica_groups={{0,3,6,1,4,7,2,5,8,11,14,9,12,15,10,13,16,19,22,17,20,23,18,21,24,27,30..., dimensions={0} | all-to-all | bytes 1048576 | tf_op jit(solution)/shard_map/all_to_all | solution.py:490
  130.7 0.1 shard_map.130
  130.8 15.6 %all_to_all.26.in_ref = bf16[12,64,128]{2,1,0:T(8,128)(2,1)S(1)} all-to-all(bf16[12,64,128]{2,1,0:T(8,128)(2,1)S(1)} %shard_map.130), channel_id=1, replica_groups={{0,320,640,192,512,64,384,704,256,576,128,448},{32,352,672,224,544,96,4..., dimensions={0} | all-to-all | bytes 393216 | tf_op jit(solution)/shard_map/all_to_all | solution.py:490
  146.4 0.1 shard_map.131
  146.4 19.7 %all_to_all.27.refs_1_ = bf16[32,72,128]{2,1,0:T(8,128)(2,1)S(1)} all-to-all(bf16[32,72,128]{2,1,0:T(8,128)(2,1)S(1)} %shard_map.131), channel_id=1, replica_groups={{0,3,6,1,4,7,2,5,8,11,14,9,12,15,10,13,16,19,22,17,20,23,18,21,24,27,30..., dimensions={0} | all-to-all | bytes 1179648 | tf_op jit(solution)/shard_map/all_to_all | solution.py:490
  166.2 8.7 %collective-permute-start.11 = (bf16[32,72,128]{2,1,0:T(8,128)(2,1)S(1)}, bf16[32,72,128]{2,1,0:T(8,128)(2,1)S(1)}, u32[]{:S(2)}, u32[]{:S(2)}) collective-permute-start(bf16[32,72,128]{2,1,0:T(8,128)(2,1)S(1)} %all_to_all.27.refs_1_), channel_id=1, source_target_pairs={{0,32},{32,0},{64,96},{96,64},{128,160},{160,128},{192,224},{224,1... | collective-permute-start | bytes 1769480 | tf_op jit(solution)/shard_map/ppermute | solution.py:701
  174.9 1.6 collective-permute-done.11.refs_2_
  176.5 1.9 %shard_map.132 = (f32[64,4096]{1,0:T(8,128)}, f32[64,4096]{1,0:T(8,128)}, f32[1,1]{1,0:T(1,128)}) custom-call(s32[3]{0:T(128)S(1)} %pad_add_fusion.refs_0_.place_ref, bf16[32,72,128]{2,1,0:T(8,128)(2,1)S(1)} %all_to_all.27.refs_1_, bf16[32,72,128]{2,1,0:T(8,128)(2,1)S(1)} %collective-permute-done.11.refs_2_), custom_call_target="tpu_custom_call" | custom-call | bytes 3500000 | tf_op jit(solution)/shard_map/pallas_call | solution.py:475
  (6 shorter events, 0.0 us)
Async XLA Ops:
  5.3 17.0 %copy-start.1 = (bf16[64,4096]{1,0:T(8,128)(2,1)}, bf16[64,4096]{1,0:T(8,128)(2,1)S(1)}, u32[]{:S(2)}) copy-start(bf16[64,4096]{1,0:T(8,128)(2,1)S(1)} %get-tuple-element.46.refs_2_.refs_5_) | copy-start | bytes 1572868
  5.3 17.0 %copy-start = (bf16[64,4096]{1,0:T(8,128)(2,1)S(1)}, bf16[64,4096]{1,0:T(8,128)(2,1)}, u32[]{:S(2)}) copy-start(bf16[64,4096]{1,0:T(8,128)(2,1)} %refs_4_.3) | copy-start | bytes 1572868
  5.3 17.0 %copy-start.4 = (s32[32,2]{0,1:T(2,128)S(1)}, s32[32,2]{0,1:T(2,128)}, u32[]{:S(2)}) copy-start(s32[32,2]{0,1:T(2,128)} %param.19) | copy-start | bytes 772
  5.3 74.7 %all-to-all-start = ((bf16[24,8,4224]{2,1,0:T(8,128)(2,1)}), bf16[24,8,4224]{2,1,0:T(8,128)(2,1)S(1)}, u32[]{:S(2)}, u32[]{:S(2)}) async-start(bf16[24,8,4224]{2,1,0:T(8,128)(2,1)} %bitcast.22), calls=%async_computation | async-start | bytes 3244032 | tf_op jit(solution)/shard_map/all_to_all | solution.py:490
  23.5 21.1 %collective-permute-start = (bf16[32,2176]{1,0:T(8,128)(2,1)S(1)}, bf16[32,2176]{1,0:T(8,128)(2,1)S(1)}, u32[]{:S(2)}, u32[]{:S(2)}) collective-permute-start(bf16[32,2176]{1,0:T(8,128)(2,1)S(1)} %get-tuple-element.49), channel_id=1, source_target_pairs={{0,1},{1,2},{2,3},{3,4},{4,5},{5,6},{6,7},{7,0},{8,9},{9,10},{10,1... | collective-permute-start | bytes 417800 | tf_op jit(solution)/shard_map/ppermute | solution.py:510
  26.7 19.8 %collective-permute-start.1 = (bf16[32,2176]{1,0:T(8,128)(2,1)S(1)}, bf16[32,2176]{1,0:T(8,128)(2,1)S(1)}, u32[]{:S(2)}, u32[]{:S(2)}) collective-permute-start(bf16[32,2176]{1,0:T(8,128)(2,1)S(1)} %get-tuple-element.50), channel_id=1, source_target_pairs={{0,7},{1,0},{2,1},{3,2},{4,3},{5,4},{6,5},{7,6},{8,15},{9,8},{10,9... | collective-permute-start | bytes 417800 | tf_op jit(solution)/shard_map/ppermute | solution.py:510
  30.6 20.4 %collective-permute-start.2 = (bf16[32,2176]{1,0:T(8,128)(2,1)S(1)}, bf16[32,2176]{1,0:T(8,128)(2,1)S(1)}, u32[]{:S(2)}, u32[]{:S(2)}) collective-permute-start(bf16[32,2176]{1,0:T(8,128)(2,1)S(1)} %get-tuple-element.51), channel_id=1, source_target_pairs={{0,4},{1,5},{2,6},{3,7},{4,0},{5,1},{6,2},{7,3},{8,12},{9,13},{10,... | collective-permute-start | bytes 417800 | tf_op jit(solution)/shard_map/ppermute | solution.py:510
  37.5 14.9 %collective-permute-start.3 = (bf16[32,2176]{1,0:T(8,128)(2,1)S(1)}, bf16[32,2176]{1,0:T(8,128)(2,1)S(1)}, u32[]{:S(2)}, u32[]{:S(2)}) collective-permute-start(bf16[32,2176]{1,0:T(8,128)(2,1)S(1)} %get-tuple-element.52), channel_id=1, source_target_pairs={{0,5},{1,6},{2,7},{3,0},{4,1},{5,2},{6,3},{7,4},{8,13},{9,14},{10,... | collective-permute-start | bytes 417800 | tf_op jit(solution)/shard_map/ppermute | solution.py:510
  39.4 14.6 %collective-permute-start.4 = (bf16[32,2176]{1,0:T(8,128)(2,1)S(1)}, bf16[32,2176]{1,0:T(8,128)(2,1)S(1)}, u32[]{:S(2)}, u32[]{:S(2)}) collective-permute-start(bf16[32,2176]{1,0:T(8,128)(2,1)S(1)} %get-tuple-element.53), channel_id=1, source_target_pairs={{0,3},{1,4},{2,5},{3,6},{4,7},{5,0},{6,1},{7,2},{8,11},{9,12},{10,... | collective-permute-start | bytes 417800 | tf_op jit(solution)/shard_map/ppermute | solution.py:510
  44.6 14.4 %collective-permute-start.5 = (bf16[32,2176]{1,0:T(8,128)(2,1)S(1)}, bf16[32,2176]{1,0:T(8,128)(2,1)S(1)}, u32[]{:S(2)}, u32[]{:S(2)}) collective-permute-start(bf16[32,2176]{1,0:T(8,128)(2,1)S(1)} %get-tuple-element.54), channel_id=1, source_target_pairs={{0,6},{1,7},{2,0},{3,1},{4,2},{5,3},{6,4},{7,5},{8,14},{9,15},{10,... | collective-permute-start | bytes 417800 | tf_op jit(solution)/shard_map/ppermute | solution.py:510
  46.6 29.8 %copy-start.2 = (bf16[64,4096]{1,0:T(8,128)(2,1)S(1)}, bf16[64,4096]{1,0:T(8,128)(2,1)}, u32[]{:S(2)}) copy-start(bf16[64,4096]{1,0:T(8,128)(2,1)} %copy-done.1) | copy-start | bytes 1572868
  46.6 29.8 %copy-start.3 = (s32[64]{0:T(128)S(1)}, s32[64]{0:T(128)}, u32[]{:S(2)}) copy-start(s32[64]{0:T(128)} %param.16) | copy-start | bytes 772
  46.6 12.4 %collective-permute-start.6 = (bf16[32,2176]{1,0:T(8,128)(2,1)S(1)}, bf16[32,2176]{1,0:T(8,128)(2,1)S(1)}, u32[]{:S(2)}, u32[]{:S(2)}) collective-permute-start(bf16[32,2176]{1,0:T(8,128)(2,1)S(1)} %get-tuple-element.55), channel_id=1, source_target_pairs={{0,2},{1,3},{2,4},{3,5},{4,6},{5,7},{6,0},{7,1},{8,10},{9,11},{10,... | collective-permute-start | bytes 417800 | tf_op jit(solution)/shard_map/ppermute | solution.py:510
  59.1 15.7 %collective-permute-start.7 = (bf16[64,2176]{1,0:T(8,128)(2,1)S(1)}, bf16[64,2176]{1,0:T(8,128)(2,1)S(1)}, u32[]{:S(2)}, u32[]{:S(2)}) collective-permute-start(bf16[64,2176]{1,0:T(8,128)(2,1)S(1)} %get-tuple-element.57), channel_id=1, source_target_pairs={{0,16},{1,17},{2,18},{3,19},{4,20},{5,21},{6,22},{7,23},{8,24},{9,... | collective-permute-start | bytes 835592 | tf_op jit(solution)/shard_map/ppermute | solution.py:520
  63.8 12.6 %collective-permute-start.8 = (bf16[64,2176]{1,0:T(8,128)(2,1)S(1)}, bf16[64,2176]{1,0:T(8,128)(2,1)S(1)}, u32[]{:S(2)}, u32[]{:S(2)}) collective-permute-start(bf16[64,2176]{1,0:T(8,128)(2,1)S(1)} %get-tuple-element.58), channel_id=1, source_target_pairs={{0,8},{1,9},{2,10},{3,11},{4,12},{5,13},{6,14},{7,15},{8,16},{9,17... | collective-permute-start | bytes 835592 | tf_op jit(solution)/shard_map/ppermute | solution.py:520
  66.0 10.4 %collective-permute-start.9 = (bf16[64,2176]{1,0:T(8,128)(2,1)S(1)}, bf16[64,2176]{1,0:T(8,128)(2,1)S(1)}, u32[]{:S(2)}, u32[]{:S(2)}) collective-permute-start(bf16[64,2176]{1,0:T(8,128)(2,1)S(1)} %get-tuple-element.59), channel_id=1, source_target_pairs={{0,24},{1,25},{2,26},{3,27},{4,28},{5,29},{6,30},{7,31},{8,0},{9,1... | collective-permute-start | bytes 835592 | tf_op jit(solution)/shard_map/ppermute | solution.py:520
  82.2 19.2 %all-to-all-start.1 = ((bf16[24,8,128]{2,1,0:T(8,128)(2,1)}), bf16[24,8,128]{2,1,0:T(8,128)(2,1)S(1)}, u32[]{:S(2)}, u32[]{:S(2)}) async-start(bf16[24,8,128]{2,1,0:T(8,128)(2,1)} %bitcast.10), calls=%async_computation.1 | async-start | bytes 98304 | tf_op jit(solution)/shard_map/all_to_all | solution.py:490
  103.6 3.8 %collective-permute-start.10 = (bf16[32,64,128]{2,1,0:T(8,128)(2,1)S(1)}, bf16[32,64,128]{2,1,0:T(8,128)(2,1)S(1)}, u32[]{:S(2)}, u32[]{:S(2)}) collective-permute-start(bf16[32,64,128]{2,1,0:T(8,128)(2,1)S(1)} %get-tuple-element.80), channel_id=1, source_target_pairs={{0,32},{32,0},{64,96},{96,64},{128,160},{160,128},{192,224},{224,1... | collective-permute-start | bytes 1572872 | tf_op jit(solution)/shard_map/ppermute | solution.py:689
  166.2 10.4 %collective-permute-start.11 = (bf16[32,72,128]{2,1,0:T(8,128)(2,1)S(1)}, bf16[32,72,128]{2,1,0:T(8,128)(2,1)S(1)}, u32[]{:S(2)}, u32[]{:S(2)}) collective-permute-start(bf16[32,72,128]{2,1,0:T(8,128)(2,1)S(1)} %all_to_all.27.refs_1_), channel_id=1, source_target_pairs={{0,32},{32,0},{64,96},{96,64},{128,160},{160,128},{192,224},{224,1... | collective-permute-start | bytes 1769480 | tf_op jit(solution)/shard_map/ppermute | solution.py:701

commit v6 on v5

--- a/solution.py
+++ b/solution.py
@@ -205,49 +205,79 @@
     size = 8
     count = refs[0].shape[0] // size
     n_in = len(order)
-    refs = [refs[order.index(dy)] for dy in range(n_in)] + list(refs[n_in:])
+    x_hbm, ext_ref, pick_ref, mate_ref = refs[n_in : n_in + 4]
+    rows, width = x_hbm.shape
+    copy = pltpu.make_async_copy(x_hbm, mate_ref.at[:, 0:width], refs[-1])
+    copy.start()
+    refs = [refs[order.index(dy)] for dy in range(n_in)] + list(refs[n_in + 4 : -1])
+    mate_ref[:, width : width + lanes] = ext_ref[...]
+    for i in range(0, pick_ref.shape[0], rows):
+        piece = dot(pick_ref[i : i + rows, :], eye(rows, lanes)).astype(bf16)
+        at = width + lanes * (1 + i // rows)
+        mate_ref[0 : piece.shape[0], at : at + lanes] = piece
     for dx in range(0, count, 2):
         for dy in range(0, n_in, 2):
             a, b = [refs[dy + i][dx * size : (dx + 2) * size, :] for i in range(2)]
             at = slice(dy * size, (dy + 2) * size)
             refs[n_in + dx][at, :] = jnp.concatenate([a[:size], b[:size]], axis=0)
             refs[n_in + dx + 1][at, :] = jnp.concatenate([a[size:], b[size:]], axis=0)
-
-
-def far_kernel(count, *refs):
+    copy.wait()
+
+
+def far_kernel(count, per_near, place_ref, *refs):
     order = far_order(count)
     far_refs = [refs[order.index(dx)] for dx in range(count)]
-    pair_ref, unit_ref, p_ext_ref, positive_ref = refs[count : count + 4]
-    o_ref, ext_ref, x_far_ref, both_ref = refs[count + 4 :]
+    pair_ref, unit_ref, p_ext_ref, positive_ref, pick_ref, mate_ref = refs[count : count + 6]
+    o_ref, ext_ref, x_far_ref, both_ref, owner_ref, mate_inv_ref = refs[count + 6 :]
     rows, width = unit_ref.shape
     half = width // 2
-    total = far_refs[0].shape[0]
-    each = total // 4
-    n_far = each * count
+    total = far_refs[0].shape[0] * count
+    n_far = total // 4
     out_row = iota((total, total), 0)
     in_row = iota((total, total), 1)
-    spot = out_row % each
+    spot = out_row % n_far
     undo = (
         (in_row // 8 == spot // 2)
         & (in_row % 2 == spot % 2)
-        & ((in_row // 2) % 4 == out_row // each)
+        & ((in_row // 2) % 4 == out_row // n_far)
     ).astype(bf16)
-    for i, far_ref in enumerate(far_refs):
-        at = slice(i * each, (i + 1) * each)
-        for cols in column_tiles(half):
-            later = slice(half + cols.start, half + cols.stop)
-            got = dot(undo, far_ref[:, cols]).astype(bf16)
-            o_ref[at, cols] = got[0:each]
-            o_ref[at, later] = got[each : 2 * each]
-            x_far_ref[at, cols] = got[2 * each : 3 * each]
-            x_far_ref[at, later] = got[3 * each :]
-        ext_ref[at, :] = dot(undo[0:each], far_ref[:, half:]).astype(bf16)
+    for cols in column_tiles(half):
+        later = slice(half + cols.start, half + cols.stop)
+        got = dot(undo, jnp.concatenate([r[:, cols] for r in far_refs], axis=0)).astype(bf16)
+        o_ref[0:n_far, cols] = got[0:n_far]
+        o_ref[0:n_far, later] = got[n_far : 2 * n_far]
+        x_far_ref[:, cols] = got[2 * n_far : 3 * n_far]
+        x_far_ref[:, later] = got[3 * n_far :]
+    tail = jnp.concatenate([r[:, half:] for r in far_refs], axis=0)
+    ext_ref[0:n_far, :] = dot(undo[0:n_far], tail).astype(bf16)
     own = (iota((rows, rows), 0) == positive_ref[...]).astype(bf16)
     own_t = flip(own)
     for cols in column_tiles(width):
         o_ref[n_far:, cols] = dot(own_t, unit_ref[:, cols]).astype(bf16)
     ext_ref[n_far:, :] = dot(own_t, p_ext_ref[...]).astype(bf16)
     both_ref[...] = dot(o_ref[...], pair_ref[...], 1, 1)
+    n_near = pick_ref.shape[0]
+    mate_ext = mate_ref[:, width : width + lanes].astype(f32)
+    rank = pair_ref.shape[0] - rows
+    mate_inv_ref[...] = jnp.broadcast_to(
+        mate_ext[:, rank : rank + 1] + mate_ext[:, rank + 1 : rank + 2], mate_inv_ref.shape
+    )
+    parts = []
+    for i in range(0, n_near, rows):
+        at = width + lanes * (1 + i // rows)
+        parts.append(mate_ref[0 : min(rows, n_near - i), at : at + lanes])
+    mate_pick = jnp.concatenate(parts, axis=0) if len(parts) > 1 else parts[0]
+    row = iota((n_near, n_near), 0)
+    col = iota((n_near, n_near), 1)
+    core = place_ref[2]
+    listed = (col // per_near) % 2 == core
+    mine = (row == col) & listed
+    shift = jnp.where(core == 0, per_near, -per_near)
+    theirs = (row == col + shift) & listed
+    own_rows = dot(mine.astype(bf16), pick_ref[...]).astype(bf16)
+    mate_rows = dot(theirs.astype(bf16), mate_pick).astype(bf16)
+    owner_ref[0:rows, :] = flip(own_rows)
+    owner_ref[rows:, :] = flip(mate_rows)[0:rows]
 
 
 def score_kernel(
@@ -346,13 +376,11 @@
     near_a = spread(dot(near_gt, q_ext) - near_ext.astype(f32) * near_radial)
     other_a = spread(dot(other_gt, q_ext) - o_ext.astype(f32) * other_radial)
     q_a = spread(dot(near_g, near_ext) + dot(other_g, o_ext) - q_ext.astype(f32) * q_radial)
+    all_a = jnp.concatenate([near_a, other_a, q_a], axis=1)
     copies[4].wait()
     for cols in column_tiles(width):
-        grad = (
-            dot(near_a, near_ref[:, cols])
-            + dot(other_a, o_ref[:, cols])
-            + dot(q_a, pair_ref[0:rows, cols])
-        )
+        stack = [near_ref[:, cols], o_ref[:, cols], pair_ref[0:rows, cols]]
+        grad = dot(all_a, jnp.concatenate(stack, axis=0))
         grad = adapter_scale * (grad[0:rank] + grad[rank:])
         top, low = grad[0:part], grad[part:]
         store_blocks(up_keep_ref, cols, jnp.where(even, top, low))
@@ -373,41 +401,49 @@
     far_ext = o_ext[0:n_far, :].astype(f32)
     far_inv = far_ext[:, rank : rank + 1] + far_ext[:, rank + 1 : rank + 2]
     dz_f = (adapter_scale * far_inv * other_back[0:n_far].astype(f32)).astype(bf16)
-    dz_qt, dz_ft = flip(dz_q), flip(dz_f)
+    dz_t = flip(jnp.concatenate([dz_q, dz_f], axis=0))
     for cols in column_tiles(width):
-        down_ref[:, cols] = dot(dz_qt, x_q_ref[:, cols]) + dot(dz_ft, x_far_ref[:, cols])
+        stack = jnp.concatenate([x_q_ref[:, cols], x_far_ref[:, cols]], axis=0)
+        down_ref[:, cols] = dot(dz_t, stack)
 
 
 def down_kernel(
-    per_near, place_ref, ret_ref, pick_ref, row_hbm, x_p_ref, down_hbm, up_keep_hbm, up_send_hbm,
-    keep_ref, send_ref, loss_ref, row_ref, down_ref, sems,
+    per_near, place_ref, ret_ref, owner_hbm, row_hbm, x_p_hbm, mate_hbm, mate_inv_hbm, down_hbm,
+    up_keep_hbm, up_send_hbm,
+    keep_ref, send_ref, loss_ref, owner_ref, row_ref, x_ref, mate_inv_ref, down_ref, sems,
 ):
-    rank = down_ref.shape[0]
+    rank, width = down_ref.shape
+    rows = row_ref.shape[0]
     part = rank // 2
     pairs = [
-        (row_hbm, row_ref), (down_hbm, down_ref),
+        (owner_hbm, owner_ref), (row_hbm, row_ref), (mate_inv_hbm, mate_inv_ref),
+        (x_p_hbm, x_ref.at[0:rows]), (mate_hbm.at[:, 0:width], x_ref.at[rows : 2 * rows]),
+        (down_hbm, down_ref),
         (up_send_hbm, send_ref.at[:, part:]), (up_keep_hbm, keep_ref.at[:, part:]),
     ]
     copies = fetch(pairs, sems)
     ret = ret_ref[...]
-    row_sum = dot(flip(pick_ref[...]), ret)[:, 0:rank]
-    copies[0].wait()
-    row_sum = row_sum + row_ref[:, 0:rank]
-    dz_t = flip((adapter_scale * row_ref[:, rank : rank + 1] * row_sum).astype(bf16))
-    copies[1].wait()
+    for c in copies[:3]:
+        c.wait()
+    row_sum = dot(owner_ref[...], ret)[:, 0:rank]
+    own = row_ref[:, rank : rank + 1] * (row_sum[0:rows] + row_ref[:, 0:rank])
+    mate = mate_inv_ref[:, 0:1] * row_sum[rows:]
+    dz_t = flip((adapter_scale * jnp.concatenate([own, mate], axis=0)).astype(bf16))
+    for c in copies[3:6]:
+        c.wait()
     even = place_ref[2] == 0
-    for cols in column_tiles(x_p_ref.shape[1]):
-        grad = dot(dz_t, x_p_ref[:, cols]) + down_ref[:, cols]
+    for cols in column_tiles(width):
+        grad = dot(dz_t, x_ref[:, cols]) + down_ref[:, cols]
         top, low = grad[0:part], grad[part:]
         store_blocks(keep_ref, cols, jnp.where(even, top, low))
         store_blocks(send_ref, cols, jnp.where(even, low, top).astype(bf16))
-    first = iota(ret.shape, 0) % per_near == 0
+    first = iota(ret.shape, 0) % (2 * per_near) == 0
     lane = iota(ret.shape, 1)
     chosen = first & ((lane == rank) | (lane == rank + 1))
     share = jnp.sum(jnp.where(chosen, ret.astype(f32), 0.0), axis=1, keepdims=True)
     loss_ref[...] = jnp.broadcast_to(jnp.sum(share, axis=0, keepdims=True), loss_ref.shape)
-    copies[2].wait()
-    copies[3].wait()
+    copies[6].wait()
+    copies[7].wait()
 
 
 def add_kernel(keep_ref, got_ref, out_ref):
@@ -455,7 +491,7 @@
         down_ref[part:, cols] = low[0:part]
         up_ref[0:part, cols] = top[part:]
         up_ref[part:, cols] = low[part:]
-        loss = loss + mine[rank:, 0:lanes]
+        loss = loss + mine[rank:, 0:lanes] + other[rank:, 0:lanes]
     loss_ref[...] = jnp.sum(loss, axis=0, keepdims=True)[:, 0:1] / queries
 
 
@@ -501,24 +537,29 @@
     return [d for i, d in enumerate(order) if d not in order[:i]]
 
 
-def far_exchange(pieces, grid_x, grid_y):
+def far_exchange(pieces, grid_x, grid_y, for_mate):
     group = [(x, y) for x in range(grid_x) for y in range(grid_y)]
     order = [0, *both_ways(grid_y)]
     got = [pieces[0]]
     for dy in order[1:]:
         pairs = [(x * grid_y + y, x * grid_y + (y + dy) % grid_y) for x, y in group]
         got.append(lax.ppermute(pieces[dy], "group", pairs))
-    lines = call(
+    x, _, pick = for_mate
+    rows, width = x.shape
+    mate_width = width + lanes * (1 + -(-pick.shape[0] // rows))
+    mate, *lines = call(
         lambda *refs: regroup_kernel(order, *refs),
-        [((grid_y * 8, got[0].shape[1]), bf16)] * grid_x,
-        got,
+        [((rows, mate_width), bf16)] + [((grid_y * 8, got[0].shape[1]), bf16)] * grid_x,
+        (*got, *for_mate),
+        [pltpu.SemaphoreType.DMA(())],
         moved=1000,
+        hbm=(len(got),),
     )
     ended = [lines[0]]
     for dx in far_order(grid_x)[1:]:
         pairs = [(x * grid_y + y, (x + dx) % grid_x * grid_y + y) for x, y in group]
         ended.append(lax.ppermute(lines[dx], "group", pairs))
-    return ended
+    return ended, mate
 
 
 def far_order(size):
@@ -589,7 +630,9 @@
         plane = [x * grid_y + y * step % grid_y for x in range(grid_x) for y in range(grid_y)]
         near = exchange(near.reshape(n_dp, per_near, width + lanes), "dp", [ring])
         near = near.reshape(n_near, width + lanes)
-        far = far_exchange(far, grid_x, grid_y)
+        far, mate = far_exchange(far, grid_x, grid_y, (passage_layer_input, p_ext, pick))
+        swap = [(i, i ^ 1) for i in range(n_dp)]
+        mate = lax.ppermute(mate, "dp", swap)
         q_pair, q_ext, q_inv, near_count, other_count, shadow = call(
             lambda *refs: query_kernel(grid_x, grid_y, per_near, *refs),
             [
@@ -616,16 +659,18 @@
             flops=1000, moved=1000, hbm=range(1, 6), out_hbm=(1, 2, 5),
         )
         positive = positive_passage_index.reshape(1, rows)
-        other, other_ext, x_far, other_both = call(
-            lambda *refs: far_kernel(grid_x, *refs),
+        other, other_ext, x_far, other_both, owner, mate_inv = call(
+            lambda *refs: far_kernel(grid_x, per_near, *refs),
             [
                 ((n_other, width), bf16),
                 ((n_other, lanes), bf16),
                 ((n_far, width), bf16),
                 ((n_other, rows + rank), f32),
-            ],
-            (*far, q_pair, p_unit, p_ext, positive),
-            flops=1000, moved=1000, out_hbm=range(4),
+                ((2 * rows, n_near), bf16),
+                ((rows, lanes), f32),
+            ],
+            (place, *far, q_pair, p_unit, p_ext, positive, pick, mate),
+            flops=1000, moved=1000, out_hbm=range(6),
         )
         ret, weights, radial, near_up = call(
             lambda *refs: score_kernel(slope, rank, *refs),
@@ -643,7 +688,9 @@
             ],
             flops=200_000_000, moved=3_000_000, hbm=(2, 5), out_hbm=(1, 2, 3),
         )
-        ret = exchange(ret.reshape(n_dp, per_near, lanes), "dp", [ring]).reshape(n_near, lanes)
+        cores = [ring[c::2] for c in range(2)]
+        ret = exchange(ret.reshape(n_dp // 2, 2 * per_near, lanes), "dp", cores)
+        ret = ret.reshape(n_near, lanes)
         up_keep, up_send, down_part, row_part = call(
             local_kernel,
             [
@@ -674,7 +721,6 @@
             ],
             flops=900_000_000, moved=9_000_000, hbm=range(3, 16), out_hbm=range(4),
         )
-        swap = [(i, i ^ 1) for i in range(n_dp)]
         keep, send, loss = call(
             lambda *refs: down_kernel(per_near, *refs),
             [
@@ -682,13 +728,22 @@
                 ((n_group, rank, block), bf16),
                 ((8, lanes), f32),
             ],
-            (place, ret, pick, row_part, passage_layer_input, down_part, up_keep, up_send),
-            [((rows, lanes), f32), ((rank, width), f32), pltpu.SemaphoreType.DMA((4,))],
-            flops=100_000_000, moved=3_000_000, hbm=(3, 5, 6, 7),
+            (
+                place, ret, owner, row_part, passage_layer_input, mate, mate_inv, down_part,
+                up_keep, up_send,
+            ),
+            [
+                (owner.shape, bf16),
+                ((rows, lanes), f32),
+                ((2 * rows, width), bf16),
+                ((rows, lanes), f32),
+                ((rank, width), f32),
+                pltpu.SemaphoreType.DMA((8,)),
+            ],
+            flops=100_000_000, moved=3_000_000, hbm=range(2, 10),
         )
         got = lax.ppermute(send, "dp", swap)
         (sums,) = call(add_kernel, [((n_group, rank, block), bf16)], (keep, got), moved=2_500_000)
-        cores = [ring[c::2] for c in range(2)]
         sums = exchange(sums, "group", [plane])
         (sums,) = call(
             spread_kernel, [((n_dp // 2, rank, block), bf16)], (sums,), moved=1_000_000

time: 179 us -> 185 us (1.034)
  starting transfers between devices: 75.2 us -> 79.8 us
  Pallas kernels: 24.1 us -> 26.1 us
    ppermute x0 -> x1, starting transfers between devices: none -> 2.97 us  [body(): mate = lax.ppermute(mate, 'dp', swap)]
    all_to_all x2, waiting for transfers between devices: 6.84 us -> 4.7 us  [exchange(): lax.all_to_all(x, axis, split_axis=0, concat_axis=0, tiled=True, axis_ind...]
    pallas_call x12, Pallas kernels: 24.1 us -> 26.1 us  [call(): pl.pallas_call(kernel, out_shape=shapes, in_specs=specs, out_specs=[pl.Bl...]
  transfers between devices with their start and end apart: 14 -> 15, of which waited for: 8 -> 7; matrix products, arithmetic and copies ran while one was open for 0% -> 0% of each run, Pallas kernels for 7% -> 8%
where the time goes in v6:
time: 185 us; the launch traced here: 184 us
  starting transfers between devices  79.8 us (43%)
  blocking collectives  58.5 us (32%)
  Pallas kernels  26.1 us (14%)
  waiting for transfers between devices  18.3 us (10%)
    all_to_all x3, blocking collectives, exchange(): lax.all_to_all(x, axis, split_axis=0, concat_axis=0, tiled=True, axis_ind...  58.5 us
    ppermute x7, starting transfers between devices, far_exchange(): got.append(lax.ppermute(pieces[dy], 'group', pairs))  27.2 us
    pallas_call x12, Pallas kernels, call(): pl.pallas_call(kernel, out_shape=shapes, in_specs=specs, out_specs=[pl.Bl...  26.1 us
    all_to_all x2, starting transfers between devices, exchange(): lax.all_to_all(x, axis, split_axis=0, concat_axis=0, tiled=True, axis_ind...  25.9 us
    ppermute x3, starting transfers between devices, far_exchange(): ended.append(lax.ppermute(lines[dx], 'group', pairs))  11.1 us
    ppermute x1, starting transfers between devices, body(): other_sums = lax.ppermute(sums, 'dp', swap)  8.71 us
    ppermute x7, waiting for transfers between devices, far_exchange(): got.append(lax.ppermute(pieces[dy], 'group', pairs))  8.15 us
    all_to_all x2, waiting for transfers between devices, exchange(): lax.all_to_all(x, axis, split_axis=0, concat_axis=0, tiled=True, axis_ind...  4.7 us
  transfers between devices with their start and end apart: 15, of which 7 were waited for; matrix products, arithmetic and copies ran while one was open for 0% of the time, Pallas kernels for 8%

profile of v6, /device:TPU:1, one launch (start us, length us, event | category | flops | bytes accessed | tf_op | source)
XLA Modules:
  0.0 183.7 jit_solution(8174422085618515742)
XLA Ops:
  0.6 4.6 %shard_map.121 = (bf16[192,4224]{1,0:T(8,128)(2,1)}, bf16[64,4096]{1,0:T(8,128)(2,1)S(1)}, bf16[64,128]{1,0:T(8,128)(2,1)S(1)}, f32[64,128]{1,0:T(8,128)}, bf16[192,64]{1,0:T(8,128)(2,1)S(1)}) custom-call(bf16[64,4096]{1,0:T(8,128)(2,1)} %refs_4_.3, bf16[64,4096]{1,0:T(8,128)(2,1)} %base_hbm.1, bf16[64,4096]{1,0:T(8,128)(2,1)} %bitcast.20, ...), custom_call_target="tpu_custom_call" | custom-call | flops 300000000 | bytes 5000000 | tf_op jit(solution)/shard_map/pallas_call | solution.py:511
  5.3 0.0 copy-start.2
  5.3 0.0 copy-start
  5.3 0.0 copy-start.5
  5.3 16.8 %all-to-all-start = ((bf16[24,8,4224]{2,1,0:T(8,128)(2,1)}), bf16[24,8,4224]{2,1,0:T(8,128)(2,1)S(1)}, u32[]{:S(2)}, u32[]{:S(2)}) async-start(bf16[24,8,4224]{2,1,0:T(8,128)(2,1)} %bitcast.22), calls=%async_computation | async-start | bytes 3244032 | tf_op jit(solution)/shard_map/all_to_all | solution.py:526
  22.2 0.1 pad_add_fusion.refs_0_.place_ref
  22.3 1.2 shard_map.123
  23.5 3.2 %collective-permute-start = (bf16[32,2176]{1,0:T(8,128)(2,1)S(1)}, bf16[32,2176]{1,0:T(8,128)(2,1)S(1)}, u32[]{:S(2)}, u32[]{:S(2)}) collective-permute-start(bf16[32,2176]{1,0:T(8,128)(2,1)S(1)} %get-tuple-element.52), channel_id=1, source_target_pairs={{0,1},{1,2},{2,3},{3,4},{4,5},{5,6},{6,7},{7,0},{8,9},{9,10},{10,1... | collective-permute-start | bytes 417800 | tf_op jit(solution)/shard_map/ppermute | solution.py:546
  26.7 3.8 %collective-permute-start.1 = (bf16[32,2176]{1,0:T(8,128)(2,1)S(1)}, bf16[32,2176]{1,0:T(8,128)(2,1)S(1)}, u32[]{:S(2)}, u32[]{:S(2)}) collective-permute-start(bf16[32,2176]{1,0:T(8,128)(2,1)S(1)} %get-tuple-element.53), channel_id=1, source_target_pairs={{0,7},{1,0},{2,1},{3,2},{4,3},{5,4},{6,5},{7,6},{8,15},{9,8},{10,9... | collective-permute-start | bytes 417800 | tf_op jit(solution)/shard_map/ppermute | solution.py:546
  30.6 6.9 %collective-permute-start.2 = (bf16[32,2176]{1,0:T(8,128)(2,1)S(1)}, bf16[32,2176]{1,0:T(8,128)(2,1)S(1)}, u32[]{:S(2)}, u32[]{:S(2)}) collective-permute-start(bf16[32,2176]{1,0:T(8,128)(2,1)S(1)} %get-tuple-element.54), channel_id=1, source_target_pairs={{0,4},{1,5},{2,6},{3,7},{4,0},{5,1},{6,2},{7,3},{8,12},{9,13},{10,... | collective-permute-start | bytes 417800 | tf_op jit(solution)/shard_map/ppermute | solution.py:546
  37.5 1.9 %collective-permute-start.3 = (bf16[32,2176]{1,0:T(8,128)(2,1)S(1)}, bf16[32,2176]{1,0:T(8,128)(2,1)S(1)}, u32[]{:S(2)}, u32[]{:S(2)}) collective-permute-start(bf16[32,2176]{1,0:T(8,128)(2,1)S(1)} %get-tuple-element.55), channel_id=1, source_target_pairs={{0,5},{1,6},{2,7},{3,0},{4,1},{5,2},{6,3},{7,4},{8,13},{9,14},{10,... | collective-permute-start | bytes 417800 | tf_op jit(solution)/shard_map/ppermute | solution.py:546
  39.4 5.2 %collective-permute-start.4 = (bf16[32,2176]{1,0:T(8,128)(2,1)S(1)}, bf16[32,2176]{1,0:T(8,128)(2,1)S(1)}, u32[]{:S(2)}, u32[]{:S(2)}) collective-permute-start(bf16[32,2176]{1,0:T(8,128)(2,1)S(1)} %get-tuple-element.56), channel_id=1, source_target_pairs={{0,3},{1,4},{2,5},{3,6},{4,7},{5,0},{6,1},{7,2},{8,11},{9,12},{10,... | collective-permute-start | bytes 417800 | tf_op jit(solution)/shard_map/ppermute | solution.py:546
  44.6 0.0 collective-permute-done.refs_1_
  44.6 2.0 %collective-permute-start.5 = (bf16[32,2176]{1,0:T(8,128)(2,1)S(1)}, bf16[32,2176]{1,0:T(8,128)(2,1)S(1)}, u32[]{:S(2)}, u32[]{:S(2)}) collective-permute-start(bf16[32,2176]{1,0:T(8,128)(2,1)S(1)} %get-tuple-element.57), channel_id=1, source_target_pairs={{0,6},{1,7},{2,0},{3,1},{4,2},{5,3},{6,4},{7,5},{8,14},{9,15},{10,... | collective-permute-start | bytes 417800 | tf_op jit(solution)/shard_map/ppermute | solution.py:546
  46.6 0.0 collective-permute-done.1.refs_2_
  46.6 4.2 %collective-permute-start.6 = (bf16[32,2176]{1,0:T(8,128)(2,1)S(1)}, bf16[32,2176]{1,0:T(8,128)(2,1)S(1)}, u32[]{:S(2)}, u32[]{:S(2)}) collective-permute-start(bf16[32,2176]{1,0:T(8,128)(2,1)S(1)} %get-tuple-element.58), channel_id=1, source_target_pairs={{0,2},{1,3},{2,4},{3,5},{4,6},{5,7},{6,0},{7,1},{8,10},{9,11},{10,... | collective-permute-start | bytes 417800 | tf_op jit(solution)/shard_map/ppermute | solution.py:546
  50.8 0.0 collective-permute-done.2.refs_3_
  50.8 1.6 collective-permute-done.3.refs_4_
  52.4 1.6 collective-permute-done.4.refs_5_
  54.0 4.9 %collective-permute-done.5.refs_6_ = bf16[32,2176]{1,0:T(8,128)(2,1)S(1)} collective-permute-done((bf16[32,2176]{1,0:T(8,128)(2,1)S(1)}, bf16[32,2176]{1,0:T(8,128)(2,1)S(1)}, u32[]{:S(2)}, u32[]{:S(2)}) %collective-permute-start.5) | collective-permute-done | bytes 139296 | tf_op jit(solution)/shard_map/ppermute | solution.py:546
  59.0 0.0 collective-permute-done.6.refs_7_
  59.0 1.1 shard_map.124
  60.1 3.0 %collective-permute-start.10 = (bf16[64,4608]{1,0:T(8,128)(2,1)S(1)}, bf16[64,4608]{1,0:T(8,128)(2,1)S(1)}, u32[]{:S(2)}, u32[]{:S(2)}) collective-permute-start(bf16[64,4608]{1,0:T(8,128)(2,1)S(1)} %get-tuple-element.64), channel_id=1, source_target_pairs={{0,32},{32,0},{64,96},{96,64},{128,160},{160,128},{192,224},{224,1... | collective-permute-start | bytes 1769480 | tf_op jit(solution)/shard_map/ppermute | solution.py:635
  63.1 4.6 %collective-permute-start.7 = (bf16[64,2176]{1,0:T(8,128)(2,1)S(1)}, bf16[64,2176]{1,0:T(8,128)(2,1)S(1)}, u32[]{:S(2)}, u32[]{:S(2)}) collective-permute-start(bf16[64,2176]{1,0:T(8,128)(2,1)S(1)} %get-tuple-element.61), channel_id=1, source_target_pairs={{0,16},{1,17},{2,18},{3,19},{4,20},{5,21},{6,22},{7,23},{8,24},{9,... | collective-permute-start | bytes 835592 | tf_op jit(solution)/shard_map/ppermute | solution.py:561
  67.7 2.2 %collective-permute-start.8 = (bf16[64,2176]{1,0:T(8,128)(2,1)S(1)}, bf16[64,2176]{1,0:T(8,128)(2,1)S(1)}, u32[]{:S(2)}, u32[]{:S(2)}) collective-permute-start(bf16[64,2176]{1,0:T(8,128)(2,1)S(1)} %get-tuple-element.62), channel_id=1, source_target_pairs={{0,8},{1,9},{2,10},{3,11},{4,12},{5,13},{6,14},{7,15},{8,16},{9,17... | collective-permute-start | bytes 835592 | tf_op jit(solution)/shard_map/ppermute | solution.py:561
  70.0 4.3 %collective-permute-start.9 = (bf16[64,2176]{1,0:T(8,128)(2,1)S(1)}, bf16[64,2176]{1,0:T(8,128)(2,1)S(1)}, u32[]{:S(2)}, u32[]{:S(2)}) collective-permute-start(bf16[64,2176]{1,0:T(8,128)(2,1)S(1)} %get-tuple-element.63), channel_id=1, source_target_pairs={{0,24},{1,25},{2,26},{3,27},{4,28},{5,29},{6,30},{7,31},{8,0},{9,1... | collective-permute-start | bytes 835592 | tf_op jit(solution)/shard_map/ppermute | solution.py:561
  74.2 4.5 %shard_map.122 = (bf16[128,4096]{1,0:T(8,128)(2,1)S(1)}, bf16[64,128]{1,0:T(8,128)(2,1)}, f32[64,128]{1,0:T(8,128)}, f32[192,64]{1,0:T(8,128)S(1)}, f32[128,64]{1,0:T(8,128)S(1)}, /*index=5*/bf16[128,64]{1,0:T(8,128)(2,1)}) custom-call(s32[3]{0:T(128)S(1)} %pad_add_fusion.refs_0_.place_ref, bf16[64,4096]{1,0:T(8,128)(2,1)} %x_q_hbm.1, ...), custom_call_target="tpu_custom_call" | custom-call | flops 1000 | bytes 1000 | tf_op jit(solution)/shard_map/pallas_call | solution.py:511
  78.7 0.0 collective-permute-done.7.refs_2_
  78.7 2.3 %collective-permute-done.8.refs_3_ = bf16[64,2176]{1,0:T(8,128)(2,1)S(1)} collective-permute-done((bf16[64,2176]{1,0:T(8,128)(2,1)S(1)}, bf16[64,2176]{1,0:T(8,128)(2,1)S(1)}, u32[]{:S(2)}, u32[]{:S(2)}) %collective-permute-start.8) | collective-permute-done | bytes 278560 | tf_op jit(solution)/shard_map/ppermute | solution.py:561
  81.0 0.0 collective-permute-done.9.refs_4_
  81.1 2.7 %shard_map.125 = (bf16[128,4096]{1,0:T(8,128)(2,1)}, bf16[128,128]{1,0:T(8,128)(2,1)}, bf16[64,4096]{1,0:T(8,128)(2,1)}, f32[128,128]{1,0:T(8,128)}, bf16[128,192]{1,0:T(8,128)(2,1)}, /*index=5*/f32[64,128]{1,0:T(8,128)}) custom-call(s32[3]{0:T(128)S(1)} %pad_add_fusion.refs_0_.place_ref, bf16[64,2176]{1,0:T(8,128)(2,1)S(1)} %get-tuple-element.60.refs_1_, ...), custom_call_target="tpu_custom_call" | custom-call | flops 1000 | bytes 1000 | tf_op jit(solution)/shard_map/pallas_call | solution.py:511
  83.8 0.0 all-to-all-done
  83.8 2.2 %shard_map.126 = (bf16[192,128]{1,0:T(8,128)(2,1)}, bf16[320,64]{1,0:T(8,128)(2,1)}, f32[384,1]{1,0:T(8,128)}, f32[192,64]{1,0:T(8,128)}) custom-call(bf16[192,4224]{1,0:T(8,128)(2,1)S(1)} %bitcast.14, bf16[128,4096]{1,0:T(8,128)(2,1)S(1)} %get-tuple-element.48.refs_5_.refs_1_.pair_ref, f32[128,128]{1,0:T(8,128)} %get-tuple-element.65.refs_2_.other_both_hbm, ...), custom_call_target="tpu_custom_call" | custom-call | flops 200000000 | bytes 3000000 | tf_op jit(solution)/shard_map/pallas_call | solution.py:511
  86.0 9.1 %all-to-all-start.1 = ((bf16[12,16,128]{2,1,0:T(8,128)(2,1)}), bf16[12,16,128]{2,1,0:T(8,128)(2,1)S(1)}, u32[]{:S(2)}, u32[]{:S(2)}) async-start(bf16[12,16,128]{2,1,0:T(8,128)(2,1)} %bitcast.10), calls=%async_computation.1 | async-start | bytes 98304 | tf_op jit(solution)/shard_map/all_to_all | solution.py:526
  95.1 5.0 %shard_map.127 = (f32[32,32,128]{2,1,0:T(8,128)}, bf16[32,32,128]{2,1,0:T(8,128)(2,1)}, f32[64,4096]{1,0:T(8,128)}, f32[64,128]{1,0:T(8,128)}) custom-call(s32[3]{0:T(128)S(1)} %pad_add_fusion.refs_0_.place_ref, bf16[192,4224]{1,0:T(8,128)(2,1)S(1)} %bitcast.15, bf16[128,4096]{1,0:T(8,128)(2,1)S(1)} %get-tuple-element.48.refs_5_.refs_1_.pair_ref, ...), custom_call_target="tpu_custom_call" | custom-call | flops 900000000 | bytes 9000000 | tf_op jit(solution)/shard_map/pallas_call | solution.py:511
  100.1 4.7 %all-to-all-done.1 = bf16[12,16,128]{2,1,0:T(8,128)(2,1)S(1)} async-done(((bf16[12,16,128]{2,1,0:T(8,128)(2,1)}), bf16[12,16,128]{2,1,0:T(8,128)(2,1)S(1)}, u32[]{:S(2)}, u32[]{:S(2)}) %all-to-all-start.1) | async-done | bytes 49184 | tf_op jit(solution)/shard_map/all_to_all | solution.py:526
  104.8 2.5 %shard_map.128 = (f32[32,64,128]{2,1,0:T(8,128)S(1)}, bf16[32,64,128]{2,1,0:T(8,128)(2,1)S(1)}, f32[8,128]{1,0:T(8,128)S(1)}) custom-call(s32[3]{0:T(128)S(1)} %pad_add_fusion.refs_0_.place_ref, bf16[192,128]{1,0:T(8,128)(2,1)S(1)} %bitcast.16, bf16[128,192]{1,0:T(8,128)(2,1)} %get-tuple-element.70.refs_2_, f32[64,128]{1,0:T(8,128)} %get-tuple-element.80.refs_3_, ...), custom_call_target="tpu_custom_call" | custom-call | flops 100000000 | bytes 3000000 | tf_op jit(solution)/shard_map/pallas_call | solution.py:511
  107.3 3.9 %collective-permute-start.11 = (bf16[32,64,128]{2,1,0:T(8,128)(2,1)S(1)}, bf16[32,64,128]{2,1,0:T(8,128)(2,1)S(1)}, u32[]{:S(2)}, u32[]{:S(2)}) collective-permute-start(bf16[32,64,128]{2,1,0:T(8,128)(2,1)S(1)} %get-tuple-element.86), channel_id=1, source_target_pairs={{0,32},{32,0},{64,96},{96,64},{128,160},{160,128},{192,224},{224,1... | collective-permute-start | bytes 1572872 | tf_op jit(solution)/shard_map/ppermute | solution.py:745
  111.2 1.5 collective-permute-done.11.got_ref
  112.7 0.1 shard_map.129
  112.8 23.5 %all_to_all.25.in_ref = bf16[32,64,128]{2,1,0:T(8,128)(2,1)S(1)} all-to-all(bf16[32,64,128]{2,1,0:T(8,128)(2,1)S(1)} %shard_map.129), channel_id=1, replica_groups={{0,3,6,1,4,7,2,5,8,11,14,9,12,15,10,13,16,19,22,17,20,23,18,21,24,27,30..., dimensions={0} | all-to-all | bytes 1048576 | tf_op jit(solution)/shard_map/all_to_all | solution.py:526
  136.3 0.1 shard_map.130
  136.4 15.2 %all_to_all.26.in_ref = bf16[12,64,128]{2,1,0:T(8,128)(2,1)S(1)} all-to-all(bf16[12,64,128]{2,1,0:T(8,128)(2,1)S(1)} %shard_map.130), channel_id=1, replica_groups={{0,320,640,192,512,64,384,704,256,576,128,448},{32,352,672,224,544,96,4..., dimensions={0} | all-to-all | bytes 393216 | tf_op jit(solution)/shard_map/all_to_all | solution.py:526
  151.6 0.1 shard_map.131
  151.6 19.8 %all_to_all.27.refs_1_ = bf16[32,72,128]{2,1,0:T(8,128)(2,1)S(1)} all-to-all(bf16[32,72,128]{2,1,0:T(8,128)(2,1)S(1)} %shard_map.131), channel_id=1, replica_groups={{0,3,6,1,4,7,2,5,8,11,14,9,12,15,10,13,16,19,22,17,20,23,18,21,24,27,30..., dimensions={0} | all-to-all | bytes 1179648 | tf_op jit(solution)/shard_map/all_to_all | solution.py:526
  171.4 8.7 %collective-permute-start.12 = (bf16[32,72,128]{2,1,0:T(8,128)(2,1)S(1)}, bf16[32,72,128]{2,1,0:T(8,128)(2,1)S(1)}, u32[]{:S(2)}, u32[]{:S(2)}) collective-permute-start(bf16[32,72,128]{2,1,0:T(8,128)(2,1)S(1)} %all_to_all.27.refs_1_), channel_id=1, source_target_pairs={{0,32},{32,0},{64,96},{96,64},{128,160},{160,128},{192,224},{224,1... | collective-permute-start | bytes 1769480 | tf_op jit(solution)/shard_map/ppermute | solution.py:756
  180.2 1.6 collective-permute-done.12.refs_2_
  181.8 1.9 %shard_map.132 = (f32[64,4096]{1,0:T(8,128)}, f32[64,4096]{1,0:T(8,128)}, f32[1,1]{1,0:T(1,128)}) custom-call(s32[3]{0:T(128)S(1)} %pad_add_fusion.refs_0_.place_ref, bf16[32,72,128]{2,1,0:T(8,128)(2,1)S(1)} %all_to_all.27.refs_1_, bf16[32,72,128]{2,1,0:T(8,128)(2,1)S(1)} %collective-permute-done.12.refs_2_), custom_call_target="tpu_custom_call" | custom-call | bytes 3500000 | tf_op jit(solution)/shard_map/pallas_call | solution.py:511
  (10 shorter events, 0.0 us)
Async XLA Ops:
  5.3 17.0 %copy-start.2 = (bf16[64,4096]{1,0:T(8,128)(2,1)}, bf16[64,4096]{1,0:T(8,128)(2,1)S(1)}, u32[]{:S(2)}) copy-start(bf16[64,4096]{1,0:T(8,128)(2,1)S(1)} %get-tuple-element.49.refs_2_.refs_6_) | copy-start | bytes 1572868
  5.3 17.0 %copy-start = (bf16[64,4096]{1,0:T(8,128)(2,1)S(1)}, bf16[64,4096]{1,0:T(8,128)(2,1)}, u32[]{:S(2)}) copy-start(bf16[64,4096]{1,0:T(8,128)(2,1)} %refs_4_.3) | copy-start | bytes 1572868
  5.3 17.0 %copy-start.5 = (s32[32,2]{0,1:T(2,128)S(1)}, s32[32,2]{0,1:T(2,128)}, u32[]{:S(2)}) copy-start(s32[32,2]{0,1:T(2,128)} %param.19) | copy-start | bytes 772
  5.3 78.5 %all-to-all-start = ((bf16[24,8,4224]{2,1,0:T(8,128)(2,1)}), bf16[24,8,4224]{2,1,0:T(8,128)(2,1)S(1)}, u32[]{:S(2)}, u32[]{:S(2)}) async-start(bf16[24,8,4224]{2,1,0:T(8,128)(2,1)} %bitcast.22), calls=%async_computation | async-start | bytes 3244032 | tf_op jit(solution)/shard_map/all_to_all | solution.py:526
  23.5 21.1 %collective-permute-start = (bf16[32,2176]{1,0:T(8,128)(2,1)S(1)}, bf16[32,2176]{1,0:T(8,128)(2,1)S(1)}, u32[]{:S(2)}, u32[]{:S(2)}) collective-permute-start(bf16[32,2176]{1,0:T(8,128)(2,1)S(1)} %get-tuple-element.52), channel_id=1, source_target_pairs={{0,1},{1,2},{2,3},{3,4},{4,5},{5,6},{6,7},{7,0},{8,9},{9,10},{10,1... | collective-permute-start | bytes 417800 | tf_op jit(solution)/shard_map/ppermute | solution.py:546
  26.7 19.8 %collective-permute-start.1 = (bf16[32,2176]{1,0:T(8,128)(2,1)S(1)}, bf16[32,2176]{1,0:T(8,128)(2,1)S(1)}, u32[]{:S(2)}, u32[]{:S(2)}) collective-permute-start(bf16[32,2176]{1,0:T(8,128)(2,1)S(1)} %get-tuple-element.53), channel_id=1, source_target_pairs={{0,7},{1,0},{2,1},{3,2},{4,3},{5,4},{6,5},{7,6},{8,15},{9,8},{10,9... | collective-permute-start | bytes 417800 | tf_op jit(solution)/shard_map/ppermute | solution.py:546
  30.6 20.3 %collective-permute-start.2 = (bf16[32,2176]{1,0:T(8,128)(2,1)S(1)}, bf16[32,2176]{1,0:T(8,128)(2,1)S(1)}, u32[]{:S(2)}, u32[]{:S(2)}) collective-permute-start(bf16[32,2176]{1,0:T(8,128)(2,1)S(1)} %get-tuple-element.54), channel_id=1, source_target_pairs={{0,4},{1,5},{2,6},{3,7},{4,0},{5,1},{6,2},{7,3},{8,12},{9,13},{10,... | collective-permute-start | bytes 417800 | tf_op jit(solution)/shard_map/ppermute | solution.py:546
  37.5 14.9 %collective-permute-start.3 = (bf16[32,2176]{1,0:T(8,128)(2,1)S(1)}, bf16[32,2176]{1,0:T(8,128)(2,1)S(1)}, u32[]{:S(2)}, u32[]{:S(2)}) collective-permute-start(bf16[32,2176]{1,0:T(8,128)(2,1)S(1)} %get-tuple-element.55), channel_id=1, source_target_pairs={{0,5},{1,6},{2,7},{3,0},{4,1},{5,2},{6,3},{7,4},{8,13},{9,14},{10,... | collective-permute-start | bytes 417800 | tf_op jit(solution)/shard_map/ppermute | solution.py:546
  39.4 14.6 %collective-permute-start.4 = (bf16[32,2176]{1,0:T(8,128)(2,1)S(1)}, bf16[32,2176]{1,0:T(8,128)(2,1)S(1)}, u32[]{:S(2)}, u32[]{:S(2)}) collective-permute-start(bf16[32,2176]{1,0:T(8,128)(2,1)S(1)} %get-tuple-element.56), channel_id=1, source_target_pairs={{0,3},{1,4},{2,5},{3,6},{4,7},{5,0},{6,1},{7,2},{8,11},{9,12},{10,... | collective-permute-start | bytes 417800 | tf_op jit(solution)/shard_map/ppermute | solution.py:546
  44.6 14.4 %collective-permute-start.5 = (bf16[32,2176]{1,0:T(8,128)(2,1)S(1)}, bf16[32,2176]{1,0:T(8,128)(2,1)S(1)}, u32[]{:S(2)}, u32[]{:S(2)}) collective-permute-start(bf16[32,2176]{1,0:T(8,128)(2,1)S(1)} %get-tuple-element.57), channel_id=1, source_target_pairs={{0,6},{1,7},{2,0},{3,1},{4,2},{5,3},{6,4},{7,5},{8,14},{9,15},{10,... | collective-permute-start | bytes 417800 | tf_op jit(solution)/shard_map/ppermute | solution.py:546
  46.6 12.4 %collective-permute-start.6 = (bf16[32,2176]{1,0:T(8,128)(2,1)S(1)}, bf16[32,2176]{1,0:T(8,128)(2,1)S(1)}, u32[]{:S(2)}, u32[]{:S(2)}) collective-permute-start(bf16[32,2176]{1,0:T(8,128)(2,1)S(1)} %get-tuple-element.58), channel_id=1, source_target_pairs={{0,2},{1,3},{2,4},{3,5},{4,6},{5,7},{6,0},{7,1},{8,10},{9,11},{10,... | collective-permute-start | bytes 417800 | tf_op jit(solution)/shard_map/ppermute | solution.py:546
  59.0 22.1 %copy-start.3 = (bf16[64,4096]{1,0:T(8,128)(2,1)S(1)}, bf16[64,4096]{1,0:T(8,128)(2,1)}, u32[]{:S(2)}) copy-start(bf16[64,4096]{1,0:T(8,128)(2,1)} %copy-done.2) | copy-start | bytes 1572868
  59.0 22.1 %copy-start.4 = (s32[64]{0:T(128)S(1)}, s32[64]{0:T(128)}, u32[]{:S(2)}) copy-start(s32[64]{0:T(128)} %param.16) | copy-start | bytes 772
  60.1 21.0 %collective-permute-start.10 = (bf16[64,4608]{1,0:T(8,128)(2,1)S(1)}, bf16[64,4608]{1,0:T(8,128)(2,1)S(1)}, u32[]{:S(2)}, u32[]{:S(2)}) collective-permute-start(bf16[64,4608]{1,0:T(8,128)(2,1)S(1)} %get-tuple-element.64), channel_id=1, source_target_pairs={{0,32},{32,0},{64,96},{96,64},{128,160},{160,128},{192,224},{224,1... | collective-permute-start | bytes 1769480 | tf_op jit(solution)/shard_map/ppermute | solution.py:635
  63.1 15.7 %collective-permute-start.7 = (bf16[64,2176]{1,0:T(8,128)(2,1)S(1)}, bf16[64,2176]{1,0:T(8,128)(2,1)S(1)}, u32[]{:S(2)}, u32[]{:S(2)}) collective-permute-start(bf16[64,2176]{1,0:T(8,128)(2,1)S(1)} %get-tuple-element.61), channel_id=1, source_target_pairs={{0,16},{1,17},{2,18},{3,19},{4,20},{5,21},{6,22},{7,23},{8,24},{9,... | collective-permute-start | bytes 835592 | tf_op jit(solution)/shard_map/ppermute | solution.py:561
  67.7 13.3 %collective-permute-start.8 = (bf16[64,2176]{1,0:T(8,128)(2,1)S(1)}, bf16[64,2176]{1,0:T(8,128)(2,1)S(1)}, u32[]{:S(2)}, u32[]{:S(2)}) collective-permute-start(bf16[64,2176]{1,0:T(8,128)(2,1)S(1)} %get-tuple-element.62), channel_id=1, source_target_pairs={{0,8},{1,9},{2,10},{3,11},{4,12},{5,13},{6,14},{7,15},{8,16},{9,17... | collective-permute-start | bytes 835592 | tf_op jit(solution)/shard_map/ppermute | solution.py:561
  70.0 11.1 %collective-permute-start.9 = (bf16[64,2176]{1,0:T(8,128)(2,1)S(1)}, bf16[64,2176]{1,0:T(8,128)(2,1)S(1)}, u32[]{:S(2)}, u32[]{:S(2)}) collective-permute-start(bf16[64,2176]{1,0:T(8,128)(2,1)S(1)} %get-tuple-element.63), channel_id=1, source_target_pairs={{0,24},{1,25},{2,26},{3,27},{4,28},{5,29},{6,30},{7,31},{8,0},{9,1... | collective-permute-start | bytes 835592 | tf_op jit(solution)/shard_map/ppermute | solution.py:561
  81.0 2.8 %copy-start.1 = (bf16[64,4608]{1,0:T(8,128)(2,1)}, bf16[64,4608]{1,0:T(8,128)(2,1)S(1)}, u32[]{:S(2)}) copy-start(bf16[64,4608]{1,0:T(8,128)(2,1)S(1)} %collective-permute-done.10.refs_10_.refs_5_) | copy-start | bytes 1769476
  86.0 18.8 %all-to-all-start.1 = ((bf16[12,16,128]{2,1,0:T(8,128)(2,1)}), bf16[12,16,128]{2,1,0:T(8,128)(2,1)S(1)}, u32[]{:S(2)}, u32[]{:S(2)}) async-start(bf16[12,16,128]{2,1,0:T(8,128)(2,1)} %bitcast.10), calls=%async_computation.1 | async-start | bytes 98304 | tf_op jit(solution)/shard_map/all_to_all | solution.py:526
  107.3 5.4 %collective-permute-start.11 = (bf16[32,64,128]{2,1,0:T(8,128)(2,1)S(1)}, bf16[32,64,128]{2,1,0:T(8,128)(2,1)S(1)}, u32[]{:S(2)}, u32[]{:S(2)}) collective-permute-start(bf16[32,64,128]{2,1,0:T(8,128)(2,1)S(1)} %get-tuple-element.86), channel_id=1, source_target_pairs={{0,32},{32,0},{64,96},{96,64},{128,160},{160,128},{192,224},{224,1... | collective-permute-start | bytes 1572872 | tf_op jit(solution)/shard_map/ppermute | solution.py:745
  171.4 10.3 %collective-permute-start.12 = (bf16[32,72,128]{2,1,0:T(8,128)(2,1)S(1)}, bf16[32,72,128]{2,1,0:T(8,128)(2,1)S(1)}, u32[]{:S(2)}, u32[]{:S(2)}) collective-permute-start(bf16[32,72,128]{2,1,0:T(8,128)(2,1)S(1)} %all_to_all.27.refs_1_), channel_id=1, source_target_pairs={{0,32},{32,0},{64,96},{96,64},{128,160},{160,128},{192,224},{224,1... | collective-permute-start | bytes 1769480 | tf_op jit(solution)/shard_map/ppermute | solution.py:756

commit v7 on v5

--- a/solution.py
+++ b/solution.py
@@ -84,19 +84,11 @@
     x_ref, base_ref, down_ref, up_ref, near_ids_ref, raw_ref, near_ref, sems, out_sems,
 ):
     pairs = [
-        (x_hbm, x_ref), (down_hbm, down_ref), (base_hbm, base_ref), (up_hbm, up_ref),
-        (near_ids_hbm, near_ids_ref),
+        (near_ids_hbm, near_ids_ref), (x_hbm, x_ref), (down_hbm, down_ref), (base_hbm, base_ref),
+        (up_hbm, up_ref),
     ]
     copies = fetch(pairs, sems)
     copies[0].wait()
-    copies[1].wait()
-
-    def ready():
-        copies[2].wait()
-        copies[3].wait()
-
-    embed(x_ref, base_ref, down_ref, up_ref, unit_ref, ext_ref, inv_ref, raw_ref, ready)
-    copies[4].wait()
     rows, width = x_ref.shape
     per_near, n_near = near_ids_ref.shape
     count = per_near * n_near
@@ -108,6 +100,14 @@
     wanted = jnp.sum(jnp.where(mine, table, 0.0), axis=1, keepdims=True).astype(jnp.int32)
     pick = (iota((count, rows), 1) == wanted).astype(bf16)
     pick_ref[...] = pick
+    copies[1].wait()
+    copies[2].wait()
+
+    def ready():
+        copies[3].wait()
+        copies[4].wait()
+
+    embed(x_ref, base_ref, down_ref, up_ref, unit_ref, ext_ref, inv_ref, raw_ref, ready)
     near_ref[:, width:] = dot(pick, ext_ref[...]).astype(bf16)
     sent = []
     for i, cols in enumerate([slice(width, width + lanes), *column_tiles(width)]):
@@ -346,13 +346,11 @@
     near_a = spread(dot(near_gt, q_ext) - near_ext.astype(f32) * near_radial)
     other_a = spread(dot(other_gt, q_ext) - o_ext.astype(f32) * other_radial)
     q_a = spread(dot(near_g, near_ext) + dot(other_g, o_ext) - q_ext.astype(f32) * q_radial)
+    all_a = jnp.concatenate([near_a, other_a, q_a], axis=1)
     copies[4].wait()
     for cols in column_tiles(width):
-        grad = (
-            dot(near_a, near_ref[:, cols])
-            + dot(other_a, o_ref[:, cols])
-            + dot(q_a, pair_ref[0:rows, cols])
-        )
+        stack = [near_ref[:, cols], o_ref[:, cols], pair_ref[0:rows, cols]]
+        grad = dot(all_a, jnp.concatenate(stack, axis=0))
         grad = adapter_scale * (grad[0:rank] + grad[rank:])
         top, low = grad[0:part], grad[part:]
         store_blocks(up_keep_ref, cols, jnp.where(even, top, low))
@@ -373,22 +371,19 @@
     far_ext = o_ext[0:n_far, :].astype(f32)
     far_inv = far_ext[:, rank : rank + 1] + far_ext[:, rank + 1 : rank + 2]
     dz_f = (adapter_scale * far_inv * other_back[0:n_far].astype(f32)).astype(bf16)
-    dz_qt, dz_ft = flip(dz_q), flip(dz_f)
+    dz_t = flip(jnp.concatenate([dz_q, dz_f], axis=0))
     for cols in column_tiles(width):
-        down_ref[:, cols] = dot(dz_qt, x_q_ref[:, cols]) + dot(dz_ft, x_far_ref[:, cols])
+        stack = jnp.concatenate([x_q_ref[:, cols], x_far_ref[:, cols]], axis=0)
+        down_ref[:, cols] = dot(dz_t, stack)
 
 
 def down_kernel(
-    per_near, place_ref, ret_ref, pick_ref, row_hbm, x_p_ref, down_hbm, up_keep_hbm, up_send_hbm,
+    per_near, place_ref, ret_ref, pick_ref, row_hbm, x_p_ref, down_hbm,
     keep_ref, send_ref, loss_ref, row_ref, down_ref, sems,
 ):
     rank = down_ref.shape[0]
     part = rank // 2
-    pairs = [
-        (row_hbm, row_ref), (down_hbm, down_ref),
-        (up_send_hbm, send_ref.at[:, part:]), (up_keep_hbm, keep_ref.at[:, part:]),
-    ]
-    copies = fetch(pairs, sems)
+    copies = fetch([(row_hbm, row_ref), (down_hbm, down_ref)], sems)
     ret = ret_ref[...]
     row_sum = dot(flip(pick_ref[...]), ret)[:, 0:rank]
     copies[0].wait()
@@ -406,13 +401,13 @@
     chosen = first & ((lane == rank) | (lane == rank + 1))
     share = jnp.sum(jnp.where(chosen, ret.astype(f32), 0.0), axis=1, keepdims=True)
     loss_ref[...] = jnp.broadcast_to(jnp.sum(share, axis=0, keepdims=True), loss_ref.shape)
-    copies[2].wait()
-    copies[3].wait()
-
-
-def add_kernel(keep_ref, got_ref, out_ref):
-    for i in range(keep_ref.shape[0]):
-        out_ref[i] = (keep_ref[i] + got_ref[i].astype(f32)).astype(bf16)
+
+
+def add_kernel(down_ref, got_down_ref, up_ref, got_up_ref, out_ref):
+    part = down_ref.shape[1]
+    for i in range(down_ref.shape[0]):
+        out_ref[i, 0:part] = (down_ref[i] + got_down_ref[i].astype(f32)).astype(bf16)
+        out_ref[i, part:] = (up_ref[i] + got_up_ref[i].astype(f32)).astype(bf16)
 
 
 def sum_blocks(ref, *at):
@@ -440,26 +435,45 @@
         out_ref[i] = value
 
 
-def output_kernel(queries, place_ref, mine_ref, other_ref, down_ref, up_ref, loss_ref):
-    rank = down_ref.shape[0]
-    part = rank // 2
-    size = mine_ref.shape[2]
-    even = place_ref[2] == 0
+def write_half(half, sums_ref, down_hbm, up_hbm, stage_ref, sems):
+    count, _, size = sums_ref.shape
+    part = stage_ref.shape[0] // 2
+    at = pl.ds(pl.multiple_of(half * part, part), part)
+    step = count // 4
+    copies = []
+    for i in range(count):
+        cols = slice(i * size, (i + 1) * size)
+        stage_ref[:, cols] = sums_ref[i, 0 : 2 * part].astype(f32)
+        if (i + 1) % step == 0:
+            k = i // step
+            cols = slice(k * step * size, (k + 1) * step * size)
+            for j, out in enumerate((down_hbm, up_hbm)):
+                rows = slice(j * part, (j + 1) * part)
+                copy = pltpu.make_async_copy(
+                    stage_ref.at[rows, cols], out.at[at, cols], sems.at[2 * k + j]
+                )
+                copy.start()
+                copies.append(copy)
+    return copies
+
+
+def own_half_kernel(queries, place_ref, mine_ref, down_hbm, up_hbm, loss_ref, stage_ref, sems):
+    copies = write_half(place_ref[2], mine_ref, down_hbm, up_hbm, stage_ref, sems)
+    rank = stage_ref.shape[0]
     loss = jnp.zeros((8, lanes), f32)
     for i in range(mine_ref.shape[0]):
-        mine, other = mine_ref[i].astype(f32), other_ref[i].astype(f32)
-        cols = slice(i * size, (i + 1) * size)
-        top = jnp.where(even, mine[0:rank], other[0:rank])
-        low = jnp.where(even, other[0:rank], mine[0:rank])
-        down_ref[0:part, cols] = top[0:part]
-        down_ref[part:, cols] = low[0:part]
-        up_ref[0:part, cols] = top[part:]
-        up_ref[part:, cols] = low[part:]
-        loss = loss + mine[rank:, 0:lanes]
+        loss = loss + mine_ref[i, rank:, 0:lanes].astype(f32)
     loss_ref[...] = jnp.sum(loss, axis=0, keepdims=True)[:, 0:1] / queries
-
-
-def call(kernel, outs, args, scratch=(), flops=0, moved=0, hbm=(), out_hbm=(), out_raw=(), limit=16):
+    for c in copies:
+        c.wait()
+
+
+def other_half_kernel(place_ref, other_ref, down_in, up_in, down_hbm, up_hbm, stage_ref, sems):
+    for c in write_half(1 - place_ref[2], other_ref, down_hbm, up_hbm, stage_ref, sems):
+        c.wait()
+
+
+def call(kernel, outs, args, scratch=(), flops=0, moved=0, hbm=(), out_hbm=(), out_raw=(), alias=None, limit=16):
     specs = []
     for i, a in enumerate(args):
         space = pltpu.SMEM if a.dtype == jnp.int32 and a.ndim == 1 else pltpu.VMEM
@@ -480,6 +494,7 @@
             pl.BlockSpec(memory_space=pltpu.HBM if i in out_raw else pltpu.VMEM)
             for i in range(len(shapes))
         ],
+        input_output_aliases=alias or {},
         scratch_shapes=[pltpu.VMEM(*s) if isinstance(s, tuple) else s for s in scratch],
         compiler_params=pltpu.CompilerParams(vmem_limit_bytes=limit * 1024 * 1024),
         cost_estimate=pl.CostEstimate(flops=flops, bytes_accessed=moved, transcendentals=0),
@@ -672,22 +687,28 @@
                 (other_both.shape, f32),
                 pltpu.SemaphoreType.DMA((13,)),
             ],
-            flops=900_000_000, moved=9_000_000, hbm=range(3, 16), out_hbm=range(4),
+            flops=900_000_000, moved=9_000_000, hbm=range(3, 16), out_hbm=(2, 3),
         )
         swap = [(i, i ^ 1) for i in range(n_dp)]
+        up_got = lax.ppermute(up_send, "dp", swap)
         keep, send, loss = call(
             lambda *refs: down_kernel(per_near, *refs),
             [
-                ((n_group, rank, block), f32),
-                ((n_group, rank, block), bf16),
+                ((n_group, part, block), f32),
+                ((n_group, part, block), bf16),
                 ((8, lanes), f32),
             ],
-            (place, ret, pick, row_part, passage_layer_input, down_part, up_keep, up_send),
-            [((rows, lanes), f32), ((rank, width), f32), pltpu.SemaphoreType.DMA((4,))],
-            flops=100_000_000, moved=3_000_000, hbm=(3, 5, 6, 7),
+            (place, ret, pick, row_part, passage_layer_input, down_part),
+            [((rows, lanes), f32), ((rank, width), f32), pltpu.SemaphoreType.DMA((2,))],
+            flops=100_000_000, moved=3_000_000, hbm=(3, 5),
         )
         got = lax.ppermute(send, "dp", swap)
-        (sums,) = call(add_kernel, [((n_group, rank, block), bf16)], (keep, got), moved=2_500_000)
+        (sums,) = call(
+            add_kernel,
+            [((n_group, rank, block), bf16)],
+            (keep, got, up_keep, up_got),
+            moved=2_500_000,
+        )
         cores = [ring[c::2] for c in range(2)]
         sums = exchange(sums, "group", [plane])
         (sums,) = call(
@@ -699,11 +720,19 @@
         )
         sums = exchange(sums, "group", [plane])
         other_sums = lax.ppermute(sums, "dp", swap)
+        halves_out = [((rank, width), f32), ((rank, width), f32)]
+        stage = [((rank, width), f32), pltpu.SemaphoreType.DMA((8,))]
         down, up, loss = call(
-            lambda *refs: output_kernel(queries, *refs),
-            [((rank, width), f32), ((rank, width), f32), ((1, 1), f32)],
-            (place, sums, other_sums),
-            moved=3_500_000,
+            lambda *refs: own_half_kernel(queries, *refs),
+            [*halves_out, ((1, 1), f32)],
+            (place, sums),
+            stage, moved=1_500_000, out_hbm=(0, 1), out_raw=(0, 1),
+        )
+        down, up = call(
+            other_half_kernel,
+            halves_out,
+            (place, other_sums, down, up),
+            stage, moved=1_500_000, hbm=(2, 3), out_hbm=(0, 1), out_raw=(0, 1), alias={2: 0, 3: 1},
         )
         return (down.T, up, loss.reshape(()))
 

time: 179 us -> 182 us (1.017)
  waiting for transfers between devices: 19.6 us -> 14.8 us
  blocking collectives: 58.6 us -> 61.8 us
  starting transfers between devices: 75.2 us -> 77.4 us
    all_to_all x3, blocking collectives: 58.6 us -> 61.8 us  [exchange(): lax.all_to_all(x, axis, split_axis=0, concat_axis=0, tiled=True, axis_ind...]
    all_to_all x2, waiting for transfers between devices: 6.84 us -> 4.09 us  [exchange(): lax.all_to_all(x, axis, split_axis=0, concat_axis=0, tiled=True, axis_ind...]
    ppermute x0 -> x1, starting transfers between devices: none -> 2.22 us  [body(): up_got = lax.ppermute(up_send, 'dp', swap)]
    pallas_call x12 -> x13, Pallas kernels: 24.1 us -> 25.3 us  [call(): pl.pallas_call(kernel, out_shape=shapes, in_specs=specs, out_specs=[pl.Bl...]
  transfers between devices with their start and end apart: 14 -> 15, of which waited for: 8 -> 7; matrix products, arithmetic and copies ran while one was open for 0% -> 0% of each run, Pallas kernels for 7% -> 9%
where the time goes in v7:
time: 182 us; the launch traced here: 181 us
  starting transfers between devices  77.4 us (43%)
  blocking collectives  61.8 us (34%)
  Pallas kernels  25.3 us (14%)
  waiting for transfers between devices  14.8 us (8%)
    all_to_all x3, blocking collectives, exchange(): lax.all_to_all(x, axis, split_axis=0, concat_axis=0, tiled=True, axis_ind...  61.8 us
    ppermute x7, starting transfers between devices, far_exchange(): got.append(lax.ppermute(pieces[dy], 'group', pairs))  27.3 us
    all_to_all x2, starting transfers between devices, exchange(): lax.all_to_all(x, axis, split_axis=0, concat_axis=0, tiled=True, axis_ind...  25.7 us
    pallas_call x13, Pallas kernels, call(): pl.pallas_call(kernel, out_shape=shapes, in_specs=specs, out_specs=[pl.Bl...  25.3 us
    ppermute x3, starting transfers between devices, far_exchange(): ended.append(lax.ppermute(lines[dx], 'group', pairs))  11.1 us
    ppermute x1, starting transfers between devices, body(): other_sums = lax.ppermute(sums, 'dp', swap)  8.66 us
    ppermute x7, waiting for transfers between devices, far_exchange(): got.append(lax.ppermute(pieces[dy], 'group', pairs))  8 us
    all_to_all x2, waiting for transfers between devices, exchange(): lax.all_to_all(x, axis, split_axis=0, concat_axis=0, tiled=True, axis_ind...  4.09 us
  transfers between devices with their start and end apart: 15, of which 7 were waited for; matrix products, arithmetic and copies ran while one was open for 0% of the time, Pallas kernels for 9%

profile of v7, /device:TPU:1, one launch (start us, length us, event | category | flops | bytes accessed | tf_op | source)
XLA Modules:
  0.0 181.2 jit_solution(16071054547150418356)
XLA Ops:
  0.6 4.4 %shard_map.121 = (bf16[192,4224]{1,0:T(8,128)(2,1)}, bf16[64,4096]{1,0:T(8,128)(2,1)S(1)}, bf16[64,128]{1,0:T(8,128)(2,1)S(1)}, f32[64,128]{1,0:T(8,128)}, bf16[192,64]{1,0:T(8,128)(2,1)S(1)}) custom-call(bf16[64,4096]{1,0:T(8,128)(2,1)} %refs_4_.3, bf16[64,4096]{1,0:T(8,128)(2,1)} %base_hbm.1, bf16[64,4096]{1,0:T(8,128)(2,1)} %bitcast.20, ...), custom_call_target="tpu_custom_call" | custom-call | flops 300000000 | bytes 5000000 | tf_op jit(solution)/shard_map/pallas_call | solution.py:489
  5.0 0.0 copy-start.1
  5.0 0.0 copy-start
  5.1 0.0 copy-start.6
  5.1 16.8 %all-to-all-start = ((bf16[24,8,4224]{2,1,0:T(8,128)(2,1)}), bf16[24,8,4224]{2,1,0:T(8,128)(2,1)S(1)}, u32[]{:S(2)}, u32[]{:S(2)}) async-start(bf16[24,8,4224]{2,1,0:T(8,128)(2,1)} %bitcast.22), calls=%async_computation | async-start | bytes 3244032 | tf_op jit(solution)/shard_map/all_to_all | solution.py:505
  22.0 0.1 pad_add_fusion.refs_0_.place_ref
  22.0 1.3 shard_map.123
  23.3 3.2 %collective-permute-start = (bf16[32,2176]{1,0:T(8,128)(2,1)S(1)}, bf16[32,2176]{1,0:T(8,128)(2,1)S(1)}, u32[]{:S(2)}, u32[]{:S(2)}) collective-permute-start(bf16[32,2176]{1,0:T(8,128)(2,1)S(1)} %get-tuple-element.51), channel_id=1, source_target_pairs={{0,1},{1,2},{2,3},{3,4},{4,5},{5,6},{6,7},{7,0},{8,9},{9,10},{10,1... | collective-permute-start | bytes 417800 | tf_op jit(solution)/shard_map/ppermute | solution.py:525
  26.5 3.8 %collective-permute-start.1 = (bf16[32,2176]{1,0:T(8,128)(2,1)S(1)}, bf16[32,2176]{1,0:T(8,128)(2,1)S(1)}, u32[]{:S(2)}, u32[]{:S(2)}) collective-permute-start(bf16[32,2176]{1,0:T(8,128)(2,1)S(1)} %get-tuple-element.52), channel_id=1, source_target_pairs={{0,7},{1,0},{2,1},{3,2},{4,3},{5,4},{6,5},{7,6},{8,15},{9,8},{10,9... | collective-permute-start | bytes 417800 | tf_op jit(solution)/shard_map/ppermute | solution.py:525
  30.3 6.9 %collective-permute-start.2 = (bf16[32,2176]{1,0:T(8,128)(2,1)S(1)}, bf16[32,2176]{1,0:T(8,128)(2,1)S(1)}, u32[]{:S(2)}, u32[]{:S(2)}) collective-permute-start(bf16[32,2176]{1,0:T(8,128)(2,1)S(1)} %get-tuple-element.53), channel_id=1, source_target_pairs={{0,4},{1,5},{2,6},{3,7},{4,0},{5,1},{6,2},{7,3},{8,12},{9,13},{10,... | collective-permute-start | bytes 417800 | tf_op jit(solution)/shard_map/ppermute | solution.py:525
  37.3 1.9 %collective-permute-start.3 = (bf16[32,2176]{1,0:T(8,128)(2,1)S(1)}, bf16[32,2176]{1,0:T(8,128)(2,1)S(1)}, u32[]{:S(2)}, u32[]{:S(2)}) collective-permute-start(bf16[32,2176]{1,0:T(8,128)(2,1)S(1)} %get-tuple-element.54), channel_id=1, source_target_pairs={{0,5},{1,6},{2,7},{3,0},{4,1},{5,2},{6,3},{7,4},{8,13},{9,14},{10,... | collective-permute-start | bytes 417800 | tf_op jit(solution)/shard_map/ppermute | solution.py:525
  39.2 5.2 %collective-permute-start.4 = (bf16[32,2176]{1,0:T(8,128)(2,1)S(1)}, bf16[32,2176]{1,0:T(8,128)(2,1)S(1)}, u32[]{:S(2)}, u32[]{:S(2)}) collective-permute-start(bf16[32,2176]{1,0:T(8,128)(2,1)S(1)} %get-tuple-element.55), channel_id=1, source_target_pairs={{0,3},{1,4},{2,5},{3,6},{4,7},{5,0},{6,1},{7,2},{8,11},{9,12},{10,... | collective-permute-start | bytes 417800 | tf_op jit(solution)/shard_map/ppermute | solution.py:525
  44.4 2.0 %collective-permute-start.5 = (bf16[32,2176]{1,0:T(8,128)(2,1)S(1)}, bf16[32,2176]{1,0:T(8,128)(2,1)S(1)}, u32[]{:S(2)}, u32[]{:S(2)}) collective-permute-start(bf16[32,2176]{1,0:T(8,128)(2,1)S(1)} %get-tuple-element.56), channel_id=1, source_target_pairs={{0,6},{1,7},{2,0},{3,1},{4,2},{5,3},{6,4},{7,5},{8,14},{9,15},{10,... | collective-permute-start | bytes 417800 | tf_op jit(solution)/shard_map/ppermute | solution.py:525
  46.4 0.0 copy-start.2
  46.4 0.0 copy-start.5
  46.4 4.4 %collective-permute-start.6 = (bf16[32,2176]{1,0:T(8,128)(2,1)S(1)}, bf16[32,2176]{1,0:T(8,128)(2,1)S(1)}, u32[]{:S(2)}, u32[]{:S(2)}) collective-permute-start(bf16[32,2176]{1,0:T(8,128)(2,1)S(1)} %get-tuple-element.57), channel_id=1, source_target_pairs={{0,2},{1,3},{2,4},{3,5},{4,6},{5,7},{6,0},{7,1},{8,10},{9,11},{10,... | collective-permute-start | bytes 417800 | tf_op jit(solution)/shard_map/ppermute | solution.py:525
  50.7 0.0 collective-permute-done.2.refs_3_
  50.8 1.4 collective-permute-done.3.refs_4_
  52.2 1.6 collective-permute-done.4.refs_5_
  53.8 4.9 %collective-permute-done.5.refs_6_ = bf16[32,2176]{1,0:T(8,128)(2,1)S(1)} collective-permute-done((bf16[32,2176]{1,0:T(8,128)(2,1)S(1)}, bf16[32,2176]{1,0:T(8,128)(2,1)S(1)}, u32[]{:S(2)}, u32[]{:S(2)}) %collective-permute-start.5) | collective-permute-done | bytes 139296 | tf_op jit(solution)/shard_map/ppermute | solution.py:525
  58.7 0.0 collective-permute-done.6.refs_7_
  58.7 0.2 shard_map.124
  58.9 4.7 %collective-permute-start.7 = (bf16[64,2176]{1,0:T(8,128)(2,1)S(1)}, bf16[64,2176]{1,0:T(8,128)(2,1)S(1)}, u32[]{:S(2)}, u32[]{:S(2)}) collective-permute-start(bf16[64,2176]{1,0:T(8,128)(2,1)S(1)} %get-tuple-element.59), channel_id=1, source_target_pairs={{0,16},{1,17},{2,18},{3,19},{4,20},{5,21},{6,22},{7,23},{8,24},{9,... | collective-permute-start | bytes 835592 | tf_op jit(solution)/shard_map/ppermute | solution.py:535
  63.6 2.2 %collective-permute-start.8 = (bf16[64,2176]{1,0:T(8,128)(2,1)S(1)}, bf16[64,2176]{1,0:T(8,128)(2,1)S(1)}, u32[]{:S(2)}, u32[]{:S(2)}) collective-permute-start(bf16[64,2176]{1,0:T(8,128)(2,1)S(1)} %get-tuple-element.60), channel_id=1, source_target_pairs={{0,8},{1,9},{2,10},{3,11},{4,12},{5,13},{6,14},{7,15},{8,16},{9,17... | collective-permute-start | bytes 835592 | tf_op jit(solution)/shard_map/ppermute | solution.py:535
  65.8 4.3 %collective-permute-start.9 = (bf16[64,2176]{1,0:T(8,128)(2,1)S(1)}, bf16[64,2176]{1,0:T(8,128)(2,1)S(1)}, u32[]{:S(2)}, u32[]{:S(2)}) collective-permute-start(bf16[64,2176]{1,0:T(8,128)(2,1)S(1)} %get-tuple-element.61), channel_id=1, source_target_pairs={{0,24},{1,25},{2,26},{3,27},{4,28},{5,29},{6,30},{7,31},{8,0},{9,1... | collective-permute-start | bytes 835592 | tf_op jit(solution)/shard_map/ppermute | solution.py:535
  70.1 4.5 %shard_map.122 = (bf16[128,4096]{1,0:T(8,128)(2,1)S(1)}, bf16[64,128]{1,0:T(8,128)(2,1)}, f32[64,128]{1,0:T(8,128)}, f32[192,64]{1,0:T(8,128)S(1)}, f32[128,64]{1,0:T(8,128)S(1)}, /*index=5*/bf16[128,64]{1,0:T(8,128)(2,1)}) custom-call(s32[3]{0:T(128)S(1)} %pad_add_fusion.refs_0_.place_ref, bf16[64,4096]{1,0:T(8,128)(2,1)} %x_q_hbm.1, ...), custom_call_target="tpu_custom_call" | custom-call | flops 1000 | bytes 1000 | tf_op jit(solution)/shard_map/pallas_call | solution.py:489
  74.6 1.6 collective-permute-done.8.refs_2_
  76.2 1.9 %shard_map.125 = (bf16[128,4096]{1,0:T(8,128)(2,1)}, bf16[128,128]{1,0:T(8,128)(2,1)}, bf16[64,4096]{1,0:T(8,128)(2,1)}, f32[128,128]{1,0:T(8,128)}) custom-call(bf16[64,2176]{1,0:T(8,128)(2,1)S(1)} %get-tuple-element.58.refs_0_, bf16[64,2176]{1,0:T(8,128)(2,1)S(1)} %collective-permute-done.7.refs_1_, bf16[64,2176]{1,0:T(8,128)(2,1)S(1)} %collective-permute-done.8.refs_2_, ...), custom_call_target="tpu_custom_call" | custom-call | flops 1000 | bytes 1000 | tf_op jit(solution)/shard_map/pallas_call | solution.py:489
  78.1 1.7 all-to-all-done
  79.8 2.2 %shard_map.126 = (bf16[192,128]{1,0:T(8,128)(2,1)}, bf16[320,64]{1,0:T(8,128)(2,1)}, f32[384,1]{1,0:T(8,128)}, f32[192,64]{1,0:T(8,128)}) custom-call(bf16[192,4224]{1,0:T(8,128)(2,1)S(1)} %bitcast.14, bf16[128,4096]{1,0:T(8,128)(2,1)S(1)} %get-tuple-element.47.refs_4_.refs_1_.pair_ref, f32[128,128]{1,0:T(8,128)} %get-tuple-element.62.refs_2_.other_both_hbm, ...), custom_call_target="tpu_custom_call" | custom-call | flops 200000000 | bytes 3000000 | tf_op jit(solution)/shard_map/pallas_call | solution.py:489
  82.0 8.9 %all-to-all-start.1 = ((bf16[24,8,128]{2,1,0:T(8,128)(2,1)}), bf16[24,8,128]{2,1,0:T(8,128)(2,1)S(1)}, u32[]{:S(2)}, u32[]{:S(2)}) async-start(bf16[24,8,128]{2,1,0:T(8,128)(2,1)} %bitcast.10), calls=%async_computation.1 | async-start | bytes 98304 | tf_op jit(solution)/shard_map/all_to_all | solution.py:505
  90.8 5.0 %shard_map.127 = (f32[32,32,128]{2,1,0:T(8,128)S(1)}, bf16[32,32,128]{2,1,0:T(8,128)(2,1)}, f32[64,4096]{1,0:T(8,128)}, f32[64,128]{1,0:T(8,128)}) custom-call(s32[3]{0:T(128)S(1)} %pad_add_fusion.refs_0_.place_ref, bf16[192,4224]{1,0:T(8,128)(2,1)S(1)} %bitcast.15, bf16[128,4096]{1,0:T(8,128)(2,1)S(1)} %get-tuple-element.47.refs_4_.refs_1_.pair_ref, ...), custom_call_target="tpu_custom_call" | custom-call | flops 900000000 | bytes 9000000 | tf_op jit(solution)/shard_map/pallas_call | solution.py:489
  95.8 0.0 copy-start.3
  95.8 0.8 copy-done.3
  96.6 2.2 %collective-permute-start.11 = (bf16[32,32,128]{2,1,0:T(8,128)(2,1)}, bf16[32,32,128]{2,1,0:T(8,128)(2,1)S(1)}, u32[]{:S(2)}, u32[]{:S(2)}) collective-permute-start(bf16[32,32,128]{2,1,0:T(8,128)(2,1)} %get-tuple-element.82), channel_id=1, source_target_pairs={{0,32},{32,0},{64,96},{96,64},{128,160},{160,128},{192,224},{224,1... | collective-permute-start | bytes 786440 | tf_op jit(solution)/shard_map/ppermute | solution.py:693
  98.8 2.4 %all-to-all-done.1 = bf16[24,8,128]{2,1,0:T(8,128)(2,1)S(1)} async-done(((bf16[24,8,128]{2,1,0:T(8,128)(2,1)}), bf16[24,8,128]{2,1,0:T(8,128)(2,1)S(1)}, u32[]{:S(2)}, u32[]{:S(2)}) %all-to-all-start.1) | async-done | bytes 49184 | tf_op jit(solution)/shard_map/all_to_all | solution.py:505
  101.2 2.1 %shard_map.128 = (f32[32,32,128]{2,1,0:T(8,128)S(1)}, bf16[32,32,128]{2,1,0:T(8,128)(2,1)S(1)}, f32[8,128]{1,0:T(8,128)S(1)}) custom-call(s32[3]{0:T(128)S(1)} %pad_add_fusion.refs_0_.place_ref, bf16[192,128]{1,0:T(8,128)(2,1)S(1)} %bitcast.16, bf16[192,64]{1,0:T(8,128)(2,1)S(1)} %get-tuple-element.67.refs_2_, f32[64,128]{1,0:T(8,128)} %get-tuple-element.77.refs_3_, ...), custom_call_target="tpu_custom_call" | custom-call | flops 100000000 | bytes 3000000 | tf_op jit(solution)/shard_map/pallas_call | solution.py:489
  103.3 2.3 %collective-permute-start.10 = (bf16[32,32,128]{2,1,0:T(8,128)(2,1)S(1)}, bf16[32,32,128]{2,1,0:T(8,128)(2,1)S(1)}, u32[]{:S(2)}, u32[]{:S(2)}) collective-permute-start(bf16[32,32,128]{2,1,0:T(8,128)(2,1)S(1)} %get-tuple-element.80), channel_id=1, source_target_pairs={{0,32},{32,0},{64,96},{96,64},{128,160},{160,128},{192,224},{224,1... | collective-permute-start | bytes 786440 | tf_op jit(solution)/shard_map/ppermute | solution.py:705
  105.6 1.1 collective-permute-done.10.got_down_ref
  106.7 0.1 shard_map.129
  106.9 23.2 %all_to_all.25.in_ref = bf16[32,64,128]{2,1,0:T(8,128)(2,1)S(1)} all-to-all(bf16[32,64,128]{2,1,0:T(8,128)(2,1)S(1)} %shard_map.129), channel_id=1, replica_groups={{0,3,6,1,4,7,2,5,8,11,14,9,12,15,10,13,16,19,22,17,20,23,18,21,24,27,30..., dimensions={0} | all-to-all | bytes 1048576 | tf_op jit(solution)/shard_map/all_to_all | solution.py:505
  130.1 0.1 shard_map.130
  130.2 18.6 %all_to_all.26.in_ref = bf16[12,64,128]{2,1,0:T(8,128)(2,1)S(1)} all-to-all(bf16[12,64,128]{2,1,0:T(8,128)(2,1)S(1)} %shard_map.130), channel_id=1, replica_groups={{0,320,640,192,512,64,384,704,256,576,128,448},{32,352,672,224,544,96,4..., dimensions={0} | all-to-all | bytes 393216 | tf_op jit(solution)/shard_map/all_to_all | solution.py:505
  148.8 0.1 shard_map.131
  148.8 20.0 %all_to_all.27.refs_1_ = bf16[32,72,128]{2,1,0:T(8,128)(2,1)S(1)} all-to-all(bf16[32,72,128]{2,1,0:T(8,128)(2,1)S(1)} %shard_map.131), channel_id=1, replica_groups={{0,3,6,1,4,7,2,5,8,11,14,9,12,15,10,13,16,19,22,17,20,23,18,21,24,27,30..., dimensions={0} | all-to-all | bytes 1179648 | tf_op jit(solution)/shard_map/all_to_all | solution.py:505
  168.8 8.7 %collective-permute-start.12 = (bf16[32,72,128]{2,1,0:T(8,128)(2,1)S(1)}, bf16[32,72,128]{2,1,0:T(8,128)(2,1)S(1)}, u32[]{:S(2)}, u32[]{:S(2)}) collective-permute-start(bf16[32,72,128]{2,1,0:T(8,128)(2,1)S(1)} %all_to_all.27.refs_1_), channel_id=1, source_target_pairs={{0,32},{32,0},{64,96},{96,64},{128,160},{160,128},{192,224},{224,1... | collective-permute-start | bytes 1769480 | tf_op jit(solution)/shard_map/ppermute | solution.py:722
  177.5 2.1 %shard_map.132 = (f32[64,4096]{1,0:T(8,128)}, f32[64,4096]{1,0:T(8,128)}, f32[1,1]{1,0:T(1,128)}) custom-call(s32[3]{0:T(128)S(1)} %pad_add_fusion.refs_0_.place_ref, bf16[32,72,128]{2,1,0:T(8,128)(2,1)S(1)} %all_to_all.27.refs_1_), custom_call_target="tpu_custom_call" | custom-call | bytes 1500000 | tf_op jit(solution)/shard_map/pallas_call | solution.py:489
  179.6 1.6 shard_map.133
  (13 shorter events, 0.0 us)
Async XLA Ops:
  5.0 17.0 %copy-start.1 = (bf16[64,4096]{1,0:T(8,128)(2,1)}, bf16[64,4096]{1,0:T(8,128)(2,1)S(1)}, u32[]{:S(2)}) copy-start(bf16[64,4096]{1,0:T(8,128)(2,1)S(1)} %get-tuple-element.48.refs_2_.refs_5_) | copy-start | bytes 1572868
  5.0 17.0 %copy-start = (bf16[64,4096]{1,0:T(8,128)(2,1)S(1)}, bf16[64,4096]{1,0:T(8,128)(2,1)}, u32[]{:S(2)}) copy-start(bf16[64,4096]{1,0:T(8,128)(2,1)} %refs_4_.3) | copy-start | bytes 1572868
  5.1 17.0 %copy-start.6 = (s32[32,2]{0,1:T(2,128)S(1)}, s32[32,2]{0,1:T(2,128)}, u32[]{:S(2)}) copy-start(s32[32,2]{0,1:T(2,128)} %param.19) | copy-start | bytes 772
  5.1 74.7 %all-to-all-start = ((bf16[24,8,4224]{2,1,0:T(8,128)(2,1)}), bf16[24,8,4224]{2,1,0:T(8,128)(2,1)S(1)}, u32[]{:S(2)}, u32[]{:S(2)}) async-start(bf16[24,8,4224]{2,1,0:T(8,128)(2,1)} %bitcast.22), calls=%async_computation | async-start | bytes 3244032 | tf_op jit(solution)/shard_map/all_to_all | solution.py:505
  23.3 21.1 %collective-permute-start = (bf16[32,2176]{1,0:T(8,128)(2,1)S(1)}, bf16[32,2176]{1,0:T(8,128)(2,1)S(1)}, u32[]{:S(2)}, u32[]{:S(2)}) collective-permute-start(bf16[32,2176]{1,0:T(8,128)(2,1)S(1)} %get-tuple-element.51), channel_id=1, source_target_pairs={{0,1},{1,2},{2,3},{3,4},{4,5},{5,6},{6,7},{7,0},{8,9},{9,10},{10,1... | collective-permute-start | bytes 417800 | tf_op jit(solution)/shard_map/ppermute | solution.py:525
  26.5 19.8 %collective-permute-start.1 = (bf16[32,2176]{1,0:T(8,128)(2,1)S(1)}, bf16[32,2176]{1,0:T(8,128)(2,1)S(1)}, u32[]{:S(2)}, u32[]{:S(2)}) collective-permute-start(bf16[32,2176]{1,0:T(8,128)(2,1)S(1)} %get-tuple-element.52), channel_id=1, source_target_pairs={{0,7},{1,0},{2,1},{3,2},{4,3},{5,4},{6,5},{7,6},{8,15},{9,8},{10,9... | collective-permute-start | bytes 417800 | tf_op jit(solution)/shard_map/ppermute | solution.py:525
  30.3 20.4 %collective-permute-start.2 = (bf16[32,2176]{1,0:T(8,128)(2,1)S(1)}, bf16[32,2176]{1,0:T(8,128)(2,1)S(1)}, u32[]{:S(2)}, u32[]{:S(2)}) collective-permute-start(bf16[32,2176]{1,0:T(8,128)(2,1)S(1)} %get-tuple-element.53), channel_id=1, source_target_pairs={{0,4},{1,5},{2,6},{3,7},{4,0},{5,1},{6,2},{7,3},{8,12},{9,13},{10,... | collective-permute-start | bytes 417800 | tf_op jit(solution)/shard_map/ppermute | solution.py:525
  37.3 14.9 %collective-permute-start.3 = (bf16[32,2176]{1,0:T(8,128)(2,1)S(1)}, bf16[32,2176]{1,0:T(8,128)(2,1)S(1)}, u32[]{:S(2)}, u32[]{:S(2)}) collective-permute-start(bf16[32,2176]{1,0:T(8,128)(2,1)S(1)} %get-tuple-element.54), channel_id=1, source_target_pairs={{0,5},{1,6},{2,7},{3,0},{4,1},{5,2},{6,3},{7,4},{8,13},{9,14},{10,... | collective-permute-start | bytes 417800 | tf_op jit(solution)/shard_map/ppermute | solution.py:525
  39.2 14.6 %collective-permute-start.4 = (bf16[32,2176]{1,0:T(8,128)(2,1)S(1)}, bf16[32,2176]{1,0:T(8,128)(2,1)S(1)}, u32[]{:S(2)}, u32[]{:S(2)}) collective-permute-start(bf16[32,2176]{1,0:T(8,128)(2,1)S(1)} %get-tuple-element.55), channel_id=1, source_target_pairs={{0,3},{1,4},{2,5},{3,6},{4,7},{5,0},{6,1},{7,2},{8,11},{9,12},{10,... | collective-permute-start | bytes 417800 | tf_op jit(solution)/shard_map/ppermute | solution.py:525
  44.4 14.4 %collective-permute-start.5 = (bf16[32,2176]{1,0:T(8,128)(2,1)S(1)}, bf16[32,2176]{1,0:T(8,128)(2,1)S(1)}, u32[]{:S(2)}, u32[]{:S(2)}) collective-permute-start(bf16[32,2176]{1,0:T(8,128)(2,1)S(1)} %get-tuple-element.56), channel_id=1, source_target_pairs={{0,6},{1,7},{2,0},{3,1},{4,2},{5,3},{6,4},{7,5},{8,14},{9,15},{10,... | collective-permute-start | bytes 417800 | tf_op jit(solution)/shard_map/ppermute | solution.py:525
  46.4 29.8 %copy-start.2 = (bf16[64,4096]{1,0:T(8,128)(2,1)S(1)}, bf16[64,4096]{1,0:T(8,128)(2,1)}, u32[]{:S(2)}) copy-start(bf16[64,4096]{1,0:T(8,128)(2,1)} %copy-done.1) | copy-start | bytes 1572868
  46.4 29.8 %copy-start.5 = (s32[64]{0:T(128)S(1)}, s32[64]{0:T(128)}, u32[]{:S(2)}) copy-start(s32[64]{0:T(128)} %param.16) | copy-start | bytes 772
  46.4 12.4 %collective-permute-start.6 = (bf16[32,2176]{1,0:T(8,128)(2,1)S(1)}, bf16[32,2176]{1,0:T(8,128)(2,1)S(1)}, u32[]{:S(2)}, u32[]{:S(2)}) collective-permute-start(bf16[32,2176]{1,0:T(8,128)(2,1)S(1)} %get-tuple-element.57), channel_id=1, source_target_pairs={{0,2},{1,3},{2,4},{3,5},{4,6},{5,7},{6,0},{7,1},{8,10},{9,11},{10,... | collective-permute-start | bytes 417800 | tf_op jit(solution)/shard_map/ppermute | solution.py:525
  58.9 15.7 %collective-permute-start.7 = (bf16[64,2176]{1,0:T(8,128)(2,1)S(1)}, bf16[64,2176]{1,0:T(8,128)(2,1)S(1)}, u32[]{:S(2)}, u32[]{:S(2)}) collective-permute-start(bf16[64,2176]{1,0:T(8,128)(2,1)S(1)} %get-tuple-element.59), channel_id=1, source_target_pairs={{0,16},{1,17},{2,18},{3,19},{4,20},{5,21},{6,22},{7,23},{8,24},{9,... | collective-permute-start | bytes 835592 | tf_op jit(solution)/shard_map/ppermute | solution.py:535
  63.6 12.6 %collective-permute-start.8 = (bf16[64,2176]{1,0:T(8,128)(2,1)S(1)}, bf16[64,2176]{1,0:T(8,128)(2,1)S(1)}, u32[]{:S(2)}, u32[]{:S(2)}) collective-permute-start(bf16[64,2176]{1,0:T(8,128)(2,1)S(1)} %get-tuple-element.60), channel_id=1, source_target_pairs={{0,8},{1,9},{2,10},{3,11},{4,12},{5,13},{6,14},{7,15},{8,16},{9,17... | collective-permute-start | bytes 835592 | tf_op jit(solution)/shard_map/ppermute | solution.py:535
  65.8 10.4 %collective-permute-start.9 = (bf16[64,2176]{1,0:T(8,128)(2,1)S(1)}, bf16[64,2176]{1,0:T(8,128)(2,1)S(1)}, u32[]{:S(2)}, u32[]{:S(2)}) collective-permute-start(bf16[64,2176]{1,0:T(8,128)(2,1)S(1)} %get-tuple-element.61), channel_id=1, source_target_pairs={{0,24},{1,25},{2,26},{3,27},{4,28},{5,29},{6,30},{7,31},{8,0},{9,1... | collective-permute-start | bytes 835592 | tf_op jit(solution)/shard_map/ppermute | solution.py:535
  82.0 19.2 %all-to-all-start.1 = ((bf16[24,8,128]{2,1,0:T(8,128)(2,1)}), bf16[24,8,128]{2,1,0:T(8,128)(2,1)S(1)}, u32[]{:S(2)}, u32[]{:S(2)}) async-start(bf16[24,8,128]{2,1,0:T(8,128)(2,1)} %bitcast.10), calls=%async_computation.1 | async-start | bytes 98304 | tf_op jit(solution)/shard_map/all_to_all | solution.py:505
  95.8 0.8 copy-start.3
  96.6 10.1 %copy-start.4 = (f32[32,32,128]{2,1,0:T(8,128)S(1)}, f32[32,32,128]{2,1,0:T(8,128)}, u32[]{:S(2)}) copy-start(f32[32,32,128]{2,1,0:T(8,128)} %copy-done.3) | copy-start | bytes 1572868
  96.6 9.0 %collective-permute-start.11 = (bf16[32,32,128]{2,1,0:T(8,128)(2,1)}, bf16[32,32,128]{2,1,0:T(8,128)(2,1)S(1)}, u32[]{:S(2)}, u32[]{:S(2)}) collective-permute-start(bf16[32,32,128]{2,1,0:T(8,128)(2,1)} %get-tuple-element.82), channel_id=1, source_target_pairs={{0,32},{32,0},{64,96},{96,64},{128,160},{160,128},{192,224},{224,1... | collective-permute-start | bytes 786440 | tf_op jit(solution)/shard_map/ppermute | solution.py:693
  103.3 3.4 %collective-permute-start.10 = (bf16[32,32,128]{2,1,0:T(8,128)(2,1)S(1)}, bf16[32,32,128]{2,1,0:T(8,128)(2,1)S(1)}, u32[]{:S(2)}, u32[]{:S(2)}) collective-permute-start(bf16[32,32,128]{2,1,0:T(8,128)(2,1)S(1)} %get-tuple-element.80), channel_id=1, source_target_pairs={{0,32},{32,0},{64,96},{96,64},{128,160},{160,128},{192,224},{224,1... | collective-permute-start | bytes 786440 | tf_op jit(solution)/shard_map/ppermute | solution.py:705
  168.8 10.8 %collective-permute-start.12 = (bf16[32,72,128]{2,1,0:T(8,128)(2,1)S(1)}, bf16[32,72,128]{2,1,0:T(8,128)(2,1)S(1)}, u32[]{:S(2)}, u32[]{:S(2)}) collective-permute-start(bf16[32,72,128]{2,1,0:T(8,128)(2,1)S(1)} %all_to_all.27.refs_1_), channel_id=1, source_target_pairs={{0,32},{32,0},{64,96},{96,64},{128,160},{160,128},{192,224},{224,1... | collective-permute-start | bytes 1769480 | tf_op jit(solution)/shard_map/ppermute | solution.py:722

commit v8 on v5

--- a/solution.py
+++ b/solution.py
@@ -84,19 +84,11 @@
     x_ref, base_ref, down_ref, up_ref, near_ids_ref, raw_ref, near_ref, sems, out_sems,
 ):
     pairs = [
-        (x_hbm, x_ref), (down_hbm, down_ref), (base_hbm, base_ref), (up_hbm, up_ref),
-        (near_ids_hbm, near_ids_ref),
+        (near_ids_hbm, near_ids_ref), (x_hbm, x_ref), (down_hbm, down_ref), (base_hbm, base_ref),
+        (up_hbm, up_ref),
     ]
     copies = fetch(pairs, sems)
     copies[0].wait()
-    copies[1].wait()
-
-    def ready():
-        copies[2].wait()
-        copies[3].wait()
-
-    embed(x_ref, base_ref, down_ref, up_ref, unit_ref, ext_ref, inv_ref, raw_ref, ready)
-    copies[4].wait()
     rows, width = x_ref.shape
     per_near, n_near = near_ids_ref.shape
     count = per_near * n_near
@@ -108,6 +100,14 @@
     wanted = jnp.sum(jnp.where(mine, table, 0.0), axis=1, keepdims=True).astype(jnp.int32)
     pick = (iota((count, rows), 1) == wanted).astype(bf16)
     pick_ref[...] = pick
+    copies[1].wait()
+    copies[2].wait()
+
+    def ready():
+        copies[3].wait()
+        copies[4].wait()
+
+    embed(x_ref, base_ref, down_ref, up_ref, unit_ref, ext_ref, inv_ref, raw_ref, ready)
     near_ref[:, width:] = dot(pick, ext_ref[...]).astype(bf16)
     sent = []
     for i, cols in enumerate([slice(width, width + lanes), *column_tiles(width)]):
@@ -346,13 +346,11 @@
     near_a = spread(dot(near_gt, q_ext) - near_ext.astype(f32) * near_radial)
     other_a = spread(dot(other_gt, q_ext) - o_ext.astype(f32) * other_radial)
     q_a = spread(dot(near_g, near_ext) + dot(other_g, o_ext) - q_ext.astype(f32) * q_radial)
+    all_a = jnp.concatenate([near_a, other_a, q_a], axis=1)
     copies[4].wait()
     for cols in column_tiles(width):
-        grad = (
-            dot(near_a, near_ref[:, cols])
-            + dot(other_a, o_ref[:, cols])
-            + dot(q_a, pair_ref[0:rows, cols])
-        )
+        stack = [near_ref[:, cols], o_ref[:, cols], pair_ref[0:rows, cols]]
+        grad = dot(all_a, jnp.concatenate(stack, axis=0))
         grad = adapter_scale * (grad[0:rank] + grad[rank:])
         top, low = grad[0:part], grad[part:]
         store_blocks(up_keep_ref, cols, jnp.where(even, top, low))
@@ -373,9 +371,10 @@
     far_ext = o_ext[0:n_far, :].astype(f32)
     far_inv = far_ext[:, rank : rank + 1] + far_ext[:, rank + 1 : rank + 2]
     dz_f = (adapter_scale * far_inv * other_back[0:n_far].astype(f32)).astype(bf16)
-    dz_qt, dz_ft = flip(dz_q), flip(dz_f)
+    dz_t = flip(jnp.concatenate([dz_q, dz_f], axis=0))
     for cols in column_tiles(width):
-        down_ref[:, cols] = dot(dz_qt, x_q_ref[:, cols]) + dot(dz_ft, x_far_ref[:, cols])
+        stack = jnp.concatenate([x_q_ref[:, cols], x_far_ref[:, cols]], axis=0)
+        down_ref[:, cols] = dot(dz_t, stack)
 
 
 def down_kernel(
@@ -688,12 +687,10 @@
         )
         got = lax.ppermute(send, "dp", swap)
         (sums,) = call(add_kernel, [((n_group, rank, block), bf16)], (keep, got), moved=2_500_000)
-        cores = [ring[c::2] for c in range(2)]
+        cores = [list(range(c, n_dp, 2)) for c in range(2)]
         sums = exchange(sums, "group", [plane])
-        (sums,) = call(
-            spread_kernel, [((n_dp // 2, rank, block), bf16)], (sums,), moved=1_000_000
-        )
-        sums = exchange(sums, "dp", cores)
+        (sums,) = call(spread_kernel, [((1, rank, block), bf16)], (sums,), moved=1_000_000)
+        sums = lax.all_gather(sums, "dp", axis=0, tiled=True, axis_index_groups=cores)
         (sums,) = call(
             finish_kernel, [((n_group, rank + 8, block), bf16)], (sums, loss), moved=1_000_000
         )

time: 179 us -> 180 us (level)
    all_to_all x3 -> x2, blocking collectives: 58.6 us -> 42.1 us  [exchange(): lax.all_to_all(x, axis, split_axis=0, concat_axis=0, tiled=True, axis_ind...]
    all_gather x0 -> x1, blocking collectives: none -> 16.1 us  [body(): lax.all_gather(sums, 'dp', axis=0, tiled=True, axis_index_groups=cores)]
where the time goes in v8:
time: 180 us; the launch traced here: 179 us
  starting transfers between devices  76.7 us (43%)
  blocking collectives  58.2 us (32%)
  Pallas kernels  23.5 us (13%)
  waiting for transfers between devices  19.9 us (11%)
    all_to_all x2, blocking collectives, exchange(): lax.all_to_all(x, axis, split_axis=0, concat_axis=0, tiled=True, axis_ind...  42.1 us
    ppermute x7, starting transfers between devices, far_exchange(): got.append(lax.ppermute(pieces[dy], 'group', pairs))  27.3 us
    all_to_all x2, starting transfers between devices, exchange(): lax.all_to_all(x, axis, split_axis=0, concat_axis=0, tiled=True, axis_ind...  25.7 us
    pallas_call x12, Pallas kernels, call(): pl.pallas_call(kernel, out_shape=shapes, in_specs=specs, out_specs=[pl.Bl...  23.5 us
    all_gather x1, blocking collectives, body(): lax.all_gather(sums, 'dp', axis=0, tiled=True, axis_index_groups=cores)  16.1 us
    ppermute x3, starting transfers between devices, far_exchange(): ended.append(lax.ppermute(lines[dx], 'group', pairs))  11.1 us
    ppermute x1, starting transfers between devices, body(): other_sums = lax.ppermute(sums, 'dp', swap)  10.2 us
    ppermute x7, waiting for transfers between devices, far_exchange(): got.append(lax.ppermute(pieces[dy], 'group', pairs))  8 us
  transfers between devices with their start and end apart: 14, of which 8 were waited for; matrix products, arithmetic and copies ran while one was open for 0% of the time, Pallas kernels for 7%

profile of v8, /device:TPU:1, one launch (start us, length us, event | category | flops | bytes accessed | tf_op | source)
XLA Modules:
  0.0 179.3 jit_solution(17082860740275825154)
XLA Ops:
  0.6 4.4 %shard_map.121 = (bf16[192,4224]{1,0:T(8,128)(2,1)}, bf16[64,4096]{1,0:T(8,128)(2,1)S(1)}, bf16[64,128]{1,0:T(8,128)(2,1)S(1)}, f32[64,128]{1,0:T(8,128)}, bf16[192,64]{1,0:T(8,128)(2,1)S(1)}) custom-call(bf16[64,4096]{1,0:T(8,128)(2,1)} %refs_4_.3, bf16[64,4096]{1,0:T(8,128)(2,1)} %base_hbm.1, bf16[64,4096]{1,0:T(8,128)(2,1)} %bitcast.20, ...), custom_call_target="tpu_custom_call" | custom-call | flops 300000000 | bytes 5000000 | tf_op jit(solution)/shard_map/pallas_call | solution.py:474
  5.0 0.0 copy-start.1
  5.0 0.0 copy-start
  5.0 0.0 copy-start.4
  5.1 16.8 %all-to-all-start = ((bf16[24,8,4224]{2,1,0:T(8,128)(2,1)}), bf16[24,8,4224]{2,1,0:T(8,128)(2,1)S(1)}, u32[]{:S(2)}, u32[]{:S(2)}) async-start(bf16[24,8,4224]{2,1,0:T(8,128)(2,1)} %bitcast.22), calls=%async_computation | async-start | bytes 3244032 | tf_op jit(solution)/shard_map/all_to_all | solution.py:489
  21.9 0.1 pad_add_fusion.refs_0_.place_ref
  22.0 1.3 shard_map.123
  23.3 3.2 %collective-permute-start = (bf16[32,2176]{1,0:T(8,128)(2,1)S(1)}, bf16[32,2176]{1,0:T(8,128)(2,1)S(1)}, u32[]{:S(2)}, u32[]{:S(2)}) collective-permute-start(bf16[32,2176]{1,0:T(8,128)(2,1)S(1)} %get-tuple-element.49), channel_id=1, source_target_pairs={{0,1},{1,2},{2,3},{3,4},{4,5},{5,6},{6,7},{7,0},{8,9},{9,10},{10,1... | collective-permute-start | bytes 417800 | tf_op jit(solution)/shard_map/ppermute | solution.py:509
  26.5 3.8 %collective-permute-start.1 = (bf16[32,2176]{1,0:T(8,128)(2,1)S(1)}, bf16[32,2176]{1,0:T(8,128)(2,1)S(1)}, u32[]{:S(2)}, u32[]{:S(2)}) collective-permute-start(bf16[32,2176]{1,0:T(8,128)(2,1)S(1)} %get-tuple-element.50), channel_id=1, source_target_pairs={{0,7},{1,0},{2,1},{3,2},{4,3},{5,4},{6,5},{7,6},{8,15},{9,8},{10,9... | collective-permute-start | bytes 417800 | tf_op jit(solution)/shard_map/ppermute | solution.py:509
  30.3 6.9 %collective-permute-start.2 = (bf16[32,2176]{1,0:T(8,128)(2,1)S(1)}, bf16[32,2176]{1,0:T(8,128)(2,1)S(1)}, u32[]{:S(2)}, u32[]{:S(2)}) collective-permute-start(bf16[32,2176]{1,0:T(8,128)(2,1)S(1)} %get-tuple-element.51), channel_id=1, source_target_pairs={{0,4},{1,5},{2,6},{3,7},{4,0},{5,1},{6,2},{7,3},{8,12},{9,13},{10,... | collective-permute-start | bytes 417800 | tf_op jit(solution)/shard_map/ppermute | solution.py:509
  37.3 1.9 %collective-permute-start.3 = (bf16[32,2176]{1,0:T(8,128)(2,1)S(1)}, bf16[32,2176]{1,0:T(8,128)(2,1)S(1)}, u32[]{:S(2)}, u32[]{:S(2)}) collective-permute-start(bf16[32,2176]{1,0:T(8,128)(2,1)S(1)} %get-tuple-element.52), channel_id=1, source_target_pairs={{0,5},{1,6},{2,7},{3,0},{4,1},{5,2},{6,3},{7,4},{8,13},{9,14},{10,... | collective-permute-start | bytes 417800 | tf_op jit(solution)/shard_map/ppermute | solution.py:509
  39.2 5.2 %collective-permute-start.4 = (bf16[32,2176]{1,0:T(8,128)(2,1)S(1)}, bf16[32,2176]{1,0:T(8,128)(2,1)S(1)}, u32[]{:S(2)}, u32[]{:S(2)}) collective-permute-start(bf16[32,2176]{1,0:T(8,128)(2,1)S(1)} %get-tuple-element.53), channel_id=1, source_target_pairs={{0,3},{1,4},{2,5},{3,6},{4,7},{5,0},{6,1},{7,2},{8,11},{9,12},{10,... | collective-permute-start | bytes 417800 | tf_op jit(solution)/shard_map/ppermute | solution.py:509
  44.3 0.0 collective-permute-done.refs_1_
  44.4 2.0 %collective-permute-start.5 = (bf16[32,2176]{1,0:T(8,128)(2,1)S(1)}, bf16[32,2176]{1,0:T(8,128)(2,1)S(1)}, u32[]{:S(2)}, u32[]{:S(2)}) collective-permute-start(bf16[32,2176]{1,0:T(8,128)(2,1)S(1)} %get-tuple-element.54), channel_id=1, source_target_pairs={{0,6},{1,7},{2,0},{3,1},{4,2},{5,3},{6,4},{7,5},{8,14},{9,15},{10,... | collective-permute-start | bytes 417800 | tf_op jit(solution)/shard_map/ppermute | solution.py:509
  46.3 0.0 collective-permute-done.1.refs_2_
  46.3 0.0 copy-start.2
  46.4 0.0 copy-start.3
  46.4 4.3 %collective-permute-start.6 = (bf16[32,2176]{1,0:T(8,128)(2,1)S(1)}, bf16[32,2176]{1,0:T(8,128)(2,1)S(1)}, u32[]{:S(2)}, u32[]{:S(2)}) collective-permute-start(bf16[32,2176]{1,0:T(8,128)(2,1)S(1)} %get-tuple-element.55), channel_id=1, source_target_pairs={{0,2},{1,3},{2,4},{3,5},{4,6},{5,7},{6,0},{7,1},{8,10},{9,11},{10,... | collective-permute-start | bytes 417800 | tf_op jit(solution)/shard_map/ppermute | solution.py:509
  50.7 0.0 collective-permute-done.2.refs_3_
  50.7 1.4 collective-permute-done.3.refs_4_
  52.2 1.6 collective-permute-done.4.refs_5_
  53.8 4.9 %collective-permute-done.5.refs_6_ = bf16[32,2176]{1,0:T(8,128)(2,1)S(1)} collective-permute-done((bf16[32,2176]{1,0:T(8,128)(2,1)S(1)}, bf16[32,2176]{1,0:T(8,128)(2,1)S(1)}, u32[]{:S(2)}, u32[]{:S(2)}) %collective-permute-start.5) | collective-permute-done | bytes 139296 | tf_op jit(solution)/shard_map/ppermute | solution.py:509
  58.7 0.0 collective-permute-done.6.refs_7_
  58.7 0.2 shard_map.124
  58.9 4.6 %collective-permute-start.7 = (bf16[64,2176]{1,0:T(8,128)(2,1)S(1)}, bf16[64,2176]{1,0:T(8,128)(2,1)S(1)}, u32[]{:S(2)}, u32[]{:S(2)}) collective-permute-start(bf16[64,2176]{1,0:T(8,128)(2,1)S(1)} %get-tuple-element.57), channel_id=1, source_target_pairs={{0,16},{1,17},{2,18},{3,19},{4,20},{5,21},{6,22},{7,23},{8,24},{9,... | collective-permute-start | bytes 835592 | tf_op jit(solution)/shard_map/ppermute | solution.py:519
  63.6 2.2 %collective-permute-start.8 = (bf16[64,2176]{1,0:T(8,128)(2,1)S(1)}, bf16[64,2176]{1,0:T(8,128)(2,1)S(1)}, u32[]{:S(2)}, u32[]{:S(2)}) collective-permute-start(bf16[64,2176]{1,0:T(8,128)(2,1)S(1)} %get-tuple-element.58), channel_id=1, source_target_pairs={{0,8},{1,9},{2,10},{3,11},{4,12},{5,13},{6,14},{7,15},{8,16},{9,17... | collective-permute-start | bytes 835592 | tf_op jit(solution)/shard_map/ppermute | solution.py:519
  65.8 4.3 %collective-permute-start.9 = (bf16[64,2176]{1,0:T(8,128)(2,1)S(1)}, bf16[64,2176]{1,0:T(8,128)(2,1)S(1)}, u32[]{:S(2)}, u32[]{:S(2)}) collective-permute-start(bf16[64,2176]{1,0:T(8,128)(2,1)S(1)} %get-tuple-element.59), channel_id=1, source_target_pairs={{0,24},{1,25},{2,26},{3,27},{4,28},{5,29},{6,30},{7,31},{8,0},{9,1... | collective-permute-start | bytes 835592 | tf_op jit(solution)/shard_map/ppermute | solution.py:519
  70.1 4.5 %shard_map.122 = (bf16[128,4096]{1,0:T(8,128)(2,1)S(1)}, bf16[64,128]{1,0:T(8,128)(2,1)}, f32[64,128]{1,0:T(8,128)}, f32[192,64]{1,0:T(8,128)S(1)}, f32[128,64]{1,0:T(8,128)S(1)}, /*index=5*/bf16[128,64]{1,0:T(8,128)(2,1)}) custom-call(s32[3]{0:T(128)S(1)} %pad_add_fusion.refs_0_.place_ref, bf16[64,4096]{1,0:T(8,128)(2,1)} %x_q_hbm.1, ...), custom_call_target="tpu_custom_call" | custom-call | flops 1000 | bytes 1000 | tf_op jit(solution)/shard_map/pallas_call | solution.py:474
  74.5 1.6 collective-permute-done.8.refs_2_
  76.2 0.0 collective-permute-done.9.refs_3_
  76.2 1.9 %shard_map.125 = (bf16[128,4096]{1,0:T(8,128)(2,1)}, bf16[128,128]{1,0:T(8,128)(2,1)}, bf16[64,4096]{1,0:T(8,128)(2,1)}, f32[128,128]{1,0:T(8,128)}) custom-call(bf16[64,2176]{1,0:T(8,128)(2,1)S(1)} %get-tuple-element.56.refs_0_, bf16[64,2176]{1,0:T(8,128)(2,1)S(1)} %collective-permute-done.7.refs_1_, bf16[64,2176]{1,0:T(8,128)(2,1)S(1)} %collective-permute-done.8.refs_2_, ...), custom_call_target="tpu_custom_call" | custom-call | flops 1000 | bytes 1000 | tf_op jit(solution)/shard_map/pallas_call | solution.py:474
  78.0 1.7 all-to-all-done
  79.8 2.2 %shard_map.126 = (bf16[192,128]{1,0:T(8,128)(2,1)}, bf16[320,64]{1,0:T(8,128)(2,1)}, f32[384,1]{1,0:T(8,128)}, f32[192,64]{1,0:T(8,128)}) custom-call(bf16[192,4224]{1,0:T(8,128)(2,1)S(1)} %bitcast.14, bf16[128,4096]{1,0:T(8,128)(2,1)S(1)} %get-tuple-element.45.refs_4_.refs_1_.pair_ref, f32[128,128]{1,0:T(8,128)} %get-tuple-element.60.refs_2_.other_both_hbm, ...), custom_call_target="tpu_custom_call" | custom-call | flops 200000000 | bytes 3000000 | tf_op jit(solution)/shard_map/pallas_call | solution.py:474
  81.9 8.9 %all-to-all-start.1 = ((bf16[24,8,128]{2,1,0:T(8,128)(2,1)}), bf16[24,8,128]{2,1,0:T(8,128)(2,1)S(1)}, u32[]{:S(2)}, u32[]{:S(2)}) async-start(bf16[24,8,128]{2,1,0:T(8,128)(2,1)} %bitcast.10), calls=%async_computation.1 | async-start | bytes 98304 | tf_op jit(solution)/shard_map/all_to_all | solution.py:489
  90.8 5.0 %shard_map.127 = (f32[32,32,128]{2,1,0:T(8,128)}, bf16[32,32,128]{2,1,0:T(8,128)(2,1)}, f32[64,4096]{1,0:T(8,128)}, f32[64,128]{1,0:T(8,128)}) custom-call(s32[3]{0:T(128)S(1)} %pad_add_fusion.refs_0_.place_ref, bf16[192,4224]{1,0:T(8,128)(2,1)S(1)} %bitcast.15, bf16[128,4096]{1,0:T(8,128)(2,1)S(1)} %get-tuple-element.45.refs_4_.refs_1_.pair_ref, ...), custom_call_target="tpu_custom_call" | custom-call | flops 900000000 | bytes 9000000 | tf_op jit(solution)/shard_map/pallas_call | solution.py:474
  95.8 5.4 %all-to-all-done.1 = bf16[24,8,128]{2,1,0:T(8,128)(2,1)S(1)} async-done(((bf16[24,8,128]{2,1,0:T(8,128)(2,1)}), bf16[24,8,128]{2,1,0:T(8,128)(2,1)S(1)}, u32[]{:S(2)}, u32[]{:S(2)}) %all-to-all-start.1) | async-done | bytes 49184 | tf_op jit(solution)/shard_map/all_to_all | solution.py:489
  101.2 2.1 %shard_map.128 = (f32[32,64,128]{2,1,0:T(8,128)S(1)}, bf16[32,64,128]{2,1,0:T(8,128)(2,1)S(1)}, f32[8,128]{1,0:T(8,128)S(1)}) custom-call(s32[3]{0:T(128)S(1)} %pad_add_fusion.refs_0_.place_ref, bf16[192,128]{1,0:T(8,128)(2,1)S(1)} %bitcast.16, bf16[192,64]{1,0:T(8,128)(2,1)S(1)} %get-tuple-element.65.refs_2_, f32[64,128]{1,0:T(8,128)} %get-tuple-element.75.refs_3_, ...), custom_call_target="tpu_custom_call" | custom-call | flops 100000000 | bytes 3000000 | tf_op jit(solution)/shard_map/pallas_call | solution.py:474
  103.3 2.3 %collective-permute-start.10 = (bf16[32,64,128]{2,1,0:T(8,128)(2,1)S(1)}, bf16[32,64,128]{2,1,0:T(8,128)(2,1)S(1)}, u32[]{:S(2)}, u32[]{:S(2)}) collective-permute-start(bf16[32,64,128]{2,1,0:T(8,128)(2,1)S(1)} %get-tuple-element.80), channel_id=1, source_target_pairs={{0,32},{32,0},{64,96},{96,64},{128,160},{160,128},{192,224},{224,1... | collective-permute-start | bytes 1572872 | tf_op jit(solution)/shard_map/ppermute | solution.py:688
  105.6 1.5 collective-permute-done.10.got_ref
  107.1 0.1 shard_map.129
  107.2 23.2 %all_to_all.20.in_ref = bf16[32,64,128]{2,1,0:T(8,128)(2,1)S(1)} all-to-all(bf16[32,64,128]{2,1,0:T(8,128)(2,1)S(1)} %shard_map.129), channel_id=1, replica_groups={{0,3,6,1,4,7,2,5,8,11,14,9,12,15,10,13,16,19,22,17,20,23,18,21,24,27,30..., dimensions={0} | all-to-all | bytes 1048576 | tf_op jit(solution)/shard_map/all_to_all | solution.py:489
  130.4 0.1 shard_map.130
  130.5 16.1 %all_gather.3.in_ref = bf16[12,64,128]{2,1,0:T(8,128)(2,1)S(1)} all-gather(bf16[1,64,128]{2,1,0:T(8,128)(2,1)S(1)} %shard_map.130), channel_id=1, replica_groups={{0,64,128,192,256,320,384,448,512,576,640,704},{32,96,160,224,288,352,4..., dimensions={0}, use_global_device_ids=true | all-gather | bytes 212992 | tf_op jit(solution)/shard_map/all_gather | solution.py:693
  146.6 0.1 shard_map.131
  146.7 18.9 %all_to_all.21.refs_1_ = bf16[32,72,128]{2,1,0:T(8,128)(2,1)S(1)} all-to-all(bf16[32,72,128]{2,1,0:T(8,128)(2,1)S(1)} %shard_map.131), channel_id=1, replica_groups={{0,3,6,1,4,7,2,5,8,11,14,9,12,15,10,13,16,19,22,17,20,23,18,21,24,27,30..., dimensions={0} | all-to-all | bytes 1179648 | tf_op jit(solution)/shard_map/all_to_all | solution.py:489
  165.5 10.2 %collective-permute-start.11 = (bf16[32,72,128]{2,1,0:T(8,128)(2,1)S(1)}, bf16[32,72,128]{2,1,0:T(8,128)(2,1)S(1)}, u32[]{:S(2)}, u32[]{:S(2)}) collective-permute-start(bf16[32,72,128]{2,1,0:T(8,128)(2,1)S(1)} %all_to_all.21.refs_1_), channel_id=1, source_target_pairs={{0,32},{32,0},{64,96},{96,64},{128,160},{160,128},{192,224},{224,1... | collective-permute-start | bytes 1769480 | tf_op jit(solution)/shard_map/ppermute | solution.py:698
  175.8 1.6 collective-permute-done.11.refs_2_
  177.4 1.9 %shard_map.132 = (f32[64,4096]{1,0:T(8,128)}, f32[64,4096]{1,0:T(8,128)}, f32[1,1]{1,0:T(1,128)}) custom-call(s32[3]{0:T(128)S(1)} %pad_add_fusion.refs_0_.place_ref, bf16[32,72,128]{2,1,0:T(8,128)(2,1)S(1)} %all_to_all.21.refs_1_, bf16[32,72,128]{2,1,0:T(8,128)(2,1)S(1)} %collective-permute-done.11.refs_2_), custom_call_target="tpu_custom_call" | custom-call | bytes 3500000 | tf_op jit(solution)/shard_map/pallas_call | solution.py:474
  (6 shorter events, 0.0 us)
Async XLA Ops:
  5.0 17.0 %copy-start.1 = (bf16[64,4096]{1,0:T(8,128)(2,1)}, bf16[64,4096]{1,0:T(8,128)(2,1)S(1)}, u32[]{:S(2)}) copy-start(bf16[64,4096]{1,0:T(8,128)(2,1)S(1)} %get-tuple-element.46.refs_2_.refs_5_) | copy-start | bytes 1572868
  5.0 17.0 %copy-start = (bf16[64,4096]{1,0:T(8,128)(2,1)S(1)}, bf16[64,4096]{1,0:T(8,128)(2,1)}, u32[]{:S(2)}) copy-start(bf16[64,4096]{1,0:T(8,128)(2,1)} %refs_4_.3) | copy-start | bytes 1572868
  5.0 17.0 %copy-start.4 = (s32[32,2]{0,1:T(2,128)S(1)}, s32[32,2]{0,1:T(2,128)}, u32[]{:S(2)}) copy-start(s32[32,2]{0,1:T(2,128)} %param.19) | copy-start | bytes 772
  5.1 74.7 %all-to-all-start = ((bf16[24,8,4224]{2,1,0:T(8,128)(2,1)}), bf16[24,8,4224]{2,1,0:T(8,128)(2,1)S(1)}, u32[]{:S(2)}, u32[]{:S(2)}) async-start(bf16[24,8,4224]{2,1,0:T(8,128)(2,1)} %bitcast.22), calls=%async_computation | async-start | bytes 3244032 | tf_op jit(solution)/shard_map/all_to_all | solution.py:489
  23.3 21.1 %collective-permute-start = (bf16[32,2176]{1,0:T(8,128)(2,1)S(1)}, bf16[32,2176]{1,0:T(8,128)(2,1)S(1)}, u32[]{:S(2)}, u32[]{:S(2)}) collective-permute-start(bf16[32,2176]{1,0:T(8,128)(2,1)S(1)} %get-tuple-element.49), channel_id=1, source_target_pairs={{0,1},{1,2},{2,3},{3,4},{4,5},{5,6},{6,7},{7,0},{8,9},{9,10},{10,1... | collective-permute-start | bytes 417800 | tf_op jit(solution)/shard_map/ppermute | solution.py:509
  26.5 19.8 %collective-permute-start.1 = (bf16[32,2176]{1,0:T(8,128)(2,1)S(1)}, bf16[32,2176]{1,0:T(8,128)(2,1)S(1)}, u32[]{:S(2)}, u32[]{:S(2)}) collective-permute-start(bf16[32,2176]{1,0:T(8,128)(2,1)S(1)} %get-tuple-element.50), channel_id=1, source_target_pairs={{0,7},{1,0},{2,1},{3,2},{4,3},{5,4},{6,5},{7,6},{8,15},{9,8},{10,9... | collective-permute-start | bytes 417800 | tf_op jit(solution)/shard_map/ppermute | solution.py:509
  30.3 20.4 %collective-permute-start.2 = (bf16[32,2176]{1,0:T(8,128)(2,1)S(1)}, bf16[32,2176]{1,0:T(8,128)(2,1)S(1)}, u32[]{:S(2)}, u32[]{:S(2)}) collective-permute-start(bf16[32,2176]{1,0:T(8,128)(2,1)S(1)} %get-tuple-element.51), channel_id=1, source_target_pairs={{0,4},{1,5},{2,6},{3,7},{4,0},{5,1},{6,2},{7,3},{8,12},{9,13},{10,... | collective-permute-start | bytes 417800 | tf_op jit(solution)/shard_map/ppermute | solution.py:509
  37.3 14.9 %collective-permute-start.3 = (bf16[32,2176]{1,0:T(8,128)(2,1)S(1)}, bf16[32,2176]{1,0:T(8,128)(2,1)S(1)}, u32[]{:S(2)}, u32[]{:S(2)}) collective-permute-start(bf16[32,2176]{1,0:T(8,128)(2,1)S(1)} %get-tuple-element.52), channel_id=1, source_target_pairs={{0,5},{1,6},{2,7},{3,0},{4,1},{5,2},{6,3},{7,4},{8,13},{9,14},{10,... | collective-permute-start | bytes 417800 | tf_op jit(solution)/shard_map/ppermute | solution.py:509
  39.2 14.6 %collective-permute-start.4 = (bf16[32,2176]{1,0:T(8,128)(2,1)S(1)}, bf16[32,2176]{1,0:T(8,128)(2,1)S(1)}, u32[]{:S(2)}, u32[]{:S(2)}) collective-permute-start(bf16[32,2176]{1,0:T(8,128)(2,1)S(1)} %get-tuple-element.53), channel_id=1, source_target_pairs={{0,3},{1,4},{2,5},{3,6},{4,7},{5,0},{6,1},{7,2},{8,11},{9,12},{10,... | collective-permute-start | bytes 417800 | tf_op jit(solution)/shard_map/ppermute | solution.py:509
  44.4 14.4 %collective-permute-start.5 = (bf16[32,2176]{1,0:T(8,128)(2,1)S(1)}, bf16[32,2176]{1,0:T(8,128)(2,1)S(1)}, u32[]{:S(2)}, u32[]{:S(2)}) collective-permute-start(bf16[32,2176]{1,0:T(8,128)(2,1)S(1)} %get-tuple-element.54), channel_id=1, source_target_pairs={{0,6},{1,7},{2,0},{3,1},{4,2},{5,3},{6,4},{7,5},{8,14},{9,15},{10,... | collective-permute-start | bytes 417800 | tf_op jit(solution)/shard_map/ppermute | solution.py:509
  46.3 29.8 %copy-start.2 = (bf16[64,4096]{1,0:T(8,128)(2,1)S(1)}, bf16[64,4096]{1,0:T(8,128)(2,1)}, u32[]{:S(2)}) copy-start(bf16[64,4096]{1,0:T(8,128)(2,1)} %copy-done.1) | copy-start | bytes 1572868
  46.4 29.8 %copy-start.3 = (s32[64]{0:T(128)S(1)}, s32[64]{0:T(128)}, u32[]{:S(2)}) copy-start(s32[64]{0:T(128)} %param.16) | copy-start | bytes 772
  46.4 12.4 %collective-permute-start.6 = (bf16[32,2176]{1,0:T(8,128)(2,1)S(1)}, bf16[32,2176]{1,0:T(8,128)(2,1)S(1)}, u32[]{:S(2)}, u32[]{:S(2)}) collective-permute-start(bf16[32,2176]{1,0:T(8,128)(2,1)S(1)} %get-tuple-element.55), channel_id=1, source_target_pairs={{0,2},{1,3},{2,4},{3,5},{4,6},{5,7},{6,0},{7,1},{8,10},{9,11},{10,... | collective-permute-start | bytes 417800 | tf_op jit(solution)/shard_map/ppermute | solution.py:509
  58.9 15.6 %collective-permute-start.7 = (bf16[64,2176]{1,0:T(8,128)(2,1)S(1)}, bf16[64,2176]{1,0:T(8,128)(2,1)S(1)}, u32[]{:S(2)}, u32[]{:S(2)}) collective-permute-start(bf16[64,2176]{1,0:T(8,128)(2,1)S(1)} %get-tuple-element.57), channel_id=1, source_target_pairs={{0,16},{1,17},{2,18},{3,19},{4,20},{5,21},{6,22},{7,23},{8,24},{9,... | collective-permute-start | bytes 835592 | tf_op jit(solution)/shard_map/ppermute | solution.py:519
  63.6 12.6 %collective-permute-start.8 = (bf16[64,2176]{1,0:T(8,128)(2,1)S(1)}, bf16[64,2176]{1,0:T(8,128)(2,1)S(1)}, u32[]{:S(2)}, u32[]{:S(2)}) collective-permute-start(bf16[64,2176]{1,0:T(8,128)(2,1)S(1)} %get-tuple-element.58), channel_id=1, source_target_pairs={{0,8},{1,9},{2,10},{3,11},{4,12},{5,13},{6,14},{7,15},{8,16},{9,17... | collective-permute-start | bytes 835592 | tf_op jit(solution)/shard_map/ppermute | solution.py:519
  65.8 10.4 %collective-permute-start.9 = (bf16[64,2176]{1,0:T(8,128)(2,1)S(1)}, bf16[64,2176]{1,0:T(8,128)(2,1)S(1)}, u32[]{:S(2)}, u32[]{:S(2)}) collective-permute-start(bf16[64,2176]{1,0:T(8,128)(2,1)S(1)} %get-tuple-element.59), channel_id=1, source_target_pairs={{0,24},{1,25},{2,26},{3,27},{4,28},{5,29},{6,30},{7,31},{8,0},{9,1... | collective-permute-start | bytes 835592 | tf_op jit(solution)/shard_map/ppermute | solution.py:519
  81.9 19.2 %all-to-all-start.1 = ((bf16[24,8,128]{2,1,0:T(8,128)(2,1)}), bf16[24,8,128]{2,1,0:T(8,128)(2,1)S(1)}, u32[]{:S(2)}, u32[]{:S(2)}) async-start(bf16[24,8,128]{2,1,0:T(8,128)(2,1)} %bitcast.10), calls=%async_computation.1 | async-start | bytes 98304 | tf_op jit(solution)/shard_map/all_to_all | solution.py:489
  103.3 3.8 %collective-permute-start.10 = (bf16[32,64,128]{2,1,0:T(8,128)(2,1)S(1)}, bf16[32,64,128]{2,1,0:T(8,128)(2,1)S(1)}, u32[]{:S(2)}, u32[]{:S(2)}) collective-permute-start(bf16[32,64,128]{2,1,0:T(8,128)(2,1)S(1)} %get-tuple-element.80), channel_id=1, source_target_pairs={{0,32},{32,0},{64,96},{96,64},{128,160},{160,128},{192,224},{224,1... | collective-permute-start | bytes 1572872 | tf_op jit(solution)/shard_map/ppermute | solution.py:688
  165.5 11.8 %collective-permute-start.11 = (bf16[32,72,128]{2,1,0:T(8,128)(2,1)S(1)}, bf16[32,72,128]{2,1,0:T(8,128)(2,1)S(1)}, u32[]{:S(2)}, u32[]{:S(2)}) collective-permute-start(bf16[32,72,128]{2,1,0:T(8,128)(2,1)S(1)} %all_to_all.21.refs_1_), channel_id=1, source_target_pairs={{0,32},{32,0},{64,96},{96,64},{128,160},{160,128},{192,224},{224,1... | collective-permute-start | bytes 1769480 | tf_op jit(solution)/shard_map/ppermute | solution.py:698

commit v9 on v8

--- a/solution.py
+++ b/solution.py
@@ -59,7 +59,8 @@
     ext = jnp.where(lane == rank, high, ext)
     ext = jnp.where(lane == rank + 1, inverse - high, ext)
     ext_ref[...] = ext.astype(bf16)
-    inv_ref[...] = jnp.broadcast_to(inverse, inv_ref.shape)
+    if inv_ref is not None:
+        inv_ref[...] = jnp.broadcast_to(inverse, inv_ref.shape)
 
 
 def fetch(pairs, sems):
@@ -80,7 +81,7 @@
 
 def passage_kernel(
     x_hbm, base_hbm, down_hbm, up_hbm, near_ids_hbm,
-    near_hbm, unit_ref, ext_ref, inv_ref, pick_ref,
+    near_hbm, unit_ref, ext_ref, pick_ref,
     x_ref, base_ref, down_ref, up_ref, near_ids_ref, raw_ref, near_ref, sems, out_sems,
 ):
     pairs = [
@@ -107,7 +108,7 @@
         copies[3].wait()
         copies[4].wait()
 
-    embed(x_ref, base_ref, down_ref, up_ref, unit_ref, ext_ref, inv_ref, raw_ref, ready)
+    embed(x_ref, base_ref, down_ref, up_ref, unit_ref, ext_ref, None, raw_ref, ready)
     near_ref[:, width:] = dot(pick, ext_ref[...]).astype(bf16)
     sent = []
     for i, cols in enumerate([slice(width, width + lanes), *column_tiles(width)]):
@@ -218,7 +219,7 @@
     order = far_order(count)
     far_refs = [refs[order.index(dx)] for dx in range(count)]
     pair_ref, unit_ref, p_ext_ref, positive_ref = refs[count : count + 4]
-    o_ref, ext_ref, x_far_ref, both_ref = refs[count + 4 :]
+    o_ref, ext_ref, x_far_ref, both_ref, p_inv_ref = refs[count + 4 :]
     rows, width = unit_ref.shape
     half = width // 2
     total = far_refs[0].shape[0]
@@ -248,6 +249,10 @@
         o_ref[n_far:, cols] = dot(own_t, unit_ref[:, cols]).astype(bf16)
     ext_ref[n_far:, :] = dot(own_t, p_ext_ref[...]).astype(bf16)
     both_ref[...] = dot(o_ref[...], pair_ref[...], 1, 1)
+    rank = pair_ref.shape[0] - rows
+    ext = p_ext_ref[...].astype(f32)
+    inverse = ext[:, rank : rank + 1] + ext[:, rank + 1 : rank + 2]
+    p_inv_ref[...] = jnp.broadcast_to(inverse, p_inv_ref.shape)
 
 
 def score_kernel(
@@ -554,13 +559,12 @@
         n_other = n_far + rows
         half = width // 2
         block = width // n_group
-        near, p_unit, p_ext, p_inv, pick = call(
+        near, p_unit, p_ext, pick = call(
             passage_kernel,
             [
                 ((n_near, width + lanes), bf16),
                 ((rows, width), bf16),
                 ((rows, lanes), bf16),
-                ((rows, lanes), f32),
                 ((n_near, rows), bf16),
             ],
             (passage_layer_input, passage_frozen_base, down_t, adapter_up_weight, near_ids),
@@ -575,7 +579,7 @@
                 pltpu.SemaphoreType.DMA((5,)),
                 pltpu.SemaphoreType.DMA((1 + len(column_tiles(width)),)),
             ],
-            flops=300_000_000, moved=5_000_000, hbm=range(5), out_hbm=(0, 3), out_raw=(0,),
+            flops=300_000_000, moved=5_000_000, hbm=range(5), out_hbm=(0,), out_raw=(0,),
         )
         far = call(
             lambda *refs: far_pick_kernel(grid_x, grid_y, *refs),
@@ -615,16 +619,17 @@
             flops=1000, moved=1000, hbm=range(1, 6), out_hbm=(1, 2, 5),
         )
         positive = positive_passage_index.reshape(1, rows)
-        other, other_ext, x_far, other_both = call(
+        other, other_ext, x_far, other_both, p_inv = call(
             lambda *refs: far_kernel(grid_x, *refs),
             [
                 ((n_other, width), bf16),
                 ((n_other, lanes), bf16),
                 ((n_far, width), bf16),
                 ((n_other, rows + rank), f32),
+                ((rows, lanes), f32),
             ],
             (*far, q_pair, p_unit, p_ext, positive),
-            flops=1000, moved=1000, out_hbm=range(4),
+            flops=1000, moved=1000, out_hbm=range(5),
         )
         ret, weights, radial, near_up = call(
             lambda *refs: score_kernel(slope, rank, *refs),
@@ -687,10 +692,12 @@
         )
         got = lax.ppermute(send, "dp", swap)
         (sums,) = call(add_kernel, [((n_group, rank, block), bf16)], (keep, got), moved=2_500_000)
-        cores = [list(range(c, n_dp, 2)) for c in range(2)]
+        cores = [ring[c::2] for c in range(2)]
         sums = exchange(sums, "group", [plane])
-        (sums,) = call(spread_kernel, [((1, rank, block), bf16)], (sums,), moved=1_000_000)
-        sums = lax.all_gather(sums, "dp", axis=0, tiled=True, axis_index_groups=cores)
+        (sums,) = call(
+            spread_kernel, [((n_dp // 2, rank, block), bf16)], (sums,), moved=1_000_000
+        )
+        sums = exchange(sums, "dp", cores)
         (sums,) = call(
             finish_kernel, [((n_group, rank + 8, block), bf16)], (sums, loss), moved=1_000_000
         )

time: 180 us -> 178 us (0.989)
    all_to_all x2 -> x3, blocking collectives: 42.1 us -> 58.3 us  [exchange(): lax.all_to_all(x, axis, split_axis=0, concat_axis=0, tiled=True, axis_ind...]
    all_gather x1 -> x0, blocking collectives: 16.1 us -> none  [body(): lax.all_gather(sums, 'dp', axis=0, tiled=True, axis_index_groups=cores)]
where the time goes in v9:
time: 178 us; the launch traced here: 177 us
  starting transfers between devices  75.3 us (42%)
  blocking collectives  58.3 us (33%)
  Pallas kernels  23 us (13%)
  waiting for transfers between devices  19.8 us (11%)
    all_to_all x3, blocking collectives, exchange(): lax.all_to_all(x, axis, split_axis=0, concat_axis=0, tiled=True, axis_ind...  58.3 us
    ppermute x7, starting transfers between devices, far_exchange(): got.append(lax.ppermute(pieces[dy], 'group', pairs))  27.4 us
    all_to_all x2, starting transfers between devices, exchange(): lax.all_to_all(x, axis, split_axis=0, concat_axis=0, tiled=True, axis_ind...  25.8 us
    pallas_call x12, Pallas kernels, call(): pl.pallas_call(kernel, out_shape=shapes, in_specs=specs, out_specs=[pl.Bl...  23 us
    ppermute x3, starting transfers between devices, far_exchange(): ended.append(lax.ppermute(lines[dx], 'group', pairs))  11.1 us
    ppermute x1, starting transfers between devices, body(): other_sums = lax.ppermute(sums, 'dp', swap)  8.74 us
    ppermute x7, waiting for transfers between devices, far_exchange(): got.append(lax.ppermute(pieces[dy], 'group', pairs))  7.99 us
    all_to_all x2, waiting for transfers between devices, exchange(): lax.all_to_all(x, axis, split_axis=0, concat_axis=0, tiled=True, axis_ind...  7.03 us
  transfers between devices with their start and end apart: 14, of which 8 were waited for; matrix products, arithmetic and copies ran while one was open for 0% of the time, Pallas kernels for 7%

profile of v9, /device:TPU:1, one launch (start us, length us, event | category | flops | bytes accessed | tf_op | source)
XLA Modules:
  0.0 177.4 jit_solution(820113476692612555)
XLA Ops:
  0.6 3.8 %shard_map.121 = (bf16[192,4224]{1,0:T(8,128)(2,1)}, bf16[64,4096]{1,0:T(8,128)(2,1)S(1)}, bf16[64,128]{1,0:T(8,128)(2,1)S(1)}, bf16[192,64]{1,0:T(8,128)(2,1)S(1)}) custom-call(bf16[64,4096]{1,0:T(8,128)(2,1)} %refs_4_.3, bf16[64,4096]{1,0:T(8,128)(2,1)} %base_hbm.1, bf16[64,4096]{1,0:T(8,128)(2,1)} %bitcast.20, bf16[64,4096]{1,0:T(8,128)(2,1)} %refs_4_.2, ...), custom_call_target="tpu_custom_call" | custom-call | flops 300000000 | bytes 5000000 | tf_op jit(solution)/shard_map/pallas_call | solution.py:479
  4.4 0.0 copy-start.1
  4.4 0.0 copy-start
  4.4 0.0 copy-start.4
  4.4 16.8 %all-to-all-start = ((bf16[24,8,4224]{2,1,0:T(8,128)(2,1)}), bf16[24,8,4224]{2,1,0:T(8,128)(2,1)S(1)}, u32[]{:S(2)}, u32[]{:S(2)}) async-start(bf16[24,8,4224]{2,1,0:T(8,128)(2,1)} %bitcast.22), calls=%async_computation | async-start | bytes 3244032 | tf_op jit(solution)/shard_map/all_to_all | solution.py:494
  21.3 0.1 pad_add_fusion.refs_0_.place_ref
  21.4 1.3 shard_map.123
  22.7 3.2 %collective-permute-start = (bf16[32,2176]{1,0:T(8,128)(2,1)S(1)}, bf16[32,2176]{1,0:T(8,128)(2,1)S(1)}, u32[]{:S(2)}, u32[]{:S(2)}) collective-permute-start(bf16[32,2176]{1,0:T(8,128)(2,1)S(1)} %get-tuple-element.49), channel_id=1, source_target_pairs={{0,1},{1,2},{2,3},{3,4},{4,5},{5,6},{6,7},{7,0},{8,9},{9,10},{10,1... | collective-permute-start | bytes 417800 | tf_op jit(solution)/shard_map/ppermute | solution.py:514
  25.9 3.8 %collective-permute-start.1 = (bf16[32,2176]{1,0:T(8,128)(2,1)S(1)}, bf16[32,2176]{1,0:T(8,128)(2,1)S(1)}, u32[]{:S(2)}, u32[]{:S(2)}) collective-permute-start(bf16[32,2176]{1,0:T(8,128)(2,1)S(1)} %get-tuple-element.50), channel_id=1, source_target_pairs={{0,7},{1,0},{2,1},{3,2},{4,3},{5,4},{6,5},{7,6},{8,15},{9,8},{10,9... | collective-permute-start | bytes 417800 | tf_op jit(solution)/shard_map/ppermute | solution.py:514
  29.7 6.9 %collective-permute-start.2 = (bf16[32,2176]{1,0:T(8,128)(2,1)S(1)}, bf16[32,2176]{1,0:T(8,128)(2,1)S(1)}, u32[]{:S(2)}, u32[]{:S(2)}) collective-permute-start(bf16[32,2176]{1,0:T(8,128)(2,1)S(1)} %get-tuple-element.51), channel_id=1, source_target_pairs={{0,4},{1,5},{2,6},{3,7},{4,0},{5,1},{6,2},{7,3},{8,12},{9,13},{10,... | collective-permute-start | bytes 417800 | tf_op jit(solution)/shard_map/ppermute | solution.py:514
  36.7 1.9 %collective-permute-start.3 = (bf16[32,2176]{1,0:T(8,128)(2,1)S(1)}, bf16[32,2176]{1,0:T(8,128)(2,1)S(1)}, u32[]{:S(2)}, u32[]{:S(2)}) collective-permute-start(bf16[32,2176]{1,0:T(8,128)(2,1)S(1)} %get-tuple-element.52), channel_id=1, source_target_pairs={{0,5},{1,6},{2,7},{3,0},{4,1},{5,2},{6,3},{7,4},{8,13},{9,14},{10,... | collective-permute-start | bytes 417800 | tf_op jit(solution)/shard_map/ppermute | solution.py:514
  38.6 5.2 %collective-permute-start.4 = (bf16[32,2176]{1,0:T(8,128)(2,1)S(1)}, bf16[32,2176]{1,0:T(8,128)(2,1)S(1)}, u32[]{:S(2)}, u32[]{:S(2)}) collective-permute-start(bf16[32,2176]{1,0:T(8,128)(2,1)S(1)} %get-tuple-element.53), channel_id=1, source_target_pairs={{0,3},{1,4},{2,5},{3,6},{4,7},{5,0},{6,1},{7,2},{8,11},{9,12},{10,... | collective-permute-start | bytes 417800 | tf_op jit(solution)/shard_map/ppermute | solution.py:514
  43.8 0.0 collective-permute-done.refs_1_
  43.8 2.0 %collective-permute-start.5 = (bf16[32,2176]{1,0:T(8,128)(2,1)S(1)}, bf16[32,2176]{1,0:T(8,128)(2,1)S(1)}, u32[]{:S(2)}, u32[]{:S(2)}) collective-permute-start(bf16[32,2176]{1,0:T(8,128)(2,1)S(1)} %get-tuple-element.54), channel_id=1, source_target_pairs={{0,6},{1,7},{2,0},{3,1},{4,2},{5,3},{6,4},{7,5},{8,14},{9,15},{10,... | collective-permute-start | bytes 417800 | tf_op jit(solution)/shard_map/ppermute | solution.py:514
  45.7 0.0 collective-permute-done.1.refs_2_
  45.7 0.0 copy-start.2
  45.7 0.0 copy-start.3
  45.8 4.4 %collective-permute-start.6 = (bf16[32,2176]{1,0:T(8,128)(2,1)S(1)}, bf16[32,2176]{1,0:T(8,128)(2,1)S(1)}, u32[]{:S(2)}, u32[]{:S(2)}) collective-permute-start(bf16[32,2176]{1,0:T(8,128)(2,1)S(1)} %get-tuple-element.55), channel_id=1, source_target_pairs={{0,2},{1,3},{2,4},{3,5},{4,6},{5,7},{6,0},{7,1},{8,10},{9,11},{10,... | collective-permute-start | bytes 417800 | tf_op jit(solution)/shard_map/ppermute | solution.py:514
  50.1 0.0 collective-permute-done.2.refs_3_
  50.1 1.4 collective-permute-done.3.refs_4_
  51.6 1.6 collective-permute-done.4.refs_5_
  53.2 4.9 %collective-permute-done.5.refs_6_ = bf16[32,2176]{1,0:T(8,128)(2,1)S(1)} collective-permute-done((bf16[32,2176]{1,0:T(8,128)(2,1)S(1)}, bf16[32,2176]{1,0:T(8,128)(2,1)S(1)}, u32[]{:S(2)}, u32[]{:S(2)}) %collective-permute-start.5) | collective-permute-done | bytes 139296 | tf_op jit(solution)/shard_map/ppermute | solution.py:514
  58.1 0.0 collective-permute-done.6.refs_7_
  58.1 0.2 shard_map.124
  58.3 4.7 %collective-permute-start.7 = (bf16[64,2176]{1,0:T(8,128)(2,1)S(1)}, bf16[64,2176]{1,0:T(8,128)(2,1)S(1)}, u32[]{:S(2)}, u32[]{:S(2)}) collective-permute-start(bf16[64,2176]{1,0:T(8,128)(2,1)S(1)} %get-tuple-element.57), channel_id=1, source_target_pairs={{0,16},{1,17},{2,18},{3,19},{4,20},{5,21},{6,22},{7,23},{8,24},{9,... | collective-permute-start | bytes 835592 | tf_op jit(solution)/shard_map/ppermute | solution.py:524
  62.9 2.2 %collective-permute-start.8 = (bf16[64,2176]{1,0:T(8,128)(2,1)S(1)}, bf16[64,2176]{1,0:T(8,128)(2,1)S(1)}, u32[]{:S(2)}, u32[]{:S(2)}) collective-permute-start(bf16[64,2176]{1,0:T(8,128)(2,1)S(1)} %get-tuple-element.58), channel_id=1, source_target_pairs={{0,8},{1,9},{2,10},{3,11},{4,12},{5,13},{6,14},{7,15},{8,16},{9,17... | collective-permute-start | bytes 835592 | tf_op jit(solution)/shard_map/ppermute | solution.py:524
  65.2 4.3 %collective-permute-start.9 = (bf16[64,2176]{1,0:T(8,128)(2,1)S(1)}, bf16[64,2176]{1,0:T(8,128)(2,1)S(1)}, u32[]{:S(2)}, u32[]{:S(2)}) collective-permute-start(bf16[64,2176]{1,0:T(8,128)(2,1)S(1)} %get-tuple-element.59), channel_id=1, source_target_pairs={{0,24},{1,25},{2,26},{3,27},{4,28},{5,29},{6,30},{7,31},{8,0},{9,1... | collective-permute-start | bytes 835592 | tf_op jit(solution)/shard_map/ppermute | solution.py:524
  69.5 4.5 %shard_map.122 = (bf16[128,4096]{1,0:T(8,128)(2,1)S(1)}, bf16[64,128]{1,0:T(8,128)(2,1)}, f32[64,128]{1,0:T(8,128)}, f32[192,64]{1,0:T(8,128)S(1)}, f32[128,64]{1,0:T(8,128)S(1)}, /*index=5*/bf16[128,64]{1,0:T(8,128)(2,1)}) custom-call(s32[3]{0:T(128)S(1)} %pad_add_fusion.refs_0_.place_ref, bf16[64,4096]{1,0:T(8,128)(2,1)} %x_q_hbm.1, ...), custom_call_target="tpu_custom_call" | custom-call | flops 1000 | bytes 1000 | tf_op jit(solution)/shard_map/pallas_call | solution.py:479
  73.9 1.6 collective-permute-done.8.refs_2_
  75.5 0.0 collective-permute-done.9.refs_3_
  75.6 2.0 %shard_map.125 = (bf16[128,4096]{1,0:T(8,128)(2,1)}, bf16[128,128]{1,0:T(8,128)(2,1)}, bf16[64,4096]{1,0:T(8,128)(2,1)}, f32[128,128]{1,0:T(8,128)}, f32[64,128]{1,0:T(8,128)}) custom-call(bf16[64,2176]{1,0:T(8,128)(2,1)S(1)} %get-tuple-element.56.refs_0_, bf16[64,2176]{1,0:T(8,128)(2,1)S(1)} %collective-permute-done.7.refs_1_, ...), custom_call_target="tpu_custom_call" | custom-call | flops 1000 | bytes 1000 | tf_op jit(solution)/shard_map/pallas_call | solution.py:479
  77.5 1.6 all-to-all-done
  79.2 2.2 %shard_map.126 = (bf16[192,128]{1,0:T(8,128)(2,1)}, bf16[320,64]{1,0:T(8,128)(2,1)}, f32[384,1]{1,0:T(8,128)}, f32[192,64]{1,0:T(8,128)}) custom-call(bf16[192,4224]{1,0:T(8,128)(2,1)S(1)} %bitcast.14, bf16[128,4096]{1,0:T(8,128)(2,1)S(1)} %get-tuple-element.45.refs_4_.refs_1_.pair_ref, f32[128,128]{1,0:T(8,128)} %get-tuple-element.60.refs_2_.other_both_hbm, ...), custom_call_target="tpu_custom_call" | custom-call | flops 200000000 | bytes 3000000 | tf_op jit(solution)/shard_map/pallas_call | solution.py:479
  81.3 9.0 %all-to-all-start.1 = ((bf16[24,8,128]{2,1,0:T(8,128)(2,1)}), bf16[24,8,128]{2,1,0:T(8,128)(2,1)S(1)}, u32[]{:S(2)}, u32[]{:S(2)}) async-start(bf16[24,8,128]{2,1,0:T(8,128)(2,1)} %bitcast.10), calls=%async_computation.1 | async-start | bytes 98304 | tf_op jit(solution)/shard_map/all_to_all | solution.py:494
  90.3 5.0 %shard_map.127 = (f32[32,32,128]{2,1,0:T(8,128)}, bf16[32,32,128]{2,1,0:T(8,128)(2,1)}, f32[64,4096]{1,0:T(8,128)}, f32[64,128]{1,0:T(8,128)}) custom-call(s32[3]{0:T(128)S(1)} %pad_add_fusion.refs_0_.place_ref, bf16[192,4224]{1,0:T(8,128)(2,1)S(1)} %bitcast.15, bf16[128,4096]{1,0:T(8,128)(2,1)S(1)} %get-tuple-element.45.refs_4_.refs_1_.pair_ref, ...), custom_call_target="tpu_custom_call" | custom-call | flops 900000000 | bytes 9000000 | tf_op jit(solution)/shard_map/pallas_call | solution.py:479
  95.3 5.4 %all-to-all-done.1 = bf16[24,8,128]{2,1,0:T(8,128)(2,1)S(1)} async-done(((bf16[24,8,128]{2,1,0:T(8,128)(2,1)}), bf16[24,8,128]{2,1,0:T(8,128)(2,1)S(1)}, u32[]{:S(2)}, u32[]{:S(2)}) %all-to-all-start.1) | async-done | bytes 49184 | tf_op jit(solution)/shard_map/all_to_all | solution.py:494
  100.7 2.1 %shard_map.128 = (f32[32,64,128]{2,1,0:T(8,128)S(1)}, bf16[32,64,128]{2,1,0:T(8,128)(2,1)S(1)}, f32[8,128]{1,0:T(8,128)S(1)}) custom-call(s32[3]{0:T(128)S(1)} %pad_add_fusion.refs_0_.place_ref, bf16[192,128]{1,0:T(8,128)(2,1)S(1)} %bitcast.16, bf16[192,64]{1,0:T(8,128)(2,1)S(1)} %get-tuple-element.65.refs_2_, f32[64,128]{1,0:T(8,128)} %get-tuple-element.75.refs_3_, ...), custom_call_target="tpu_custom_call" | custom-call | flops 100000000 | bytes 3000000 | tf_op jit(solution)/shard_map/pallas_call | solution.py:479
  102.8 2.3 %collective-permute-start.10 = (bf16[32,64,128]{2,1,0:T(8,128)(2,1)S(1)}, bf16[32,64,128]{2,1,0:T(8,128)(2,1)S(1)}, u32[]{:S(2)}, u32[]{:S(2)}) collective-permute-start(bf16[32,64,128]{2,1,0:T(8,128)(2,1)S(1)} %get-tuple-element.80), channel_id=1, source_target_pairs={{0,32},{32,0},{64,96},{96,64},{128,160},{160,128},{192,224},{224,1... | collective-permute-start | bytes 1572872 | tf_op jit(solution)/shard_map/ppermute | solution.py:693
  105.1 1.5 collective-permute-done.10.got_ref
  106.6 0.1 shard_map.129
  106.7 23.2 %all_to_all.25.in_ref = bf16[32,64,128]{2,1,0:T(8,128)(2,1)S(1)} all-to-all(bf16[32,64,128]{2,1,0:T(8,128)(2,1)S(1)} %shard_map.129), channel_id=1, replica_groups={{0,3,6,1,4,7,2,5,8,11,14,9,12,15,10,13,16,19,22,17,20,23,18,21,24,27,30..., dimensions={0} | all-to-all | bytes 1048576 | tf_op jit(solution)/shard_map/all_to_all | solution.py:494
  129.9 0.1 shard_map.130
  130.0 15.3 %all_to_all.26.in_ref = bf16[12,64,128]{2,1,0:T(8,128)(2,1)S(1)} all-to-all(bf16[12,64,128]{2,1,0:T(8,128)(2,1)S(1)} %shard_map.130), channel_id=1, replica_groups={{0,320,640,192,512,64,384,704,256,576,128,448},{32,352,672,224,544,96,4..., dimensions={0} | all-to-all | bytes 393216 | tf_op jit(solution)/shard_map/all_to_all | solution.py:494
  145.3 0.1 shard_map.131
  145.4 19.7 %all_to_all.27.refs_1_ = bf16[32,72,128]{2,1,0:T(8,128)(2,1)S(1)} all-to-all(bf16[32,72,128]{2,1,0:T(8,128)(2,1)S(1)} %shard_map.131), channel_id=1, replica_groups={{0,3,6,1,4,7,2,5,8,11,14,9,12,15,10,13,16,19,22,17,20,23,18,21,24,27,30..., dimensions={0} | all-to-all | bytes 1179648 | tf_op jit(solution)/shard_map/all_to_all | solution.py:494
  165.1 8.7 %collective-permute-start.11 = (bf16[32,72,128]{2,1,0:T(8,128)(2,1)S(1)}, bf16[32,72,128]{2,1,0:T(8,128)(2,1)S(1)}, u32[]{:S(2)}, u32[]{:S(2)}) collective-permute-start(bf16[32,72,128]{2,1,0:T(8,128)(2,1)S(1)} %all_to_all.27.refs_1_), channel_id=1, source_target_pairs={{0,32},{32,0},{64,96},{96,64},{128,160},{160,128},{192,224},{224,1... | collective-permute-start | bytes 1769480 | tf_op jit(solution)/shard_map/ppermute | solution.py:705
  173.9 1.6 collective-permute-done.11.refs_2_
  175.5 1.9 %shard_map.132 = (f32[64,4096]{1,0:T(8,128)}, f32[64,4096]{1,0:T(8,128)}, f32[1,1]{1,0:T(1,128)}) custom-call(s32[3]{0:T(128)S(1)} %pad_add_fusion.refs_0_.place_ref, bf16[32,72,128]{2,1,0:T(8,128)(2,1)S(1)} %all_to_all.27.refs_1_, bf16[32,72,128]{2,1,0:T(8,128)(2,1)S(1)} %collective-permute-done.11.refs_2_), custom_call_target="tpu_custom_call" | custom-call | bytes 3500000 | tf_op jit(solution)/shard_map/pallas_call | solution.py:479
  (6 shorter events, 0.0 us)
Async XLA Ops:
  4.4 17.0 %copy-start.1 = (bf16[64,4096]{1,0:T(8,128)(2,1)}, bf16[64,4096]{1,0:T(8,128)(2,1)S(1)}, u32[]{:S(2)}) copy-start(bf16[64,4096]{1,0:T(8,128)(2,1)S(1)} %get-tuple-element.46.refs_2_.refs_5_) | copy-start | bytes 1572868
  4.4 17.0 %copy-start = (bf16[64,4096]{1,0:T(8,128)(2,1)S(1)}, bf16[64,4096]{1,0:T(8,128)(2,1)}, u32[]{:S(2)}) copy-start(bf16[64,4096]{1,0:T(8,128)(2,1)} %refs_4_.3) | copy-start | bytes 1572868
  4.4 17.0 %copy-start.4 = (s32[32,2]{0,1:T(2,128)S(1)}, s32[32,2]{0,1:T(2,128)}, u32[]{:S(2)}) copy-start(s32[32,2]{0,1:T(2,128)} %param.19) | copy-start | bytes 772
  4.4 74.7 %all-to-all-start = ((bf16[24,8,4224]{2,1,0:T(8,128)(2,1)}), bf16[24,8,4224]{2,1,0:T(8,128)(2,1)S(1)}, u32[]{:S(2)}, u32[]{:S(2)}) async-start(bf16[24,8,4224]{2,1,0:T(8,128)(2,1)} %bitcast.22), calls=%async_computation | async-start | bytes 3244032 | tf_op jit(solution)/shard_map/all_to_all | solution.py:494
  22.7 21.1 %collective-permute-start = (bf16[32,2176]{1,0:T(8,128)(2,1)S(1)}, bf16[32,2176]{1,0:T(8,128)(2,1)S(1)}, u32[]{:S(2)}, u32[]{:S(2)}) collective-permute-start(bf16[32,2176]{1,0:T(8,128)(2,1)S(1)} %get-tuple-element.49), channel_id=1, source_target_pairs={{0,1},{1,2},{2,3},{3,4},{4,5},{5,6},{6,7},{7,0},{8,9},{9,10},{10,1... | collective-permute-start | bytes 417800 | tf_op jit(solution)/shard_map/ppermute | solution.py:514
  25.9 19.8 %collective-permute-start.1 = (bf16[32,2176]{1,0:T(8,128)(2,1)S(1)}, bf16[32,2176]{1,0:T(8,128)(2,1)S(1)}, u32[]{:S(2)}, u32[]{:S(2)}) collective-permute-start(bf16[32,2176]{1,0:T(8,128)(2,1)S(1)} %get-tuple-element.50), channel_id=1, source_target_pairs={{0,7},{1,0},{2,1},{3,2},{4,3},{5,4},{6,5},{7,6},{8,15},{9,8},{10,9... | collective-permute-start | bytes 417800 | tf_op jit(solution)/shard_map/ppermute | solution.py:514
  29.7 20.4 %collective-permute-start.2 = (bf16[32,2176]{1,0:T(8,128)(2,1)S(1)}, bf16[32,2176]{1,0:T(8,128)(2,1)S(1)}, u32[]{:S(2)}, u32[]{:S(2)}) collective-permute-start(bf16[32,2176]{1,0:T(8,128)(2,1)S(1)} %get-tuple-element.51), channel_id=1, source_target_pairs={{0,4},{1,5},{2,6},{3,7},{4,0},{5,1},{6,2},{7,3},{8,12},{9,13},{10,... | collective-permute-start | bytes 417800 | tf_op jit(solution)/shard_map/ppermute | solution.py:514
  36.7 14.9 %collective-permute-start.3 = (bf16[32,2176]{1,0:T(8,128)(2,1)S(1)}, bf16[32,2176]{1,0:T(8,128)(2,1)S(1)}, u32[]{:S(2)}, u32[]{:S(2)}) collective-permute-start(bf16[32,2176]{1,0:T(8,128)(2,1)S(1)} %get-tuple-element.52), channel_id=1, source_target_pairs={{0,5},{1,6},{2,7},{3,0},{4,1},{5,2},{6,3},{7,4},{8,13},{9,14},{10,... | collective-permute-start | bytes 417800 | tf_op jit(solution)/shard_map/ppermute | solution.py:514
  38.6 14.6 %collective-permute-start.4 = (bf16[32,2176]{1,0:T(8,128)(2,1)S(1)}, bf16[32,2176]{1,0:T(8,128)(2,1)S(1)}, u32[]{:S(2)}, u32[]{:S(2)}) collective-permute-start(bf16[32,2176]{1,0:T(8,128)(2,1)S(1)} %get-tuple-element.53), channel_id=1, source_target_pairs={{0,3},{1,4},{2,5},{3,6},{4,7},{5,0},{6,1},{7,2},{8,11},{9,12},{10,... | collective-permute-start | bytes 417800 | tf_op jit(solution)/shard_map/ppermute | solution.py:514
  43.8 14.4 %collective-permute-start.5 = (bf16[32,2176]{1,0:T(8,128)(2,1)S(1)}, bf16[32,2176]{1,0:T(8,128)(2,1)S(1)}, u32[]{:S(2)}, u32[]{:S(2)}) collective-permute-start(bf16[32,2176]{1,0:T(8,128)(2,1)S(1)} %get-tuple-element.54), channel_id=1, source_target_pairs={{0,6},{1,7},{2,0},{3,1},{4,2},{5,3},{6,4},{7,5},{8,14},{9,15},{10,... | collective-permute-start | bytes 417800 | tf_op jit(solution)/shard_map/ppermute | solution.py:514
  45.7 29.8 %copy-start.2 = (bf16[64,4096]{1,0:T(8,128)(2,1)S(1)}, bf16[64,4096]{1,0:T(8,128)(2,1)}, u32[]{:S(2)}) copy-start(bf16[64,4096]{1,0:T(8,128)(2,1)} %copy-done.1) | copy-start | bytes 1572868
  45.7 29.8 %copy-start.3 = (s32[64]{0:T(128)S(1)}, s32[64]{0:T(128)}, u32[]{:S(2)}) copy-start(s32[64]{0:T(128)} %param.16) | copy-start | bytes 772
  45.8 12.4 %collective-permute-start.6 = (bf16[32,2176]{1,0:T(8,128)(2,1)S(1)}, bf16[32,2176]{1,0:T(8,128)(2,1)S(1)}, u32[]{:S(2)}, u32[]{:S(2)}) collective-permute-start(bf16[32,2176]{1,0:T(8,128)(2,1)S(1)} %get-tuple-element.55), channel_id=1, source_target_pairs={{0,2},{1,3},{2,4},{3,5},{4,6},{5,7},{6,0},{7,1},{8,10},{9,11},{10,... | collective-permute-start | bytes 417800 | tf_op jit(solution)/shard_map/ppermute | solution.py:514
  58.3 15.7 %collective-permute-start.7 = (bf16[64,2176]{1,0:T(8,128)(2,1)S(1)}, bf16[64,2176]{1,0:T(8,128)(2,1)S(1)}, u32[]{:S(2)}, u32[]{:S(2)}) collective-permute-start(bf16[64,2176]{1,0:T(8,128)(2,1)S(1)} %get-tuple-element.57), channel_id=1, source_target_pairs={{0,16},{1,17},{2,18},{3,19},{4,20},{5,21},{6,22},{7,23},{8,24},{9,... | collective-permute-start | bytes 835592 | tf_op jit(solution)/shard_map/ppermute | solution.py:524
  62.9 12.6 %collective-permute-start.8 = (bf16[64,2176]{1,0:T(8,128)(2,1)S(1)}, bf16[64,2176]{1,0:T(8,128)(2,1)S(1)}, u32[]{:S(2)}, u32[]{:S(2)}) collective-permute-start(bf16[64,2176]{1,0:T(8,128)(2,1)S(1)} %get-tuple-element.58), channel_id=1, source_target_pairs={{0,8},{1,9},{2,10},{3,11},{4,12},{5,13},{6,14},{7,15},{8,16},{9,17... | collective-permute-start | bytes 835592 | tf_op jit(solution)/shard_map/ppermute | solution.py:524
  65.2 10.4 %collective-permute-start.9 = (bf16[64,2176]{1,0:T(8,128)(2,1)S(1)}, bf16[64,2176]{1,0:T(8,128)(2,1)S(1)}, u32[]{:S(2)}, u32[]{:S(2)}) collective-permute-start(bf16[64,2176]{1,0:T(8,128)(2,1)S(1)} %get-tuple-element.59), channel_id=1, source_target_pairs={{0,24},{1,25},{2,26},{3,27},{4,28},{5,29},{6,30},{7,31},{8,0},{9,1... | collective-permute-start | bytes 835592 | tf_op jit(solution)/shard_map/ppermute | solution.py:524
  81.3 19.3 %all-to-all-start.1 = ((bf16[24,8,128]{2,1,0:T(8,128)(2,1)}), bf16[24,8,128]{2,1,0:T(8,128)(2,1)S(1)}, u32[]{:S(2)}, u32[]{:S(2)}) async-start(bf16[24,8,128]{2,1,0:T(8,128)(2,1)} %bitcast.10), calls=%async_computation.1 | async-start | bytes 98304 | tf_op jit(solution)/shard_map/all_to_all | solution.py:494
  102.8 3.8 %collective-permute-start.10 = (bf16[32,64,128]{2,1,0:T(8,128)(2,1)S(1)}, bf16[32,64,128]{2,1,0:T(8,128)(2,1)S(1)}, u32[]{:S(2)}, u32[]{:S(2)}) collective-permute-start(bf16[32,64,128]{2,1,0:T(8,128)(2,1)S(1)} %get-tuple-element.80), channel_id=1, source_target_pairs={{0,32},{32,0},{64,96},{96,64},{128,160},{160,128},{192,224},{224,1... | collective-permute-start | bytes 1572872 | tf_op jit(solution)/shard_map/ppermute | solution.py:693
  165.1 10.4 %collective-permute-start.11 = (bf16[32,72,128]{2,1,0:T(8,128)(2,1)S(1)}, bf16[32,72,128]{2,1,0:T(8,128)(2,1)S(1)}, u32[]{:S(2)}, u32[]{:S(2)}) collective-permute-start(bf16[32,72,128]{2,1,0:T(8,128)(2,1)S(1)} %all_to_all.27.refs_1_), channel_id=1, source_target_pairs={{0,32},{32,0},{64,96},{96,64},{128,160},{160,128},{192,224},{224,1... | collective-permute-start | bytes 1769480 | tf_op jit(solution)/shard_map/ppermute | solution.py:705

commit v10 on v9

--- a/solution.py
+++ b/solution.py
@@ -257,14 +257,18 @@
 
 def score_kernel(
     slope, rank, near_ref, pair_ref, other_both_hbm, near_count_ref, other_count_ref, shadow_hbm,
-    ret_ref, g_ref, radial_ref, near_up_ref, other_both_ref, shadow_ref, sems,
+    ret_ref, g_hbm, radial_hbm, near_up_hbm, other_both_ref, shadow_ref, g_ref, radial_ref,
+    near_up_ref, sems,
 ):
+    outs = [(near_up_ref, near_up_hbm), (g_ref, g_hbm), (radial_ref, radial_hbm)]
+    sent = [pltpu.make_async_copy(a, b, sems.at[2 + i]) for i, (a, b) in enumerate(outs)]
     copies = fetch([(other_both_hbm, other_both_ref), (shadow_hbm, shadow_ref)], sems)
     width = pair_ref.shape[1]
     n_near, rows = near_count_ref.shape
     both = dot(near_ref[:, :width], pair_ref[...], 1, 1)
     near_raw, near_up = both[:, 0:rows], both[:, rows:]
     near_up_ref[...] = near_up
+    sent[0].start()
     for c in copies:
         c.wait()
     other_raw = other_both_ref[:, 0:rows]
@@ -282,6 +286,7 @@
     other_g = ((other_exp / partition - same.astype(f32)) * slope).astype(bf16)
     g_ref[0:n_near, :] = near_g
     g_ref[n_near:, :] = other_g
+    sent[1].start()
     near_part = near_g.astype(f32) * near_raw
     other_part = other_g.astype(f32) * other_raw
     near_radial = jnp.sum(near_part, axis=1, keepdims=True)
@@ -294,6 +299,7 @@
     radial_ref[n_near + n_other :, :] = jnp.sum(
         jnp.where(square, q_radial, 0.0), axis=1, keepdims=True
     )
+    sent[2].start()
     back = dot(near_g, shadow_ref[0:rows, :]) + dot(near_g, shadow_ref[rows:, :])
     back = back - near_radial * near_up
     back = dot(back.astype(bf16), eye(rank, lanes))
@@ -302,6 +308,8 @@
     back = jnp.where(lane == rank, high, back)
     back = jnp.where(lane == rank + 1, loss - high, back)
     ret_ref[...] = back.astype(bf16)
+    for c in sent:
+        c.wait()
 
 
 def halves(value):
@@ -643,9 +651,12 @@
             [
                 ((n_other, rows + rank), f32),
                 (shadow.shape, bf16),
-                pltpu.SemaphoreType.DMA((2,)),
-            ],
-            flops=200_000_000, moved=3_000_000, hbm=(2, 5), out_hbm=(1, 2, 3),
+                ((n_near + n_other, rows), bf16),
+                ((n_near + n_other + rows, 1), f32),
+                ((n_near, rank), f32),
+                pltpu.SemaphoreType.DMA((5,)),
+            ],
+            flops=200_000_000, moved=3_000_000, hbm=(2, 5), out_hbm=(1, 2, 3), out_raw=(1, 2, 3),
         )
         ret = exchange(ret.reshape(n_dp, per_near, lanes), "dp", [ring]).reshape(n_near, lanes)
         up_keep, up_send, down_part, row_part = call(

time: 178 us -> 179 us (level)
  no operation moved by 1% of the time
where the time goes in v10:
time: 179 us; the launch traced here: 178 us
  starting transfers between devices  75.3 us (42%)
  blocking collectives  58.3 us (33%)
  Pallas kernels  23.6 us (13%)
  waiting for transfers between devices  19.8 us (11%)
    all_to_all x3, blocking collectives, exchange(): lax.all_to_all(x, axis, split_axis=0, concat_axis=0, tiled=True, axis_ind...  58.3 us
    ppermute x7, starting transfers between devices, far_exchange(): got.append(lax.ppermute(pieces[dy], 'group', pairs))  27.4 us
    all_to_all x2, starting transfers between devices, exchange(): lax.all_to_all(x, axis, split_axis=0, concat_axis=0, tiled=True, axis_ind...  25.8 us
    pallas_call x12, Pallas kernels, call(): pl.pallas_call(kernel, out_shape=shapes, in_specs=specs, out_specs=[pl.Bl...  23.6 us
    ppermute x3, starting transfers between devices, far_exchange(): ended.append(lax.ppermute(lines[dx], 'group', pairs))  11.1 us
    ppermute x1, starting transfers between devices, body(): other_sums = lax.ppermute(sums, 'dp', swap)  8.74 us
    ppermute x7, waiting for transfers between devices, far_exchange(): got.append(lax.ppermute(pieces[dy], 'group', pairs))  7.99 us
    all_to_all x2, waiting for transfers between devices, exchange(): lax.all_to_all(x, axis, split_axis=0, concat_axis=0, tiled=True, axis_ind...  7.03 us
  transfers between devices with their start and end apart: 14, of which 8 were waited for; matrix products, arithmetic and copies ran while one was open for 0% of the time, Pallas kernels for 7%

profile of v10, /device:TPU:1, one launch (start us, length us, event | category | flops | bytes accessed | tf_op | source)
XLA Modules:
  0.0 178.0 jit_solution(15217648198893819223)
XLA Ops:
  0.6 3.8 %shard_map.121 = (bf16[192,4224]{1,0:T(8,128)(2,1)}, bf16[64,4096]{1,0:T(8,128)(2,1)S(1)}, bf16[64,128]{1,0:T(8,128)(2,1)S(1)}, bf16[192,64]{1,0:T(8,128)(2,1)S(1)}) custom-call(bf16[64,4096]{1,0:T(8,128)(2,1)} %refs_4_.3, bf16[64,4096]{1,0:T(8,128)(2,1)} %base_hbm.1, bf16[64,4096]{1,0:T(8,128)(2,1)} %bitcast.20, bf16[64,4096]{1,0:T(8,128)(2,1)} %refs_4_.2, ...), custom_call_target="tpu_custom_call" | custom-call | flops 300000000 | bytes 5000000 | tf_op jit(solution)/shard_map/pallas_call | solution.py:487
  4.4 0.0 copy-start.1
  4.4 0.0 copy-start
  4.4 0.0 copy-start.4
  4.4 16.8 %all-to-all-start = ((bf16[24,8,4224]{2,1,0:T(8,128)(2,1)}), bf16[24,8,4224]{2,1,0:T(8,128)(2,1)S(1)}, u32[]{:S(2)}, u32[]{:S(2)}) async-start(bf16[24,8,4224]{2,1,0:T(8,128)(2,1)} %bitcast.22), calls=%async_computation | async-start | bytes 3244032 | tf_op jit(solution)/shard_map/all_to_all | solution.py:502
  21.3 0.1 pad_add_fusion.refs_0_.place_ref
  21.4 1.3 shard_map.123
  22.7 3.2 %collective-permute-start = (bf16[32,2176]{1,0:T(8,128)(2,1)S(1)}, bf16[32,2176]{1,0:T(8,128)(2,1)S(1)}, u32[]{:S(2)}, u32[]{:S(2)}) collective-permute-start(bf16[32,2176]{1,0:T(8,128)(2,1)S(1)} %get-tuple-element.49), channel_id=1, source_target_pairs={{0,1},{1,2},{2,3},{3,4},{4,5},{5,6},{6,7},{7,0},{8,9},{9,10},{10,1... | collective-permute-start | bytes 417800 | tf_op jit(solution)/shard_map/ppermute | solution.py:522
  25.9 3.8 %collective-permute-start.1 = (bf16[32,2176]{1,0:T(8,128)(2,1)S(1)}, bf16[32,2176]{1,0:T(8,128)(2,1)S(1)}, u32[]{:S(2)}, u32[]{:S(2)}) collective-permute-start(bf16[32,2176]{1,0:T(8,128)(2,1)S(1)} %get-tuple-element.50), channel_id=1, source_target_pairs={{0,7},{1,0},{2,1},{3,2},{4,3},{5,4},{6,5},{7,6},{8,15},{9,8},{10,9... | collective-permute-start | bytes 417800 | tf_op jit(solution)/shard_map/ppermute | solution.py:522
  29.7 6.9 %collective-permute-start.2 = (bf16[32,2176]{1,0:T(8,128)(2,1)S(1)}, bf16[32,2176]{1,0:T(8,128)(2,1)S(1)}, u32[]{:S(2)}, u32[]{:S(2)}) collective-permute-start(bf16[32,2176]{1,0:T(8,128)(2,1)S(1)} %get-tuple-element.51), channel_id=1, source_target_pairs={{0,4},{1,5},{2,6},{3,7},{4,0},{5,1},{6,2},{7,3},{8,12},{9,13},{10,... | collective-permute-start | bytes 417800 | tf_op jit(solution)/shard_map/ppermute | solution.py:522
  36.7 1.9 %collective-permute-start.3 = (bf16[32,2176]{1,0:T(8,128)(2,1)S(1)}, bf16[32,2176]{1,0:T(8,128)(2,1)S(1)}, u32[]{:S(2)}, u32[]{:S(2)}) collective-permute-start(bf16[32,2176]{1,0:T(8,128)(2,1)S(1)} %get-tuple-element.52), channel_id=1, source_target_pairs={{0,5},{1,6},{2,7},{3,0},{4,1},{5,2},{6,3},{7,4},{8,13},{9,14},{10,... | collective-permute-start | bytes 417800 | tf_op jit(solution)/shard_map/ppermute | solution.py:522
  38.6 5.2 %collective-permute-start.4 = (bf16[32,2176]{1,0:T(8,128)(2,1)S(1)}, bf16[32,2176]{1,0:T(8,128)(2,1)S(1)}, u32[]{:S(2)}, u32[]{:S(2)}) collective-permute-start(bf16[32,2176]{1,0:T(8,128)(2,1)S(1)} %get-tuple-element.53), channel_id=1, source_target_pairs={{0,3},{1,4},{2,5},{3,6},{4,7},{5,0},{6,1},{7,2},{8,11},{9,12},{10,... | collective-permute-start | bytes 417800 | tf_op jit(solution)/shard_map/ppermute | solution.py:522
  43.8 0.0 collective-permute-done.refs_1_
  43.8 2.0 %collective-permute-start.5 = (bf16[32,2176]{1,0:T(8,128)(2,1)S(1)}, bf16[32,2176]{1,0:T(8,128)(2,1)S(1)}, u32[]{:S(2)}, u32[]{:S(2)}) collective-permute-start(bf16[32,2176]{1,0:T(8,128)(2,1)S(1)} %get-tuple-element.54), channel_id=1, source_target_pairs={{0,6},{1,7},{2,0},{3,1},{4,2},{5,3},{6,4},{7,5},{8,14},{9,15},{10,... | collective-permute-start | bytes 417800 | tf_op jit(solution)/shard_map/ppermute | solution.py:522
  45.7 0.0 collective-permute-done.1.refs_2_
  45.7 0.0 copy-start.2
  45.7 0.0 copy-start.3
  45.8 4.4 %collective-permute-start.6 = (bf16[32,2176]{1,0:T(8,128)(2,1)S(1)}, bf16[32,2176]{1,0:T(8,128)(2,1)S(1)}, u32[]{:S(2)}, u32[]{:S(2)}) collective-permute-start(bf16[32,2176]{1,0:T(8,128)(2,1)S(1)} %get-tuple-element.55), channel_id=1, source_target_pairs={{0,2},{1,3},{2,4},{3,5},{4,6},{5,7},{6,0},{7,1},{8,10},{9,11},{10,... | collective-permute-start | bytes 417800 | tf_op jit(solution)/shard_map/ppermute | solution.py:522
  50.1 0.0 collective-permute-done.2.refs_3_
  50.1 1.4 collective-permute-done.3.refs_4_
  51.6 1.6 collective-permute-done.4.refs_5_
  53.2 4.9 %collective-permute-done.5.refs_6_ = bf16[32,2176]{1,0:T(8,128)(2,1)S(1)} collective-permute-done((bf16[32,2176]{1,0:T(8,128)(2,1)S(1)}, bf16[32,2176]{1,0:T(8,128)(2,1)S(1)}, u32[]{:S(2)}, u32[]{:S(2)}) %collective-permute-start.5) | collective-permute-done | bytes 139296 | tf_op jit(solution)/shard_map/ppermute | solution.py:522
  58.1 0.0 collective-permute-done.6.refs_7_
  58.1 0.2 shard_map.124
  58.3 4.7 %collective-permute-start.7 = (bf16[64,2176]{1,0:T(8,128)(2,1)S(1)}, bf16[64,2176]{1,0:T(8,128)(2,1)S(1)}, u32[]{:S(2)}, u32[]{:S(2)}) collective-permute-start(bf16[64,2176]{1,0:T(8,128)(2,1)S(1)} %get-tuple-element.57), channel_id=1, source_target_pairs={{0,16},{1,17},{2,18},{3,19},{4,20},{5,21},{6,22},{7,23},{8,24},{9,... | collective-permute-start | bytes 835592 | tf_op jit(solution)/shard_map/ppermute | solution.py:532
  62.9 2.2 %collective-permute-start.8 = (bf16[64,2176]{1,0:T(8,128)(2,1)S(1)}, bf16[64,2176]{1,0:T(8,128)(2,1)S(1)}, u32[]{:S(2)}, u32[]{:S(2)}) collective-permute-start(bf16[64,2176]{1,0:T(8,128)(2,1)S(1)} %get-tuple-element.58), channel_id=1, source_target_pairs={{0,8},{1,9},{2,10},{3,11},{4,12},{5,13},{6,14},{7,15},{8,16},{9,17... | collective-permute-start | bytes 835592 | tf_op jit(solution)/shard_map/ppermute | solution.py:532
  65.2 4.3 %collective-permute-start.9 = (bf16[64,2176]{1,0:T(8,128)(2,1)S(1)}, bf16[64,2176]{1,0:T(8,128)(2,1)S(1)}, u32[]{:S(2)}, u32[]{:S(2)}) collective-permute-start(bf16[64,2176]{1,0:T(8,128)(2,1)S(1)} %get-tuple-element.59), channel_id=1, source_target_pairs={{0,24},{1,25},{2,26},{3,27},{4,28},{5,29},{6,30},{7,31},{8,0},{9,1... | collective-permute-start | bytes 835592 | tf_op jit(solution)/shard_map/ppermute | solution.py:532
  69.5 4.5 %shard_map.122 = (bf16[128,4096]{1,0:T(8,128)(2,1)S(1)}, bf16[64,128]{1,0:T(8,128)(2,1)}, f32[64,128]{1,0:T(8,128)}, f32[192,64]{1,0:T(8,128)S(1)}, f32[128,64]{1,0:T(8,128)S(1)}, /*index=5*/bf16[128,64]{1,0:T(8,128)(2,1)}) custom-call(s32[3]{0:T(128)S(1)} %pad_add_fusion.refs_0_.place_ref, bf16[64,4096]{1,0:T(8,128)(2,1)} %x_q_hbm.1, ...), custom_call_target="tpu_custom_call" | custom-call | flops 1000 | bytes 1000 | tf_op jit(solution)/shard_map/pallas_call | solution.py:487
  73.9 1.6 collective-permute-done.8.refs_2_
  75.5 0.0 collective-permute-done.9.refs_3_
  75.6 2.0 %shard_map.125 = (bf16[128,4096]{1,0:T(8,128)(2,1)}, bf16[128,128]{1,0:T(8,128)(2,1)}, bf16[64,4096]{1,0:T(8,128)(2,1)}, f32[128,128]{1,0:T(8,128)}, f32[64,128]{1,0:T(8,128)}) custom-call(bf16[64,2176]{1,0:T(8,128)(2,1)S(1)} %get-tuple-element.56.refs_0_, bf16[64,2176]{1,0:T(8,128)(2,1)S(1)} %collective-permute-done.7.refs_1_, ...), custom_call_target="tpu_custom_call" | custom-call | flops 1000 | bytes 1000 | tf_op jit(solution)/shard_map/pallas_call | solution.py:487
  77.5 1.6 all-to-all-done
  79.2 2.8 %shard_map.126 = (bf16[192,128]{1,0:T(8,128)(2,1)}, bf16[320,64]{1,0:T(8,128)(2,1)}, f32[384,1]{1,0:T(8,128)}, f32[192,64]{1,0:T(8,128)}) custom-call(bf16[192,4224]{1,0:T(8,128)(2,1)S(1)} %bitcast.14, bf16[128,4096]{1,0:T(8,128)(2,1)S(1)} %get-tuple-element.45.refs_4_.refs_1_.pair_ref, f32[128,128]{1,0:T(8,128)} %get-tuple-element.60.refs_2_.other_both_hbm, ...), custom_call_target="tpu_custom_call" | custom-call | flops 200000000 | bytes 3000000 | tf_op jit(solution)/shard_map/pallas_call | solution.py:487
  81.9 9.0 %all-to-all-start.1 = ((bf16[24,8,128]{2,1,0:T(8,128)(2,1)}), bf16[24,8,128]{2,1,0:T(8,128)(2,1)S(1)}, u32[]{:S(2)}, u32[]{:S(2)}) async-start(bf16[24,8,128]{2,1,0:T(8,128)(2,1)} %bitcast.10), calls=%async_computation.1 | async-start | bytes 98304 | tf_op jit(solution)/shard_map/all_to_all | solution.py:502
  90.9 5.0 %shard_map.127 = (f32[32,32,128]{2,1,0:T(8,128)}, bf16[32,32,128]{2,1,0:T(8,128)(2,1)}, f32[64,4096]{1,0:T(8,128)}, f32[64,128]{1,0:T(8,128)}) custom-call(s32[3]{0:T(128)S(1)} %pad_add_fusion.refs_0_.place_ref, bf16[192,4224]{1,0:T(8,128)(2,1)S(1)} %bitcast.15, bf16[128,4096]{1,0:T(8,128)(2,1)S(1)} %get-tuple-element.45.refs_4_.refs_1_.pair_ref, ...), custom_call_target="tpu_custom_call" | custom-call | flops 900000000 | bytes 9000000 | tf_op jit(solution)/shard_map/pallas_call | solution.py:487
  95.9 5.4 %all-to-all-done.1 = bf16[24,8,128]{2,1,0:T(8,128)(2,1)S(1)} async-done(((bf16[24,8,128]{2,1,0:T(8,128)(2,1)}), bf16[24,8,128]{2,1,0:T(8,128)(2,1)S(1)}, u32[]{:S(2)}, u32[]{:S(2)}) %all-to-all-start.1) | async-done | bytes 49184 | tf_op jit(solution)/shard_map/all_to_all | solution.py:502
  101.3 2.1 %shard_map.128 = (f32[32,64,128]{2,1,0:T(8,128)S(1)}, bf16[32,64,128]{2,1,0:T(8,128)(2,1)S(1)}, f32[8,128]{1,0:T(8,128)S(1)}) custom-call(s32[3]{0:T(128)S(1)} %pad_add_fusion.refs_0_.place_ref, bf16[192,128]{1,0:T(8,128)(2,1)S(1)} %bitcast.16, bf16[192,64]{1,0:T(8,128)(2,1)S(1)} %get-tuple-element.65.refs_2_, f32[64,128]{1,0:T(8,128)} %get-tuple-element.75.refs_3_, ...), custom_call_target="tpu_custom_call" | custom-call | flops 100000000 | bytes 3000000 | tf_op jit(solution)/shard_map/pallas_call | solution.py:487
  103.4 2.3 %collective-permute-start.10 = (bf16[32,64,128]{2,1,0:T(8,128)(2,1)S(1)}, bf16[32,64,128]{2,1,0:T(8,128)(2,1)S(1)}, u32[]{:S(2)}, u32[]{:S(2)}) collective-permute-start(bf16[32,64,128]{2,1,0:T(8,128)(2,1)S(1)} %get-tuple-element.80), channel_id=1, source_target_pairs={{0,32},{32,0},{64,96},{96,64},{128,160},{160,128},{192,224},{224,1... | collective-permute-start | bytes 1572872 | tf_op jit(solution)/shard_map/ppermute | solution.py:704
  105.7 1.5 collective-permute-done.10.got_ref
  107.2 0.1 shard_map.129
  107.3 23.2 %all_to_all.25.in_ref = bf16[32,64,128]{2,1,0:T(8,128)(2,1)S(1)} all-to-all(bf16[32,64,128]{2,1,0:T(8,128)(2,1)S(1)} %shard_map.129), channel_id=1, replica_groups={{0,3,6,1,4,7,2,5,8,11,14,9,12,15,10,13,16,19,22,17,20,23,18,21,24,27,30..., dimensions={0} | all-to-all | bytes 1048576 | tf_op jit(solution)/shard_map/all_to_all | solution.py:502
  130.5 0.1 shard_map.130
  130.6 15.3 %all_to_all.26.in_ref = bf16[12,64,128]{2,1,0:T(8,128)(2,1)S(1)} all-to-all(bf16[12,64,128]{2,1,0:T(8,128)(2,1)S(1)} %shard_map.130), channel_id=1, replica_groups={{0,320,640,192,512,64,384,704,256,576,128,448},{32,352,672,224,544,96,4..., dimensions={0} | all-to-all | bytes 393216 | tf_op jit(solution)/shard_map/all_to_all | solution.py:502
  145.9 0.1 shard_map.131
  146.0 19.7 %all_to_all.27.refs_1_ = bf16[32,72,128]{2,1,0:T(8,128)(2,1)S(1)} all-to-all(bf16[32,72,128]{2,1,0:T(8,128)(2,1)S(1)} %shard_map.131), channel_id=1, replica_groups={{0,3,6,1,4,7,2,5,8,11,14,9,12,15,10,13,16,19,22,17,20,23,18,21,24,27,30..., dimensions={0} | all-to-all | bytes 1179648 | tf_op jit(solution)/shard_map/all_to_all | solution.py:502
  165.7 8.7 %collective-permute-start.11 = (bf16[32,72,128]{2,1,0:T(8,128)(2,1)S(1)}, bf16[32,72,128]{2,1,0:T(8,128)(2,1)S(1)}, u32[]{:S(2)}, u32[]{:S(2)}) collective-permute-start(bf16[32,72,128]{2,1,0:T(8,128)(2,1)S(1)} %all_to_all.27.refs_1_), channel_id=1, source_target_pairs={{0,32},{32,0},{64,96},{96,64},{128,160},{160,128},{192,224},{224,1... | collective-permute-start | bytes 1769480 | tf_op jit(solution)/shard_map/ppermute | solution.py:716
  174.5 1.6 collective-permute-done.11.refs_2_
  176.1 1.9 %shard_map.132 = (f32[64,4096]{1,0:T(8,128)}, f32[64,4096]{1,0:T(8,128)}, f32[1,1]{1,0:T(1,128)}) custom-call(s32[3]{0:T(128)S(1)} %pad_add_fusion.refs_0_.place_ref, bf16[32,72,128]{2,1,0:T(8,128)(2,1)S(1)} %all_to_all.27.refs_1_, bf16[32,72,128]{2,1,0:T(8,128)(2,1)S(1)} %collective-permute-done.11.refs_2_), custom_call_target="tpu_custom_call" | custom-call | bytes 3500000 | tf_op jit(solution)/shard_map/pallas_call | solution.py:487
  (6 shorter events, 0.0 us)
Async XLA Ops:
  4.4 17.0 %copy-start.1 = (bf16[64,4096]{1,0:T(8,128)(2,1)}, bf16[64,4096]{1,0:T(8,128)(2,1)S(1)}, u32[]{:S(2)}) copy-start(bf16[64,4096]{1,0:T(8,128)(2,1)S(1)} %get-tuple-element.46.refs_2_.refs_5_) | copy-start | bytes 1572868
  4.4 17.0 %copy-start = (bf16[64,4096]{1,0:T(8,128)(2,1)S(1)}, bf16[64,4096]{1,0:T(8,128)(2,1)}, u32[]{:S(2)}) copy-start(bf16[64,4096]{1,0:T(8,128)(2,1)} %refs_4_.3) | copy-start | bytes 1572868
  4.4 17.0 %copy-start.4 = (s32[32,2]{0,1:T(2,128)S(1)}, s32[32,2]{0,1:T(2,128)}, u32[]{:S(2)}) copy-start(s32[32,2]{0,1:T(2,128)} %param.19) | copy-start | bytes 772
  4.4 74.7 %all-to-all-start = ((bf16[24,8,4224]{2,1,0:T(8,128)(2,1)}), bf16[24,8,4224]{2,1,0:T(8,128)(2,1)S(1)}, u32[]{:S(2)}, u32[]{:S(2)}) async-start(bf16[24,8,4224]{2,1,0:T(8,128)(2,1)} %bitcast.22), calls=%async_computation | async-start | bytes 3244032 | tf_op jit(solution)/shard_map/all_to_all | solution.py:502
  22.7 21.1 %collective-permute-start = (bf16[32,2176]{1,0:T(8,128)(2,1)S(1)}, bf16[32,2176]{1,0:T(8,128)(2,1)S(1)}, u32[]{:S(2)}, u32[]{:S(2)}) collective-permute-start(bf16[32,2176]{1,0:T(8,128)(2,1)S(1)} %get-tuple-element.49), channel_id=1, source_target_pairs={{0,1},{1,2},{2,3},{3,4},{4,5},{5,6},{6,7},{7,0},{8,9},{9,10},{10,1... | collective-permute-start | bytes 417800 | tf_op jit(solution)/shard_map/ppermute | solution.py:522
  25.9 19.8 %collective-permute-start.1 = (bf16[32,2176]{1,0:T(8,128)(2,1)S(1)}, bf16[32,2176]{1,0:T(8,128)(2,1)S(1)}, u32[]{:S(2)}, u32[]{:S(2)}) collective-permute-start(bf16[32,2176]{1,0:T(8,128)(2,1)S(1)} %get-tuple-element.50), channel_id=1, source_target_pairs={{0,7},{1,0},{2,1},{3,2},{4,3},{5,4},{6,5},{7,6},{8,15},{9,8},{10,9... | collective-permute-start | bytes 417800 | tf_op jit(solution)/shard_map/ppermute | solution.py:522
  29.7 20.4 %collective-permute-start.2 = (bf16[32,2176]{1,0:T(8,128)(2,1)S(1)}, bf16[32,2176]{1,0:T(8,128)(2,1)S(1)}, u32[]{:S(2)}, u32[]{:S(2)}) collective-permute-start(bf16[32,2176]{1,0:T(8,128)(2,1)S(1)} %get-tuple-element.51), channel_id=1, source_target_pairs={{0,4},{1,5},{2,6},{3,7},{4,0},{5,1},{6,2},{7,3},{8,12},{9,13},{10,... | collective-permute-start | bytes 417800 | tf_op jit(solution)/shard_map/ppermute | solution.py:522
  36.7 14.9 %collective-permute-start.3 = (bf16[32,2176]{1,0:T(8,128)(2,1)S(1)}, bf16[32,2176]{1,0:T(8,128)(2,1)S(1)}, u32[]{:S(2)}, u32[]{:S(2)}) collective-permute-start(bf16[32,2176]{1,0:T(8,128)(2,1)S(1)} %get-tuple-element.52), channel_id=1, source_target_pairs={{0,5},{1,6},{2,7},{3,0},{4,1},{5,2},{6,3},{7,4},{8,13},{9,14},{10,... | collective-permute-start | bytes 417800 | tf_op jit(solution)/shard_map/ppermute | solution.py:522
  38.6 14.6 %collective-permute-start.4 = (bf16[32,2176]{1,0:T(8,128)(2,1)S(1)}, bf16[32,2176]{1,0:T(8,128)(2,1)S(1)}, u32[]{:S(2)}, u32[]{:S(2)}) collective-permute-start(bf16[32,2176]{1,0:T(8,128)(2,1)S(1)} %get-tuple-element.53), channel_id=1, source_target_pairs={{0,3},{1,4},{2,5},{3,6},{4,7},{5,0},{6,1},{7,2},{8,11},{9,12},{10,... | collective-permute-start | bytes 417800 | tf_op jit(solution)/shard_map/ppermute | solution.py:522
  43.8 14.4 %collective-permute-start.5 = (bf16[32,2176]{1,0:T(8,128)(2,1)S(1)}, bf16[32,2176]{1,0:T(8,128)(2,1)S(1)}, u32[]{:S(2)}, u32[]{:S(2)}) collective-permute-start(bf16[32,2176]{1,0:T(8,128)(2,1)S(1)} %get-tuple-element.54), channel_id=1, source_target_pairs={{0,6},{1,7},{2,0},{3,1},{4,2},{5,3},{6,4},{7,5},{8,14},{9,15},{10,... | collective-permute-start | bytes 417800 | tf_op jit(solution)/shard_map/ppermute | solution.py:522
  45.7 29.8 %copy-start.2 = (bf16[64,4096]{1,0:T(8,128)(2,1)S(1)}, bf16[64,4096]{1,0:T(8,128)(2,1)}, u32[]{:S(2)}) copy-start(bf16[64,4096]{1,0:T(8,128)(2,1)} %copy-done.1) | copy-start | bytes 1572868
  45.7 29.8 %copy-start.3 = (s32[64]{0:T(128)S(1)}, s32[64]{0:T(128)}, u32[]{:S(2)}) copy-start(s32[64]{0:T(128)} %param.16) | copy-start | bytes 772
  45.8 12.4 %collective-permute-start.6 = (bf16[32,2176]{1,0:T(8,128)(2,1)S(1)}, bf16[32,2176]{1,0:T(8,128)(2,1)S(1)}, u32[]{:S(2)}, u32[]{:S(2)}) collective-permute-start(bf16[32,2176]{1,0:T(8,128)(2,1)S(1)} %get-tuple-element.55), channel_id=1, source_target_pairs={{0,2},{1,3},{2,4},{3,5},{4,6},{5,7},{6,0},{7,1},{8,10},{9,11},{10,... | collective-permute-start | bytes 417800 | tf_op jit(solution)/shard_map/ppermute | solution.py:522
  58.3 15.7 %collective-permute-start.7 = (bf16[64,2176]{1,0:T(8,128)(2,1)S(1)}, bf16[64,2176]{1,0:T(8,128)(2,1)S(1)}, u32[]{:S(2)}, u32[]{:S(2)}) collective-permute-start(bf16[64,2176]{1,0:T(8,128)(2,1)S(1)} %get-tuple-element.57), channel_id=1, source_target_pairs={{0,16},{1,17},{2,18},{3,19},{4,20},{5,21},{6,22},{7,23},{8,24},{9,... | collective-permute-start | bytes 835592 | tf_op jit(solution)/shard_map/ppermute | solution.py:532
  62.9 12.6 %collective-permute-start.8 = (bf16[64,2176]{1,0:T(8,128)(2,1)S(1)}, bf16[64,2176]{1,0:T(8,128)(2,1)S(1)}, u32[]{:S(2)}, u32[]{:S(2)}) collective-permute-start(bf16[64,2176]{1,0:T(8,128)(2,1)S(1)} %get-tuple-element.58), channel_id=1, source_target_pairs={{0,8},{1,9},{2,10},{3,11},{4,12},{5,13},{6,14},{7,15},{8,16},{9,17... | collective-permute-start | bytes 835592 | tf_op jit(solution)/shard_map/ppermute | solution.py:532
  65.2 10.4 %collective-permute-start.9 = (bf16[64,2176]{1,0:T(8,128)(2,1)S(1)}, bf16[64,2176]{1,0:T(8,128)(2,1)S(1)}, u32[]{:S(2)}, u32[]{:S(2)}) collective-permute-start(bf16[64,2176]{1,0:T(8,128)(2,1)S(1)} %get-tuple-element.59), channel_id=1, source_target_pairs={{0,24},{1,25},{2,26},{3,27},{4,28},{5,29},{6,30},{7,31},{8,0},{9,1... | collective-permute-start | bytes 835592 | tf_op jit(solution)/shard_map/ppermute | solution.py:532
  81.9 19.3 %all-to-all-start.1 = ((bf16[24,8,128]{2,1,0:T(8,128)(2,1)}), bf16[24,8,128]{2,1,0:T(8,128)(2,1)S(1)}, u32[]{:S(2)}, u32[]{:S(2)}) async-start(bf16[24,8,128]{2,1,0:T(8,128)(2,1)} %bitcast.10), calls=%async_computation.1 | async-start | bytes 98304 | tf_op jit(solution)/shard_map/all_to_all | solution.py:502
  103.4 3.8 %collective-permute-start.10 = (bf16[32,64,128]{2,1,0:T(8,128)(2,1)S(1)}, bf16[32,64,128]{2,1,0:T(8,128)(2,1)S(1)}, u32[]{:S(2)}, u32[]{:S(2)}) collective-permute-start(bf16[32,64,128]{2,1,0:T(8,128)(2,1)S(1)} %get-tuple-element.80), channel_id=1, source_target_pairs={{0,32},{32,0},{64,96},{96,64},{128,160},{160,128},{192,224},{224,1... | collective-permute-start | bytes 1572872 | tf_op jit(solution)/shard_map/ppermute | solution.py:704
  165.7 10.4 %collective-permute-start.11 = (bf16[32,72,128]{2,1,0:T(8,128)(2,1)S(1)}, bf16[32,72,128]{2,1,0:T(8,128)(2,1)S(1)}, u32[]{:S(2)}, u32[]{:S(2)}) collective-permute-start(bf16[32,72,128]{2,1,0:T(8,128)(2,1)S(1)} %all_to_all.27.refs_1_), channel_id=1, source_target_pairs={{0,32},{32,0},{64,96},{96,64},{128,160},{160,128},{192,224},{224,1... | collective-permute-start | bytes 1769480 | tf_op jit(solution)/shard_map/ppermute | solution.py:716
